TPU v7x, 32 devices: a whole 2x2x4 slice. The times are simulated.
32 devices in a mesh: src: 4 (over x, core), tgt: 8 (over z, y).
Axes of the slice: x: 2, y: 2, z: 4, core: 2. Of those that a mesh axis runs over, the one named last changes fastest.
Arguments:
- source_fields: float32 [7, 131072], P(None, ('src', 'tgt'))
- slot_source: int32 [524288], P(('src', 'tgt')), may hold values from 0 to 4095
- slot_weight: float32 [524288], P(('src', 'tgt')), may hold values from 0.05 to 1
- slot_target: int32 [524288], P(('src', 'tgt')), may hold values from -1 to 8191, as said below
- cell_mass: float32 [16, 128, 128], P('src', 'tgt'), may hold values from 0.5 to 2
- send_order: int32 [32, 8192], P(('src', 'tgt')), may hold values from 0 to 8191, each once within a row
- place_order: int32 [32, 8192], P(('src', 'tgt')), may hold values from 0 to 8191, each once within a row
Outputs:
- projected: float32 [7, 16, 128, 128], P(None, 'src', 'tgt')
- moduli: float32 [3, 262144], P(None, ('src', 'tgt'))
Inputs may be any that keep to these rules, and one draw needn't show every extreme that they name: `slot_target`: within each sending partition's block of 512 slots at an owner, the live slots come first and there are 128 or more of them; some owner has all 512 slots live from every sender.
All inputs are finite; a program needn't handle non-finite values.
Results may differ from a plain program's by a relative error of at most 0.00007.
Values sent between devices are 32-bit elements; how exact they have to be, the bound alone decides.
No kernel may reach another device: no remote copies, remote signals or barrier semaphores. Data moves between devices by JAX's collectives and lax.ppermute only.
A program may use at most 64 MiB of HBM per device.

v0:
```python
import math

import jax
import jax.numpy as jnp
from jax import lax
from jax.sharding import PartitionSpec as P

ITERS = 4


def padded_2(x, sides, width):
    for axis, dim in sides:
        count, length = (lax.axis_size(axis), x.shape[dim])
        up = [(i, (i + 1) % count) for i in range(count - 1)]
        down = [(j, i) for i, j in up]
        last = lax.slice_in_dim(x, length - width, length, axis=dim)
        first = lax.slice_in_dim(x, 0, width, axis=dim)
        before = lax.ppermute(last, axis, up)
        after = lax.ppermute(first, axis, down)
        x = jnp.concatenate([before, x, after], axis=dim)
    return x


def cell_moduli(vals):
    phi = vals[0]
    mean = (vals[1] + vals[2] + vals[3]) / 3.0
    q2 = 1.5 * (
        (vals[1] - mean) ** 2
        + (vals[2] - mean) ** 2
        + (vals[3] - mean) ** 2
        + 2.0 * (vals[4] ** 2 + vals[5] ** 2 + vals[6] ** 2)
    )
    bulk = 1.6 * jnp.exp(-3.0 * phi) * (1.0 + 0.25 * jnp.tanh(mean))
    shear = 0.9 * jnp.exp(-2.0 * phi) / (1.0 + q2 / 0.5)
    soften = shear * q2 / (0.5 + q2)
    return jnp.stack([bulk, shear, soften])


def lookup_columns(table, index):
    rows, width = table.shape
    groups = width // 32
    folded = table.reshape(rows, groups, 32).transpose(0, 2, 1).reshape(rows * 32, groups)
    count = index.shape[0]
    block = math.gcd(count, 4096)
    group_ids = jnp.arange(groups, dtype=jnp.int32)
    lane_ids = jnp.arange(32, dtype=jnp.int32)

    def one_block(piece):
        onehot = (piece[None, :] // 32 == group_ids[:, None]).astype(jnp.float32)
        picked = jnp.dot(
            folded, onehot, precision=lax.Precision.HIGHEST, preferred_element_type=jnp.float32
        ).reshape(rows, 32, piece.shape[0])
        lanes = (piece[None, :] % 32 == lane_ids[:, None]).astype(jnp.float32)
        return jnp.sum(picked * lanes[None], axis=1)

    pieces = lax.map(one_block, index.reshape(count // block, block))
    return pieces.transpose(1, 0, 2).reshape(rows, count)


def spread_columns(values, index, width):
    rows, count = values.shape
    groups = width // 32
    block = math.gcd(count, 4096)
    blocks = count // block
    group_ids = jnp.arange(groups, dtype=jnp.int32)
    lane_ids = jnp.arange(32, dtype=jnp.int32)
    value_blocks = values.reshape(rows, blocks, block).transpose(1, 0, 2)
    index_blocks = index.reshape(blocks, block)

    def add_block(total, inputs):
        vals, piece = inputs
        onehot = (piece[:, None] // 32 == group_ids[None, :]).astype(jnp.float32)
        lanes = (piece[:, None] % 32 == lane_ids[None, :]).astype(jnp.float32)
        spread = (vals.T[:, :, None] * lanes[:, None, :]).reshape(block, rows * 32)
        added = lax.dot_general(
            onehot,
            spread,
            (((0,), (0,)), ((), ())),
            precision=lax.Precision.HIGHEST,
            preferred_element_type=jnp.float32,
        )
        return (total + added, None)

    start = jnp.zeros((groups, rows * 32), jnp.float32)
    total, _ = lax.scan(add_block, start, (value_blocks, index_blocks))
    return total.reshape(groups, rows, 32).transpose(1, 0, 2).reshape(rows, width)


def mass_apply(field, root):
    w = root[None] * field
    padded = padded_2(w, (("src", 1), ("tgt", 2)), 1)
    deep = jnp.pad(w, ((0, 0), (0, 0), (0, 0), (1, 1)))
    nb = padded[:, 2:, 1:-1] + padded[:, :-2, 1:-1]
    nb = nb + padded[:, 1:-1, 2:] + padded[:, 1:-1, :-2]
    nb = nb + deep[:, :, :, 2:] + deep[:, :, :, :-2]
    return root[None] * (w + 0.125 * nb)


def on_device(
    source_fields, slot_source, slot_weight, slot_target, cell_mass, send_order, place_order
):
    n_src = lax.axis_size("src")
    n_tgt = lax.axis_size("tgt")
    owners = n_src * n_tgt
    per_owner = slot_source.shape[0] // owners
    hx_cells, hy_cells, hz_cells = cell_mass.shape
    cells = hx_cells * hy_cells * hz_cells
    quota = cells // owners
    values = slot_weight[None, :] * lookup_columns(source_fields, slot_source)
    values = values.reshape(7, owners, per_owner)
    arrived = lax.all_to_all(values, ("src", "tgt"), split_axis=1, concat_axis=1, tiled=True)
    arrived = arrived.reshape(7, owners * per_owner)
    rhs = spread_columns(arrived, slot_target, cells)
    rhs = rhs.reshape(7, hx_cells, hy_cells, hz_cells)
    root = jnp.sqrt(cell_mass)
    theta = 1.0
    delta = 0.75
    sigma = theta / delta
    rho = 1.0 / sigma
    solution = jnp.zeros_like(rhs)
    resid = rhs
    direction = resid / (theta * cell_mass[None])
    for sweep in range(ITERS):
        image = mass_apply(direction, root)
        solution = solution + direction
        resid = resid - image
        rho_new = 1.0 / (2.0 * sigma - rho)
        direction = rho_new * rho * direction + 2.0 * rho_new / delta * resid / cell_mass[None]
        rho = rho_new
    projected = solution + direction
    flat = projected.reshape(7, cells)
    payload = cell_moduli(flat)
    rows = payload.shape[0]
    outgoing = lookup_columns(payload, send_order[0])
    incoming = lax.all_to_all(
        outgoing.reshape(rows, owners, quota),
        ("src", "tgt"),
        split_axis=1,
        concat_axis=1,
        tiled=True,
    )
    placed = lookup_columns(incoming.reshape(rows, cells), place_order[0])
    return (projected, placed)


def solution(mesh):
    placed = (
        P(None, ("src", "tgt")),
        P(("src", "tgt")),
        P(("src", "tgt")),
        P(("src", "tgt")),
        P("src", "tgt", None),
        P(("src", "tgt"), None),
        P(("src", "tgt"), None),
    )
    return jax.shard_map(
        on_device,
        mesh=mesh,
        in_specs=placed,
        out_specs=(P(None, "src", "tgt", None), P(None, ("src", "tgt"))),
        check_vma=False,
    )
```

profile of v0, /device:TPU:0, one launch (start us, length us, event | category | flops | bytes accessed | tf_op | source)
XLA Modules:
  0.0 159.0 jit_solution(8292236593482730444)
XLA Ops:
  2.8 9.7 %while.52 = (s32[]{:T(128)}, f32[4,7,4096]{2,1,0:T(8,128)S(1)}, s32[4,4096]{1,0:T(4,128)S(1)}, f32[224,128]{1,0:T(8,128)S(1)}, s32[]{:T(128)}) while((s32[]{:T(128)}, f32[4,7,4096]{2,1,0:T(8,128)S(1)}, s32[4,4096]{1,0:T(4,128)S(1)}, f32[224,128]{1,0:T(8,128)S(1)}, s32[]{:T(128)}) %tuple.153), condition=%wide.region_2.3_spmd.clone, body=%wide.region_0.2_spmd.clone.sunk | while | flops 1411973120 | bytes 9011273 | solution.py:56
  2.9 1.6 %fusion.99 = f32[4096,224]{0,1:T(8,128)S(1)} fusion(f32[224,128]{1,0:T(8,128)S(1)} %get-tuple-element.595, s32[4096]{0:T(1024)S(1)} %bitcast.111), kind=kOutput, calls=%fused_computation.10.clone.1 | convolution fusion | flops 1409810432 | bytes 3801088 | tf_op jit(solution)/shard_map/while/body/eval_jaxpr/dot_general | solution.py:50
  5.4 1.6 %fusion.99 = f32[4096,224]{0,1:T(8,128)S(1)} fusion(f32[224,128]{1,0:T(8,128)S(1)} %get-tuple-element.595, s32[4096]{0:T(1024)S(1)} %bitcast.111), kind=kOutput, calls=%fused_computation.10.clone.1 | convolution fusion | flops 1409810432 | bytes 3801088 | tf_op jit(solution)/shard_map/while/body/eval_jaxpr/dot_general | solution.py:50
  7.8 1.6 %fusion.99 = f32[4096,224]{0,1:T(8,128)S(1)} fusion(f32[224,128]{1,0:T(8,128)S(1)} %get-tuple-element.595, s32[4096]{0:T(1024)S(1)} %bitcast.111), kind=kOutput, calls=%fused_computation.10.clone.1 | convolution fusion | flops 1409810432 | bytes 3801088 | tf_op jit(solution)/shard_map/while/body/eval_jaxpr/dot_general | solution.py:50
  10.2 1.6 %fusion.99 = f32[4096,224]{0,1:T(8,128)S(1)} fusion(f32[224,128]{1,0:T(8,128)S(1)} %get-tuple-element.595, s32[4096]{0:T(1024)S(1)} %bitcast.111), kind=kOutput, calls=%fused_computation.10.clone.1 | convolution fusion | flops 1409810432 | bytes 3801088 | tf_op jit(solution)/shard_map/while/body/eval_jaxpr/dot_general | solution.py:50
  14.3 7.3 %all-to-all-start = ((f32[7,32,512]{2,0,1:T(8,128)}), f32[7,32,512]{2,0,1:T(8,128)S(1)}, u32[]{:S(2)}, u32[]{:S(2)}) async-start(f32[7,32,512]{2,0,1:T(8,128)} %copy.42), calls=%async_computation | async-start | bytes 1048576 | tf_op jit(solution)/shard_map/all_to_all | solution.py:111
  21.7 16.3 %all-to-all-done = f32[7,32,512]{2,0,1:T(8,128)S(1)} async-done(((f32[7,32,512]{2,0,1:T(8,128)}), f32[7,32,512]{2,0,1:T(8,128)S(1)}, u32[]{:S(2)}, u32[]{:S(2)}) %all-to-all-start) | async-done | bytes 458784 | tf_op jit(solution)/shard_map/all_to_all | solution.py:111
  38.5 28.1 %while.55 = (s32[]{:T(128)}, f32[256,224]{0,1:T(8,128)S(1)}, s32[4,4096]{1,0:T(4,128)S(1)}, f32[4,7,4096]{2,0,1:T(4,128)S(1)}, s32[]{:T(128)}, /*index=5*/s32[]{:T(128)}) while((s32[]{:T(128)}, f32[256,224]{0,1:T(8,128)S(1)}, s32[4,4096]{1,0:T(4,128)S(1)}, f32[4,7,4096]{2,0,1:T(4,128)S(1)}, s32[]{:T(128)}, ...), condition=%wide.region_4.5_spmd.clone, body=%wide.region_3.4_spmd.clone.sunk | while | flops 2820993024 | bytes 9535575 | solution.py:85
  38.9 2.2 %broadcast_multiply_fusion.6 = f32[4096,7,32]{0,2,1:T(8,128)} fusion(f32[4096,32]{0,1:T(8,128)S(1)} %fusion.108, f32[4096,7]{0,1:T(8,128)S(1)} %bitcast.103), kind=kLoop, calls=%fused_computation.47.clone.1 | loop fusion | flops 917504 | bytes 4308992 | tf_op jit(solution)/shard_map/while/body/eval_jaxpr/mul | solution.py:74
  41.1 4.5 %fusion.109 = f32[256,224]{0,1:T(8,128)S(1)} fusion(f32[4096,224]{0,1:T(8,128)} %bitcast.99, s32[4096]{0:T(1024)S(1)} %get-tuple-element.581, f32[256,224]{0,1:T(8,128)S(1)} %get-tuple-element.604, pred[]{:T(512)S(6)} %compare.42), kind=kOutput, calls=%fused_computation.48.clone.1 | convolution fusion | flops 2819735552 | bytes 4145153 | tf_op jit(solution)/shard_map/while/body/eval_jaxpr/dot_general | solution.py:75
  45.9 2.2 %broadcast_multiply_fusion.6 = f32[4096,7,32]{0,2,1:T(8,128)} fusion(f32[4096,32]{0,1:T(8,128)S(1)} %fusion.108, f32[4096,7]{0,1:T(8,128)S(1)} %bitcast.103), kind=kLoop, calls=%fused_computation.47.clone.1 | loop fusion | flops 917504 | bytes 4308992 | tf_op jit(solution)/shard_map/while/body/eval_jaxpr/mul | solution.py:74
  48.1 4.5 %fusion.109 = f32[256,224]{0,1:T(8,128)S(1)} fusion(f32[4096,224]{0,1:T(8,128)} %bitcast.99, s32[4096]{0:T(1024)S(1)} %get-tuple-element.581, f32[256,224]{0,1:T(8,128)S(1)} %get-tuple-element.604, pred[]{:T(512)S(6)} %compare.42), kind=kOutput, calls=%fused_computation.48.clone.1 | convolution fusion | flops 2819735552 | bytes 4145153 | tf_op jit(solution)/shard_map/while/body/eval_jaxpr/dot_general | solution.py:75
  52.9 2.2 %broadcast_multiply_fusion.6 = f32[4096,7,32]{0,2,1:T(8,128)} fusion(f32[4096,32]{0,1:T(8,128)S(1)} %fusion.108, f32[4096,7]{0,1:T(8,128)S(1)} %bitcast.103), kind=kLoop, calls=%fused_computation.47.clone.1 | loop fusion | flops 917504 | bytes 4308992 | tf_op jit(solution)/shard_map/while/body/eval_jaxpr/mul | solution.py:74
  55.1 4.5 %fusion.109 = f32[256,224]{0,1:T(8,128)S(1)} fusion(f32[4096,224]{0,1:T(8,128)} %bitcast.99, s32[4096]{0:T(1024)S(1)} %get-tuple-element.581, f32[256,224]{0,1:T(8,128)S(1)} %get-tuple-element.604, pred[]{:T(512)S(6)} %compare.42), kind=kOutput, calls=%fused_computation.48.clone.1 | convolution fusion | flops 2819735552 | bytes 4145153 | tf_op jit(solution)/shard_map/while/body/eval_jaxpr/dot_general | solution.py:75
  60.0 2.2 %broadcast_multiply_fusion.6 = f32[4096,7,32]{0,2,1:T(8,128)} fusion(f32[4096,32]{0,1:T(8,128)S(1)} %fusion.108, f32[4096,7]{0,1:T(8,128)S(1)} %bitcast.103), kind=kLoop, calls=%fused_computation.47.clone.1 | loop fusion | flops 917504 | bytes 4308992 | tf_op jit(solution)/shard_map/while/body/eval_jaxpr/mul | solution.py:74
  62.2 4.5 %fusion.109 = f32[256,224]{0,1:T(8,128)S(1)} fusion(f32[4096,224]{0,1:T(8,128)} %bitcast.99, s32[4096]{0:T(1024)S(1)} %get-tuple-element.581, f32[256,224]{0,1:T(8,128)S(1)} %get-tuple-element.604, pred[]{:T(512)S(6)} %compare.42), kind=kOutput, calls=%fused_computation.48.clone.1 | convolution fusion | flops 2819735552 | bytes 4145153 | tf_op jit(solution)/shard_map/while/body/eval_jaxpr/dot_general | solution.py:75
  68.6 3.0 %collective-permute-start.1 = (f32[7,1,16,128]{3,2,1,0:T(8,128)S(1)}, f32[7,1,16,128]{3,2,1,0:T(8,128)S(1)}, u32[]{:S(2)}, u32[]{:S(2)}) collective-permute-start(f32[7,1,16,128]{3,2,1,0:T(8,128)S(1)} %get-tuple-element.463), channel_id=1, source_target_pairs={{0,8},{8,16},{16,24},{1,9},{9,17},{17,25},{2,10},{10,18},{18,26},{... | collective-permute-start | bytes 172040 | tf_op jit(solution)/shard_map/ppermute | solution.py:18
  73.9 4.5 %collective-permute-start.3 = (f32[7,6,1,128]{3,2,1,0:T(1,128)S(1)}, f32[7,6,1,128]{3,2,1,0:T(1,128)S(1)}, u32[]{:S(2)}, u32[]{:S(2)}) collective-permute-start(f32[7,6,1,128]{3,2,1,0:T(1,128)S(1)} %get-tuple-element.450), channel_id=1, source_target_pairs={{0,1},{1,2},{2,3},{3,4},{4,5},{5,6},{6,7},{8,9},{9,10},{10,11},{11... | collective-permute-start | bytes 64520 | tf_op jit(solution)/shard_map/ppermute | solution.py:18
  81.5 3.0 %collective-permute-start.5 = (f32[7,1,16,128]{3,2,1,0:T(8,128)S(1)}, f32[7,1,16,128]{3,2,1,0:T(8,128)S(1)}, u32[]{:S(2)}, u32[]{:S(2)}) collective-permute-start(f32[7,1,16,128]{3,2,1,0:T(8,128)S(1)} %get-tuple-element.461), channel_id=1, source_target_pairs={{0,8},{8,16},{16,24},{1,9},{9,17},{17,25},{2,10},{10,18},{18,26},{... | collective-permute-start | bytes 172040 | tf_op jit(solution)/shard_map/ppermute | solution.py:18
  86.7 5.0 %collective-permute-start.7 = (f32[7,6,1,128]{3,2,1,0:T(1,128)S(1)}, f32[7,6,1,128]{3,2,1,0:T(1,128)S(1)}, u32[]{:S(2)}, u32[]{:S(2)}) collective-permute-start(f32[7,6,1,128]{3,2,1,0:T(1,128)S(1)} %get-tuple-element.448), channel_id=1, source_target_pairs={{0,1},{1,2},{2,3},{3,4},{4,5},{5,6},{6,7},{8,9},{9,10},{10,11},{11... | collective-permute-start | bytes 64520 | tf_op jit(solution)/shard_map/ppermute | solution.py:18
  94.8 5.0 %collective-permute-start.9 = (f32[7,1,16,128]{3,2,1,0:T(8,128)S(1)}, f32[7,1,16,128]{3,2,1,0:T(8,128)S(1)}, u32[]{:S(2)}, u32[]{:S(2)}) collective-permute-start(f32[7,1,16,128]{3,2,1,0:T(8,128)S(1)} %get-tuple-element.459), channel_id=1, source_target_pairs={{0,8},{8,16},{16,24},{1,9},{9,17},{17,25},{2,10},{10,18},{18,26},{... | collective-permute-start | bytes 172040 | tf_op jit(solution)/shard_map/ppermute | solution.py:18
  101.9 5.6 %collective-permute-start.11 = (f32[7,6,1,128]{3,2,1,0:T(1,128)S(1)}, f32[7,6,1,128]{3,2,1,0:T(1,128)S(1)}, u32[]{:S(2)}, u32[]{:S(2)}) collective-permute-start(f32[7,6,1,128]{3,2,1,0:T(1,128)S(1)} %get-tuple-element.446), channel_id=1, source_target_pairs={{0,1},{1,2},{2,3},{3,4},{4,5},{5,6},{6,7},{8,9},{9,10},{10,11},{11... | collective-permute-start | bytes 64520 | tf_op jit(solution)/shard_map/ppermute | solution.py:18
  110.6 5.2 %collective-permute-start.13 = (f32[7,1,16,128]{3,2,1,0:T(8,128)S(1)}, f32[7,1,16,128]{3,2,1,0:T(8,128)S(1)}, u32[]{:S(2)}, u32[]{:S(2)}) collective-permute-start(f32[7,1,16,128]{3,2,1,0:T(8,128)S(1)} %get-tuple-element.457), channel_id=1, source_target_pairs={{0,8},{8,16},{16,24},{1,9},{9,17},{17,25},{2,10},{10,18},{18,26},{... | collective-permute-start | bytes 172040 | tf_op jit(solution)/shard_map/ppermute | solution.py:18
  118.0 5.9 %collective-permute-start.15 = (f32[7,6,1,128]{3,2,1,0:T(1,128)S(1)}, f32[7,6,1,128]{3,2,1,0:T(1,128)S(1)}, u32[]{:S(2)}, u32[]{:S(2)}) collective-permute-start(f32[7,6,1,128]{3,2,1,0:T(1,128)S(1)} %get-tuple-element.444), channel_id=1, source_target_pairs={{0,1},{1,2},{2,3},{3,4},{4,5},{5,6},{6,7},{8,9},{9,10},{10,11},{11... | collective-permute-start | bytes 64520 | tf_op jit(solution)/shard_map/ppermute | solution.py:18
  127.4 5.5 %while.53 = (s32[]{:T(128)}, f32[2,3,4096]{2,1,0:T(4,128)}, s32[2,4096]{1,0:T(2,128)S(1)}, f32[96,256]{1,0:T(8,128)S(1)}, s32[]{:T(128)}) while((s32[]{:T(128)}, f32[2,3,4096]{2,1,0:T(4,128)}, s32[2,4096]{1,0:T(2,128)S(1)}, f32[96,256]{1,0:T(8,128)S(1)}, s32[]{:T(128)}) %tuple.154), condition=%wide.region_7.8_spmd.clone, body=%wide.region_5.7_spmd.clone.sunk | while | flops 1210138624 | bytes 4588101 | solution.py:56
  127.6 1.6 %fusion.102 = f32[4096,96]{0,1:T(8,128)S(1)} fusion(f32[96,256]{1,0:T(8,128)S(1)} %get-tuple-element.628, s32[4096]{0:T(1024)S(1)} %bitcast.112), kind=kOutput, calls=%fused_computation.21.clone.1 | convolution fusion | flops 1209008128 | bytes 1687552 | tf_op jit(solution)/shard_map/while/body/eval_jaxpr/dot_general | solution.py:50
  130.3 1.6 %fusion.102 = f32[4096,96]{0,1:T(8,128)S(1)} fusion(f32[96,256]{1,0:T(8,128)S(1)} %get-tuple-element.628, s32[4096]{0:T(1024)S(1)} %bitcast.112), kind=kOutput, calls=%fused_computation.21.clone.1 | convolution fusion | flops 1209008128 | bytes 1687552 | tf_op jit(solution)/shard_map/while/body/eval_jaxpr/dot_general | solution.py:50
  132.9 13.0 %all-to-all-start.1 = ((f32[3,32,256]{2,0,1:T(4,128)}), f32[3,32,256]{2,0,1:T(4,128)S(1)}, u32[]{:S(2)}, u32[]{:S(2)}) async-start(f32[3,32,256]{2,0,1:T(4,128)} %bitcast.9), calls=%async_computation.1 | async-start | bytes 262144 | tf_op jit(solution)/shard_map/all_to_all | solution.py:135
  146.7 7.0 %all-to-all-done.1 = f32[3,32,256]{2,0,1:T(4,128)S(1)} async-done(((f32[3,32,256]{2,0,1:T(4,128)}), f32[3,32,256]{2,0,1:T(4,128)S(1)}, u32[]{:S(2)}, u32[]{:S(2)}) %all-to-all-start.1) | async-done | bytes 98336 | tf_op jit(solution)/shard_map/all_to_all | solution.py:135
  154.0 4.3 %while.54 = (s32[]{:T(128)}, f32[2,3,4096]{2,1,0:T(4,128)S(1)}, s32[2,4096]{1,0:T(2,128)S(1)}, f32[96,256]{1,0:T(8,128)S(1)}, s32[]{:T(128)}) while((s32[]{:T(128)}, f32[2,3,4096]{2,1,0:T(4,128)S(1)}, s32[2,4096]{1,0:T(2,128)S(1)}, f32[96,256]{1,0:T(8,128)S(1)}, s32[]{:T(128)}) %tuple.155), condition=%wide.region_10.11_spmd.clone, body=%wide.region_8.10_spmd.clone.sunk | while | flops 1210138624 | bytes 4603977 | solution.py:56
  154.2 1.6 %fusion.105 = f32[4096,96]{0,1:T(8,128)S(1)} fusion(f32[96,256]{1,0:T(8,128)S(1)} %get-tuple-element.643, s32[4096]{0:T(1024)S(1)} %bitcast.113), kind=kOutput, calls=%fused_computation.33.clone.1 | convolution fusion | flops 1209008128 | bytes 1687552 | tf_op jit(solution)/shard_map/while/body/eval_jaxpr/dot_general | solution.py:50
  156.3 1.6 %fusion.105 = f32[4096,96]{0,1:T(8,128)S(1)} fusion(f32[96,256]{1,0:T(8,128)S(1)} %get-tuple-element.643, s32[4096]{0:T(1024)S(1)} %bitcast.113), kind=kOutput, calls=%fused_computation.33.clone.1 | convolution fusion | flops 1209008128 | bytes 1687552 | tf_op jit(solution)/shard_map/while/body/eval_jaxpr/dot_general | solution.py:50
  (153 shorter events, 36.3 us)
Async XLA Ops:
  2.7 10.4 %copy-start.3 = (f32[16384]{0:T(1024)S(1)}, f32[16384]{0:T(1024)}, u32[]{:S(2)}) copy-start(f32[16384]{0:T(1024)} %param.17) | copy-start | bytes 196612
  12.5 9.1 %copy-start.4 = (s32[16384]{0:T(1024)S(1)}, s32[16384]{0:T(1024)}, u32[]{:S(2)}) copy-start(s32[16384]{0:T(1024)} %param.18) | copy-start | bytes 196612
  12.5 9.1 %copy-start = (f32[4,16,128]{2,1,0:T(8,128)S(1)}, f32[4,16,128]{2,1,0:T(8,128)}, u32[]{:S(2)}) copy-start(f32[4,16,128]{2,1,0:T(8,128)} %param.19) | copy-start | bytes 98308
  14.3 23.7 %all-to-all-start = ((f32[7,32,512]{2,0,1:T(8,128)}), f32[7,32,512]{2,0,1:T(8,128)S(1)}, u32[]{:S(2)}, u32[]{:S(2)}) async-start(f32[7,32,512]{2,0,1:T(8,128)} %copy.42), calls=%async_computation | async-start | bytes 1048576 | tf_op jit(solution)/shard_map/all_to_all | solution.py:111
  67.3 57.3 %copy-start.5 = (s32[1,8192]{1,0:T(1,128)S(1)}, s32[1,8192]{1,0:T(1,128)}, u32[]{:S(2)}) copy-start(s32[1,8192]{1,0:T(1,128)} %param.20) | copy-start | bytes 98308
  67.3 4.3 %collective-permute-start = (f32[7,1,16,128]{3,2,1,0:T(8,128)S(1)}, f32[7,1,16,128]{3,2,1,0:T(8,128)S(1)}, u32[]{:S(2)}, u32[]{:S(2)}) collective-permute-start(f32[7,1,16,128]{3,2,1,0:T(8,128)S(1)} %get-tuple-element.464), channel_id=1, source_target_pairs={{8,0},{16,8},{24,16},{9,1},{17,9},{25,17},{10,2},{18,10},{26,18},{... | collective-permute-start | bytes 172040 | tf_op jit(solution)/shard_map/ppermute | solution.py:19
  68.6 3.9 %collective-permute-start.1 = (f32[7,1,16,128]{3,2,1,0:T(8,128)S(1)}, f32[7,1,16,128]{3,2,1,0:T(8,128)S(1)}, u32[]{:S(2)}, u32[]{:S(2)}) collective-permute-start(f32[7,1,16,128]{3,2,1,0:T(8,128)S(1)} %get-tuple-element.463), channel_id=1, source_target_pairs={{0,8},{8,16},{16,24},{1,9},{9,17},{17,25},{2,10},{10,18},{18,26},{... | collective-permute-start | bytes 172040 | tf_op jit(solution)/shard_map/ppermute | solution.py:18
  72.6 5.9 %collective-permute-start.2 = (f32[7,6,1,128]{3,2,1,0:T(1,128)S(1)}, f32[7,6,1,128]{3,2,1,0:T(1,128)S(1)}, u32[]{:S(2)}, u32[]{:S(2)}) collective-permute-start(f32[7,6,1,128]{3,2,1,0:T(1,128)S(1)} %get-tuple-element.449), channel_id=1, source_target_pairs={{1,0},{2,1},{3,2},{4,3},{5,4},{6,5},{7,6},{9,8},{10,9},{11,10},{12... | collective-permute-start | bytes 64520 | tf_op jit(solution)/shard_map/ppermute | solution.py:19
  73.9 6.1 %collective-permute-start.3 = (f32[7,6,1,128]{3,2,1,0:T(1,128)S(1)}, f32[7,6,1,128]{3,2,1,0:T(1,128)S(1)}, u32[]{:S(2)}, u32[]{:S(2)}) collective-permute-start(f32[7,6,1,128]{3,2,1,0:T(1,128)S(1)} %get-tuple-element.450), channel_id=1, source_target_pairs={{0,1},{1,2},{2,3},{3,4},{4,5},{5,6},{6,7},{8,9},{9,10},{10,11},{11... | collective-permute-start | bytes 64520 | tf_op jit(solution)/shard_map/ppermute | solution.py:18
  80.2 4.3 %collective-permute-start.4 = (f32[7,1,16,128]{3,2,1,0:T(8,128)S(1)}, f32[7,1,16,128]{3,2,1,0:T(8,128)S(1)}, u32[]{:S(2)}, u32[]{:S(2)}) collective-permute-start(f32[7,1,16,128]{3,2,1,0:T(8,128)S(1)} %get-tuple-element.462), channel_id=1, source_target_pairs={{8,0},{16,8},{24,16},{9,1},{17,9},{25,17},{10,2},{18,10},{26,18},{... | collective-permute-start | bytes 172040 | tf_op jit(solution)/shard_map/ppermute | solution.py:19
  81.5 3.9 %collective-permute-start.5 = (f32[7,1,16,128]{3,2,1,0:T(8,128)S(1)}, f32[7,1,16,128]{3,2,1,0:T(8,128)S(1)}, u32[]{:S(2)}, u32[]{:S(2)}) collective-permute-start(f32[7,1,16,128]{3,2,1,0:T(8,128)S(1)} %get-tuple-element.461), channel_id=1, source_target_pairs={{0,8},{8,16},{16,24},{1,9},{9,17},{17,25},{2,10},{10,18},{18,26},{... | collective-permute-start | bytes 172040 | tf_op jit(solution)/shard_map/ppermute | solution.py:18
  85.4 6.3 %collective-permute-start.6 = (f32[7,6,1,128]{3,2,1,0:T(1,128)S(1)}, f32[7,6,1,128]{3,2,1,0:T(1,128)S(1)}, u32[]{:S(2)}, u32[]{:S(2)}) collective-permute-start(f32[7,6,1,128]{3,2,1,0:T(1,128)S(1)} %get-tuple-element.447), channel_id=1, source_target_pairs={{1,0},{2,1},{3,2},{4,3},{5,4},{6,5},{7,6},{9,8},{10,9},{11,10},{12... | collective-permute-start | bytes 64520 | tf_op jit(solution)/shard_map/ppermute | solution.py:19
  86.7 6.5 %collective-permute-start.7 = (f32[7,6,1,128]{3,2,1,0:T(1,128)S(1)}, f32[7,6,1,128]{3,2,1,0:T(1,128)S(1)}, u32[]{:S(2)}, u32[]{:S(2)}) collective-permute-start(f32[7,6,1,128]{3,2,1,0:T(1,128)S(1)} %get-tuple-element.448), channel_id=1, source_target_pairs={{0,1},{1,2},{2,3},{3,4},{4,5},{5,6},{6,7},{8,9},{9,10},{10,11},{11... | collective-permute-start | bytes 64520 | tf_op jit(solution)/shard_map/ppermute | solution.py:18
  93.5 6.3 %collective-permute-start.8 = (f32[7,1,16,128]{3,2,1,0:T(8,128)S(1)}, f32[7,1,16,128]{3,2,1,0:T(8,128)S(1)}, u32[]{:S(2)}, u32[]{:S(2)}) collective-permute-start(f32[7,1,16,128]{3,2,1,0:T(8,128)S(1)} %get-tuple-element.460), channel_id=1, source_target_pairs={{8,0},{16,8},{24,16},{9,1},{17,9},{25,17},{10,2},{18,10},{26,18},{... | collective-permute-start | bytes 172040 | tf_op jit(solution)/shard_map/ppermute | solution.py:19
  94.8 5.8 %collective-permute-start.9 = (f32[7,1,16,128]{3,2,1,0:T(8,128)S(1)}, f32[7,1,16,128]{3,2,1,0:T(8,128)S(1)}, u32[]{:S(2)}, u32[]{:S(2)}) collective-permute-start(f32[7,1,16,128]{3,2,1,0:T(8,128)S(1)} %get-tuple-element.459), channel_id=1, source_target_pairs={{0,8},{8,16},{16,24},{1,9},{9,17},{17,25},{2,10},{10,18},{18,26},{... | collective-permute-start | bytes 172040 | tf_op jit(solution)/shard_map/ppermute | solution.py:18
  100.6 6.9 %collective-permute-start.10 = (f32[7,6,1,128]{3,2,1,0:T(1,128)S(1)}, f32[7,6,1,128]{3,2,1,0:T(1,128)S(1)}, u32[]{:S(2)}, u32[]{:S(2)}) collective-permute-start(f32[7,6,1,128]{3,2,1,0:T(1,128)S(1)} %get-tuple-element.445), channel_id=1, source_target_pairs={{1,0},{2,1},{3,2},{4,3},{5,4},{6,5},{7,6},{9,8},{10,9},{11,10},{12... | collective-permute-start | bytes 64520 | tf_op jit(solution)/shard_map/ppermute | solution.py:19
  101.9 7.1 %collective-permute-start.11 = (f32[7,6,1,128]{3,2,1,0:T(1,128)S(1)}, f32[7,6,1,128]{3,2,1,0:T(1,128)S(1)}, u32[]{:S(2)}, u32[]{:S(2)}) collective-permute-start(f32[7,6,1,128]{3,2,1,0:T(1,128)S(1)} %get-tuple-element.446), channel_id=1, source_target_pairs={{0,1},{1,2},{2,3},{3,4},{4,5},{5,6},{6,7},{8,9},{9,10},{10,11},{11... | collective-permute-start | bytes 64520 | tf_op jit(solution)/shard_map/ppermute | solution.py:18
  109.3 6.6 %collective-permute-start.12 = (f32[7,1,16,128]{3,2,1,0:T(8,128)S(1)}, f32[7,1,16,128]{3,2,1,0:T(8,128)S(1)}, u32[]{:S(2)}, u32[]{:S(2)}) collective-permute-start(f32[7,1,16,128]{3,2,1,0:T(8,128)S(1)} %get-tuple-element.458), channel_id=1, source_target_pairs={{8,0},{16,8},{24,16},{9,1},{17,9},{25,17},{10,2},{18,10},{26,18},{... | collective-permute-start | bytes 172040 | tf_op jit(solution)/shard_map/ppermute | solution.py:19
  110.6 6.1 %collective-permute-start.13 = (f32[7,1,16,128]{3,2,1,0:T(8,128)S(1)}, f32[7,1,16,128]{3,2,1,0:T(8,128)S(1)}, u32[]{:S(2)}, u32[]{:S(2)}) collective-permute-start(f32[7,1,16,128]{3,2,1,0:T(8,128)S(1)} %get-tuple-element.457), channel_id=1, source_target_pairs={{0,8},{8,16},{16,24},{1,9},{9,17},{17,25},{2,10},{10,18},{18,26},{... | collective-permute-start | bytes 172040 | tf_op jit(solution)/shard_map/ppermute | solution.py:18
  116.7 8.6 %collective-permute-start.14 = (f32[7,6,1,128]{3,2,1,0:T(1,128)S(1)}, f32[7,6,1,128]{3,2,1,0:T(1,128)S(1)}, u32[]{:S(2)}, u32[]{:S(2)}) collective-permute-start(f32[7,6,1,128]{3,2,1,0:T(1,128)S(1)} %get-tuple-element.443), channel_id=1, source_target_pairs={{1,0},{2,1},{3,2},{4,3},{5,4},{6,5},{7,6},{9,8},{10,9},{11,10},{12... | collective-permute-start | bytes 64520 | tf_op jit(solution)/shard_map/ppermute | solution.py:19
  118.0 7.3 %collective-permute-start.15 = (f32[7,6,1,128]{3,2,1,0:T(1,128)S(1)}, f32[7,6,1,128]{3,2,1,0:T(1,128)S(1)}, u32[]{:S(2)}, u32[]{:S(2)}) collective-permute-start(f32[7,6,1,128]{3,2,1,0:T(1,128)S(1)} %get-tuple-element.444), channel_id=1, source_target_pairs={{0,1},{1,2},{2,3},{3,4},{4,5},{5,6},{6,7},{8,9},{9,10},{10,11},{11... | collective-permute-start | bytes 64520 | tf_op jit(solution)/shard_map/ppermute | solution.py:18
  125.6 1.8 %copy-start.1 = (f32[7,4,16,128]{3,2,1,0:T(8,128)}, f32[7,4,16,128]{3,2,1,0:T(8,128)S(1)}, u32[]{:S(2)}) copy-start(f32[7,4,16,128]{3,2,1,0:T(8,128)S(1)} %fusion.58) | copy-start | bytes 688132
  127.4 18.5 %copy-start.6 = (s32[1,8192]{1,0:T(1,128)S(1)}, s32[1,8192]{1,0:T(1,128)}, u32[]{:S(2)}) copy-start(s32[1,8192]{1,0:T(1,128)} %param.21) | copy-start | bytes 98308
  132.9 20.8 %all-to-all-start.1 = ((f32[3,32,256]{2,0,1:T(4,128)}), f32[3,32,256]{2,0,1:T(4,128)S(1)}, u32[]{:S(2)}, u32[]{:S(2)}) async-start(f32[3,32,256]{2,0,1:T(4,128)} %bitcast.9), calls=%async_computation.1 | async-start | bytes 262144 | tf_op jit(solution)/shard_map/all_to_all | solution.py:135
  158.3 0.7 copy-start.2
where the time goes:
time: 160 us; the launch traced here: 159 us
  starting transfers between devices  68 us (42%)
  waiting for transfers between devices  31.1 us (19%)
  matrix products  31 us (19%)
  other arithmetic  16.4 us (10%)
  local copies, waits for them, and re-layouts  10.5 us (7%)
    ppermute x8, starting transfers between devices, padded_2(): before = lax.ppermute(last, axis, up)  37.4 us
    dot_general x4, matrix products, add_block(): lax.dot_general(onehot, spread, (((0,), (0,)), ((), ())), precision=lax.P...  18 us
    all_to_all x1, waiting for transfers between devices, on_device(): lax.all_to_all(values, ('src', 'tgt'), split_axis=1, concat_axis=1, tiled...  16.3 us
    all_to_all x1, starting transfers between devices, on_device(): lax.all_to_all(outgoing.reshape(rows, owners, quota), ('src', 'tgt'), spl...  13 us
    dot_general x8, matrix products, one_block(): jnp.dot(folded, onehot, precision=lax.Precision.HIGHEST, preferred_elemen...  13 us
    ppermute x8, starting transfers between devices, padded_2(): after = lax.ppermute(first, axis, down)  10.3 us
    mul x4, other arithmetic, add_block(): spread = (vals.T[:, :, None] * lanes[:, None, :]).reshape(block, rows * 32)  8.81 us
    ppermute x8, waiting for transfers between devices, padded_2(): before = lax.ppermute(last, axis, up)  7.86 us
  transfers between devices with their start and end apart: 18, of which 9 were waited for; matrix products, arithmetic and copies ran while one was open for 1% of the time, Pallas kernels for 0%

commit v1 on v0

v1 whole, which is shorter than its diff:
```python
import numpy as np

import jax
import jax.numpy as jnp
from jax import lax
from jax.experimental import pallas as pl
from jax.experimental.pallas import tpu as pltpu
from jax.sharding import PartitionSpec as P

ITERS = 4
FIELDS = 7
WIDE = 256
BF16 = jnp.bfloat16
F32 = jnp.float32
NT = (((1,), (1,)), ((), ()))


def sweep_polynomial(iters, theta, delta):
    sigma = theta / delta
    rho = 1.0 / sigma
    mass = np.array([1.0, 0.125])
    poly = np.polynomial.polynomial
    resid = np.array([1.0])
    step = resid / theta
    total = np.array([0.0])
    for _ in range(iters):
        total = poly.polyadd(total, step)
        resid = poly.polysub(resid, poly.polymul(mass, step))
        rho_new = 1.0 / (2.0 * sigma - rho)
        step = poly.polyadd(rho_new * rho * step, 2.0 * rho_new / delta * resid)
        rho = rho_new
    return [float(c) for c in poly.polyadd(total, step)]


COEFS = sweep_polynomial(ITERS, 1.0, 0.75)


def halves(x):
    high = x.astype(BF16)
    return high, (x - high.astype(F32)).astype(BF16)


def log2(n):
    assert n & (n - 1) == 0
    return n.bit_length() - 1


def row_ids(rows, lanes):
    return lax.broadcasted_iota(jnp.int32, (rows, lanes), 0)


def low_onehot(low, ids):
    return jnp.where(ids == low.astype(F32).astype(BF16), jnp.ones((), BF16), jnp.zeros((), BF16))


def gather_kernel(fields_ref, index_ref, weight_ref, out_ref, table):
    owners, tiles, _, lanes = out_ref.shape
    span = tiles * lanes
    groups = fields_ref.shape[1] // WIDE
    table[...] = jnp.zeros_like(table)
    for g in range(groups):
        table[g * 8 : g * 8 + FIELDS, :] = fields_ref[:, g * WIDE : (g + 1) * WIDE]
    high, low = halves(table[...])
    both = jnp.concatenate([high, low], axis=0)
    ids = row_ids(WIDE, span).astype(F32).astype(BF16)
    rows = groups * 8

    @pl.loop(0, owners)
    def _(q):
        at = pl.multiple_of(q * span, span)
        index = index_ref[:, pl.ds(at, span)]
        weight = weight_ref[:, pl.ds(at, span)]
        onehot = low_onehot(index & (WIDE - 1), ids)
        got = jnp.dot(both, onehot, preferred_element_type=F32)
        group = jnp.broadcast_to(index >> log2(WIDE), (8, span))
        value = jnp.zeros((8, span), F32)
        for g in range(groups):
            part = got[g * 8 : (g + 1) * 8] + got[rows + g * 8 : rows + (g + 1) * 8]
            value = jnp.where(group == g, part, value)
        value = value * weight
        for t in range(tiles):
            out_ref[q, t] = value[:, t * lanes : (t + 1) * lanes]


def gather_call(fields, index, weight, owners):
    tiles = index.shape[1] // owners // 128
    return pl.pallas_call(
        gather_kernel,
        out_shape=jax.ShapeDtypeStruct((owners, tiles, 8, 128), F32),
        in_specs=[pl.BlockSpec(memory_space=pltpu.VMEM)] * 3,
        out_specs=pl.BlockSpec(memory_space=pltpu.VMEM),
        scratch_shapes=[pltpu.VMEM((fields.shape[1] // WIDE * 8, WIDE), F32)],
        compiler_params=pltpu.CompilerParams(vmem_limit_bytes=40 << 20),
    )(fields, index, weight)


def scatter_kernel(value_ref, target_ref, mass_ref, v_ref, first_ref, last_ref, total):
    owners, tiles, _, lanes = value_ref.shape
    span = tiles * lanes
    hx, hy, hz = mass_ref.shape
    groups = hx * hy * hz // WIDE
    total[...] = jnp.zeros_like(total)
    ids = row_ids(WIDE, span).astype(F32).astype(BF16)
    group_ids = row_ids(groups, span).astype(F32).astype(BF16)

    @pl.loop(0, owners)
    def _(p):
        at = pl.multiple_of(p * span, span)
        target = target_ref[:, pl.ds(at, span)]
        low = ((target >> log2(groups * hz)) << log2(hz)) + (target & (hz - 1))
        onehot = low_onehot(jnp.where(target < 0, -1, low), ids)
        group = ((target >> log2(hz)) & (groups - 1)).astype(F32).astype(BF16)
        here = group_ids == group
        value = jnp.concatenate([value_ref[p, t] for t in range(tiles)], axis=1)
        parts = []
        for half in halves(value):
            for f in range(FIELDS):
                parts.append(jnp.where(here, half[f : f + 1], jnp.zeros((), BF16)))
        spread = jnp.concatenate(parts, axis=0)
        total[...] += lax.dot_general(spread, onehot, NT, preferred_element_type=F32)

    scale = lax.rsqrt(mass_ref[...])
    half_x = hx // 2
    for f in range(FIELDS):
        s = total[f * groups : (f + 1) * groups] + total[(FIELDS + f) * groups : (FIELDS + f + 1) * groups]
        for b in range(2):
            for x in range(half_x):
                at = b * half_x + x
                v = s[x * hy : (x + 1) * hy, b * hz : (b + 1) * hz] * scale[at]
                v_ref[f, at] = v
                first_ref[f, at] = v[:ITERS]
                last_ref[f, at] = v[hy - ITERS :]


def scatter_call(values, target, mass):
    hx, hy, hz = mass.shape
    groups = hx * hy * hz // WIDE
    side = jax.ShapeDtypeStruct((FIELDS, hx, ITERS, hz), F32)
    return pl.pallas_call(
        scatter_kernel,
        out_shape=(jax.ShapeDtypeStruct((FIELDS, hx, hy, hz), F32), side, side),
        in_specs=[pl.BlockSpec(memory_space=pltpu.VMEM)] * 3,
        out_specs=(pl.BlockSpec(memory_space=pltpu.VMEM),) * 3,
        scratch_shapes=[pltpu.VMEM((2 * FIELDS * groups, WIDE), F32)],
        compiler_params=pltpu.CompilerParams(vmem_limit_bytes=40 << 20),
    )(values, target, mass)


def lookup_rows(table, index, ids, group_ids, groups, at_parts):
    group, low = at_parts(index)
    got = jnp.dot(table, low_onehot(low, ids), preferred_element_type=F32)
    here = group_ids == group
    rows = 3 * groups
    out = []
    for m in range(3):
        part = got[m * groups : (m + 1) * groups] + got[rows + m * groups : rows + (m + 1) * groups]
        out.append(jnp.sum(jnp.where(here, part, 0.0), axis=0, keepdims=True))
    return out


def cell_moduli(vals):
    phi = vals[0]
    mean = (vals[1] + vals[2] + vals[3]) / 3.0
    q2 = 1.5 * (
        (vals[1] - mean) ** 2
        + (vals[2] - mean) ** 2
        + (vals[3] - mean) ** 2
        + 2.0 * (vals[4] ** 2 + vals[5] ** 2 + vals[6] ** 2)
    )
    bulk = 1.6 * jnp.exp(-3.0 * phi) * (1.0 + 0.25 * jnp.tanh(mean))
    shear = 0.9 * jnp.exp(-2.0 * phi) / (1.0 + q2 / 0.5)
    soften = shear * q2 / (0.5 + q2)
    return [bulk, shear, soften]


def solve_kernel(
    mesh_shape, v_ref, xl_ref, xr_ref, yl_ref, yr_ref, ll_ref, lr_ref, rl_ref, rr_ref, mass_ref, order_ref,
    projected_ref, out_ref, wide,
):
    n_src, n_tgt = mesh_shape
    hx, hy, hz = mass_ref.shape
    k = ITERS
    rows = hy + 2 * k
    a, b = lax.axis_index("src"), lax.axis_index("tgt")
    wide[...] = jnp.zeros_like(wide)
    for f in range(FIELDS):
        for x in range(hx):
            wide[f, k + x, :hy] = v_ref[f, x]
            wide[f, k + x, hy : hy + k] = yr_ref[f, x]
            wide[f, k + x, hy + k :] = yl_ref[f, x]
        for x in range(k):
            wide[f, x, :hy] = xl_ref[f, hx - k + x]
            wide[f, k + hx + x, :hy] = xr_ref[f, x]
        for x in range(k - 1):
            wide[f, 1 + x, hy + k :] = ll_ref[f, x]
            wide[f, 1 + x, hy : hy + k] = lr_ref[f, x]
            wide[f, k + hx + x, hy + k :] = rl_ref[f, x]
            wide[f, k + hx + x, hy : hy + k] = rr_ref[f, x]

    def exists(flag):
        return jnp.where(flag, 1.0, 0.0).astype(F32)

    row = row_ids(rows, hz)
    lane = lax.broadcasted_iota(jnp.int32, (rows, hz), 1)
    inside = jnp.where(row < hy, 1.0, jnp.where(row < hy + k, exists(b < n_tgt - 1), exists(b > 0)))
    inside_left = inside * exists(a > 0)
    inside_right = inside * exists(a < n_src - 1)
    not_first = jnp.where(lane == 0, 0.0, 1.0)
    not_last = jnp.where(lane == hz - 1, 0.0, 1.0)
    scale = lax.rsqrt(mass_ref[...])

    @pl.loop(0, FIELDS)
    def _(f):
        base = [wide[f, x] for x in range(hx + 2 * k)]
        u = [COEFS[k] * e for e in base]
        for sweep in range(1, k + 1):
            new = list(u)
            for x in range(sweep, hx + 2 * k - sweep):
                w = u[x]
                near = u[x - 1] + u[x + 1]
                near = near + pltpu.roll(w, 1, 0) + pltpu.roll(w, rows - 1, 0)
                near = near + pltpu.roll(w, 1, 1) * not_first + pltpu.roll(w, hz - 1, 1) * not_last
                if x < k:
                    near = near * inside_left
                elif x < k + hx:
                    near = near * inside
                else:
                    near = near * inside_right
                new[x] = COEFS[k - sweep] * base[x] + near
            u = new
        for x in range(hx):
            projected_ref[f, x] = u[k + x][:hy] * scale[x]

    groups = hx * hy * hz // WIDE
    payload = cell_moduli([projected_ref[f].reshape(hx * hy, hz) for f in range(FIELDS)])
    table = jnp.concatenate([jnp.concatenate([m[:groups], m[groups:]], axis=1) for m in payload], axis=0)
    table = jnp.concatenate(halves(table), axis=0)
    ids = row_ids(WIDE, WIDE).astype(F32).astype(BF16)
    group_ids = row_ids(groups, WIDE)

    def at_parts(index):
        return (index >> log2(hz)) & (groups - 1), ((index >> log2(groups * hz)) << log2(hz)) + (index & (hz - 1))

    @pl.loop(0, out_ref.shape[0])
    def _(q):
        index = order_ref[:, pl.ds(pl.multiple_of(q * WIDE, WIDE), WIDE)]
        got = lookup_rows(table, index, ids, group_ids, groups, at_parts)
        lines = [line[:, c * 128 : (c + 1) * 128] for line in got for c in range(2)]
        out_ref[q] = jnp.concatenate(lines + [jnp.zeros((2, 128), F32)], axis=0)


def solve_call(mesh_shape, v, halos, mass, order):
    hx, hy, hz = mass.shape

    def kernel(*refs):
        solve_kernel(mesh_shape, *refs)

    return pl.pallas_call(
        kernel,
        out_shape=(
            jax.ShapeDtypeStruct((FIELDS, hx, hy, hz), F32),
            jax.ShapeDtypeStruct((order.shape[1] // WIDE, 8, 128), F32),
        ),
        in_specs=[pl.BlockSpec(memory_space=pltpu.VMEM)] * 11,
        out_specs=(pl.BlockSpec(memory_space=pltpu.VMEM),) * 2,
        scratch_shapes=[pltpu.VMEM((FIELDS, hx + 2 * ITERS, hy + 2 * ITERS, hz), F32)],
        compiler_params=pltpu.CompilerParams(vmem_limit_bytes=40 << 20),
    )(v, *halos, mass, order)


def place_kernel(arrived_ref, order_ref, out_ref, lines):
    groups = arrived_ref.shape[0]
    lines[...] = arrived_ref[...].reshape(groups * 8, 128)
    table = jnp.concatenate(
        [
            jnp.concatenate([lines[pl.ds(2 * m + c, groups, stride=8), :] for c in range(2)], axis=1)
            for m in range(3)
        ],
        axis=0,
    )
    table = jnp.concatenate(halves(table), axis=0)
    ids = row_ids(WIDE, WIDE).astype(F32).astype(BF16)
    group_ids = row_ids(groups, WIDE)

    @pl.loop(0, groups)
    def _(q):
        at = pl.ds(pl.multiple_of(q * WIDE, WIDE), WIDE)
        got = lookup_rows(
            table, order_ref[:, at], ids, group_ids, groups, lambda index: (index >> log2(WIDE), index & (WIDE - 1))
        )
        out_ref[:, at] = jnp.concatenate(got, axis=0)


def place_call(arrived, order):
    return pl.pallas_call(
        place_kernel,
        out_shape=jax.ShapeDtypeStruct((3, order.shape[1]), F32),
        in_specs=[pl.BlockSpec(memory_space=pltpu.VMEM)] * 2,
        out_specs=pl.BlockSpec(memory_space=pltpu.VMEM),
        scratch_shapes=[pltpu.VMEM((arrived.shape[0] * 8, 128), F32)],
        compiler_params=pltpu.CompilerParams(vmem_limit_bytes=40 << 20),
    )(arrived, order)


def neighbours(n_src, n_tgt, da, db):
    pairs = []
    for a in range(n_src):
        for b in range(n_tgt):
            if 0 <= a + da < n_src and 0 <= b + db < n_tgt:
                pairs.append(((a + da) * n_tgt + b + db, a * n_tgt + b))
    return pairs


def on_device(source_fields, slot_source, slot_weight, slot_target, cell_mass, send_order, place_order):
    n_src, n_tgt = lax.axis_size("src"), lax.axis_size("tgt")
    both = ("src", "tgt")
    owners = n_src * n_tgt
    cells = cell_mass.size
    quota = cells // owners

    values = gather_call(source_fields, slot_source.reshape(1, -1), slot_weight.reshape(1, -1), owners)
    values = lax.all_to_all(values, both, split_axis=0, concat_axis=0, tiled=True)
    v, first, last = scatter_call(values, slot_target.reshape(1, -1), cell_mass)

    def bring(x, da, db):
        return lax.ppermute(x, both, neighbours(n_src, n_tgt, da, db))

    hx = cell_mass.shape[0]
    halos = (
        bring(v, -1, 0),
        bring(v, 1, 0),
        bring(last, 0, -1),
        bring(first, 0, 1),
        bring(last[:, hx - ITERS + 1 :], -1, -1),
        bring(first[:, hx - ITERS + 1 :], -1, 1),
        bring(last[:, : ITERS - 1], 1, -1),
        bring(first[:, : ITERS - 1], 1, 1),
    )
    projected, outgoing = solve_call((n_src, n_tgt), v, halos, cell_mass, send_order)

    if quota == WIDE:
        incoming = lax.all_to_all(outgoing, both, split_axis=0, concat_axis=0, tiled=True)
    else:
        groups = cells // WIDE
        flat = outgoing[:, :6].reshape(groups, 3, WIDE).transpose(1, 0, 2).reshape(3, owners, quota)
        flat = lax.all_to_all(flat, both, split_axis=1, concat_axis=1, tiled=True)
        flat = flat.reshape(3, groups, WIDE).transpose(1, 0, 2).reshape(groups, 6, 128)
        incoming = jnp.pad(flat, ((0, 0), (0, 2), (0, 0)))
    return projected, place_call(incoming, place_order)


def solution(mesh):
    split = P(("src", "tgt"))
    rows = P(("src", "tgt"), None)
    return jax.shard_map(
        on_device,
        mesh=mesh,
        in_specs=(P(None, ("src", "tgt")), split, split, split, P("src", "tgt", None), rows, rows),
        out_specs=(P(None, "src", "tgt", None), P(None, ("src", "tgt"))),
        check_vma=False,
    )
```

time: 160 us -> 100 us (0.62)
  starting transfers between devices: 68 us -> 16.4 us
  blocking collectives: 0 us -> 41 us
  Pallas kernels: 0 us -> 34.7 us
  matrix products: 31 us -> 0 us
  waiting for transfers between devices: 31.1 us -> 4.09 us
  other arithmetic: 16.4 us -> 0 us
  local copies, waits for them, and re-layouts: 10.5 us -> 2.63 us
    all_to_all x0 -> x2, blocking collectives: none -> 41 us  [the longest x1 23.4 us: on_device(): lax.all_to_all(values, both, split_axis=0, concat_axis=0, tiled=True)]
    pallas_call x0 -> x4, Pallas kernels: none -> 34.7 us  [the longest x1 10.5 us: scatter_call(): pl.pallas_call(scatter_kernel, out_shape=(jax.ShapeDtypeStruct((FIELDS, h...]
    ppermute x16 -> x8, starting transfers between devices: 47.7 us -> 16.4 us  [bring(): return lax.ppermute(x, both, neighbours(n_src, n_tgt, da, db))]
    dot_general x12 -> x0, matrix products: 31 us -> none  [the longest x4 18 us: add_block(): lax.dot_general(onehot, spread, (((0,), (0,)), ((), ())), precision=lax.P...]
    all_to_all x2 -> x0, waiting for transfers between devices: 23.3 us -> none  [the longest x1 16.3 us: on_device(): lax.all_to_all(values, ('src', 'tgt'), split_axis=1, concat_axis=1, tiled...]
    all_to_all x2 -> x0, starting transfers between devices: 20.3 us -> none  [the longest x1 13 us: on_device(): lax.all_to_all(outgoing.reshape(rows, owners, quota), ('src', 'tgt'), spl...]
    mul x10 -> x0, other arithmetic: 9.59 us -> none  [the longest x4 8.81 us: add_block(): spread = (vals.T[:, :, None] * lanes[:, None, :]).reshape(block, rows * 32)]
    ppermute x16 -> x8, waiting for transfers between devices: 7.88 us -> 4.09 us  [bring(): return lax.ppermute(x, both, neighbours(n_src, n_tgt, da, db))]
  transfers between devices with their start and end apart: 18 -> 8, of which waited for: 9 -> 1; matrix products, arithmetic and copies ran while one was open for 1% -> 0% of each run, Pallas kernels for 0% -> 0%
where the time goes in v1:
time: 100 us; the launch traced here: 99.7 us
  blocking collectives  41 us (41%)
  Pallas kernels  34.7 us (35%)
  starting transfers between devices  16.4 us (16%)
  waiting for transfers between devices  4.09 us (4%)
  local copies, waits for them, and re-layouts  2.63 us (3%)
    all_to_all x1, blocking collectives, on_device(): lax.all_to_all(values, both, split_axis=0, concat_axis=0, tiled=True)  23.4 us
    all_to_all x1, blocking collectives, on_device(): lax.all_to_all(outgoing, both, split_axis=0, concat_axis=0, tiled=True)  17.5 us
    ppermute x8, starting transfers between devices, bring(): return lax.ppermute(x, both, neighbours(n_src, n_tgt, da, db))  16.4 us
    pallas_call x1, Pallas kernels, scatter_call(): pl.pallas_call(scatter_kernel, out_shape=(jax.ShapeDtypeStruct((FIELDS, h...  10.5 us
    pallas_call x1, Pallas kernels, solve_call(): pl.pallas_call(kernel, out_shape=(jax.ShapeDtypeStruct((FIELDS, hx, hy, h...  9.42 us
    pallas_call x1, Pallas kernels, gather_call(): pl.pallas_call(gather_kernel, out_shape=jax.ShapeDtypeStruct((owners, til...  7.72 us
    pallas_call x1, Pallas kernels, place_call(): pl.pallas_call(place_kernel, out_shape=jax.ShapeDtypeStruct((3, order.sha...  7.09 us
    ppermute x8, waiting for transfers between devices, bring(): return lax.ppermute(x, both, neighbours(n_src, n_tgt, da, db))  4.09 us
  transfers between devices with their start and end apart: 8, of which 1 were waited for; matrix products, arithmetic and copies ran while one was open for 0% of the time, Pallas kernels for 0%

profile of v1, /device:TPU:0, one launch (start us, length us, event | category | flops | bytes accessed | tf_op | source)
XLA Modules:
  0.0 99.7 jit_solution(17015496031946174302)
XLA Ops:
  0.6 0.0 copy-start.1
  0.6 0.9 copy-done.1
  1.5 0.8 copy-done.2
  2.4 0.8 copy-done.3
  3.2 7.7 %shard_map.86 = f32[32,4,8,128]{3,2,1,0:T(8,128)S(1)} custom-call(f32[7,4096]{1,0:T(8,128)S(1)} %copy-done.1, s32[1,16384]{1,0:T(1,128)S(1)} %bitcast.3, f32[1,16384]{1,0:T(1,128)S(1)} %bitcast.4), custom_call_target="tpu_custom_call" | custom-call | tf_op jit(solution)/shard_map/pallas_call | solution.py:87
  10.9 0.0 copy-start
  11.0 0.0 copy-start.4
  11.0 23.4 %all_to_all.10.value_ref = f32[32,4,8,128]{3,2,1,0:T(8,128)S(1)} all-to-all(f32[32,4,8,128]{3,2,1,0:T(8,128)S(1)} %shard_map.86), channel_id=1, replica_groups=mesh['src'=4,'tgt'=8] {'src','tgt'}, dimensions={0} | all-to-all | bytes 1048576 | tf_op jit(solution)/shard_map/all_to_all | solution.py:322
  34.4 0.0 copy-done
  34.4 0.0 copy-done.4
  34.4 10.5 %shard_map.87 = (f32[7,4,16,128]{3,2,1,0:T(8,128)S(1)}, f32[7,4,4,128]{3,2,1,0:T(4,128)S(1)}, f32[7,4,4,128]{3,2,1,0:T(4,128)S(1)}) custom-call(f32[32,4,8,128]{3,2,1,0:T(8,128)S(1)} %all_to_all.10.value_ref, s32[1,16384]{1,0:T(1,128)S(1)} %bitcast.5, f32[4,16,128]{2,1,0:T(8,128)S(1)} %copy-done), custom_call_target="tpu_custom_call" | custom-call | tf_op jit(solution)/shard_map/pallas_call | solution.py:139
  44.9 1.3 %collective-permute-start.1 = (f32[7,4,16,128]{3,2,1,0:T(8,128)S(1)}, f32[7,4,16,128]{3,2,1,0:T(8,128)S(1)}, u32[]{:S(2)}, u32[]{:S(2)}) collective-permute-start(f32[7,4,16,128]{3,2,1,0:T(8,128)S(1)} %get-tuple-element.7.refs_0_), channel_id=1, source_target_pairs={{8,0},{9,1},{10,2},{11,3},{12,4},{13,5},{14,6},{15,7},{16,8},{17,9... | collective-permute-start | bytes 688136 | tf_op jit(solution)/shard_map/ppermute | solution.py:326
  46.2 3.0 %collective-permute-start = (f32[7,4,16,128]{3,2,1,0:T(8,128)S(1)}, f32[7,4,16,128]{3,2,1,0:T(8,128)S(1)}, u32[]{:S(2)}, u32[]{:S(2)}) collective-permute-start(f32[7,4,16,128]{3,2,1,0:T(8,128)S(1)} %get-tuple-element.7.refs_0_), channel_id=1, source_target_pairs={{0,8},{1,9},{2,10},{3,11},{4,12},{5,13},{6,14},{7,15},{8,16},{9,17... | collective-permute-start | bytes 688136 | tf_op jit(solution)/shard_map/ppermute | solution.py:326
  49.3 0.7 collective-permute-start.6
  50.0 5.1 %collective-permute-start.4 = (f32[7,3,4,128]{3,2,1,0:T(4,128)S(1)}, f32[7,3,4,128]{3,2,1,0:T(4,128)S(1)}, u32[]{:S(2)}, u32[]{:S(2)}) collective-permute-start(f32[7,3,4,128]{3,2,1,0:T(4,128)S(1)} %get-tuple-element.15), channel_id=1, source_target_pairs={{0,9},{1,10},{2,11},{3,12},{4,13},{5,14},{6,15},{8,17},{9,18},{10,... | collective-permute-start | bytes 129032 | tf_op jit(solution)/shard_map/ppermute | solution.py:326
  55.1 0.0 copy-start.5
  55.1 1.3 %collective-permute-start.7 = (f32[7,3,4,128]{3,2,1,0:T(4,128)S(1)}, f32[7,3,4,128]{3,2,1,0:T(4,128)S(1)}, u32[]{:S(2)}, u32[]{:S(2)}) collective-permute-start(f32[7,3,4,128]{3,2,1,0:T(4,128)S(1)} %get-tuple-element.12), channel_id=1, source_target_pairs={{9,0},{10,1},{11,2},{12,3},{13,4},{14,5},{15,6},{17,8},{18,9},{19,... | collective-permute-start | bytes 129032 | tf_op jit(solution)/shard_map/ppermute | solution.py:326
  56.4 0.0 collective-permute-done.6.refs_7_
  56.4 3.1 %collective-permute-start.2 = (f32[7,4,4,128]{3,2,1,0:T(4,128)S(1)}, f32[7,4,4,128]{3,2,1,0:T(4,128)S(1)}, u32[]{:S(2)}, u32[]{:S(2)}) collective-permute-start(f32[7,4,4,128]{3,2,1,0:T(4,128)S(1)} %get-tuple-element.8), channel_id=1, source_target_pairs={{0,1},{1,2},{2,3},{3,4},{4,5},{5,6},{6,7},{8,9},{9,10},{10,11},{11... | collective-permute-start | bytes 172040 | tf_op jit(solution)/shard_map/ppermute | solution.py:326
  59.5 0.0 collective-permute-done.4.refs_5_
  59.5 1.3 %collective-permute-start.3 = (f32[7,4,4,128]{3,2,1,0:T(4,128)S(1)}, f32[7,4,4,128]{3,2,1,0:T(4,128)S(1)}, u32[]{:S(2)}, u32[]{:S(2)}) collective-permute-start(f32[7,4,4,128]{3,2,1,0:T(4,128)S(1)} %get-tuple-element.9), channel_id=1, source_target_pairs={{1,0},{2,1},{3,2},{4,3},{5,4},{6,5},{7,6},{9,8},{10,9},{11,10},{12... | collective-permute-start | bytes 172040 | tf_op jit(solution)/shard_map/ppermute | solution.py:326
  60.8 0.0 collective-permute-done.7.refs_8_
  60.8 0.7 collective-permute-start.5
  61.5 0.0 collective-permute-done.5.refs_6_
  61.5 0.0 collective-permute-done.2.refs_3_
  61.5 4.1 %collective-permute-done.3.refs_4_ = f32[7,4,4,128]{3,2,1,0:T(4,128)S(1)} collective-permute-done((f32[7,4,4,128]{3,2,1,0:T(4,128)S(1)}, f32[7,4,4,128]{3,2,1,0:T(4,128)S(1)}, u32[]{:S(2)}, u32[]{:S(2)}) %collective-permute-start.3) | collective-permute-done | bytes 57376 | tf_op jit(solution)/shard_map/ppermute | solution.py:326
  65.6 0.0 collective-permute-done.1.refs_2_
  65.6 0.0 collective-permute-done.refs_1_
  65.6 0.0 copy-done.5
  65.6 9.4 %shard_map.88 = (f32[7,4,16,128]{3,2,1,0:T(8,128)}, f32[32,8,128]{2,1,0:T(8,128)S(1)}) custom-call(f32[7,4,16,128]{3,2,1,0:T(8,128)S(1)} %get-tuple-element.7.refs_0_, f32[7,4,16,128]{3,2,1,0:T(8,128)S(1)} %collective-permute-done.refs_1_, f32[7,4,16,128]{3,2,1,0:T(8,128)S(1)} %collective-permute-done.1.refs_2_, ...), custom_call_target="tpu_custom_call" | custom-call | tf_op jit(solution)/shard_map/pallas_call | solution.py:258
  75.0 17.5 %all_to_all.11.arrived_ref = f32[32,8,128]{2,1,0:T(8,128)S(1)} all-to-all(f32[32,8,128]{2,1,0:T(8,128)S(1)} %get-tuple-element.11), channel_id=1, replica_groups=mesh['src'=4,'tgt'=8] {'src','tgt'}, dimensions={0} | all-to-all | bytes 262144 | tf_op jit(solution)/shard_map/all_to_all | solution.py:342
  92.6 7.1 %shard_map.89 = f32[3,8192]{1,0:T(4,128)} custom-call(f32[32,8,128]{2,1,0:T(8,128)S(1)} %all_to_all.11.arrived_ref, s32[1,8192]{1,0:T(1,128)S(1)} %copy-done.6), custom_call_target="tpu_custom_call" | custom-call | tf_op jit(solution)/shard_map/pallas_call | solution.py:295
  (6 shorter events, 0.0 us)
Async XLA Ops:
  0.6 0.9 copy-start.1
  1.5 0.8 copy-start.2
  2.4 0.8 copy-start.3
  10.9 23.5 %copy-start = (f32[4,16,128]{2,1,0:T(8,128)S(1)}, f32[4,16,128]{2,1,0:T(8,128)}, u32[]{:S(2)}) copy-start(f32[4,16,128]{2,1,0:T(8,128)} %refs_9_.1) | copy-start | bytes 98308
  11.0 23.5 %copy-start.4 = (s32[16384]{0:T(1024)S(1)}, s32[16384]{0:T(1024)}, u32[]{:S(2)}) copy-start(s32[16384]{0:T(1024)} %param.10) | copy-start | bytes 196612
  44.9 20.7 %collective-permute-start.1 = (f32[7,4,16,128]{3,2,1,0:T(8,128)S(1)}, f32[7,4,16,128]{3,2,1,0:T(8,128)S(1)}, u32[]{:S(2)}, u32[]{:S(2)}) collective-permute-start(f32[7,4,16,128]{3,2,1,0:T(8,128)S(1)} %get-tuple-element.7.refs_0_), channel_id=1, source_target_pairs={{8,0},{9,1},{10,2},{11,3},{12,4},{13,5},{14,6},{15,7},{16,8},{17,9... | collective-permute-start | bytes 688136 | tf_op jit(solution)/shard_map/ppermute | solution.py:326
  46.2 19.4 %collective-permute-start = (f32[7,4,16,128]{3,2,1,0:T(8,128)S(1)}, f32[7,4,16,128]{3,2,1,0:T(8,128)S(1)}, u32[]{:S(2)}, u32[]{:S(2)}) collective-permute-start(f32[7,4,16,128]{3,2,1,0:T(8,128)S(1)} %get-tuple-element.7.refs_0_), channel_id=1, source_target_pairs={{0,8},{1,9},{2,10},{3,11},{4,12},{5,13},{6,14},{7,15},{8,16},{9,17... | collective-permute-start | bytes 688136 | tf_op jit(solution)/shard_map/ppermute | solution.py:326
  49.3 7.1 %collective-permute-start.6 = (f32[7,3,4,128]{3,2,1,0:T(4,128)S(1)}, f32[7,3,4,128]{3,2,1,0:T(4,128)S(1)}, u32[]{:S(2)}, u32[]{:S(2)}) collective-permute-start(f32[7,3,4,128]{3,2,1,0:T(4,128)S(1)} %get-tuple-element.14), channel_id=1, source_target_pairs={{8,1},{9,2},{10,3},{11,4},{12,5},{13,6},{14,7},{16,9},{17,10},{18,... | collective-permute-start | bytes 129032 | tf_op jit(solution)/shard_map/ppermute | solution.py:326
  50.0 9.5 %collective-permute-start.4 = (f32[7,3,4,128]{3,2,1,0:T(4,128)S(1)}, f32[7,3,4,128]{3,2,1,0:T(4,128)S(1)}, u32[]{:S(2)}, u32[]{:S(2)}) collective-permute-start(f32[7,3,4,128]{3,2,1,0:T(4,128)S(1)} %get-tuple-element.15), channel_id=1, source_target_pairs={{0,9},{1,10},{2,11},{3,12},{4,13},{5,14},{6,15},{8,17},{9,18},{10,... | collective-permute-start | bytes 129032 | tf_op jit(solution)/shard_map/ppermute | solution.py:326
  55.1 10.5 %copy-start.5 = (s32[1,8192]{1,0:T(1,128)S(1)}, s32[1,8192]{1,0:T(1,128)}, u32[]{:S(2)}) copy-start(s32[1,8192]{1,0:T(1,128)} %refs_10_.1) | copy-start | bytes 98308
  55.1 5.7 %collective-permute-start.7 = (f32[7,3,4,128]{3,2,1,0:T(4,128)S(1)}, f32[7,3,4,128]{3,2,1,0:T(4,128)S(1)}, u32[]{:S(2)}, u32[]{:S(2)}) collective-permute-start(f32[7,3,4,128]{3,2,1,0:T(4,128)S(1)} %get-tuple-element.12), channel_id=1, source_target_pairs={{9,0},{10,1},{11,2},{12,3},{13,4},{14,5},{15,6},{17,8},{18,9},{19,... | collective-permute-start | bytes 129032 | tf_op jit(solution)/shard_map/ppermute | solution.py:326
  56.4 5.1 %collective-permute-start.2 = (f32[7,4,4,128]{3,2,1,0:T(4,128)S(1)}, f32[7,4,4,128]{3,2,1,0:T(4,128)S(1)}, u32[]{:S(2)}, u32[]{:S(2)}) collective-permute-start(f32[7,4,4,128]{3,2,1,0:T(4,128)S(1)} %get-tuple-element.8), channel_id=1, source_target_pairs={{0,1},{1,2},{2,3},{3,4},{4,5},{5,6},{6,7},{8,9},{9,10},{10,11},{11... | collective-permute-start | bytes 172040 | tf_op jit(solution)/shard_map/ppermute | solution.py:326
  59.5 6.1 %collective-permute-start.3 = (f32[7,4,4,128]{3,2,1,0:T(4,128)S(1)}, f32[7,4,4,128]{3,2,1,0:T(4,128)S(1)}, u32[]{:S(2)}, u32[]{:S(2)}) collective-permute-start(f32[7,4,4,128]{3,2,1,0:T(4,128)S(1)} %get-tuple-element.9), channel_id=1, source_target_pairs={{1,0},{2,1},{3,2},{4,3},{5,4},{6,5},{7,6},{9,8},{10,9},{11,10},{12... | collective-permute-start | bytes 172040 | tf_op jit(solution)/shard_map/ppermute | solution.py:326
  60.8 0.7 collective-permute-start.5
  75.0 17.6 %copy-start.6 = (s32[1,8192]{1,0:T(1,128)S(1)}, s32[1,8192]{1,0:T(1,128)}, u32[]{:S(2)}) copy-start(s32[1,8192]{1,0:T(1,128)} %order_ref.1) | copy-start | bytes 98308

commit v2 on v1

--- a/solution.py
+++ b/solution.py
@@ -9,6 +9,7 @@
 
 ITERS = 4
 FIELDS = 7
+TOGETHER = 4
 WIDE = 256
 BF16 = jnp.bfloat16
 F32 = jnp.float32
@@ -53,11 +54,17 @@
     return jnp.where(ids == low.astype(F32).astype(BF16), jnp.ones((), BF16), jnp.zeros((), BF16))
 
 
-def gather_kernel(fields_ref, index_ref, weight_ref, out_ref, table):
+def gather_kernel(fields_hbm, index_hbm, weight_hbm, out_ref, table, fields_ref, index_ref, weight_ref, sems):
+    pairs = ((fields_hbm, fields_ref), (index_hbm, index_ref), (weight_hbm, weight_ref))
+    copies = [pltpu.make_async_copy(src, dst, sems.at[i]) for i, (src, dst) in enumerate(pairs)]
+    for copy in copies:
+        copy.start()
     owners, tiles, _, lanes = out_ref.shape
     span = tiles * lanes
     groups = fields_ref.shape[1] // WIDE
     table[...] = jnp.zeros_like(table)
+    for copy in copies:
+        copy.wait()
     for g in range(groups):
         table[g * 8 : g * 8 + FIELDS, :] = fields_ref[:, g * WIDE : (g + 1) * WIDE]
     high, low = halves(table[...])
@@ -65,7 +72,7 @@
     ids = row_ids(WIDE, span).astype(F32).astype(BF16)
     rows = groups * 8
 
-    @pl.loop(0, owners)
+    @pl.loop(0, owners, unroll=8)
     def _(q):
         at = pl.multiple_of(q * span, span)
         index = index_ref[:, pl.ds(at, span)]
@@ -87,23 +94,29 @@
     return pl.pallas_call(
         gather_kernel,
         out_shape=jax.ShapeDtypeStruct((owners, tiles, 8, 128), F32),
-        in_specs=[pl.BlockSpec(memory_space=pltpu.VMEM)] * 3,
+        in_specs=[pl.BlockSpec(memory_space=pltpu.HBM)] * 3,
         out_specs=pl.BlockSpec(memory_space=pltpu.VMEM),
-        scratch_shapes=[pltpu.VMEM((fields.shape[1] // WIDE * 8, WIDE), F32)],
+        scratch_shapes=[
+            pltpu.VMEM((fields.shape[1] // WIDE * 8, WIDE), F32),
+            pltpu.VMEM(fields.shape, F32),
+            pltpu.VMEM(index.shape, jnp.int32),
+            pltpu.VMEM(weight.shape, F32),
+            pltpu.SemaphoreType.DMA((3,)),
+        ],
         compiler_params=pltpu.CompilerParams(vmem_limit_bytes=40 << 20),
     )(fields, index, weight)
 
 
-def scatter_kernel(value_ref, target_ref, mass_ref, v_ref, first_ref, last_ref, total):
+def scatter_kernel(value_ref, target_ref, mass_ref, v_ref, even_ref, odd_ref, total):
     owners, tiles, _, lanes = value_ref.shape
-    span = tiles * lanes
+    span = TOGETHER * tiles * lanes
     hx, hy, hz = mass_ref.shape
     groups = hx * hy * hz // WIDE
     total[...] = jnp.zeros_like(total)
     ids = row_ids(WIDE, span).astype(F32).astype(BF16)
     group_ids = row_ids(groups, span).astype(F32).astype(BF16)
 
-    @pl.loop(0, owners)
+    @pl.loop(0, owners // TOGETHER)
     def _(p):
         at = pl.multiple_of(p * span, span)
         target = target_ref[:, pl.ds(at, span)]
@@ -111,7 +124,7 @@
         onehot = low_onehot(jnp.where(target < 0, -1, low), ids)
         group = ((target >> log2(hz)) & (groups - 1)).astype(F32).astype(BF16)
         here = group_ids == group
-        value = jnp.concatenate([value_ref[p, t] for t in range(tiles)], axis=1)
+        value = jnp.concatenate([value_ref[p * TOGETHER + i, t] for i in range(TOGETHER) for t in range(tiles)], axis=1)
         parts = []
         for half in halves(value):
             for f in range(FIELDS):
@@ -121,6 +134,7 @@
 
     scale = lax.rsqrt(mass_ref[...])
     half_x = hx // 2
+    odd = lax.axis_index("tgt") % 2 == 1
     for f in range(FIELDS):
         s = total[f * groups : (f + 1) * groups] + total[(FIELDS + f) * groups : (FIELDS + f + 1) * groups]
         for b in range(2):
@@ -128,8 +142,9 @@
                 at = b * half_x + x
                 v = s[x * hy : (x + 1) * hy, b * hz : (b + 1) * hz] * scale[at]
                 v_ref[f, at] = v
-                first_ref[f, at] = v[:ITERS]
-                last_ref[f, at] = v[hy - ITERS :]
+                first, last = v[:ITERS], v[hy - ITERS :]
+                even_ref[f, at] = jnp.where(odd, first, last)
+                odd_ref[f, at] = jnp.where(odd, last, first)
 
 
 def scatter_call(values, target, mass):
@@ -173,29 +188,33 @@
     return [bulk, shear, soften]
 
 
-def solve_kernel(
-    mesh_shape, v_ref, xl_ref, xr_ref, yl_ref, yr_ref, ll_ref, lr_ref, rl_ref, rr_ref, mass_ref, order_ref,
-    projected_ref, out_ref, wide,
-):
+def widen_kernel(v_ref, even_ref, odd_ref, wide_ref):
+    hy = v_ref.shape[2]
+    odd = lax.axis_index("tgt") % 2 == 1
+    for f in range(FIELDS):
+        for x in range(v_ref.shape[1]):
+            even_side, odd_side = even_ref[f, x], odd_ref[f, x]
+            wide_ref[f, x, :hy] = v_ref[f, x]
+            wide_ref[f, x, hy : hy + ITERS] = jnp.where(odd, odd_side, even_side)
+            wide_ref[f, x, hy + ITERS :] = jnp.where(odd, even_side, odd_side)
+
+
+def widen_call(v, even, odd):
+    fields, hx, hy, hz = v.shape
+    return pl.pallas_call(
+        widen_kernel,
+        out_shape=jax.ShapeDtypeStruct((fields, hx, hy + 2 * ITERS, hz), F32),
+        in_specs=[pl.BlockSpec(memory_space=pltpu.VMEM)] * 3,
+        out_specs=pl.BlockSpec(memory_space=pltpu.VMEM),
+    )(v, even, odd)
+
+
+def solve_kernel(mesh_shape, wide_ref, even_ref, odd_ref, mass_ref, order_ref, projected_ref, out_ref):
     n_src, n_tgt = mesh_shape
     hx, hy, hz = mass_ref.shape
     k = ITERS
     rows = hy + 2 * k
     a, b = lax.axis_index("src"), lax.axis_index("tgt")
-    wide[...] = jnp.zeros_like(wide)
-    for f in range(FIELDS):
-        for x in range(hx):
-            wide[f, k + x, :hy] = v_ref[f, x]
-            wide[f, k + x, hy : hy + k] = yr_ref[f, x]
-            wide[f, k + x, hy + k :] = yl_ref[f, x]
-        for x in range(k):
-            wide[f, x, :hy] = xl_ref[f, hx - k + x]
-            wide[f, k + hx + x, :hy] = xr_ref[f, x]
-        for x in range(k - 1):
-            wide[f, 1 + x, hy + k :] = ll_ref[f, x]
-            wide[f, 1 + x, hy : hy + k] = lr_ref[f, x]
-            wide[f, k + hx + x, hy + k :] = rl_ref[f, x]
-            wide[f, k + hx + x, hy : hy + k] = rr_ref[f, x]
 
     def exists(flag):
         return jnp.where(flag, 1.0, 0.0).astype(F32)
@@ -211,7 +230,11 @@
 
     @pl.loop(0, FIELDS)
     def _(f):
-        base = [wide[f, x] for x in range(hx + 2 * k)]
+        even = [even_ref[f, x] for x in range(hx)]
+        odd = [odd_ref[f, x] for x in range(hx)]
+        left = [jnp.where(a % 2 == 1, p, q) for p, q in zip(even, odd)]
+        right = [jnp.where(a % 2 == 1, q, p) for p, q in zip(even, odd)]
+        base = left[hx - k :] + [wide_ref[f, x] for x in range(hx)] + right[:k]
         u = [COEFS[k] * e for e in base]
         for sweep in range(1, k + 1):
             new = list(u)
@@ -241,7 +264,7 @@
     def at_parts(index):
         return (index >> log2(hz)) & (groups - 1), ((index >> log2(groups * hz)) << log2(hz)) + (index & (hz - 1))
 
-    @pl.loop(0, out_ref.shape[0])
+    @pl.loop(0, out_ref.shape[0], unroll=8)
     def _(q):
         index = order_ref[:, pl.ds(pl.multiple_of(q * WIDE, WIDE), WIDE)]
         got = lookup_rows(table, index, ids, group_ids, groups, at_parts)
@@ -249,7 +272,7 @@
         out_ref[q] = jnp.concatenate(lines + [jnp.zeros((2, 128), F32)], axis=0)
 
 
-def solve_call(mesh_shape, v, halos, mass, order):
+def solve_call(mesh_shape, wide, even, odd, mass, order):
     hx, hy, hz = mass.shape
 
     def kernel(*refs):
@@ -261,11 +284,10 @@
             jax.ShapeDtypeStruct((FIELDS, hx, hy, hz), F32),
             jax.ShapeDtypeStruct((order.shape[1] // WIDE, 8, 128), F32),
         ),
-        in_specs=[pl.BlockSpec(memory_space=pltpu.VMEM)] * 11,
+        in_specs=[pl.BlockSpec(memory_space=pltpu.VMEM)] * 5,
         out_specs=(pl.BlockSpec(memory_space=pltpu.VMEM),) * 2,
-        scratch_shapes=[pltpu.VMEM((FIELDS, hx + 2 * ITERS, hy + 2 * ITERS, hz), F32)],
         compiler_params=pltpu.CompilerParams(vmem_limit_bytes=40 << 20),
-    )(v, *halos, mass, order)
+    )(wide, even, odd, mass, order)
 
 
 def place_kernel(arrived_ref, order_ref, out_ref, lines):
@@ -282,7 +304,7 @@
     ids = row_ids(WIDE, WIDE).astype(F32).astype(BF16)
     group_ids = row_ids(groups, WIDE)
 
-    @pl.loop(0, groups)
+    @pl.loop(0, groups, unroll=8)
     def _(q):
         at = pl.ds(pl.multiple_of(q * WIDE, WIDE), WIDE)
         got = lookup_rows(
@@ -302,13 +324,13 @@
     )(arrived, order)
 
 
-def neighbours(n_src, n_tgt, da, db):
-    pairs = []
-    for a in range(n_src):
-        for b in range(n_tgt):
-            if 0 <= a + da < n_src and 0 <= b + db < n_tgt:
-                pairs.append(((a + da) * n_tgt + b + db, a * n_tgt + b))
-    return pairs
+def swap(x, axis):
+    count = lax.axis_size(axis)
+    out = []
+    for start, part in enumerate(x):
+        pairs = [(i, i + 1) for i in range(start, count - 1, 2)]
+        out.append(lax.ppermute(part, axis, pairs + [(j, i) for i, j in pairs]))
+    return out
 
 
 def on_device(source_fields, slot_source, slot_weight, slot_target, cell_mass, send_order, place_order):
@@ -320,23 +342,9 @@
 
     values = gather_call(source_fields, slot_source.reshape(1, -1), slot_weight.reshape(1, -1), owners)
     values = lax.all_to_all(values, both, split_axis=0, concat_axis=0, tiled=True)
-    v, first, last = scatter_call(values, slot_target.reshape(1, -1), cell_mass)
-
-    def bring(x, da, db):
-        return lax.ppermute(x, both, neighbours(n_src, n_tgt, da, db))
-
-    hx = cell_mass.shape[0]
-    halos = (
-        bring(v, -1, 0),
-        bring(v, 1, 0),
-        bring(last, 0, -1),
-        bring(first, 0, 1),
-        bring(last[:, hx - ITERS + 1 :], -1, -1),
-        bring(first[:, hx - ITERS + 1 :], -1, 1),
-        bring(last[:, : ITERS - 1], 1, -1),
-        bring(first[:, : ITERS - 1], 1, 1),
-    )
-    projected, outgoing = solve_call((n_src, n_tgt), v, halos, cell_mass, send_order)
+    v, even, odd = scatter_call(values, slot_target.reshape(1, -1), cell_mass)
+    wide = widen_call(v, *swap((even, odd), "tgt"))
+    projected, outgoing = solve_call((n_src, n_tgt), wide, *swap((wide, wide), "src"), cell_mass, send_order)
 
     if quota == WIDE:
         incoming = lax.all_to_all(outgoing, both, split_axis=0, concat_axis=0, tiled=True)

time: 100 us -> 72.6 us (0.73)
  Pallas kernels: 34.7 us -> 17.4 us
  starting transfers between devices: 16.4 us -> 4.11 us
  local copies, waits for them, and re-layouts: 2.63 us -> 4.89 us
    ppermute x8 -> x4, starting transfers between devices: 16.4 us -> 4.11 us  [swap(): out.append(lax.ppermute(part, axis, pairs + [(j, i) for i, j in pairs]))]
    pallas_call x1, Pallas kernels: 9.42 us -> 4.5 us  [solve_call(): pl.pallas_call(kernel, out_shape=(jax.ShapeDtypeStruct((FIELDS, hx, hy, h...]
    pallas_call x1, Pallas kernels: 10.5 us -> 5.59 us  [scatter_call(): pl.pallas_call(scatter_kernel, out_shape=(jax.ShapeDtypeStruct((FIELDS, h...]
    pallas_call x1, Pallas kernels: 7.09 us -> 2.3 us  [place_call(): pl.pallas_call(place_kernel, out_shape=jax.ShapeDtypeStruct((3, order.sha...]
    pallas_call x1, Pallas kernels: 7.72 us -> 3.27 us  [gather_call(): pl.pallas_call(gather_kernel, out_shape=jax.ShapeDtypeStruct((owners, til...]
    unnamed x14 -> x22, local copies, waits for them, and re-layouts: 2.6 us -> 4.89 us
    pallas_call x0 -> x1, Pallas kernels: none -> 1.74 us  [widen_call(): pl.pallas_call(widen_kernel, out_shape=jax.ShapeDtypeStruct((fields, hx,...]
    ppermute x8 -> x4, waiting for transfers between devices: 4.09 us -> 4.17 us  [swap(): out.append(lax.ppermute(part, axis, pairs + [(j, i) for i, j in pairs]))]
  transfers between devices with their start and end apart: 8 -> 4, of which waited for: 1 -> 2; matrix products, arithmetic and copies ran while one was open for 0% -> 0% of each run, Pallas kernels for 0% -> 0%
where the time goes in v2:
time: 72.6 us; the launch traced here: 72.2 us
  blocking collectives  40.9 us (56%)
  Pallas kernels  17.4 us (24%)
  local copies, waits for them, and re-layouts  4.89 us (7%)
  waiting for transfers between devices  4.17 us (6%)
  starting transfers between devices  4.11 us (6%)
    all_to_all x1, blocking collectives, on_device(): lax.all_to_all(values, both, split_axis=0, concat_axis=0, tiled=True)  23.5 us
    all_to_all x1, blocking collectives, on_device(): lax.all_to_all(outgoing, both, split_axis=0, concat_axis=0, tiled=True)  17.5 us
    pallas_call x1, Pallas kernels, scatter_call(): pl.pallas_call(scatter_kernel, out_shape=(jax.ShapeDtypeStruct((FIELDS, h...  5.59 us
    unnamed x22, local copies, waits for them, and re-layouts  4.89 us
    pallas_call x1, Pallas kernels, solve_call(): pl.pallas_call(kernel, out_shape=(jax.ShapeDtypeStruct((FIELDS, hx, hy, h...  4.5 us
    ppermute x4, waiting for transfers between devices, swap(): out.append(lax.ppermute(part, axis, pairs + [(j, i) for i, j in pairs]))  4.17 us
    ppermute x4, starting transfers between devices, swap(): out.append(lax.ppermute(part, axis, pairs + [(j, i) for i, j in pairs]))  4.11 us
    pallas_call x1, Pallas kernels, gather_call(): pl.pallas_call(gather_kernel, out_shape=jax.ShapeDtypeStruct((owners, til...  3.27 us
  transfers between devices with their start and end apart: 4, of which 2 were waited for; matrix products, arithmetic and copies ran while one was open for 0% of the time, Pallas kernels for 0%

profile of v2, /device:TPU:0, one launch (start us, length us, event | category | flops | bytes accessed | tf_op | source)
XLA Modules:
  0.0 72.2 jit_solution(528699448611060806)
XLA Ops:
  0.6 0.0 copy-start.3
  0.6 0.9 %copy-done.3 = f32[7,4096]{1,0:T(8,128)S(1)} copy-done((f32[7,4096]{1,0:T(8,128)S(1)}, f32[7,4096]{1,0:T(8,128)}, u32[]{:S(2)}) %copy-start.3) | copy-done | bytes 114712
  1.5 0.0 copy-start.4
  1.5 0.8 %copy-done.4 = s32[16384]{0:T(1024)S(1)} copy-done((s32[16384]{0:T(1024)S(1)}, s32[16384]{0:T(1024)}, u32[]{:S(2)}) %copy-start.4) | copy-done | bytes 65560
  2.4 0.0 copy-start.5
  2.4 0.8 %copy-done.5 = f32[16384]{0:T(1024)S(1)} copy-done((f32[16384]{0:T(1024)S(1)}, f32[16384]{0:T(1024)}, u32[]{:S(2)}) %copy-start.5) | copy-done | bytes 65560
  3.2 3.3 %shard_map.86 = f32[32,4,8,128]{3,2,1,0:T(8,128)S(1)} custom-call(f32[7,4096]{1,0:T(8,128)S(1)} %copy-done.3, s32[1,16384]{1,0:T(1,128)S(1)} %bitcast.3, f32[1,16384]{1,0:T(1,128)S(1)} %bitcast.4), custom_call_target="tpu_custom_call" | custom-call | tf_op jit(solution)/shard_map/pallas_call | solution.py:94
  6.5 0.0 copy-start.2
  6.5 0.0 copy-start.6
  6.5 23.5 %all_to_all.10.value_ref = f32[32,4,8,128]{3,2,1,0:T(8,128)S(1)} all-to-all(f32[32,4,8,128]{3,2,1,0:T(8,128)S(1)} %shard_map.86), channel_id=1, replica_groups=mesh['src'=4,'tgt'=8] {'src','tgt'}, dimensions={0} | all-to-all | bytes 1048576 | tf_op jit(solution)/shard_map/all_to_all | solution.py:344
  30.0 0.0 copy-done.2
  30.0 0.0 copy-done.6
  30.0 5.6 %shard_map.87 = (f32[7,4,16,128]{3,2,1,0:T(8,128)S(1)}, f32[7,4,4,128]{3,2,1,0:T(4,128)S(1)}, f32[7,4,4,128]{3,2,1,0:T(4,128)S(1)}) custom-call(f32[32,4,8,128]{3,2,1,0:T(8,128)S(1)} %all_to_all.10.value_ref, s32[1,16384]{1,0:T(1,128)S(1)} %bitcast.5, f32[4,16,128]{2,1,0:T(8,128)S(1)} %copy-done.2), custom_call_target="tpu_custom_call" | custom-call | tf_op jit(solution)/shard_map/pallas_call | solution.py:154
  35.6 0.0 copy-start.1
  35.6 0.7 copy-done.1
  36.3 0.8 %collective-permute-start = (f32[7,4,4,128]{3,2,1,0:T(4,128)S(1)}, f32[7,4,4,128]{3,2,1,0:T(4,128)S(1)}, u32[]{:S(2)}, u32[]{:S(2)}) collective-permute-start(f32[7,4,4,128]{3,2,1,0:T(4,128)S(1)} %get-tuple-element.8), channel_id=1, source_target_pairs={{0,1},{2,3},{4,5},{6,7},{1,0},{3,2},{5,4},{7,6},{8,9},{10,11},{12,... | collective-permute-start | bytes 172040 | tf_op jit(solution)/shard_map/ppermute | solution.py:332
  37.1 0.7 collective-permute-start.1
  37.8 2.7 %collective-permute-done.even_ref = f32[7,4,4,128]{3,2,1,0:T(4,128)S(1)} collective-permute-done((f32[7,4,4,128]{3,2,1,0:T(4,128)S(1)}, f32[7,4,4,128]{3,2,1,0:T(4,128)S(1)}, u32[]{:S(2)}, u32[]{:S(2)}) %collective-permute-start) | collective-permute-done | bytes 57376 | tf_op jit(solution)/shard_map/ppermute | solution.py:332
  40.4 0.0 collective-permute-done.1.odd_ref
  40.5 0.6 copy-done.9
  41.1 0.0 copy-done.10
  41.1 1.7 %shard_map.88.refs_0_ = f32[7,4,24,128]{3,2,1,0:T(8,128)} custom-call(f32[7,4,16,128]{3,2,1,0:T(8,128)} %copy-done.1, f32[7,4,4,128]{3,2,1,0:T(4,128)} %copy-done.9, f32[7,4,4,128]{3,2,1,0:T(4,128)} %copy-done.10), custom_call_target="tpu_custom_call" | custom-call | tf_op jit(solution)/shard_map/pallas_call | solution.py:204
  42.8 0.7 collective-permute-start.3
  43.5 2.0 %collective-permute-start.2 = (f32[7,4,24,128]{3,2,1,0:T(8,128)}, f32[7,4,24,128]{3,2,1,0:T(8,128)S(1)}, u32[]{:S(2)}, u32[]{:S(2)}) collective-permute-start(f32[7,4,24,128]{3,2,1,0:T(8,128)} %shard_map.88.refs_0_), channel_id=1, source_target_pairs={{0,8},{16,24},{8,0},{24,16},{1,9},{17,25},{9,1},{25,17},{2,10},{18... | collective-permute-start | bytes 1032200 | tf_op jit(solution)/shard_map/ppermute | solution.py:332
  45.5 0.0 collective-permute-done.3.refs_2_
  45.5 1.5 %collective-permute-done.2.refs_1_ = f32[7,4,24,128]{3,2,1,0:T(8,128)S(1)} collective-permute-done((f32[7,4,24,128]{3,2,1,0:T(8,128)}, f32[7,4,24,128]{3,2,1,0:T(8,128)S(1)}, u32[]{:S(2)}, u32[]{:S(2)}) %collective-permute-start.2) | collective-permute-done | bytes 344096 | tf_op jit(solution)/shard_map/ppermute | solution.py:332
  46.9 0.0 copy-done.7
  46.9 1.0 %copy-done = f32[7,4,24,128]{3,2,1,0:T(8,128)S(1)} copy-done((f32[7,4,24,128]{3,2,1,0:T(8,128)S(1)}, f32[7,4,24,128]{3,2,1,0:T(8,128)}, u32[]{:S(2)}) %copy-start) | copy-done | bytes 344088
  47.9 4.5 %shard_map.89 = (f32[7,4,16,128]{3,2,1,0:T(8,128)}, f32[32,8,128]{2,1,0:T(8,128)S(1)}) custom-call(f32[7,4,24,128]{3,2,1,0:T(8,128)S(1)} %copy-done, f32[7,4,24,128]{3,2,1,0:T(8,128)S(1)} %collective-permute-done.2.refs_1_, f32[7,4,24,128]{3,2,1,0:T(8,128)S(1)} %collective-permute-done.3.refs_2_, f32[4,16,128]{2,1,0:T(8,128)S(1)} %copy-done.2, ...), custom_call_target="tpu_custom_call" | custom-call | tf_op jit(solution)/shard_map/pallas_call | solution.py:281
  52.4 17.5 %all_to_all.11.arrived_ref = f32[32,8,128]{2,1,0:T(8,128)S(1)} all-to-all(f32[32,8,128]{2,1,0:T(8,128)S(1)} %get-tuple-element.11), channel_id=1, replica_groups=mesh['src'=4,'tgt'=8] {'src','tgt'}, dimensions={0} | all-to-all | bytes 262144 | tf_op jit(solution)/shard_map/all_to_all | solution.py:350
  69.9 0.0 copy-done.8
  69.9 2.3 %shard_map.90 = f32[3,8192]{1,0:T(4,128)} custom-call(f32[32,8,128]{2,1,0:T(8,128)S(1)} %all_to_all.11.arrived_ref, s32[1,8192]{1,0:T(1,128)S(1)} %copy-done.8), custom_call_target="tpu_custom_call" | custom-call | tf_op jit(solution)/shard_map/pallas_call | solution.py:317
  (5 shorter events, 0.0 us)
Async XLA Ops:
  0.6 0.9 %copy-start.3 = (f32[7,4096]{1,0:T(8,128)S(1)}, f32[7,4096]{1,0:T(8,128)}, u32[]{:S(2)}) copy-start(f32[7,4096]{1,0:T(8,128)} %fields_hbm.1) | copy-start | bytes 344068
  1.5 0.8 %copy-start.4 = (s32[16384]{0:T(1024)S(1)}, s32[16384]{0:T(1024)}, u32[]{:S(2)}) copy-start(s32[16384]{0:T(1024)} %param.8) | copy-start | bytes 196612
  2.4 0.8 %copy-start.5 = (f32[16384]{0:T(1024)S(1)}, f32[16384]{0:T(1024)}, u32[]{:S(2)}) copy-start(f32[16384]{0:T(1024)} %param.9) | copy-start | bytes 196612
  6.5 23.5 %copy-start.2 = (f32[4,16,128]{2,1,0:T(8,128)S(1)}, f32[4,16,128]{2,1,0:T(8,128)}, u32[]{:S(2)}) copy-start(f32[4,16,128]{2,1,0:T(8,128)} %refs_3_.1) | copy-start | bytes 98308
  6.5 23.5 %copy-start.6 = (s32[16384]{0:T(1024)S(1)}, s32[16384]{0:T(1024)}, u32[]{:S(2)}) copy-start(s32[16384]{0:T(1024)} %param.10) | copy-start | bytes 196612
  35.6 0.7 copy-start.1
  36.3 4.2 %collective-permute-start = (f32[7,4,4,128]{3,2,1,0:T(4,128)S(1)}, f32[7,4,4,128]{3,2,1,0:T(4,128)S(1)}, u32[]{:S(2)}, u32[]{:S(2)}) collective-permute-start(f32[7,4,4,128]{3,2,1,0:T(4,128)S(1)} %get-tuple-element.8), channel_id=1, source_target_pairs={{0,1},{2,3},{4,5},{6,7},{1,0},{3,2},{5,4},{7,6},{8,9},{10,11},{12,... | collective-permute-start | bytes 172040 | tf_op jit(solution)/shard_map/ppermute | solution.py:332
  37.1 3.3 %collective-permute-start.1 = (f32[7,4,4,128]{3,2,1,0:T(4,128)S(1)}, f32[7,4,4,128]{3,2,1,0:T(4,128)S(1)}, u32[]{:S(2)}, u32[]{:S(2)}) collective-permute-start(f32[7,4,4,128]{3,2,1,0:T(4,128)S(1)} %get-tuple-element.9), channel_id=1, source_target_pairs={{1,2},{3,4},{5,6},{2,1},{4,3},{6,5},{9,10},{11,12},{13,14},{10,9},... | collective-permute-start | bytes 172040 | tf_op jit(solution)/shard_map/ppermute | solution.py:332
  40.4 0.6 copy-start.9
  40.5 0.6 copy-start.10
  41.1 5.9 %copy-start.7 = (s32[1,8192]{1,0:T(1,128)S(1)}, s32[1,8192]{1,0:T(1,128)}, u32[]{:S(2)}) copy-start(s32[1,8192]{1,0:T(1,128)} %refs_4_.1) | copy-start | bytes 98308
  42.8 2.6 %collective-permute-start.3 = (f32[7,4,24,128]{3,2,1,0:T(8,128)}, f32[7,4,24,128]{3,2,1,0:T(8,128)S(1)}, u32[]{:S(2)}, u32[]{:S(2)}) collective-permute-start(f32[7,4,24,128]{3,2,1,0:T(8,128)} %shard_map.88.refs_0_), channel_id=1, source_target_pairs={{8,16},{16,8},{9,17},{17,9},{10,18},{18,10},{11,19},{19,11},{12,20... | collective-permute-start | bytes 1032200 | tf_op jit(solution)/shard_map/ppermute | solution.py:332
  43.5 3.4 %collective-permute-start.2 = (f32[7,4,24,128]{3,2,1,0:T(8,128)}, f32[7,4,24,128]{3,2,1,0:T(8,128)S(1)}, u32[]{:S(2)}, u32[]{:S(2)}) collective-permute-start(f32[7,4,24,128]{3,2,1,0:T(8,128)} %shard_map.88.refs_0_), channel_id=1, source_target_pairs={{0,8},{16,24},{8,0},{24,16},{1,9},{17,25},{9,1},{25,17},{2,10},{18... | collective-permute-start | bytes 1032200 | tf_op jit(solution)/shard_map/ppermute | solution.py:332
  46.9 1.0 %copy-start = (f32[7,4,24,128]{3,2,1,0:T(8,128)S(1)}, f32[7,4,24,128]{3,2,1,0:T(8,128)}, u32[]{:S(2)}) copy-start(f32[7,4,24,128]{3,2,1,0:T(8,128)} %shard_map.88.refs_0_) | copy-start | bytes 1032196
  52.4 17.5 %copy-start.8 = (s32[1,8192]{1,0:T(1,128)S(1)}, s32[1,8192]{1,0:T(1,128)}, u32[]{:S(2)}) copy-start(s32[1,8192]{1,0:T(1,128)} %order_ref.1) | copy-start | bytes 98308

commit v3 on v2

--- a/solution.py
+++ b/solution.py
@@ -9,6 +9,7 @@
 
 ITERS = 4
 FIELDS = 7
+AT_ONCE = 8
 TOGETHER = 4
 WIDE = 256
 BF16 = jnp.bfloat16
@@ -54,7 +55,7 @@
     return jnp.where(ids == low.astype(F32).astype(BF16), jnp.ones((), BF16), jnp.zeros((), BF16))
 
 
-def gather_kernel(fields_hbm, index_hbm, weight_hbm, out_ref, table, fields_ref, index_ref, weight_ref, sems):
+def gather_kernel(fields_hbm, index_hbm, weight_hbm, out_hbm, table, fields_ref, index_ref, weight_ref, out_ref, sems, done):
     pairs = ((fields_hbm, fields_ref), (index_hbm, index_ref), (weight_hbm, weight_ref))
     copies = [pltpu.make_async_copy(src, dst, sems.at[i]) for i, (src, dst) in enumerate(pairs)]
     for copy in copies:
@@ -72,8 +73,7 @@
     ids = row_ids(WIDE, span).astype(F32).astype(BF16)
     rows = groups * 8
 
-    @pl.loop(0, owners, unroll=8)
-    def _(q):
+    def one_owner(q):
         at = pl.multiple_of(q * span, span)
         index = index_ref[:, pl.ds(at, span)]
         weight = weight_ref[:, pl.ds(at, span)]
@@ -88,6 +88,20 @@
         for t in range(tiles):
             out_ref[q, t] = value[:, t * lanes : (t + 1) * lanes]
 
+    def send_off(n):
+        part = pl.ds(n * AT_ONCE, AT_ONCE)
+        return pltpu.make_async_copy(out_ref.at[part], out_hbm.at[part], done.at[n])
+
+    @pl.loop(0, owners // AT_ONCE)
+    def _(n):
+        for i in range(AT_ONCE):
+            one_owner(n * AT_ONCE + i)
+        send_off(n).start()
+
+    @pl.loop(0, owners // AT_ONCE)
+    def _(n):
+        send_off(n).wait()
+
 
 def gather_call(fields, index, weight, owners):
     tiles = index.shape[1] // owners // 128
@@ -95,15 +109,17 @@
         gather_kernel,
         out_shape=jax.ShapeDtypeStruct((owners, tiles, 8, 128), F32),
         in_specs=[pl.BlockSpec(memory_space=pltpu.HBM)] * 3,
-        out_specs=pl.BlockSpec(memory_space=pltpu.VMEM),
+        out_specs=pl.BlockSpec(memory_space=pltpu.HBM),
         scratch_shapes=[
             pltpu.VMEM((fields.shape[1] // WIDE * 8, WIDE), F32),
             pltpu.VMEM(fields.shape, F32),
             pltpu.VMEM(index.shape, jnp.int32),
             pltpu.VMEM(weight.shape, F32),
+            pltpu.VMEM((owners, tiles, 8, 128), F32),
             pltpu.SemaphoreType.DMA((3,)),
+            pltpu.SemaphoreType.DMA((owners // AT_ONCE,)),
         ],
-        compiler_params=pltpu.CompilerParams(vmem_limit_bytes=40 << 20),
+        compiler_params=pltpu.CompilerParams(vmem_limit_bytes=60 << 20),
     )(fields, index, weight)
 
 
@@ -188,24 +204,42 @@
     return [bulk, shear, soften]
 
 
-def widen_kernel(v_ref, even_ref, odd_ref, wide_ref):
-    hy = v_ref.shape[2]
-    odd = lax.axis_index("tgt") % 2 == 1
+def widen_kernel(v_ref, even_ref, odd_ref, wide_ref, to_even_ref, to_odd_ref):
+    hx, hy = v_ref.shape[1], v_ref.shape[2]
+    own = hx * hy
+    b_odd = lax.axis_index("tgt") % 2 == 1
+    a_odd = lax.axis_index("src") % 2 == 1
+    line = row_ids(2 * ITERS, v_ref.shape[3])
     for f in range(FIELDS):
-        for x in range(v_ref.shape[1]):
+        sides = []
+        for x in range(hx):
             even_side, odd_side = even_ref[f, x], odd_ref[f, x]
+            right = jnp.where(b_odd, odd_side, even_side)
+            left = jnp.where(b_odd, even_side, odd_side)
+            sides.append(jnp.concatenate([right, left], axis=0))
             wide_ref[f, x, :hy] = v_ref[f, x]
-            wide_ref[f, x, hy : hy + ITERS] = jnp.where(odd, odd_side, even_side)
-            wide_ref[f, x, hy + ITERS :] = jnp.where(odd, even_side, odd_side)
+            wide_ref[f, x, hy:] = sides[x]
+            to_even_ref[f, x * hy : (x + 1) * hy] = v_ref[f, x]
+            to_odd_ref[f, x * hy : (x + 1) * hy] = v_ref[f, x]
+        extra = []
+        for first, second, third in ((sides[hx - 1], sides[hx - 2], sides[hx - 3]), (sides[0], sides[1], sides[2])):
+            far = jnp.where(line < 4, pltpu.roll(third, 2, 0), pltpu.roll(third, 6, 0))
+            extra.append((first, jnp.where((line < 2) | (line > 5), second, far)))
+        for i in range(2):
+            at = own + i * 2 * ITERS
+            to_even_ref[f, at : at + 2 * ITERS] = jnp.where(a_odd, extra[1][i], extra[0][i])
+            to_odd_ref[f, at : at + 2 * ITERS] = jnp.where(a_odd, extra[0][i], extra[1][i])
 
 
 def widen_call(v, even, odd):
     fields, hx, hy, hz = v.shape
+    payload = jax.ShapeDtypeStruct((fields, hx * hy + 4 * ITERS, hz), F32)
     return pl.pallas_call(
         widen_kernel,
-        out_shape=jax.ShapeDtypeStruct((fields, hx, hy + 2 * ITERS, hz), F32),
+        out_shape=(jax.ShapeDtypeStruct((fields, hx, hy + 2 * ITERS, hz), F32), payload, payload),
         in_specs=[pl.BlockSpec(memory_space=pltpu.VMEM)] * 3,
-        out_specs=pl.BlockSpec(memory_space=pltpu.VMEM),
+        out_specs=(pl.BlockSpec(memory_space=pltpu.VMEM),) * 3,
+        compiler_params=pltpu.CompilerParams(vmem_limit_bytes=40 << 20),
     )(v, even, odd)
 
 
@@ -228,13 +262,22 @@
     not_last = jnp.where(lane == hz - 1, 0.0, 1.0)
     scale = lax.rsqrt(mass_ref[...])
 
+    line = row_ids(2 * k, hz)
+
+    def slabs(payload, from_left):
+        first = payload[hx * hy : hx * hy + 2 * k]
+        second = payload[hx * hy + 2 * k :]
+        third = jnp.where(line < 4, pltpu.roll(second, 6, 0), pltpu.roll(second, 2, 0))
+        sides = [first, second, third] + [jnp.zeros((2 * k, hz), F32)] * (hx - 3)
+        order = reversed(sides) if from_left else sides
+        return [jnp.concatenate([payload[x * hy : (x + 1) * hy], side], axis=0) for x, side in enumerate(order)]
+
     @pl.loop(0, FIELDS)
     def _(f):
-        even = [even_ref[f, x] for x in range(hx)]
-        odd = [odd_ref[f, x] for x in range(hx)]
-        left = [jnp.where(a % 2 == 1, p, q) for p, q in zip(even, odd)]
-        right = [jnp.where(a % 2 == 1, q, p) for p, q in zip(even, odd)]
-        base = left[hx - k :] + [wide_ref[f, x] for x in range(hx)] + right[:k]
+        even, odd = even_ref[f], odd_ref[f]
+        left = slabs(jnp.where(a % 2 == 1, even, odd), True)
+        right = slabs(jnp.where(a % 2 == 1, odd, even), False)
+        base = left + [wide_ref[f, x] for x in range(hx)] + right
         u = [COEFS[k] * e for e in base]
         for sweep in range(1, k + 1):
             new = list(u)
@@ -343,8 +386,8 @@
     values = gather_call(source_fields, slot_source.reshape(1, -1), slot_weight.reshape(1, -1), owners)
     values = lax.all_to_all(values, both, split_axis=0, concat_axis=0, tiled=True)
     v, even, odd = scatter_call(values, slot_target.reshape(1, -1), cell_mass)
-    wide = widen_call(v, *swap((even, odd), "tgt"))
-    projected, outgoing = solve_call((n_src, n_tgt), wide, *swap((wide, wide), "src"), cell_mass, send_order)
+    wide, even, odd = widen_call(v, *swap((even, odd), "tgt"))
+    projected, outgoing = solve_call((n_src, n_tgt), wide, *swap((even, odd), "src"), cell_mass, send_order)
 
     if quota == WIDE:
         incoming = lax.all_to_all(outgoing, both, split_axis=0, concat_axis=0, tiled=True)

time: 72.6 us -> 67.1 us (0.924)
  local copies, waits for them, and re-layouts: 4.89 us -> 0.02 us
  blocking collectives: 40.9 us -> 43.1 us
  starting transfers between devices: 4.11 us -> 2.3 us
    unnamed x22 -> x8, local copies, waits for them, and re-layouts: 4.89 us -> 0.02 us
    all_to_all x1, blocking collectives: 17.5 us -> 19.5 us  [on_device(): lax.all_to_all(outgoing, both, split_axis=0, concat_axis=0, tiled=True)]
    ppermute x4, starting transfers between devices: 4.11 us -> 2.3 us  [swap(): out.append(lax.ppermute(part, axis, pairs + [(j, i) for i, j in pairs]))]
    pallas_call x1, Pallas kernels: 1.74 us -> 0.07 us  [widen_call(): pl.pallas_call(widen_kernel, out_shape=(jax.ShapeDtypeStruct((fields, hx,...]
    pallas_call x1, Pallas kernels: 3.27 us -> 4.57 us  [gather_call(): pl.pallas_call(gather_kernel, out_shape=jax.ShapeDtypeStruct((owners, til...]
where the time goes in v3:
time: 67.1 us; the launch traced here: 66.7 us
  blocking collectives  43.1 us (64%)
  Pallas kernels  17 us (25%)
  waiting for transfers between devices  3.56 us (5%)
  starting transfers between devices  2.3 us (3%)
  between operations  0.7 us (1%)
    all_to_all x1, blocking collectives, on_device(): lax.all_to_all(values, both, split_axis=0, concat_axis=0, tiled=True)  23.7 us
    all_to_all x1, blocking collectives, on_device(): lax.all_to_all(outgoing, both, split_axis=0, concat_axis=0, tiled=True)  19.5 us
    pallas_call x1, Pallas kernels, scatter_call(): pl.pallas_call(scatter_kernel, out_shape=(jax.ShapeDtypeStruct((FIELDS, h...  5.6 us
    pallas_call x1, Pallas kernels, gather_call(): pl.pallas_call(gather_kernel, out_shape=jax.ShapeDtypeStruct((owners, til...  4.57 us
    pallas_call x1, Pallas kernels, solve_call(): pl.pallas_call(kernel, out_shape=(jax.ShapeDtypeStruct((FIELDS, hx, hy, h...  4.49 us
    ppermute x4, waiting for transfers between devices, swap(): out.append(lax.ppermute(part, axis, pairs + [(j, i) for i, j in pairs]))  3.56 us
    ppermute x4, starting transfers between devices, swap(): out.append(lax.ppermute(part, axis, pairs + [(j, i) for i, j in pairs]))  2.3 us
    pallas_call x1, Pallas kernels, place_call(): pl.pallas_call(place_kernel, out_shape=jax.ShapeDtypeStruct((3, order.sha...  2.29 us
  transfers between devices with their start and end apart: 4, of which 2 were waited for; matrix products, arithmetic and copies ran while one was open for 0% of the time, Pallas kernels for 0%

profile of v3, /device:TPU:0, one launch (start us, length us, event | category | flops | bytes accessed | tf_op | source)
XLA Modules:
  0.0 66.7 jit_solution(6519009515233984795)
XLA Ops:
  0.6 4.6 %shard_map.86 = f32[32,4,8,128]{3,2,1,0:T(8,128)} custom-call(f32[7,4096]{1,0:T(8,128)} %fields_hbm.1, s32[1,16384]{1,0:T(1,128)} %bitcast.4, f32[1,16384]{1,0:T(1,128)} %bitcast.5), custom_call_target="tpu_custom_call" | custom-call | tf_op jit(solution)/shard_map/pallas_call | solution.py:108
  5.2 0.0 copy-start
  5.2 0.0 copy-start.1
  5.2 23.7 %all_to_all.10.value_ref = f32[32,4,8,128]{3,2,1,0:T(8,128)S(1)} all-to-all(f32[32,4,8,128]{3,2,1,0:T(8,128)} %shard_map.86), channel_id=1, replica_groups=mesh['src'=4,'tgt'=8] {'src','tgt'}, dimensions={0} | all-to-all | bytes 1048576 | tf_op jit(solution)/shard_map/all_to_all | solution.py:387
  28.9 0.0 copy-done
  28.9 0.0 copy-done.1
  28.9 5.6 %shard_map.87 = (f32[7,4,16,128]{3,2,1,0:T(8,128)S(1)}, f32[7,4,4,128]{3,2,1,0:T(4,128)S(1)}, f32[7,4,4,128]{3,2,1,0:T(4,128)S(1)}) custom-call(f32[32,4,8,128]{3,2,1,0:T(8,128)S(1)} %all_to_all.10.value_ref, s32[1,16384]{1,0:T(1,128)S(1)} %bitcast.3, f32[4,16,128]{2,1,0:T(8,128)S(1)} %copy-done), custom_call_target="tpu_custom_call" | custom-call | tf_op jit(solution)/shard_map/pallas_call | solution.py:170
  34.5 0.9 %collective-permute-start = (f32[7,4,4,128]{3,2,1,0:T(4,128)S(1)}, f32[7,4,4,128]{3,2,1,0:T(4,128)S(1)}, u32[]{:S(2)}, u32[]{:S(2)}) collective-permute-start(f32[7,4,4,128]{3,2,1,0:T(4,128)S(1)} %get-tuple-element.11), channel_id=1, source_target_pairs={{0,1},{2,3},{4,5},{6,7},{1,0},{3,2},{5,4},{7,6},{8,9},{10,11},{12,... | collective-permute-start | bytes 172040 | tf_op jit(solution)/shard_map/ppermute | solution.py:375
  35.4 0.7 collective-permute-start.1
  36.1 2.7 %collective-permute-done.even_ref = f32[7,4,4,128]{3,2,1,0:T(4,128)S(1)} collective-permute-done((f32[7,4,4,128]{3,2,1,0:T(4,128)S(1)}, f32[7,4,4,128]{3,2,1,0:T(4,128)S(1)}, u32[]{:S(2)}, u32[]{:S(2)}) %collective-permute-start) | collective-permute-done | bytes 57376 | tf_op jit(solution)/shard_map/ppermute | solution.py:375
  38.8 0.0 collective-permute-done.1.odd_ref
  38.8 0.0 copy-start.2
  38.8 0.1 shard_map.88
  38.8 0.1 collective-permute-start.2
  38.9 0.7 %collective-permute-start.3 = (f32[7,80,128]{2,1,0:T(8,128)S(1)}, f32[7,80,128]{2,1,0:T(8,128)S(1)}, u32[]{:S(2)}, u32[]{:S(2)}) collective-permute-start(f32[7,80,128]{2,1,0:T(8,128)S(1)} %get-tuple-element.15), channel_id=1, source_target_pairs={{8,16},{16,8},{9,17},{17,9},{10,18},{18,10},{11,19},{19,11},{12,20... | collective-permute-start | bytes 860168 | tf_op jit(solution)/shard_map/ppermute | solution.py:375
  39.6 0.9 %collective-permute-done.2.refs_1_ = f32[7,80,128]{2,1,0:T(8,128)S(1)} collective-permute-done((f32[7,80,128]{2,1,0:T(8,128)S(1)}, f32[7,80,128]{2,1,0:T(8,128)S(1)}, u32[]{:S(2)}, u32[]{:S(2)}) %collective-permute-start.2) | collective-permute-done | bytes 286752 | tf_op jit(solution)/shard_map/ppermute | solution.py:375
  40.5 0.0 collective-permute-done.3.refs_2_
  40.5 0.0 copy-done.2
  40.5 4.5 %shard_map.89 = (f32[7,4,16,128]{3,2,1,0:T(8,128)}, f32[32,8,128]{2,1,0:T(8,128)S(1)}) custom-call(f32[7,4,24,128]{3,2,1,0:T(8,128)S(1)} %get-tuple-element.13.refs_0_, f32[7,80,128]{2,1,0:T(8,128)S(1)} %collective-permute-done.2.refs_1_, f32[7,80,128]{2,1,0:T(8,128)S(1)} %collective-permute-done.3.refs_2_, f32[4,16,128]{2,1,0:T(8,128)S(1)} %copy-done, ...), custom_call_target="tpu_custom_call" | custom-call | tf_op jit(solution)/shard_map/pallas_call | solution.py:324
  45.0 0.0 copy-start.3
  45.0 19.5 %all_to_all.11.arrived_ref = f32[32,8,128]{2,1,0:T(8,128)S(1)} all-to-all(f32[32,8,128]{2,1,0:T(8,128)S(1)} %get-tuple-element.17), channel_id=1, replica_groups=mesh['src'=4,'tgt'=8] {'src','tgt'}, dimensions={0} | all-to-all | bytes 262144 | tf_op jit(solution)/shard_map/all_to_all | solution.py:393
  64.4 0.0 copy-done.3
  64.4 2.3 %shard_map.90 = f32[3,8192]{1,0:T(4,128)} custom-call(f32[32,8,128]{2,1,0:T(8,128)S(1)} %all_to_all.11.arrived_ref, s32[1,8192]{1,0:T(1,128)S(1)} %copy-done.3), custom_call_target="tpu_custom_call" | custom-call | tf_op jit(solution)/shard_map/pallas_call | solution.py:360
Async XLA Ops:
  5.2 23.7 %copy-start = (f32[4,16,128]{2,1,0:T(8,128)S(1)}, f32[4,16,128]{2,1,0:T(8,128)}, u32[]{:S(2)}) copy-start(f32[4,16,128]{2,1,0:T(8,128)} %refs_3_.1) | copy-start | bytes 98308
  5.2 23.7 %copy-start.1 = (s32[16384]{0:T(1024)S(1)}, s32[16384]{0:T(1024)}, u32[]{:S(2)}) copy-start(s32[16384]{0:T(1024)} %param.10) | copy-start | bytes 196612
  34.5 4.2 %collective-permute-start = (f32[7,4,4,128]{3,2,1,0:T(4,128)S(1)}, f32[7,4,4,128]{3,2,1,0:T(4,128)S(1)}, u32[]{:S(2)}, u32[]{:S(2)}) collective-permute-start(f32[7,4,4,128]{3,2,1,0:T(4,128)S(1)} %get-tuple-element.11), channel_id=1, source_target_pairs={{0,1},{2,3},{4,5},{6,7},{1,0},{3,2},{5,4},{7,6},{8,9},{10,11},{12,... | collective-permute-start | bytes 172040 | tf_op jit(solution)/shard_map/ppermute | solution.py:375
  35.4 3.3 %collective-permute-start.1 = (f32[7,4,4,128]{3,2,1,0:T(4,128)S(1)}, f32[7,4,4,128]{3,2,1,0:T(4,128)S(1)}, u32[]{:S(2)}, u32[]{:S(2)}) collective-permute-start(f32[7,4,4,128]{3,2,1,0:T(4,128)S(1)} %get-tuple-element.12), channel_id=1, source_target_pairs={{1,2},{3,4},{5,6},{2,1},{4,3},{6,5},{9,10},{11,12},{13,14},{10,9},... | collective-permute-start | bytes 172040 | tf_op jit(solution)/shard_map/ppermute | solution.py:375
  38.8 1.7 %copy-start.2 = (s32[1,8192]{1,0:T(1,128)S(1)}, s32[1,8192]{1,0:T(1,128)}, u32[]{:S(2)}) copy-start(s32[1,8192]{1,0:T(1,128)} %refs_4_.1) | copy-start | bytes 98308
  38.8 1.6 %collective-permute-start.2 = (f32[7,80,128]{2,1,0:T(8,128)S(1)}, f32[7,80,128]{2,1,0:T(8,128)S(1)}, u32[]{:S(2)}, u32[]{:S(2)}) collective-permute-start(f32[7,80,128]{2,1,0:T(8,128)S(1)} %get-tuple-element.14), channel_id=1, source_target_pairs={{0,8},{16,24},{8,0},{24,16},{1,9},{17,25},{9,1},{25,17},{2,10},{18... | collective-permute-start | bytes 860168 | tf_op jit(solution)/shard_map/ppermute | solution.py:375
  38.9 1.6 %collective-permute-start.3 = (f32[7,80,128]{2,1,0:T(8,128)S(1)}, f32[7,80,128]{2,1,0:T(8,128)S(1)}, u32[]{:S(2)}, u32[]{:S(2)}) collective-permute-start(f32[7,80,128]{2,1,0:T(8,128)S(1)} %get-tuple-element.15), channel_id=1, source_target_pairs={{8,16},{16,8},{9,17},{17,9},{10,18},{18,10},{11,19},{19,11},{12,20... | collective-permute-start | bytes 860168 | tf_op jit(solution)/shard_map/ppermute | solution.py:375
  45.0 19.5 %copy-start.3 = (s32[1,8192]{1,0:T(1,128)S(1)}, s32[1,8192]{1,0:T(1,128)}, u32[]{:S(2)}) copy-start(s32[1,8192]{1,0:T(1,128)} %order_ref.1) | copy-start | bytes 98308

commit v4 on v3

--- a/solution.py
+++ b/solution.py
@@ -123,7 +123,7 @@
     )(fields, index, weight)
 
 
-def scatter_kernel(value_ref, target_ref, mass_ref, v_ref, even_ref, odd_ref, total):
+def scatter_kernel(value_ref, target_ref, mass_ref, v_ref, odd_ref, total):
     owners, tiles, _, lanes = value_ref.shape
     span = TOGETHER * tiles * lanes
     hx, hy, hz = mass_ref.shape
@@ -158,9 +158,7 @@
                 at = b * half_x + x
                 v = s[x * hy : (x + 1) * hy, b * hz : (b + 1) * hz] * scale[at]
                 v_ref[f, at] = v
-                first, last = v[:ITERS], v[hy - ITERS :]
-                even_ref[f, at] = jnp.where(odd, first, last)
-                odd_ref[f, at] = jnp.where(odd, last, first)
+                odd_ref[f, at] = jnp.where(odd, v[hy - ITERS :], v[:ITERS])
 
 
 def scatter_call(values, target, mass):
@@ -169,9 +167,9 @@
     side = jax.ShapeDtypeStruct((FIELDS, hx, ITERS, hz), F32)
     return pl.pallas_call(
         scatter_kernel,
-        out_shape=(jax.ShapeDtypeStruct((FIELDS, hx, hy, hz), F32), side, side),
+        out_shape=(jax.ShapeDtypeStruct((FIELDS, hx, hy, hz), F32), side),
         in_specs=[pl.BlockSpec(memory_space=pltpu.VMEM)] * 3,
-        out_specs=(pl.BlockSpec(memory_space=pltpu.VMEM),) * 3,
+        out_specs=(pl.BlockSpec(memory_space=pltpu.VMEM),) * 2,
         scratch_shapes=[pltpu.VMEM((2 * FIELDS * groups, WIDE), F32)],
         compiler_params=pltpu.CompilerParams(vmem_limit_bytes=40 << 20),
     )(values, target, mass)
@@ -204,12 +202,36 @@
     return [bulk, shear, soften]
 
 
-def widen_kernel(v_ref, even_ref, odd_ref, wide_ref, to_even_ref, to_odd_ref):
-    hx, hy = v_ref.shape[1], v_ref.shape[2]
-    own = hx * hy
+def strips_kernel(v_ref, even_ref):
+    odd = lax.axis_index("tgt") % 2 == 1
+    hy = v_ref.shape[2]
+    for f in range(FIELDS):
+        for x in range(v_ref.shape[1]):
+            even_ref[f, x] = jnp.where(odd, v_ref[f, x, :ITERS], v_ref[f, x, hy - ITERS :])
+
+
+def strips_call(v):
+    fields, hx, _, hz = v.shape
+    return pl.pallas_call(
+        strips_kernel,
+        out_shape=jax.ShapeDtypeStruct((fields, hx, ITERS, hz), F32),
+        in_specs=[pl.BlockSpec(memory_space=pltpu.VMEM)],
+        out_specs=pl.BlockSpec(memory_space=pltpu.VMEM),
+        compiler_params=pltpu.CompilerParams(vmem_limit_bytes=4 << 20),
+    )(v)
+
+
+def corners(sides):
+    line = row_ids(2 * ITERS, sides[0].shape[1])
+    far = jnp.where(line < 4, pltpu.roll(sides[2], 2, 0), pltpu.roll(sides[2], 6, 0))
+    return sides[0], jnp.where((line < 2) | (line > 5), sides[1], far)
+
+
+def sides_kernel(even_ref, odd_ref, block_ref, sides_ref, to_odd_ref):
+    del block_ref
     b_odd = lax.axis_index("tgt") % 2 == 1
     a_odd = lax.axis_index("src") % 2 == 1
-    line = row_ids(2 * ITERS, v_ref.shape[3])
+    hx = even_ref.shape[1]
     for f in range(FIELDS):
         sides = []
         for x in range(hx):
@@ -217,33 +239,51 @@
             right = jnp.where(b_odd, odd_side, even_side)
             left = jnp.where(b_odd, even_side, odd_side)
             sides.append(jnp.concatenate([right, left], axis=0))
-            wide_ref[f, x, :hy] = v_ref[f, x]
-            wide_ref[f, x, hy:] = sides[x]
+            sides_ref[f, x] = sides[x]
+        for i, (first, last) in enumerate(zip(corners(sides), corners(sides[::-1]))):
+            to_odd_ref[f, i * 2 * ITERS : (i + 1) * 2 * ITERS] = jnp.where(a_odd, last, first)
+
+
+def sides_call(even, odd, block):
+    fields, hx, _, hz = even.shape
+    return pl.pallas_call(
+        sides_kernel,
+        out_shape=(
+            jax.ShapeDtypeStruct((fields, hx, 2 * ITERS, hz), F32),
+            jax.ShapeDtypeStruct((fields, 4 * ITERS, hz), F32),
+        ),
+        in_specs=[pl.BlockSpec(memory_space=pltpu.VMEM)] * 3,
+        out_specs=(pl.BlockSpec(memory_space=pltpu.VMEM),) * 2,
+        compiler_params=pltpu.CompilerParams(vmem_limit_bytes=4 << 20),
+    )(even, odd, block)
+
+
+def payload_kernel(v_ref, sides_ref, to_even_ref):
+    a_odd = lax.axis_index("src") % 2 == 1
+    hx, hy = v_ref.shape[1], v_ref.shape[2]
+    for f in range(FIELDS):
+        for x in range(hx):
             to_even_ref[f, x * hy : (x + 1) * hy] = v_ref[f, x]
-            to_odd_ref[f, x * hy : (x + 1) * hy] = v_ref[f, x]
-        extra = []
-        for first, second, third in ((sides[hx - 1], sides[hx - 2], sides[hx - 3]), (sides[0], sides[1], sides[2])):
-            far = jnp.where(line < 4, pltpu.roll(third, 2, 0), pltpu.roll(third, 6, 0))
-            extra.append((first, jnp.where((line < 2) | (line > 5), second, far)))
-        for i in range(2):
-            at = own + i * 2 * ITERS
-            to_even_ref[f, at : at + 2 * ITERS] = jnp.where(a_odd, extra[1][i], extra[0][i])
-            to_odd_ref[f, at : at + 2 * ITERS] = jnp.where(a_odd, extra[0][i], extra[1][i])
-
-
-def widen_call(v, even, odd):
+        sides = [sides_ref[f, x] for x in range(hx)]
+        for i, (first, last) in enumerate(zip(corners(sides), corners(sides[::-1]))):
+            at = hx * hy + i * 2 * ITERS
+            to_even_ref[f, at : at + 2 * ITERS] = jnp.where(a_odd, first, last)
+
+
+def payload_call(v, sides):
     fields, hx, hy, hz = v.shape
-    payload = jax.ShapeDtypeStruct((fields, hx * hy + 4 * ITERS, hz), F32)
-    return pl.pallas_call(
-        widen_kernel,
-        out_shape=(jax.ShapeDtypeStruct((fields, hx, hy + 2 * ITERS, hz), F32), payload, payload),
-        in_specs=[pl.BlockSpec(memory_space=pltpu.VMEM)] * 3,
-        out_specs=(pl.BlockSpec(memory_space=pltpu.VMEM),) * 3,
-        compiler_params=pltpu.CompilerParams(vmem_limit_bytes=40 << 20),
-    )(v, even, odd)
-
-
-def solve_kernel(mesh_shape, wide_ref, even_ref, odd_ref, mass_ref, order_ref, projected_ref, out_ref):
+    return pl.pallas_call(
+        payload_kernel,
+        out_shape=jax.ShapeDtypeStruct((fields, hx * hy + 4 * ITERS, hz), F32),
+        in_specs=[pl.BlockSpec(memory_space=pltpu.VMEM)] * 2,
+        out_specs=pl.BlockSpec(memory_space=pltpu.VMEM),
+        compiler_params=pltpu.CompilerParams(vmem_limit_bytes=4 << 20),
+    )(v, sides)
+
+
+def solve_kernel(
+    mesh_shape, v_ref, sides_ref, even_ref, odd_ref, odd_sides_ref, mass_ref, order_ref, projected_ref, out_ref
+):
     n_src, n_tgt = mesh_shape
     hx, hy, hz = mass_ref.shape
     k = ITERS
@@ -264,20 +304,22 @@
 
     line = row_ids(2 * k, hz)
 
-    def slabs(payload, from_left):
-        first = payload[hx * hy : hx * hy + 2 * k]
-        second = payload[hx * hy + 2 * k :]
+    def slabs(own, sides, from_left):
+        second = sides[2 * k :]
         third = jnp.where(line < 4, pltpu.roll(second, 6, 0), pltpu.roll(second, 2, 0))
-        sides = [first, second, third] + [jnp.zeros((2 * k, hz), F32)] * (hx - 3)
+        sides = [sides[: 2 * k], second, third] + [jnp.zeros((2 * k, hz), F32)] * (hx - 3)
         order = reversed(sides) if from_left else sides
-        return [jnp.concatenate([payload[x * hy : (x + 1) * hy], side], axis=0) for x, side in enumerate(order)]
+        return [jnp.concatenate([own[x * hy : (x + 1) * hy], side], axis=0) for x, side in enumerate(order)]
 
     @pl.loop(0, FIELDS)
     def _(f):
-        even, odd = even_ref[f], odd_ref[f]
-        left = slabs(jnp.where(a % 2 == 1, even, odd), True)
-        right = slabs(jnp.where(a % 2 == 1, odd, even), False)
-        base = left + [wide_ref[f, x] for x in range(hx)] + right
+        even, even_sides = even_ref[f, : hx * hy], even_ref[f, hx * hy :]
+        odd, odd_sides = odd_ref[f].reshape(hx * hy, hz), odd_sides_ref[f]
+        a_odd = a % 2 == 1
+        left = slabs(jnp.where(a_odd, even, odd), jnp.where(a_odd, even_sides, odd_sides), True)
+        right = slabs(jnp.where(a_odd, odd, even), jnp.where(a_odd, odd_sides, even_sides), False)
+        own = [jnp.concatenate([v_ref[f, x], sides_ref[f, x]], axis=0) for x in range(hx)]
+        base = left + own + right
         u = [COEFS[k] * e for e in base]
         for sweep in range(1, k + 1):
             new = list(u)
@@ -315,7 +357,7 @@
         out_ref[q] = jnp.concatenate(lines + [jnp.zeros((2, 128), F32)], axis=0)
 
 
-def solve_call(mesh_shape, wide, even, odd, mass, order):
+def solve_call(mesh_shape, v, sides, even, odd, odd_sides, mass, order):
     hx, hy, hz = mass.shape
 
     def kernel(*refs):
@@ -327,10 +369,10 @@
             jax.ShapeDtypeStruct((FIELDS, hx, hy, hz), F32),
             jax.ShapeDtypeStruct((order.shape[1] // WIDE, 8, 128), F32),
         ),
-        in_specs=[pl.BlockSpec(memory_space=pltpu.VMEM)] * 5,
+        in_specs=[pl.BlockSpec(memory_space=pltpu.VMEM)] * 7,
         out_specs=(pl.BlockSpec(memory_space=pltpu.VMEM),) * 2,
         compiler_params=pltpu.CompilerParams(vmem_limit_bytes=40 << 20),
-    )(wide, even, odd, mass, order)
+    )(v, sides, even, odd, odd_sides, mass, order)
 
 
 def place_kernel(arrived_ref, order_ref, out_ref, lines):
@@ -367,13 +409,9 @@
     )(arrived, order)
 
 
-def swap(x, axis):
-    count = lax.axis_size(axis)
-    out = []
-    for start, part in enumerate(x):
-        pairs = [(i, i + 1) for i in range(start, count - 1, 2)]
-        out.append(lax.ppermute(part, axis, pairs + [(j, i) for i, j in pairs]))
-    return out
+def swap(x, axis, start):
+    pairs = [(i, i + 1) for i in range(start, lax.axis_size(axis) - 1, 2)]
+    return lax.ppermute(x, axis, pairs + [(j, i) for i, j in pairs])
 
 
 def on_device(source_fields, slot_source, slot_weight, slot_target, cell_mass, send_order, place_order):
@@ -385,9 +423,14 @@
 
     values = gather_call(source_fields, slot_source.reshape(1, -1), slot_weight.reshape(1, -1), owners)
     values = lax.all_to_all(values, both, split_axis=0, concat_axis=0, tiled=True)
-    v, even, odd = scatter_call(values, slot_target.reshape(1, -1), cell_mass)
-    wide, even, odd = widen_call(v, *swap((even, odd), "tgt"))
-    projected, outgoing = solve_call((n_src, n_tgt), wide, *swap((even, odd), "src"), cell_mass, send_order)
+    v, odd_strips = scatter_call(values, slot_target.reshape(1, -1), cell_mass)
+    odd_strips = swap(odd_strips, "tgt", 1)
+    odd = swap(v, "src", 1)
+    even_strips = swap(strips_call(v), "tgt", 0)
+    sides, odd_sides = sides_call(even_strips, odd_strips, odd)
+    odd_sides = swap(odd_sides, "src", 1)
+    even = swap(payload_call(v, sides), "src", 0)
+    projected, outgoing = solve_call((n_src, n_tgt), v, sides, even, odd, odd_sides, cell_mass, send_order)
 
     if quota == WIDE:
         incoming = lax.all_to_all(outgoing, both, split_axis=0, concat_axis=0, tiled=True)

time: 67.1 us -> 67.6 us (level)
  starting transfers between devices: 2.3 us -> 4.99 us
  blocking collectives: 43.1 us -> 41.2 us
    ppermute x4 -> x5, starting transfers between devices: 2.3 us -> 4.99 us  [swap(): return lax.ppermute(x, axis, pairs + [(j, i) for i, j in pairs])]
    all_to_all x1, blocking collectives: 19.5 us -> 17.5 us  [on_device(): lax.all_to_all(outgoing, both, split_axis=0, concat_axis=0, tiled=True)]
    ppermute x4 -> x5, waiting for transfers between devices: 3.56 us -> 3.22 us  [swap(): return lax.ppermute(x, axis, pairs + [(j, i) for i, j in pairs])]
  transfers between devices with their start and end apart: 4 -> 5, of which waited for: 2 -> 2; matrix products, arithmetic and copies ran while one was open for 0% -> 0% of each run, Pallas kernels for 0% -> 0%
where the time goes in v4:
time: 67.6 us; the launch traced here: 67.2 us
  blocking collectives  41.2 us (61%)
  Pallas kernels  17 us (25%)
  starting transfers between devices  4.99 us (7%)
  waiting for transfers between devices  3.22 us (5%)
  between operations  0.73 us (1%)
    all_to_all x1, blocking collectives, on_device(): lax.all_to_all(values, both, split_axis=0, concat_axis=0, tiled=True)  23.7 us
    all_to_all x1, blocking collectives, on_device(): lax.all_to_all(outgoing, both, split_axis=0, concat_axis=0, tiled=True)  17.5 us
    pallas_call x1, Pallas kernels, scatter_call(): pl.pallas_call(scatter_kernel, out_shape=(jax.ShapeDtypeStruct((FIELDS, h...  5.59 us
    ppermute x5, starting transfers between devices, swap(): return lax.ppermute(x, axis, pairs + [(j, i) for i, j in pairs])  4.99 us
    pallas_call x1, Pallas kernels, gather_call(): pl.pallas_call(gather_kernel, out_shape=jax.ShapeDtypeStruct((owners, til...  4.56 us
    pallas_call x1, Pallas kernels, solve_call(): pl.pallas_call(kernel, out_shape=(jax.ShapeDtypeStruct((FIELDS, hx, hy, h...  4.5 us
    ppermute x5, waiting for transfers between devices, swap(): return lax.ppermute(x, axis, pairs + [(j, i) for i, j in pairs])  3.22 us
    pallas_call x1, Pallas kernels, place_call(): pl.pallas_call(place_kernel, out_shape=jax.ShapeDtypeStruct((3, order.sha...  2.29 us
  transfers between devices with their start and end apart: 5, of which 2 were waited for; matrix products, arithmetic and copies ran while one was open for 0% of the time, Pallas kernels for 0%

profile of v4, /device:TPU:0, one launch (start us, length us, event | category | flops | bytes accessed | tf_op | source)
XLA Modules:
  0.0 67.2 jit_solution(12337925958571628752)
XLA Ops:
  0.6 4.6 %shard_map.86 = f32[32,4,8,128]{3,2,1,0:T(8,128)} custom-call(f32[7,4096]{1,0:T(8,128)} %fields_hbm.1, s32[1,16384]{1,0:T(1,128)} %bitcast.4, f32[1,16384]{1,0:T(1,128)} %bitcast.5), custom_call_target="tpu_custom_call" | custom-call | tf_op jit(solution)/shard_map/pallas_call | solution.py:108
  5.2 0.0 copy-start
  5.2 0.0 copy-start.1
  5.2 23.7 %all_to_all.10.value_ref = f32[32,4,8,128]{3,2,1,0:T(8,128)S(1)} all-to-all(f32[32,4,8,128]{3,2,1,0:T(8,128)} %shard_map.86), channel_id=1, replica_groups=mesh['src'=4,'tgt'=8] {'src','tgt'}, dimensions={0} | all-to-all | bytes 1048576 | tf_op jit(solution)/shard_map/all_to_all | solution.py:425
  28.9 0.0 copy-done
  28.9 0.0 copy-done.1
  28.9 5.6 %shard_map.87 = (f32[7,4,16,128]{3,2,1,0:T(8,128)S(1)}, f32[7,4,4,128]{3,2,1,0:T(4,128)S(1)}) custom-call(f32[32,4,8,128]{3,2,1,0:T(8,128)S(1)} %all_to_all.10.value_ref, s32[1,16384]{1,0:T(1,128)S(1)} %bitcast.3, f32[4,16,128]{2,1,0:T(8,128)S(1)} %copy-done), custom_call_target="tpu_custom_call" | custom-call | tf_op jit(solution)/shard_map/pallas_call | solution.py:168
  34.5 0.7 %collective-permute-start.2 = (f32[7,4,16,128]{3,2,1,0:T(8,128)S(1)}, f32[7,4,16,128]{3,2,1,0:T(8,128)S(1)}, u32[]{:S(2)}, u32[]{:S(2)}) collective-permute-start(f32[7,4,16,128]{3,2,1,0:T(8,128)S(1)} %get-tuple-element.8.v_ref.refs_0_), channel_id=1, source_target_pairs={{8,16},{16,8},{9,17},{17,9},{10,18},{18,10},{11,19},{19,11},{12,20... | collective-permute-start | bytes 688136 | tf_op jit(solution)/shard_map/ppermute | solution.py:414
  35.2 0.9 %collective-permute-start = (f32[7,4,4,128]{3,2,1,0:T(4,128)S(1)}, f32[7,4,4,128]{3,2,1,0:T(4,128)S(1)}, u32[]{:S(2)}, u32[]{:S(2)}) collective-permute-start(f32[7,4,4,128]{3,2,1,0:T(4,128)S(1)} %shard_map.88), channel_id=1, source_target_pairs={{0,1},{2,3},{4,5},{6,7},{1,0},{3,2},{5,4},{7,6},{8,9},{10,11},{12,... | collective-permute-start | bytes 172040 | tf_op jit(solution)/shard_map/ppermute | solution.py:414
  36.1 0.7 collective-permute-start.1
  36.8 2.7 %collective-permute-done.even_ref = f32[7,4,4,128]{3,2,1,0:T(4,128)S(1)} collective-permute-done((f32[7,4,4,128]{3,2,1,0:T(4,128)S(1)}, f32[7,4,4,128]{3,2,1,0:T(4,128)S(1)}, u32[]{:S(2)}, u32[]{:S(2)}) %collective-permute-start) | collective-permute-done | bytes 57376 | tf_op jit(solution)/shard_map/ppermute | solution.py:414
  39.4 0.0 collective-permute-done.1.odd_ref
  39.5 0.0 collective-permute-done.2.block_ref.refs_3_
  39.5 0.0 copy-start.2
  39.5 2.1 %collective-permute-start.3 = (f32[7,80,128]{2,1,0:T(8,128)S(1)}, f32[7,80,128]{2,1,0:T(8,128)S(1)}, u32[]{:S(2)}, u32[]{:S(2)}) collective-permute-start(f32[7,80,128]{2,1,0:T(8,128)S(1)} %shard_map.90), channel_id=1, source_target_pairs={{0,8},{16,24},{8,0},{24,16},{1,9},{17,25},{9,1},{25,17},{2,10},{18... | collective-permute-start | bytes 860168 | tf_op jit(solution)/shard_map/ppermute | solution.py:414
  41.7 0.7 collective-permute-start.4
  42.3 0.0 collective-permute-done.4.refs_4_
  42.3 0.5 collective-permute-done.3.refs_2_
  42.9 0.0 copy-done.2
  42.9 4.5 %shard_map.91 = (f32[7,4,16,128]{3,2,1,0:T(8,128)}, f32[32,8,128]{2,1,0:T(8,128)S(1)}) custom-call(f32[7,4,16,128]{3,2,1,0:T(8,128)S(1)} %get-tuple-element.8.v_ref.refs_0_, f32[7,4,8,128]{3,2,1,0:T(8,128)S(1)} %get-tuple-element.10.sides_ref.refs_1_, f32[7,80,128]{2,1,0:T(8,128)S(1)} %collective-permute-done.3.refs_2_, ...), custom_call_target="tpu_custom_call" | custom-call | tf_op jit(solution)/shard_map/pallas_call | solution.py:366
  47.4 0.0 copy-start.3
  47.4 17.5 %all_to_all.11.arrived_ref = f32[32,8,128]{2,1,0:T(8,128)S(1)} all-to-all(f32[32,8,128]{2,1,0:T(8,128)S(1)} %get-tuple-element.13), channel_id=1, replica_groups=mesh['src'=4,'tgt'=8] {'src','tgt'}, dimensions={0} | all-to-all | bytes 262144 | tf_op jit(solution)/shard_map/all_to_all | solution.py:436
  64.9 0.0 copy-done.3
  64.9 2.3 %shard_map.92 = f32[3,8192]{1,0:T(4,128)} custom-call(f32[32,8,128]{2,1,0:T(8,128)S(1)} %all_to_all.11.arrived_ref, s32[1,8192]{1,0:T(1,128)S(1)} %copy-done.3), custom_call_target="tpu_custom_call" | custom-call | tf_op jit(solution)/shard_map/pallas_call | solution.py:402
  (3 shorter events, 0.1 us)
Async XLA Ops:
  5.2 23.7 %copy-start = (f32[4,16,128]{2,1,0:T(8,128)S(1)}, f32[4,16,128]{2,1,0:T(8,128)}, u32[]{:S(2)}) copy-start(f32[4,16,128]{2,1,0:T(8,128)} %refs_5_.1) | copy-start | bytes 98308
  5.2 23.7 %copy-start.1 = (s32[16384]{0:T(1024)S(1)}, s32[16384]{0:T(1024)}, u32[]{:S(2)}) copy-start(s32[16384]{0:T(1024)} %param.10) | copy-start | bytes 196612
  34.5 5.0 %collective-permute-start.2 = (f32[7,4,16,128]{3,2,1,0:T(8,128)S(1)}, f32[7,4,16,128]{3,2,1,0:T(8,128)S(1)}, u32[]{:S(2)}, u32[]{:S(2)}) collective-permute-start(f32[7,4,16,128]{3,2,1,0:T(8,128)S(1)} %get-tuple-element.8.v_ref.refs_0_), channel_id=1, source_target_pairs={{8,16},{16,8},{9,17},{17,9},{10,18},{18,10},{11,19},{19,11},{12,20... | collective-permute-start | bytes 688136 | tf_op jit(solution)/shard_map/ppermute | solution.py:414
  35.2 4.2 %collective-permute-start = (f32[7,4,4,128]{3,2,1,0:T(4,128)S(1)}, f32[7,4,4,128]{3,2,1,0:T(4,128)S(1)}, u32[]{:S(2)}, u32[]{:S(2)}) collective-permute-start(f32[7,4,4,128]{3,2,1,0:T(4,128)S(1)} %shard_map.88), channel_id=1, source_target_pairs={{0,1},{2,3},{4,5},{6,7},{1,0},{3,2},{5,4},{7,6},{8,9},{10,11},{12,... | collective-permute-start | bytes 172040 | tf_op jit(solution)/shard_map/ppermute | solution.py:414
  36.1 3.3 %collective-permute-start.1 = (f32[7,4,4,128]{3,2,1,0:T(4,128)S(1)}, f32[7,4,4,128]{3,2,1,0:T(4,128)S(1)}, u32[]{:S(2)}, u32[]{:S(2)}) collective-permute-start(f32[7,4,4,128]{3,2,1,0:T(4,128)S(1)} %get-tuple-element.9), channel_id=1, source_target_pairs={{1,2},{3,4},{5,6},{2,1},{4,3},{6,5},{9,10},{11,12},{13,14},{10,9},... | collective-permute-start | bytes 172040 | tf_op jit(solution)/shard_map/ppermute | solution.py:414
  39.5 3.4 %copy-start.2 = (s32[1,8192]{1,0:T(1,128)S(1)}, s32[1,8192]{1,0:T(1,128)}, u32[]{:S(2)}) copy-start(s32[1,8192]{1,0:T(1,128)} %refs_6_.1) | copy-start | bytes 98308
  39.5 3.3 %collective-permute-start.3 = (f32[7,80,128]{2,1,0:T(8,128)S(1)}, f32[7,80,128]{2,1,0:T(8,128)S(1)}, u32[]{:S(2)}, u32[]{:S(2)}) collective-permute-start(f32[7,80,128]{2,1,0:T(8,128)S(1)} %shard_map.90), channel_id=1, source_target_pairs={{0,8},{16,24},{8,0},{24,16},{1,9},{17,25},{9,1},{25,17},{2,10},{18... | collective-permute-start | bytes 860168 | tf_op jit(solution)/shard_map/ppermute | solution.py:414
  41.7 0.7 collective-permute-start.4
  47.4 17.5 %copy-start.3 = (s32[1,8192]{1,0:T(1,128)S(1)}, s32[1,8192]{1,0:T(1,128)}, u32[]{:S(2)}) copy-start(s32[1,8192]{1,0:T(1,128)} %order_ref.1) | copy-start | bytes 98308

commit v5 on v3

--- a/solution.py
+++ b/solution.py
@@ -9,6 +9,7 @@
 
 ITERS = 4
 FIELDS = 7
+SPAN = 512
 AT_ONCE = 8
 TOGETHER = 4
 WIDE = 256
@@ -60,8 +61,10 @@
     copies = [pltpu.make_async_copy(src, dst, sems.at[i]) for i, (src, dst) in enumerate(pairs)]
     for copy in copies:
         copy.start()
-    owners, tiles, _, lanes = out_ref.shape
-    span = tiles * lanes
+    lanes = out_ref.shape[1]
+    span = SPAN
+    tiles = span // lanes
+    owners = index_ref.shape[1] // span
     groups = fields_ref.shape[1] // WIDE
     table[...] = jnp.zeros_like(table)
     for copy in copies:
@@ -86,10 +89,13 @@
             value = jnp.where(group == g, part, value)
         value = value * weight
         for t in range(tiles):
-            out_ref[q, t] = value[:, t * lanes : (t + 1) * lanes]
+            out_ref[pl.ds(q * (FIELDS * tiles) + t, FIELDS, stride=tiles), :] = value[
+                :FIELDS, t * lanes : (t + 1) * lanes
+            ]
 
     def send_off(n):
-        part = pl.ds(n * AT_ONCE, AT_ONCE)
+        rows = AT_ONCE * FIELDS * tiles
+        part = pl.ds(pl.multiple_of(n * rows, 8), rows)
         return pltpu.make_async_copy(out_ref.at[part], out_hbm.at[part], done.at[n])
 
     @pl.loop(0, owners // AT_ONCE)
@@ -103,11 +109,12 @@
         send_off(n).wait()
 
 
-def gather_call(fields, index, weight, owners):
-    tiles = index.shape[1] // owners // 128
+def gather_call(fields, index, weight):
+    owners = index.shape[1] // SPAN
+    rows = FIELDS * index.shape[1] // 128
     return pl.pallas_call(
         gather_kernel,
-        out_shape=jax.ShapeDtypeStruct((owners, tiles, 8, 128), F32),
+        out_shape=jax.ShapeDtypeStruct((rows, 128), F32),
         in_specs=[pl.BlockSpec(memory_space=pltpu.HBM)] * 3,
         out_specs=pl.BlockSpec(memory_space=pltpu.HBM),
         scratch_shapes=[
@@ -115,7 +122,7 @@
             pltpu.VMEM(fields.shape, F32),
             pltpu.VMEM(index.shape, jnp.int32),
             pltpu.VMEM(weight.shape, F32),
-            pltpu.VMEM((owners, tiles, 8, 128), F32),
+            pltpu.VMEM((rows, 128), F32),
             pltpu.SemaphoreType.DMA((3,)),
             pltpu.SemaphoreType.DMA((owners // AT_ONCE,)),
         ],
@@ -124,8 +131,10 @@
 
 
 def scatter_kernel(value_ref, target_ref, mass_ref, v_ref, even_ref, odd_ref, total):
-    owners, tiles, _, lanes = value_ref.shape
-    span = TOGETHER * tiles * lanes
+    lanes = value_ref.shape[1]
+    tiles = SPAN // lanes
+    owners = target_ref.shape[1] // SPAN
+    span = TOGETHER * SPAN
     hx, hy, hz = mass_ref.shape
     groups = hx * hy * hz // WIDE
     total[...] = jnp.zeros_like(total)
@@ -140,7 +149,9 @@
         onehot = low_onehot(jnp.where(target < 0, -1, low), ids)
         group = ((target >> log2(hz)) & (groups - 1)).astype(F32).astype(BF16)
         here = group_ids == group
-        value = jnp.concatenate([value_ref[p * TOGETHER + i, t] for i in range(TOGETHER) for t in range(tiles)], axis=1)
+        row = p * (TOGETHER * FIELDS * tiles)
+        pieces = [i * FIELDS * tiles + t for i in range(TOGETHER) for t in range(tiles)]
+        value = jnp.concatenate([value_ref[pl.ds(row + i, FIELDS, stride=tiles), :] for i in pieces], axis=1)
         parts = []
         for half in halves(value):
             for f in range(FIELDS):
@@ -148,6 +159,7 @@
         spread = jnp.concatenate(parts, axis=0)
         total[...] += lax.dot_general(spread, onehot, NT, preferred_element_type=F32)
 
+    odd_ref[FIELDS * hx] = jnp.zeros((ITERS, hz), F32)
     scale = lax.rsqrt(mass_ref[...])
     half_x = hx // 2
     odd = lax.axis_index("tgt") % 2 == 1
@@ -159,17 +171,18 @@
                 v = s[x * hy : (x + 1) * hy, b * hz : (b + 1) * hz] * scale[at]
                 v_ref[f, at] = v
                 first, last = v[:ITERS], v[hy - ITERS :]
-                even_ref[f, at] = jnp.where(odd, first, last)
-                odd_ref[f, at] = jnp.where(odd, last, first)
+                even_ref[f * hx + at] = jnp.where(odd, first, last)
+                odd_ref[f * hx + at] = jnp.where(odd, last, first)
 
 
 def scatter_call(values, target, mass):
     hx, hy, hz = mass.shape
     groups = hx * hy * hz // WIDE
-    side = jax.ShapeDtypeStruct((FIELDS, hx, ITERS, hz), F32)
+    even = jax.ShapeDtypeStruct((FIELDS * hx, ITERS, hz), F32)
+    odd = jax.ShapeDtypeStruct((FIELDS * hx + 1, ITERS, hz), F32)
     return pl.pallas_call(
         scatter_kernel,
-        out_shape=(jax.ShapeDtypeStruct((FIELDS, hx, hy, hz), F32), side, side),
+        out_shape=(jax.ShapeDtypeStruct((FIELDS, hx, hy, hz), F32), even, odd),
         in_specs=[pl.BlockSpec(memory_space=pltpu.VMEM)] * 3,
         out_specs=(pl.BlockSpec(memory_space=pltpu.VMEM),) * 3,
         scratch_shapes=[pltpu.VMEM((2 * FIELDS * groups, WIDE), F32)],
@@ -213,7 +226,7 @@
     for f in range(FIELDS):
         sides = []
         for x in range(hx):
-            even_side, odd_side = even_ref[f, x], odd_ref[f, x]
+            even_side, odd_side = even_ref[f * hx + x], odd_ref[f * hx + x]
             right = jnp.where(b_odd, odd_side, even_side)
             left = jnp.where(b_odd, even_side, odd_side)
             sides.append(jnp.concatenate([right, left], axis=0))
@@ -223,20 +236,23 @@
             to_odd_ref[f, x * hy : (x + 1) * hy] = v_ref[f, x]
         extra = []
         for first, second, third in ((sides[hx - 1], sides[hx - 2], sides[hx - 3]), (sides[0], sides[1], sides[2])):
-            far = jnp.where(line < 4, pltpu.roll(third, 2, 0), pltpu.roll(third, 6, 0))
-            extra.append((first, jnp.where((line < 2) | (line > 5), second, far)))
-        for i in range(2):
-            at = own + i * 2 * ITERS
-            to_even_ref[f, at : at + 2 * ITERS] = jnp.where(a_odd, extra[1][i], extra[0][i])
-            to_odd_ref[f, at : at + 2 * ITERS] = jnp.where(a_odd, extra[0][i], extra[1][i])
+            near = pltpu.roll(second, 2, 0)
+            far = jnp.where(line == 4, pltpu.roll(third, 4, 0), pltpu.roll(third, 6, 0))
+            extra.append((first, jnp.where(line < 4, near, far)))
+        at = own + 2 * ITERS
+        to_even_ref[f, own:at] = jnp.where(a_odd, extra[1][0], extra[0][0])
+        to_odd_ref[f, own:at] = jnp.where(a_odd, extra[0][0], extra[1][0])
+        to_even_ref[f, at : at + 6] = jnp.where(a_odd, extra[1][1], extra[0][1])[:6]
+        to_odd_ref[f, at : at + 8] = jnp.where(a_odd, extra[0][1], extra[1][1])
 
 
 def widen_call(v, even, odd):
     fields, hx, hy, hz = v.shape
-    payload = jax.ShapeDtypeStruct((fields, hx * hy + 4 * ITERS, hz), F32)
+    even_rows = jax.ShapeDtypeStruct((fields, hx * hy + 4 * ITERS - 2, hz), F32)
+    odd_rows = jax.ShapeDtypeStruct((fields, hx * hy + 4 * ITERS, hz), F32)
     return pl.pallas_call(
         widen_kernel,
-        out_shape=(jax.ShapeDtypeStruct((fields, hx, hy + 2 * ITERS, hz), F32), payload, payload),
+        out_shape=(jax.ShapeDtypeStruct((fields, hx, hy + 2 * ITERS, hz), F32), even_rows, odd_rows),
         in_specs=[pl.BlockSpec(memory_space=pltpu.VMEM)] * 3,
         out_specs=(pl.BlockSpec(memory_space=pltpu.VMEM),) * 3,
         compiler_params=pltpu.CompilerParams(vmem_limit_bytes=40 << 20),
@@ -266,15 +282,16 @@
 
     def slabs(payload, from_left):
         first = payload[hx * hy : hx * hy + 2 * k]
-        second = payload[hx * hy + 2 * k :]
-        third = jnp.where(line < 4, pltpu.roll(second, 6, 0), pltpu.roll(second, 2, 0))
+        packed = payload[hx * hy + 2 * k :]
+        second = pltpu.roll(packed, 6, 0)
+        third = jnp.where(line < 4, pltpu.roll(packed, 4, 0), pltpu.roll(packed, 2, 0))
         sides = [first, second, third] + [jnp.zeros((2 * k, hz), F32)] * (hx - 3)
         order = reversed(sides) if from_left else sides
         return [jnp.concatenate([payload[x * hy : (x + 1) * hy], side], axis=0) for x, side in enumerate(order)]
 
     @pl.loop(0, FIELDS)
     def _(f):
-        even, odd = even_ref[f], odd_ref[f]
+        even, odd = jnp.concatenate([even_ref[f], jnp.zeros((2, hz), F32)], axis=0), odd_ref[f]
         left = slabs(jnp.where(a % 2 == 1, even, odd), True)
         right = slabs(jnp.where(a % 2 == 1, odd, even), False)
         base = left + [wide_ref[f, x] for x in range(hx)] + right
@@ -307,12 +324,14 @@
     def at_parts(index):
         return (index >> log2(hz)) & (groups - 1), ((index >> log2(groups * hz)) << log2(hz)) + (index & (hz - 1))
 
-    @pl.loop(0, out_ref.shape[0], unroll=8)
+    @pl.loop(0, groups // 4)
     def _(q):
-        index = order_ref[:, pl.ds(pl.multiple_of(q * WIDE, WIDE), WIDE)]
-        got = lookup_rows(table, index, ids, group_ids, groups, at_parts)
-        lines = [line[:, c * 128 : (c + 1) * 128] for line in got for c in range(2)]
-        out_ref[q] = jnp.concatenate(lines + [jnp.zeros((2, 128), F32)], axis=0)
+        lines = []
+        for i in range(4):
+            index = order_ref[:, pl.ds(pl.multiple_of((q * 4 + i) * WIDE, WIDE), WIDE)]
+            got = lookup_rows(table, index, ids, group_ids, groups, at_parts)
+            lines += [line[:, c * 128 : (c + 1) * 128] for line in got for c in range(2)]
+        out_ref[pl.ds(pl.multiple_of(q * 24, 8), 24), :] = jnp.concatenate(lines, axis=0)
 
 
 def solve_call(mesh_shape, wide, even, odd, mass, order):
@@ -325,7 +344,7 @@
         kernel,
         out_shape=(
             jax.ShapeDtypeStruct((FIELDS, hx, hy, hz), F32),
-            jax.ShapeDtypeStruct((order.shape[1] // WIDE, 8, 128), F32),
+            jax.ShapeDtypeStruct((order.shape[1] // WIDE * 6, 128), F32),
         ),
         in_specs=[pl.BlockSpec(memory_space=pltpu.VMEM)] * 5,
         out_specs=(pl.BlockSpec(memory_space=pltpu.VMEM),) * 2,
@@ -333,12 +352,11 @@
     )(wide, even, odd, mass, order)
 
 
-def place_kernel(arrived_ref, order_ref, out_ref, lines):
-    groups = arrived_ref.shape[0]
-    lines[...] = arrived_ref[...].reshape(groups * 8, 128)
+def place_kernel(arrived_ref, order_ref, out_ref):
+    groups = arrived_ref.shape[0] // 6
     table = jnp.concatenate(
         [
-            jnp.concatenate([lines[pl.ds(2 * m + c, groups, stride=8), :] for c in range(2)], axis=1)
+            jnp.concatenate([arrived_ref[pl.ds(2 * m + c, groups, stride=6), :] for c in range(2)], axis=1)
             for m in range(3)
         ],
         axis=0,
@@ -362,7 +380,6 @@
         out_shape=jax.ShapeDtypeStruct((3, order.shape[1]), F32),
         in_specs=[pl.BlockSpec(memory_space=pltpu.VMEM)] * 2,
         out_specs=pl.BlockSpec(memory_space=pltpu.VMEM),
-        scratch_shapes=[pltpu.VMEM((arrived.shape[0] * 8, 128), F32)],
         compiler_params=pltpu.CompilerParams(vmem_limit_bytes=40 << 20),
     )(arrived, order)
 
@@ -383,20 +400,22 @@
     cells = cell_mass.size
     quota = cells // owners
 
-    values = gather_call(source_fields, slot_source.reshape(1, -1), slot_weight.reshape(1, -1), owners)
-    values = lax.all_to_all(values, both, split_axis=0, concat_axis=0, tiled=True)
+    values = gather_call(source_fields, slot_source.reshape(1, -1), slot_weight.reshape(1, -1))
+    values = values.reshape(owners, FIELDS, SPAN // 128, 128)
+    values = lax.all_to_all(values, both, split_axis=0, concat_axis=0, tiled=True).reshape(-1, 128)
     v, even, odd = scatter_call(values, slot_target.reshape(1, -1), cell_mass)
     wide, even, odd = widen_call(v, *swap((even, odd), "tgt"))
     projected, outgoing = solve_call((n_src, n_tgt), wide, *swap((even, odd), "src"), cell_mass, send_order)
 
     if quota == WIDE:
+        outgoing = outgoing.reshape(owners, 3, 2, 128)
         incoming = lax.all_to_all(outgoing, both, split_axis=0, concat_axis=0, tiled=True)
     else:
         groups = cells // WIDE
-        flat = outgoing[:, :6].reshape(groups, 3, WIDE).transpose(1, 0, 2).reshape(3, owners, quota)
+        flat = outgoing.reshape(groups, 3, WIDE).transpose(1, 0, 2).reshape(3, owners, quota)
         flat = lax.all_to_all(flat, both, split_axis=1, concat_axis=1, tiled=True)
-        flat = flat.reshape(3, groups, WIDE).transpose(1, 0, 2).reshape(groups, 6, 128)
-        incoming = jnp.pad(flat, ((0, 0), (0, 2), (0, 0)))
+        incoming = flat.reshape(3, groups, WIDE).transpose(1, 0, 2)
+    incoming = incoming.reshape(-1, 128)
     return projected, place_call(incoming, place_order)
 
 

time: 67.1 us -> 66.2 us (0.987)
  blocking collectives: 43.1 us -> 37.2 us
  starting transfers between devices: 2.3 us -> 6.81 us
    ppermute x4, starting transfers between devices: 2.3 us -> 6.81 us  [swap(): out.append(lax.ppermute(part, axis, pairs + [(j, i) for i, j in pairs]))]
    all_to_all x1, blocking collectives: 19.5 us -> 15 us  [on_device(): lax.all_to_all(outgoing, both, split_axis=0, concat_axis=0, tiled=True)]
    all_to_all x1, blocking collectives: 23.7 us -> 22.3 us  [on_device(): lax.all_to_all(values, both, split_axis=0, concat_axis=0, tiled=True)]
where the time goes in v5:
time: 66.2 us; the launch traced here: 65.8 us
  blocking collectives  37.2 us (56%)
  Pallas kernels  17.6 us (27%)
  starting transfers between devices  6.81 us (10%)
  waiting for transfers between devices  3.41 us (5%)
  between operations  0.69 us (1%)
    all_to_all x1, blocking collectives, on_device(): lax.all_to_all(values, both, split_axis=0, concat_axis=0, tiled=True)  22.3 us
    all_to_all x1, blocking collectives, on_device(): lax.all_to_all(outgoing, both, split_axis=0, concat_axis=0, tiled=True)  15 us
    ppermute x4, starting transfers between devices, swap(): out.append(lax.ppermute(part, axis, pairs + [(j, i) for i, j in pairs]))  6.81 us
    pallas_call x1, Pallas kernels, scatter_call(): pl.pallas_call(scatter_kernel, out_shape=(jax.ShapeDtypeStruct((FIELDS, h...  5.58 us
    pallas_call x1, Pallas kernels, solve_call(): pl.pallas_call(kernel, out_shape=(jax.ShapeDtypeStruct((FIELDS, hx, hy, h...  5.13 us
    pallas_call x1, Pallas kernels, gather_call(): pl.pallas_call(gather_kernel, out_shape=jax.ShapeDtypeStruct((rows, 128),...  4.57 us
    ppermute x4, waiting for transfers between devices, swap(): out.append(lax.ppermute(part, axis, pairs + [(j, i) for i, j in pairs]))  3.41 us
    pallas_call x1, Pallas kernels, place_call(): pl.pallas_call(place_kernel, out_shape=jax.ShapeDtypeStruct((3, order.sha...  2.28 us
  transfers between devices with their start and end apart: 4, of which 2 were waited for; matrix products, arithmetic and copies ran while one was open for 0% of the time, Pallas kernels for 0%

profile of v5, /device:TPU:0, one launch (start us, length us, event | category | flops | bytes accessed | tf_op | source)
XLA Modules:
  0.0 65.8 jit_solution(9976409078668919804)
XLA Ops:
  0.6 4.6 %shard_map.86 = f32[896,128]{1,0:T(8,128)} custom-call(f32[7,4096]{1,0:T(8,128)} %fields_hbm.1, s32[1,16384]{1,0:T(1,128)} %bitcast.12, f32[1,16384]{1,0:T(1,128)} %bitcast.13), custom_call_target="tpu_custom_call" | custom-call | tf_op jit(solution)/shard_map/pallas_call | solution.py:115
  5.2 0.0 copy-start
  5.2 0.0 copy-start.1
  5.2 22.3 %all_to_all.10 = f32[32,7,4,128]{3,2,1,0:T(4,128)S(1)} all-to-all(f32[32,7,4,128]{3,2,1,0:T(4,128)} %bitcast.11), channel_id=1, replica_groups=mesh['src'=4,'tgt'=8] {'src','tgt'}, dimensions={0} | all-to-all | bytes 917504 | tf_op jit(solution)/shard_map/all_to_all | solution.py:405
  27.5 0.0 copy-done
  27.5 0.0 copy-done.1
  27.5 5.6 %shard_map.87 = (f32[7,4,16,128]{3,2,1,0:T(8,128)S(1)}, f32[28,4,128]{2,1,0:T(4,128)S(1)}, f32[29,4,128]{2,1,0:T(4,128)S(1)}) custom-call(f32[896,128]{1,0:T(8,128)S(1)} %bitcast.7, s32[1,16384]{1,0:T(1,128)S(1)} %bitcast.10, f32[4,16,128]{2,1,0:T(8,128)S(1)} %copy-done), custom_call_target="tpu_custom_call" | custom-call | tf_op jit(solution)/shard_map/pallas_call | solution.py:183
  33.1 0.7 %collective-permute-start.1 = (f32[29,4,128]{2,1,0:T(4,128)S(1)}, f32[29,4,128]{2,1,0:T(4,128)S(1)}, u32[]{:S(2)}, u32[]{:S(2)}) collective-permute-start(f32[29,4,128]{2,1,0:T(4,128)S(1)} %get-tuple-element.12), channel_id=1, source_target_pairs={{1,2},{3,4},{5,6},{2,1},{4,3},{6,5},{9,10},{11,12},{13,14},{10,9},... | collective-permute-start | bytes 178184 | tf_op jit(solution)/shard_map/ppermute | solution.py:392
  33.8 3.5 %collective-permute-start = (f32[28,4,128]{2,1,0:T(4,128)S(1)}, f32[28,4,128]{2,1,0:T(4,128)S(1)}, u32[]{:S(2)}, u32[]{:S(2)}) collective-permute-start(f32[28,4,128]{2,1,0:T(4,128)S(1)} %get-tuple-element.11), channel_id=1, source_target_pairs={{0,1},{2,3},{4,5},{6,7},{1,0},{3,2},{5,4},{7,6},{8,9},{10,11},{12,... | collective-permute-start | bytes 172040 | tf_op jit(solution)/shard_map/ppermute | solution.py:392
  37.3 2.2 %collective-permute-done.even_ref = f32[28,4,128]{2,1,0:T(4,128)S(1)} collective-permute-done((f32[28,4,128]{2,1,0:T(4,128)S(1)}, f32[28,4,128]{2,1,0:T(4,128)S(1)}, u32[]{:S(2)}, u32[]{:S(2)}) %collective-permute-start) | collective-permute-done | bytes 57376 | tf_op jit(solution)/shard_map/ppermute | solution.py:392
  39.5 0.0 collective-permute-done.1.odd_ref
  39.5 0.0 copy-start.2
  39.5 0.1 shard_map.88
  39.5 0.7 %collective-permute-start.3 = (f32[7,80,128]{2,1,0:T(8,128)S(1)}, f32[7,80,128]{2,1,0:T(8,128)S(1)}, u32[]{:S(2)}, u32[]{:S(2)}) collective-permute-start(f32[7,80,128]{2,1,0:T(8,128)S(1)} %get-tuple-element.15), channel_id=1, source_target_pairs={{8,16},{16,8},{9,17},{17,9},{10,18},{18,10},{11,19},{19,11},{12,20... | collective-permute-start | bytes 860168 | tf_op jit(solution)/shard_map/ppermute | solution.py:392
  40.2 2.0 %collective-permute-start.2 = (f32[7,78,128]{2,1,0:T(8,128)S(1)}, f32[7,78,128]{2,1,0:T(8,128)S(1)}, u32[]{:S(2)}, u32[]{:S(2)}) collective-permute-start(f32[7,78,128]{2,1,0:T(8,128)S(1)} %get-tuple-element.14), channel_id=1, source_target_pairs={{0,8},{16,24},{8,0},{24,16},{1,9},{17,25},{9,1},{25,17},{2,10},{18... | collective-permute-start | bytes 838664 | tf_op jit(solution)/shard_map/ppermute | solution.py:392
  42.2 1.2 %collective-permute-done.2.refs_1_ = f32[7,78,128]{2,1,0:T(8,128)S(1)} collective-permute-done((f32[7,78,128]{2,1,0:T(8,128)S(1)}, f32[7,78,128]{2,1,0:T(8,128)S(1)}, u32[]{:S(2)}, u32[]{:S(2)}) %collective-permute-start.2) | collective-permute-done | bytes 279584 | tf_op jit(solution)/shard_map/ppermute | solution.py:392
  43.4 0.0 collective-permute-done.3.refs_2_
  43.4 0.0 copy-done.2
  43.4 5.1 %shard_map.89 = (f32[7,4,16,128]{3,2,1,0:T(8,128)}, f32[192,128]{1,0:T(8,128)S(1)}) custom-call(f32[7,4,24,128]{3,2,1,0:T(8,128)S(1)} %get-tuple-element.13.refs_0_, f32[7,78,128]{2,1,0:T(8,128)S(1)} %collective-permute-done.2.refs_1_, f32[7,80,128]{2,1,0:T(8,128)S(1)} %collective-permute-done.3.refs_2_, f32[4,16,128]{2,1,0:T(8,128)S(1)} %copy-done, ...), custom_call_target="tpu_custom_call" | custom-call | tf_op jit(solution)/shard_map/pallas_call | solution.py:343
  48.5 0.0 copy-start.3
  48.5 15.0 %all_to_all.11 = f32[32,3,2,128]{3,2,1,0:T(2,128)S(1)} all-to-all(f32[32,3,2,128]{3,2,1,0:T(2,128)S(1)} %bitcast.9), channel_id=1, replica_groups=mesh['src'=4,'tgt'=8] {'src','tgt'}, dimensions={0} | all-to-all | bytes 196608 | tf_op jit(solution)/shard_map/all_to_all | solution.py:412
  63.5 0.0 copy-done.3
  63.5 2.3 %shard_map.90 = f32[3,8192]{1,0:T(4,128)} custom-call(f32[192,128]{1,0:T(8,128)S(1)} %bitcast.8, s32[1,8192]{1,0:T(1,128)S(1)} %copy-done.3), custom_call_target="tpu_custom_call" | custom-call | tf_op jit(solution)/shard_map/pallas_call | solution.py:378
Async XLA Ops:
  5.2 22.3 %copy-start = (f32[4,16,128]{2,1,0:T(8,128)S(1)}, f32[4,16,128]{2,1,0:T(8,128)}, u32[]{:S(2)}) copy-start(f32[4,16,128]{2,1,0:T(8,128)} %refs_3_.1) | copy-start | bytes 98308
  5.2 22.3 %copy-start.1 = (s32[16384]{0:T(1024)S(1)}, s32[16384]{0:T(1024)}, u32[]{:S(2)}) copy-start(s32[16384]{0:T(1024)} %param.10) | copy-start | bytes 196612
  33.1 6.4 %collective-permute-start.1 = (f32[29,4,128]{2,1,0:T(4,128)S(1)}, f32[29,4,128]{2,1,0:T(4,128)S(1)}, u32[]{:S(2)}, u32[]{:S(2)}) collective-permute-start(f32[29,4,128]{2,1,0:T(4,128)S(1)} %get-tuple-element.12), channel_id=1, source_target_pairs={{1,2},{3,4},{5,6},{2,1},{4,3},{6,5},{9,10},{11,12},{13,14},{10,9},... | collective-permute-start | bytes 178184 | tf_op jit(solution)/shard_map/ppermute | solution.py:392
  33.8 5.7 %collective-permute-start = (f32[28,4,128]{2,1,0:T(4,128)S(1)}, f32[28,4,128]{2,1,0:T(4,128)S(1)}, u32[]{:S(2)}, u32[]{:S(2)}) collective-permute-start(f32[28,4,128]{2,1,0:T(4,128)S(1)} %get-tuple-element.11), channel_id=1, source_target_pairs={{0,1},{2,3},{4,5},{6,7},{1,0},{3,2},{5,4},{7,6},{8,9},{10,11},{12,... | collective-permute-start | bytes 172040 | tf_op jit(solution)/shard_map/ppermute | solution.py:392
  39.5 3.9 %copy-start.2 = (s32[1,8192]{1,0:T(1,128)S(1)}, s32[1,8192]{1,0:T(1,128)}, u32[]{:S(2)}) copy-start(s32[1,8192]{1,0:T(1,128)} %refs_4_.1) | copy-start | bytes 98308
  39.5 3.9 %collective-permute-start.3 = (f32[7,80,128]{2,1,0:T(8,128)S(1)}, f32[7,80,128]{2,1,0:T(8,128)S(1)}, u32[]{:S(2)}, u32[]{:S(2)}) collective-permute-start(f32[7,80,128]{2,1,0:T(8,128)S(1)} %get-tuple-element.15), channel_id=1, source_target_pairs={{8,16},{16,8},{9,17},{17,9},{10,18},{18,10},{11,19},{19,11},{12,20... | collective-permute-start | bytes 860168 | tf_op jit(solution)/shard_map/ppermute | solution.py:392
  40.2 3.2 %collective-permute-start.2 = (f32[7,78,128]{2,1,0:T(8,128)S(1)}, f32[7,78,128]{2,1,0:T(8,128)S(1)}, u32[]{:S(2)}, u32[]{:S(2)}) collective-permute-start(f32[7,78,128]{2,1,0:T(8,128)S(1)} %get-tuple-element.14), channel_id=1, source_target_pairs={{0,8},{16,24},{8,0},{24,16},{1,9},{17,25},{9,1},{25,17},{2,10},{18... | collective-permute-start | bytes 838664 | tf_op jit(solution)/shard_map/ppermute | solution.py:392
  48.5 15.0 %copy-start.3 = (s32[1,8192]{1,0:T(1,128)S(1)}, s32[1,8192]{1,0:T(1,128)}, u32[]{:S(2)}) copy-start(s32[1,8192]{1,0:T(1,128)} %order_ref.1) | copy-start | bytes 98308

commit v6 on v5

--- a/solution.py
+++ b/solution.py
@@ -1,3 +1,5 @@
+import functools
+
 import numpy as np
 
 import jax
@@ -9,9 +11,10 @@
 
 ITERS = 4
 FIELDS = 7
+HALVES = 2
 SPAN = 512
 AT_ONCE = 8
-TOGETHER = 4
+TOGETHER = 8
 WIDE = 256
 BF16 = jnp.bfloat16
 F32 = jnp.float32
@@ -48,6 +51,10 @@
     return n.bit_length() - 1
 
 
+def cost(flops):
+    return pl.CostEstimate(flops=flops, bytes_accessed=1 << 20, transcendentals=0)
+
+
 def row_ids(rows, lanes):
     return lax.broadcasted_iota(jnp.int32, (rows, lanes), 0)
 
@@ -56,15 +63,15 @@
     return jnp.where(ids == low.astype(F32).astype(BF16), jnp.ones((), BF16), jnp.zeros((), BF16))
 
 
-def gather_kernel(fields_hbm, index_hbm, weight_hbm, out_hbm, table, fields_ref, index_ref, weight_ref, out_ref, sems, done):
+def gather_kernel(first, fields_hbm, index_hbm, weight_hbm, out_hbm, table, fields_ref, index_ref, weight_ref, out_ref, sems, done):
     pairs = ((fields_hbm, fields_ref), (index_hbm, index_ref), (weight_hbm, weight_ref))
     copies = [pltpu.make_async_copy(src, dst, sems.at[i]) for i, (src, dst) in enumerate(pairs)]
     for copy in copies:
         copy.start()
     lanes = out_ref.shape[1]
-    span = SPAN
+    span = SPAN // HALVES
     tiles = span // lanes
-    owners = index_ref.shape[1] // span
+    owners = index_ref.shape[1] // SPAN
     groups = fields_ref.shape[1] // WIDE
     table[...] = jnp.zeros_like(table)
     for copy in copies:
@@ -77,7 +84,7 @@
     rows = groups * 8
 
     def one_owner(q):
-        at = pl.multiple_of(q * span, span)
+        at = pl.multiple_of(q * SPAN + first, span)
         index = index_ref[:, pl.ds(at, span)]
         weight = weight_ref[:, pl.ds(at, span)]
         onehot = low_onehot(index & (WIDE - 1), ids)
@@ -109,11 +116,11 @@
         send_off(n).wait()
 
 
-def gather_call(fields, index, weight):
+def gather_call(fields, index, weight, half):
     owners = index.shape[1] // SPAN
-    rows = FIELDS * index.shape[1] // 128
-    return pl.pallas_call(
-        gather_kernel,
+    rows = FIELDS * index.shape[1] // HALVES // 128
+    return pl.pallas_call(
+        functools.partial(gather_kernel, half * SPAN // HALVES),
         out_shape=jax.ShapeDtypeStruct((rows, 128), F32),
         in_specs=[pl.BlockSpec(memory_space=pltpu.HBM)] * 3,
         out_specs=pl.BlockSpec(memory_space=pltpu.HBM),
@@ -127,24 +134,23 @@
             pltpu.SemaphoreType.DMA((owners // AT_ONCE,)),
         ],
         compiler_params=pltpu.CompilerParams(vmem_limit_bytes=60 << 20),
+        cost_estimate=cost(2 * 2 * 8 * fields.shape[1] * index.shape[1] // HALVES),
     )(fields, index, weight)
 
 
-def scatter_kernel(value_ref, target_ref, mass_ref, v_ref, even_ref, odd_ref, total):
+def add_slots(first, value_ref, target_ref, total, groups, hz):
     lanes = value_ref.shape[1]
-    tiles = SPAN // lanes
+    part = SPAN // HALVES
+    tiles = part // lanes
     owners = target_ref.shape[1] // SPAN
-    span = TOGETHER * SPAN
-    hx, hy, hz = mass_ref.shape
-    groups = hx * hy * hz // WIDE
     total[...] = jnp.zeros_like(total)
-    ids = row_ids(WIDE, span).astype(F32).astype(BF16)
-    group_ids = row_ids(groups, span).astype(F32).astype(BF16)
+    ids = row_ids(WIDE, TOGETHER * part).astype(F32).astype(BF16)
+    group_ids = row_ids(groups, TOGETHER * part).astype(F32).astype(BF16)
 
     @pl.loop(0, owners // TOGETHER)
     def _(p):
-        at = pl.multiple_of(p * span, span)
-        target = target_ref[:, pl.ds(at, span)]
+        starts = [pl.multiple_of((p * TOGETHER + i) * SPAN + first, part) for i in range(TOGETHER)]
+        target = jnp.concatenate([target_ref[:, pl.ds(at, part)] for at in starts], axis=1)
         low = ((target >> log2(groups * hz)) << log2(hz)) + (target & (hz - 1))
         onehot = low_onehot(jnp.where(target < 0, -1, low), ids)
         group = ((target >> log2(hz)) & (groups - 1)).astype(F32).astype(BF16)
@@ -159,7 +165,27 @@
         spread = jnp.concatenate(parts, axis=0)
         total[...] += lax.dot_general(spread, onehot, NT, preferred_element_type=F32)
 
-    odd_ref[FIELDS * hx] = jnp.zeros((ITERS, hz), F32)
+
+def first_sums_kernel(hz, value_ref, target_ref, total_ref):
+    add_slots(0, value_ref, target_ref, total_ref, total_ref.shape[0] // (2 * FIELDS), hz)
+
+
+def first_sums_call(values, target, mass):
+    return pl.pallas_call(
+        functools.partial(first_sums_kernel, mass.shape[2]),
+        out_shape=jax.ShapeDtypeStruct((2 * FIELDS * mass.size // WIDE, WIDE), F32),
+        in_specs=[pl.BlockSpec(memory_space=pltpu.VMEM)] * 2,
+        out_specs=pl.BlockSpec(memory_space=pltpu.VMEM),
+        compiler_params=pltpu.CompilerParams(vmem_limit_bytes=40 << 20),
+        cost_estimate=cost(4 * FIELDS * mass.size * target.shape[1] // HALVES),
+    )(values, target)
+
+
+def scatter_kernel(value_ref, target_ref, before_ref, mass_ref, v_ref, even_ref, odd_ref, total):
+    hx, hy, hz = mass_ref.shape
+    groups = hx * hy * hz // WIDE
+    add_slots(SPAN // HALVES, value_ref, target_ref, total, groups, hz)
+    total[...] += before_ref[...]
     scale = lax.rsqrt(mass_ref[...])
     half_x = hx // 2
     odd = lax.axis_index("tgt") % 2 == 1
@@ -175,7 +201,7 @@
                 odd_ref[f * hx + at] = jnp.where(odd, last, first)
 
 
-def scatter_call(values, target, mass):
+def scatter_call(values, target, before, mass):
     hx, hy, hz = mass.shape
     groups = hx * hy * hz // WIDE
     even = jax.ShapeDtypeStruct((FIELDS * hx, ITERS, hz), F32)
@@ -183,11 +209,12 @@
     return pl.pallas_call(
         scatter_kernel,
         out_shape=(jax.ShapeDtypeStruct((FIELDS, hx, hy, hz), F32), even, odd),
-        in_specs=[pl.BlockSpec(memory_space=pltpu.VMEM)] * 3,
+        in_specs=[pl.BlockSpec(memory_space=pltpu.VMEM)] * 4,
         out_specs=(pl.BlockSpec(memory_space=pltpu.VMEM),) * 3,
         scratch_shapes=[pltpu.VMEM((2 * FIELDS * groups, WIDE), F32)],
         compiler_params=pltpu.CompilerParams(vmem_limit_bytes=40 << 20),
-    )(values, target, mass)
+        cost_estimate=cost(4 * FIELDS * mass.size * target.shape[1] // HALVES),
+    )(values, target, before, mass)
 
 
 def lookup_rows(table, index, ids, group_ids, groups, at_parts):
@@ -324,14 +351,14 @@
     def at_parts(index):
         return (index >> log2(hz)) & (groups - 1), ((index >> log2(groups * hz)) << log2(hz)) + (index & (hz - 1))
 
-    @pl.loop(0, groups // 4)
+    @pl.loop(0, groups // 8)
     def _(q):
         lines = []
-        for i in range(4):
-            index = order_ref[:, pl.ds(pl.multiple_of((q * 4 + i) * WIDE, WIDE), WIDE)]
+        for i in range(8):
+            index = order_ref[:, pl.ds(pl.multiple_of((q * 8 + i) * WIDE, WIDE), WIDE)]
             got = lookup_rows(table, index, ids, group_ids, groups, at_parts)
             lines += [line[:, c * 128 : (c + 1) * 128] for line in got for c in range(2)]
-        out_ref[pl.ds(pl.multiple_of(q * 24, 8), 24), :] = jnp.concatenate(lines, axis=0)
+        out_ref[pl.ds(pl.multiple_of(q * 48, 8), 48), :] = jnp.concatenate(lines, axis=0)
 
 
 def solve_call(mesh_shape, wide, even, odd, mass, order):
@@ -400,10 +427,15 @@
     cells = cell_mass.size
     quota = cells // owners
 
-    values = gather_call(source_fields, slot_source.reshape(1, -1), slot_weight.reshape(1, -1))
-    values = values.reshape(owners, FIELDS, SPAN // 128, 128)
-    values = lax.all_to_all(values, both, split_axis=0, concat_axis=0, tiled=True).reshape(-1, 128)
-    v, even, odd = scatter_call(values, slot_target.reshape(1, -1), cell_mass)
+    arrived = []
+    for half in range(HALVES):
+        values = gather_call(source_fields, slot_source.reshape(1, -1), slot_weight.reshape(1, -1), half)
+        values = values.reshape(owners, FIELDS, SPAN // HALVES // 128, 128)
+        values = lax.all_to_all(values, both, split_axis=0, concat_axis=0, tiled=True)
+        arrived.append(values.reshape(-1, 128))
+    target = slot_target.reshape(1, -1)
+    before = first_sums_call(arrived[0], target, cell_mass)
+    v, even, odd = scatter_call(arrived[1], target, before, cell_mass)
     wide, even, odd = widen_call(v, *swap((even, odd), "tgt"))
     projected, outgoing = solve_call((n_src, n_tgt), wide, *swap((even, odd), "src"), cell_mass, send_order)
 

time: 66.2 us -> 69.3 us (1.047)
  blocking collectives: 37.2 us -> 14.8 us
  waiting for transfers between devices: 3.41 us -> 16.7 us
  starting transfers between devices: 6.81 us -> 17.2 us
  Pallas kernels: 17.6 us -> 19.4 us
    all_to_all x1 -> x0, blocking collectives: 22.3 us -> none  [on_device(): lax.all_to_all(values, both, split_axis=0, concat_axis=0, tiled=True)]
    all_to_all x0 -> x2, waiting for transfers between devices: none -> 13.3 us  [on_device(): lax.all_to_all(values, both, split_axis=0, concat_axis=0, tiled=True)]
    all_to_all x0 -> x2, starting transfers between devices: none -> 10 us  [on_device(): lax.all_to_all(values, both, split_axis=0, concat_axis=0, tiled=True)]
    pallas_call x1 -> x3, Pallas kernels: 4.57 us -> 9.69 us  [the longest x2 6.92 us: gather_call(): pl.pallas_call(functools.partial(gather_kernel, half * SPAN // HALVES), o...]
    pallas_call x1, Pallas kernels: 5.58 us -> 2.84 us  [scatter_call(): pl.pallas_call(scatter_kernel, out_shape=(jax.ShapeDtypeStruct((FIELDS, h...]
  transfers between devices with their start and end apart: 4 -> 6, of which waited for: 2 -> 4; matrix products, arithmetic and copies ran while one was open for 0% -> 0% of each run, Pallas kernels for 0% -> 9%
where the time goes in v6:
time: 69.3 us; the launch traced here: 68.8 us
  Pallas kernels  19.4 us (28%)
  starting transfers between devices  17.2 us (25%)
  waiting for transfers between devices  16.7 us (24%)
  blocking collectives  14.8 us (21%)
  between operations  0.72 us (1%)
    all_to_all x1, blocking collectives, on_device(): lax.all_to_all(outgoing, both, split_axis=0, concat_axis=0, tiled=True)  14.8 us
    all_to_all x2, waiting for transfers between devices, on_device(): lax.all_to_all(values, both, split_axis=0, concat_axis=0, tiled=True)  13.3 us
    all_to_all x2, starting transfers between devices, on_device(): lax.all_to_all(values, both, split_axis=0, concat_axis=0, tiled=True)  10 us
    ppermute x4, starting transfers between devices, swap(): out.append(lax.ppermute(part, axis, pairs + [(j, i) for i, j in pairs]))  7.21 us
    pallas_call x2, Pallas kernels, gather_call(): pl.pallas_call(functools.partial(gather_kernel, half * SPAN // HALVES), o...  6.92 us
    pallas_call x1, Pallas kernels, solve_call(): pl.pallas_call(kernel, out_shape=(jax.ShapeDtypeStruct((FIELDS, hx, hy, h...  4.53 us
    ppermute x4, waiting for transfers between devices, swap(): out.append(lax.ppermute(part, axis, pairs + [(j, i) for i, j in pairs]))  3.36 us
    pallas_call x1, Pallas kernels, scatter_call(): pl.pallas_call(scatter_kernel, out_shape=(jax.ShapeDtypeStruct((FIELDS, h...  2.84 us
  transfers between devices with their start and end apart: 6, of which 4 were waited for; matrix products, arithmetic and copies ran while one was open for 0% of the time, Pallas kernels for 9%

profile of v6, /device:TPU:0, one launch (start us, length us, event | category | flops | bytes accessed | tf_op | source)
XLA Modules:
  0.0 68.8 jit_solution(11207658645514244195)
XLA Ops:
  0.6 3.5 %shard_map.87 = f32[448,128]{1,0:T(8,128)} custom-call(f32[7,4096]{1,0:T(8,128)} %fields_hbm.3, s32[1,16384]{1,0:T(1,128)} %bitcast.17, f32[1,16384]{1,0:T(1,128)} %bitcast.19), custom_call_target="tpu_custom_call" | custom-call | flops 1073741824 | bytes 1048576 | tf_op jit(solution)/shard_map/pallas_call | solution.py:122
  4.1 7.3 %all-to-all-start.1 = ((f32[32,7,2,128]{3,2,1,0:T(2,128)}), f32[32,7,2,128]{3,2,1,0:T(2,128)S(1)}, u32[]{:S(2)}, u32[]{:S(2)}) async-start(f32[32,7,2,128]{3,2,1,0:T(2,128)} %bitcast.16), calls=%async_computation.1 | async-start | bytes 458752 | tf_op jit(solution)/shard_map/all_to_all | solution.py:434
  11.4 3.5 %shard_map.86 = f32[448,128]{1,0:T(8,128)} custom-call(f32[7,4096]{1,0:T(8,128)} %fields_hbm.3, s32[1,16384]{1,0:T(1,128)} %bitcast.18, f32[1,16384]{1,0:T(1,128)} %bitcast.20), custom_call_target="tpu_custom_call" | custom-call | flops 1073741824 | bytes 1048576 | tf_op jit(solution)/shard_map/pallas_call | solution.py:122
  14.9 6.3 %all-to-all-done.1 = f32[32,7,2,128]{3,2,1,0:T(2,128)S(1)} async-done(((f32[32,7,2,128]{3,2,1,0:T(2,128)}), f32[32,7,2,128]{3,2,1,0:T(2,128)S(1)}, u32[]{:S(2)}, u32[]{:S(2)}) %all-to-all-start.1) | async-done | bytes 229408 | tf_op jit(solution)/shard_map/all_to_all | solution.py:434
  21.2 0.0 copy-start.3
  21.2 2.7 %all-to-all-start = ((f32[32,7,2,128]{3,2,1,0:T(2,128)}), f32[32,7,2,128]{3,2,1,0:T(2,128)S(1)}, u32[]{:S(2)}, u32[]{:S(2)}) async-start(f32[32,7,2,128]{3,2,1,0:T(2,128)} %bitcast.15), calls=%async_computation | async-start | bytes 458752 | tf_op jit(solution)/shard_map/all_to_all | solution.py:434
  23.9 0.0 copy-done.3
  23.9 0.0 copy-start
  23.9 2.8 %shard_map.88.before_ref = f32[448,256]{1,0:T(8,128)S(1)} custom-call(f32[448,128]{1,0:T(8,128)S(1)} %bitcast.10, s32[1,16384]{1,0:T(1,128)S(1)} %bitcast.13), custom_call_target="tpu_custom_call" | custom-call | flops 1879048192 | bytes 1048576 | tf_op jit(solution)/shard_map/pallas_call | solution.py:174
  26.7 7.0 %all-to-all-done = f32[32,7,2,128]{3,2,1,0:T(2,128)S(1)} async-done(((f32[32,7,2,128]{3,2,1,0:T(2,128)}), f32[32,7,2,128]{3,2,1,0:T(2,128)S(1)}, u32[]{:S(2)}, u32[]{:S(2)}) %all-to-all-start) | async-done | bytes 229408 | tf_op jit(solution)/shard_map/all_to_all | solution.py:434
  33.7 0.0 copy-done
  33.7 2.8 %shard_map.89 = (f32[7,4,16,128]{3,2,1,0:T(8,128)S(1)}, f32[28,4,128]{2,1,0:T(4,128)S(1)}, f32[29,4,128]{2,1,0:T(4,128)S(1)}) custom-call(f32[448,128]{1,0:T(8,128)S(1)} %bitcast.11, s32[1,16384]{1,0:T(1,128)S(1)} %bitcast.14, f32[448,256]{1,0:T(8,128)S(1)} %shard_map.88.before_ref, f32[4,16,128]{2,1,0:T(8,128)S(1)} %copy-done), custom_call_target="tpu_custom_call" | custom-call | flops 1879048192 | bytes 1048576 | tf_op jit(solution)/shard_map/pallas_call | solution.py:209
  36.6 0.7 collective-permute-start.1
  37.2 3.9 %collective-permute-start = (f32[28,4,128]{2,1,0:T(4,128)S(1)}, f32[28,4,128]{2,1,0:T(4,128)S(1)}, u32[]{:S(2)}, u32[]{:S(2)}) collective-permute-start(f32[28,4,128]{2,1,0:T(4,128)S(1)} %get-tuple-element.11), channel_id=1, source_target_pairs={{0,1},{2,3},{4,5},{6,7},{1,0},{3,2},{5,4},{7,6},{8,9},{10,11},{12,... | collective-permute-start | bytes 172040 | tf_op jit(solution)/shard_map/ppermute | solution.py:419
  41.1 2.2 %collective-permute-done.even_ref = f32[28,4,128]{2,1,0:T(4,128)S(1)} collective-permute-done((f32[28,4,128]{2,1,0:T(4,128)S(1)}, f32[28,4,128]{2,1,0:T(4,128)S(1)}, u32[]{:S(2)}, u32[]{:S(2)}) %collective-permute-start) | collective-permute-done | bytes 57376 | tf_op jit(solution)/shard_map/ppermute | solution.py:419
  43.3 0.0 collective-permute-done.1.odd_ref
  43.3 0.0 copy-start.1
  43.3 0.1 shard_map.90
  43.4 0.7 collective-permute-start.3
  44.1 2.0 %collective-permute-start.2 = (f32[7,78,128]{2,1,0:T(8,128)S(1)}, f32[7,78,128]{2,1,0:T(8,128)S(1)}, u32[]{:S(2)}, u32[]{:S(2)}) collective-permute-start(f32[7,78,128]{2,1,0:T(8,128)S(1)} %get-tuple-element.14), channel_id=1, source_target_pairs={{0,8},{16,24},{8,0},{24,16},{1,9},{17,25},{9,1},{25,17},{2,10},{18... | collective-permute-start | bytes 838664 | tf_op jit(solution)/shard_map/ppermute | solution.py:419
  46.0 1.2 %collective-permute-done.2.refs_1_ = f32[7,78,128]{2,1,0:T(8,128)S(1)} collective-permute-done((f32[7,78,128]{2,1,0:T(8,128)S(1)}, f32[7,78,128]{2,1,0:T(8,128)S(1)}, u32[]{:S(2)}, u32[]{:S(2)}) %collective-permute-start.2) | collective-permute-done | bytes 279584 | tf_op jit(solution)/shard_map/ppermute | solution.py:419
  47.2 0.0 collective-permute-done.3.refs_2_
  47.2 0.0 copy-done.1
  47.2 4.5 %shard_map.91 = (f32[7,4,16,128]{3,2,1,0:T(8,128)}, f32[192,128]{1,0:T(8,128)S(1)}) custom-call(f32[7,4,24,128]{3,2,1,0:T(8,128)S(1)} %get-tuple-element.13.refs_0_, f32[7,78,128]{2,1,0:T(8,128)S(1)} %collective-permute-done.2.refs_1_, f32[7,80,128]{2,1,0:T(8,128)S(1)} %collective-permute-done.3.refs_2_, f32[4,16,128]{2,1,0:T(8,128)S(1)} %copy-done, ...), custom_call_target="tpu_custom_call" | custom-call | tf_op jit(solution)/shard_map/pallas_call | solution.py:370
  51.8 0.0 copy-start.2
  51.8 14.8 %all_to_all.15 = f32[32,3,2,128]{3,2,1,0:T(2,128)S(1)} all-to-all(f32[32,3,2,128]{3,2,1,0:T(2,128)S(1)} %bitcast.12), channel_id=1, replica_groups=mesh['src'=4,'tgt'=8] {'src','tgt'}, dimensions={0} | all-to-all | bytes 196608 | tf_op jit(solution)/shard_map/all_to_all | solution.py:444
  66.5 0.0 copy-done.2
  66.5 2.3 %shard_map.92 = f32[3,8192]{1,0:T(4,128)} custom-call(f32[192,128]{1,0:T(8,128)S(1)} %bitcast.9, s32[1,8192]{1,0:T(1,128)S(1)} %copy-done.2), custom_call_target="tpu_custom_call" | custom-call | tf_op jit(solution)/shard_map/pallas_call | solution.py:405
Async XLA Ops:
  4.1 17.1 %all-to-all-start.1 = ((f32[32,7,2,128]{3,2,1,0:T(2,128)}), f32[32,7,2,128]{3,2,1,0:T(2,128)S(1)}, u32[]{:S(2)}, u32[]{:S(2)}) async-start(f32[32,7,2,128]{3,2,1,0:T(2,128)} %bitcast.16), calls=%async_computation.1 | async-start | bytes 458752 | tf_op jit(solution)/shard_map/all_to_all | solution.py:434
  21.2 2.7 %copy-start.3 = (s32[16384]{0:T(1024)S(1)}, s32[16384]{0:T(1024)}, u32[]{:S(2)}) copy-start(s32[16384]{0:T(1024)} %param.10) | copy-start | bytes 196612
  21.2 12.5 %all-to-all-start = ((f32[32,7,2,128]{3,2,1,0:T(2,128)}), f32[32,7,2,128]{3,2,1,0:T(2,128)S(1)}, u32[]{:S(2)}, u32[]{:S(2)}) async-start(f32[32,7,2,128]{3,2,1,0:T(2,128)} %bitcast.15), calls=%async_computation | async-start | bytes 458752 | tf_op jit(solution)/shard_map/all_to_all | solution.py:434
  23.9 9.8 %copy-start = (f32[4,16,128]{2,1,0:T(8,128)S(1)}, f32[4,16,128]{2,1,0:T(8,128)}, u32[]{:S(2)}) copy-start(f32[4,16,128]{2,1,0:T(8,128)} %refs_3_.1) | copy-start | bytes 98308
  36.6 6.7 %collective-permute-start.1 = (f32[29,4,128]{2,1,0:T(4,128)S(1)}, f32[29,4,128]{2,1,0:T(4,128)S(1)}, u32[]{:S(2)}, u32[]{:S(2)}) collective-permute-start(f32[29,4,128]{2,1,0:T(4,128)S(1)} %get-tuple-element.12), channel_id=1, source_target_pairs={{1,2},{3,4},{5,6},{2,1},{4,3},{6,5},{9,10},{11,12},{13,14},{10,9},... | collective-permute-start | bytes 178184 | tf_op jit(solution)/shard_map/ppermute | solution.py:419
  37.2 6.1 %collective-permute-start = (f32[28,4,128]{2,1,0:T(4,128)S(1)}, f32[28,4,128]{2,1,0:T(4,128)S(1)}, u32[]{:S(2)}, u32[]{:S(2)}) collective-permute-start(f32[28,4,128]{2,1,0:T(4,128)S(1)} %get-tuple-element.11), channel_id=1, source_target_pairs={{0,1},{2,3},{4,5},{6,7},{1,0},{3,2},{5,4},{7,6},{8,9},{10,11},{12,... | collective-permute-start | bytes 172040 | tf_op jit(solution)/shard_map/ppermute | solution.py:419
  43.3 3.9 %copy-start.1 = (s32[1,8192]{1,0:T(1,128)S(1)}, s32[1,8192]{1,0:T(1,128)}, u32[]{:S(2)}) copy-start(s32[1,8192]{1,0:T(1,128)} %refs_4_.1) | copy-start | bytes 98308
  43.4 3.9 %collective-permute-start.3 = (f32[7,80,128]{2,1,0:T(8,128)S(1)}, f32[7,80,128]{2,1,0:T(8,128)S(1)}, u32[]{:S(2)}, u32[]{:S(2)}) collective-permute-start(f32[7,80,128]{2,1,0:T(8,128)S(1)} %get-tuple-element.15), channel_id=1, source_target_pairs={{8,16},{16,8},{9,17},{17,9},{10,18},{18,10},{11,19},{19,11},{12,20... | collective-permute-start | bytes 860168 | tf_op jit(solution)/shard_map/ppermute | solution.py:419
  44.1 3.2 %collective-permute-start.2 = (f32[7,78,128]{2,1,0:T(8,128)S(1)}, f32[7,78,128]{2,1,0:T(8,128)S(1)}, u32[]{:S(2)}, u32[]{:S(2)}) collective-permute-start(f32[7,78,128]{2,1,0:T(8,128)S(1)} %get-tuple-element.14), channel_id=1, source_target_pairs={{0,8},{16,24},{8,0},{24,16},{1,9},{17,25},{9,1},{25,17},{2,10},{18... | collective-permute-start | bytes 838664 | tf_op jit(solution)/shard_map/ppermute | solution.py:419
  51.8 14.8 %copy-start.2 = (s32[1,8192]{1,0:T(1,128)S(1)}, s32[1,8192]{1,0:T(1,128)}, u32[]{:S(2)}) copy-start(s32[1,8192]{1,0:T(1,128)} %order_ref.1) | copy-start | bytes 98308

commit v7 on v5

--- a/solution.py
+++ b/solution.py
@@ -1,3 +1,5 @@
+import functools
+
 import numpy as np
 
 import jax
@@ -9,6 +11,8 @@
 
 ITERS = 4
 FIELDS = 7
+VMEM = 28 << 20
+READY = 16384
 SPAN = 512
 AT_ONCE = 8
 TOGETHER = 4
@@ -46,6 +50,10 @@
 def log2(n):
     assert n & (n - 1) == 0
     return n.bit_length() - 1
+
+
+def cost(flops):
+    return pl.CostEstimate(flops=flops, bytes_accessed=1 << 20, transcendentals=0)
 
 
 def row_ids(rows, lanes):
@@ -130,7 +138,43 @@
     )(fields, index, weight)
 
 
-def scatter_kernel(value_ref, target_ref, mass_ref, v_ref, even_ref, odd_ref, total):
+def cell_parts(cell, groups, hz):
+    return (cell >> log2(hz)) & (groups - 1), ((cell >> log2(groups * hz)) << log2(hz)) + (cell & (hz - 1))
+
+
+def prepare_kernel(groups, hz, target_ref, send_ref, place_ref, target_hot, send_hot, place_hot):
+    span = 1024
+    ids = row_ids(WIDE, span).astype(F32).astype(BF16)
+
+    def build(index_ref, hot_ref, low_of):
+        @pl.loop(0, hot_ref.shape[1] // span)
+        def _(n):
+            at = pl.ds(pl.multiple_of(n * span, span), span)
+            hot_ref[:, at] = low_onehot(low_of(index_ref[:, at]), ids)
+
+    def low_of_cell(cell):
+        return jnp.where(cell < 0, -1, cell_parts(cell, groups, hz)[1])
+
+    build(target_ref, target_hot, low_of_cell)
+    build(send_ref, send_hot, low_of_cell)
+    build(place_ref, place_hot, lambda index: index & (WIDE - 1))
+
+
+def prepare_call(target, send, place, mass):
+    hz = mass.shape[2]
+    columns = (min(target.shape[1], READY), send.shape[1], place.shape[1])
+    out = [jax.ShapeDtypeStruct((WIDE, n), BF16) for n in columns]
+    return pl.pallas_call(
+        functools.partial(prepare_kernel, mass.size // WIDE, hz),
+        out_shape=out,
+        in_specs=[pl.BlockSpec(memory_space=pltpu.VMEM)] * 3,
+        out_specs=[pl.BlockSpec(memory_space=pltpu.VMEM)] * 3,
+        compiler_params=pltpu.CompilerParams(vmem_limit_bytes=VMEM),
+        cost_estimate=cost(4 * 10**9),
+    )(target, send, place)
+
+
+def scatter_kernel(value_ref, target_ref, hot_ref, mass_ref, v_ref, even_ref, odd_ref, total):
     lanes = value_ref.shape[1]
     tiles = SPAN // lanes
     owners = target_ref.shape[1] // SPAN
@@ -138,17 +182,13 @@
     hx, hy, hz = mass_ref.shape
     groups = hx * hy * hz // WIDE
     total[...] = jnp.zeros_like(total)
-    ids = row_ids(WIDE, span).astype(F32).astype(BF16)
     group_ids = row_ids(groups, span).astype(F32).astype(BF16)
 
-    @pl.loop(0, owners // TOGETHER)
-    def _(p):
-        at = pl.multiple_of(p * span, span)
-        target = target_ref[:, pl.ds(at, span)]
-        low = ((target >> log2(groups * hz)) << log2(hz)) + (target & (hz - 1))
-        onehot = low_onehot(jnp.where(target < 0, -1, low), ids)
-        group = ((target >> log2(hz)) & (groups - 1)).astype(F32).astype(BF16)
-        here = group_ids == group
+    def step(p, onehot_at):
+        at = pl.ds(pl.multiple_of(p * span, span), span)
+        target = target_ref[:, at]
+        group, low = cell_parts(target, groups, hz)
+        here = group_ids == group.astype(F32).astype(BF16)
         row = p * (TOGETHER * FIELDS * tiles)
         pieces = [i * FIELDS * tiles + t for i in range(TOGETHER) for t in range(tiles)]
         value = jnp.concatenate([value_ref[pl.ds(row + i, FIELDS, stride=tiles), :] for i in pieces], axis=1)
@@ -157,7 +197,21 @@
             for f in range(FIELDS):
                 parts.append(jnp.where(here, half[f : f + 1], jnp.zeros((), BF16)))
         spread = jnp.concatenate(parts, axis=0)
+        onehot = onehot_at(at, jnp.where(target < 0, -1, low))
         total[...] += lax.dot_general(spread, onehot, NT, preferred_element_type=F32)
+
+    ready = hot_ref.shape[1] // span
+
+    @pl.loop(0, ready)
+    def _(p):
+        step(p, lambda at, low: hot_ref[:, at])
+
+    if ready < owners // TOGETHER:
+        ids = row_ids(WIDE, span).astype(F32).astype(BF16)
+
+        @pl.loop(ready, owners // TOGETHER)
+        def _(p):
+            step(p, lambda at, low: low_onehot(low, ids))
 
     odd_ref[FIELDS * hx] = jnp.zeros((ITERS, hz), F32)
     scale = lax.rsqrt(mass_ref[...])
@@ -175,7 +229,7 @@
                 odd_ref[f * hx + at] = jnp.where(odd, last, first)
 
 
-def scatter_call(values, target, mass):
+def scatter_call(values, target, hot, mass):
     hx, hy, hz = mass.shape
     groups = hx * hy * hz // WIDE
     even = jax.ShapeDtypeStruct((FIELDS * hx, ITERS, hz), F32)
@@ -183,16 +237,15 @@
     return pl.pallas_call(
         scatter_kernel,
         out_shape=(jax.ShapeDtypeStruct((FIELDS, hx, hy, hz), F32), even, odd),
-        in_specs=[pl.BlockSpec(memory_space=pltpu.VMEM)] * 3,
+        in_specs=[pl.BlockSpec(memory_space=pltpu.VMEM)] * 4,
         out_specs=(pl.BlockSpec(memory_space=pltpu.VMEM),) * 3,
         scratch_shapes=[pltpu.VMEM((2 * FIELDS * groups, WIDE), F32)],
-        compiler_params=pltpu.CompilerParams(vmem_limit_bytes=40 << 20),
-    )(values, target, mass)
-
-
-def lookup_rows(table, index, ids, group_ids, groups, at_parts):
-    group, low = at_parts(index)
-    got = jnp.dot(table, low_onehot(low, ids), preferred_element_type=F32)
+        compiler_params=pltpu.CompilerParams(vmem_limit_bytes=VMEM),
+    )(values, target, hot, mass)
+
+
+def lookup_rows(table, group, hot, group_ids, groups):
+    got = jnp.dot(table, hot, preferred_element_type=F32)
     here = group_ids == group
     rows = 3 * groups
     out = []
@@ -255,11 +308,13 @@
         out_shape=(jax.ShapeDtypeStruct((fields, hx, hy + 2 * ITERS, hz), F32), even_rows, odd_rows),
         in_specs=[pl.BlockSpec(memory_space=pltpu.VMEM)] * 3,
         out_specs=(pl.BlockSpec(memory_space=pltpu.VMEM),) * 3,
-        compiler_params=pltpu.CompilerParams(vmem_limit_bytes=40 << 20),
+        compiler_params=pltpu.CompilerParams(vmem_limit_bytes=VMEM),
     )(v, even, odd)
 
 
-def solve_kernel(mesh_shape, wide_ref, even_ref, odd_ref, mass_ref, order_ref, projected_ref, out_ref):
+def solve_kernel(
+    mesh_shape, wide_ref, even_ref, odd_ref, mass_ref, order_ref, hot_ref, projected_ref, out_ref
+):
     n_src, n_tgt = mesh_shape
     hx, hy, hz = mass_ref.shape
     k = ITERS
@@ -318,23 +373,20 @@
     payload = cell_moduli([projected_ref[f].reshape(hx * hy, hz) for f in range(FIELDS)])
     table = jnp.concatenate([jnp.concatenate([m[:groups], m[groups:]], axis=1) for m in payload], axis=0)
     table = jnp.concatenate(halves(table), axis=0)
-    ids = row_ids(WIDE, WIDE).astype(F32).astype(BF16)
     group_ids = row_ids(groups, WIDE)
 
-    def at_parts(index):
-        return (index >> log2(hz)) & (groups - 1), ((index >> log2(groups * hz)) << log2(hz)) + (index & (hz - 1))
-
-    @pl.loop(0, groups // 4)
+    @pl.loop(0, groups // 8)
     def _(q):
         lines = []
-        for i in range(4):
-            index = order_ref[:, pl.ds(pl.multiple_of((q * 4 + i) * WIDE, WIDE), WIDE)]
-            got = lookup_rows(table, index, ids, group_ids, groups, at_parts)
+        for i in range(8):
+            at = pl.ds(pl.multiple_of((q * 8 + i) * WIDE, WIDE), WIDE)
+            group, _ = cell_parts(order_ref[:, at], groups, hz)
+            got = lookup_rows(table, group, hot_ref[:, at], group_ids, groups)
             lines += [line[:, c * 128 : (c + 1) * 128] for line in got for c in range(2)]
-        out_ref[pl.ds(pl.multiple_of(q * 24, 8), 24), :] = jnp.concatenate(lines, axis=0)
-
-
-def solve_call(mesh_shape, wide, even, odd, mass, order):
+        out_ref[pl.ds(pl.multiple_of(q * 48, 8), 48), :] = jnp.concatenate(lines, axis=0)
+
+
+def solve_call(mesh_shape, wide, even, odd, mass, order, hot):
     hx, hy, hz = mass.shape
 
     def kernel(*refs):
@@ -346,13 +398,13 @@
             jax.ShapeDtypeStruct((FIELDS, hx, hy, hz), F32),
             jax.ShapeDtypeStruct((order.shape[1] // WIDE * 6, 128), F32),
         ),
-        in_specs=[pl.BlockSpec(memory_space=pltpu.VMEM)] * 5,
+        in_specs=[pl.BlockSpec(memory_space=pltpu.VMEM)] * 6,
         out_specs=(pl.BlockSpec(memory_space=pltpu.VMEM),) * 2,
-        compiler_params=pltpu.CompilerParams(vmem_limit_bytes=40 << 20),
-    )(wide, even, odd, mass, order)
-
-
-def place_kernel(arrived_ref, order_ref, out_ref):
+        compiler_params=pltpu.CompilerParams(vmem_limit_bytes=VMEM),
+    )(wide, even, odd, mass, order, hot)
+
+
+def place_kernel(arrived_ref, order_ref, hot_ref, out_ref):
     groups = arrived_ref.shape[0] // 6
     table = jnp.concatenate(
         [
@@ -362,26 +414,23 @@
         axis=0,
     )
     table = jnp.concatenate(halves(table), axis=0)
-    ids = row_ids(WIDE, WIDE).astype(F32).astype(BF16)
     group_ids = row_ids(groups, WIDE)
 
     @pl.loop(0, groups, unroll=8)
     def _(q):
         at = pl.ds(pl.multiple_of(q * WIDE, WIDE), WIDE)
-        got = lookup_rows(
-            table, order_ref[:, at], ids, group_ids, groups, lambda index: (index >> log2(WIDE), index & (WIDE - 1))
-        )
+        got = lookup_rows(table, order_ref[:, at] >> log2(WIDE), hot_ref[:, at], group_ids, groups)
         out_ref[:, at] = jnp.concatenate(got, axis=0)
 
 
-def place_call(arrived, order):
+def place_call(arrived, order, hot):
     return pl.pallas_call(
         place_kernel,
         out_shape=jax.ShapeDtypeStruct((3, order.shape[1]), F32),
-        in_specs=[pl.BlockSpec(memory_space=pltpu.VMEM)] * 2,
+        in_specs=[pl.BlockSpec(memory_space=pltpu.VMEM)] * 3,
         out_specs=pl.BlockSpec(memory_space=pltpu.VMEM),
-        compiler_params=pltpu.CompilerParams(vmem_limit_bytes=40 << 20),
-    )(arrived, order)
+        compiler_params=pltpu.CompilerParams(vmem_limit_bytes=VMEM),
+    )(arrived, order, hot)
 
 
 def swap(x, axis):
@@ -403,9 +452,11 @@
     values = gather_call(source_fields, slot_source.reshape(1, -1), slot_weight.reshape(1, -1))
     values = values.reshape(owners, FIELDS, SPAN // 128, 128)
     values = lax.all_to_all(values, both, split_axis=0, concat_axis=0, tiled=True).reshape(-1, 128)
-    v, even, odd = scatter_call(values, slot_target.reshape(1, -1), cell_mass)
+    target = slot_target.reshape(1, -1)
+    target_hot, send_hot, place_hot = prepare_call(target, send_order, place_order, cell_mass)
+    v, even, odd = scatter_call(values, target, target_hot, cell_mass)
     wide, even, odd = widen_call(v, *swap((even, odd), "tgt"))
-    projected, outgoing = solve_call((n_src, n_tgt), wide, *swap((even, odd), "src"), cell_mass, send_order)
+    projected, outgoing = solve_call((n_src, n_tgt), wide, *swap((even, odd), "src"), cell_mass, send_order, send_hot)
 
     if quota == WIDE:
         outgoing = outgoing.reshape(owners, 3, 2, 128)
@@ -416,7 +467,7 @@
         flat = lax.all_to_all(flat, both, split_axis=1, concat_axis=1, tiled=True)
         incoming = flat.reshape(3, groups, WIDE).transpose(1, 0, 2)
     incoming = incoming.reshape(-1, 128)
-    return projected, place_call(incoming, place_order)
+    return projected, place_call(incoming, place_order, place_hot)
 
 
 def solution(mesh):

time: 66.2 us -> 69.1 us (1.044)
  blocking collectives: 37.2 us -> 15 us
  local copies, waits for them, and re-layouts: 0.02 us -> 12.9 us
  starting transfers between devices: 6.81 us -> 14.4 us
  waiting for transfers between devices: 3.41 us -> 6.82 us
  Pallas kernels: 17.6 us -> 18.8 us
    all_to_all x1 -> x0, blocking collectives: 22.3 us -> none  [on_device(): lax.all_to_all(values, both, split_axis=0, concat_axis=0, tiled=True)]
    unnamed x8 -> x26, local copies, waits for them, and re-layouts: 0.02 us -> 12.9 us
    all_to_all x0 -> x1, starting transfers between devices: none -> 7.3 us  [on_device(): lax.all_to_all(values, both, split_axis=0, concat_axis=0, tiled=True)]
    all_to_all x0 -> x1, waiting for transfers between devices: none -> 3.41 us  [on_device(): lax.all_to_all(values, both, split_axis=0, concat_axis=0, tiled=True)]
    pallas_call x0 -> x1, Pallas kernels: none -> 2 us  [prepare_call(): pl.pallas_call(functools.partial(prepare_kernel, mass.size // WIDE, hz),...]
    pallas_call x1, Pallas kernels: 5.13 us -> 4.4 us  [solve_call(): pl.pallas_call(kernel, out_shape=(jax.ShapeDtypeStruct((FIELDS, hx, hy, h...]
  transfers between devices with their start and end apart: 4 -> 5, of which waited for: 2 -> 3; matrix products, arithmetic and copies ran while one was open for 0% -> 0% of each run, Pallas kernels for 0% -> 3%
where the time goes in v7:
time: 69.1 us; the launch traced here: 68.6 us
  Pallas kernels  18.8 us (27%)
  blocking collectives  15 us (22%)
  starting transfers between devices  14.4 us (21%)
  local copies, waits for them, and re-layouts  12.9 us (19%)
  waiting for transfers between devices  6.82 us (10%)
  between operations  0.73 us (1%)
    all_to_all x1, blocking collectives, on_device(): lax.all_to_all(outgoing, both, split_axis=0, concat_axis=0, tiled=True)  15 us
    unnamed x26, local copies, waits for them, and re-layouts  12.9 us
    all_to_all x1, starting transfers between devices, on_device(): lax.all_to_all(values, both, split_axis=0, concat_axis=0, tiled=True)  7.3 us
    ppermute x4, starting transfers between devices, swap(): out.append(lax.ppermute(part, axis, pairs + [(j, i) for i, j in pairs]))  7.09 us
    pallas_call x1, Pallas kernels, scatter_call(): pl.pallas_call(scatter_kernel, out_shape=(jax.ShapeDtypeStruct((FIELDS, h...  5.48 us
    pallas_call x1, Pallas kernels, gather_call(): pl.pallas_call(gather_kernel, out_shape=jax.ShapeDtypeStruct((rows, 128),...  4.55 us
    pallas_call x1, Pallas kernels, solve_call(): pl.pallas_call(kernel, out_shape=(jax.ShapeDtypeStruct((FIELDS, hx, hy, h...  4.4 us
    all_to_all x1, waiting for transfers between devices, on_device(): lax.all_to_all(values, both, split_axis=0, concat_axis=0, tiled=True)  3.41 us
  transfers between devices with their start and end apart: 5, of which 3 were waited for; matrix products, arithmetic and copies ran while one was open for 0% of the time, Pallas kernels for 3%

profile of v7, /device:TPU:0, one launch (start us, length us, event | category | flops | bytes accessed | tf_op | source)
XLA Modules:
  0.0 68.6 jit_solution(8222069955703844173)
XLA Ops:
  0.6 4.6 %shard_map.86 = f32[896,128]{1,0:T(8,128)} custom-call(f32[7,4096]{1,0:T(8,128)} %fields_hbm.1, s32[1,16384]{1,0:T(1,128)} %bitcast.13, f32[1,16384]{1,0:T(1,128)} %bitcast.14), custom_call_target="tpu_custom_call" | custom-call | tf_op jit(solution)/shard_map/pallas_call | solution.py:123
  5.2 7.3 %all-to-all-start = ((f32[32,7,4,128]{3,2,1,0:T(4,128)}), f32[32,7,4,128]{3,2,1,0:T(4,128)S(1)}, u32[]{:S(2)}, u32[]{:S(2)}) async-start(f32[32,7,4,128]{3,2,1,0:T(4,128)} %bitcast.12), calls=%async_computation | async-start | bytes 917504 | tf_op jit(solution)/shard_map/all_to_all | solution.py:454
  12.5 0.0 copy-start.7
  12.5 0.8 %copy-done.7 = s32[16384]{0:T(1024)S(1)} copy-done((s32[16384]{0:T(1024)S(1)}, s32[16384]{0:T(1024)}, u32[]{:S(2)}) %copy-start.7) | copy-done | bytes 65560
  13.3 0.8 %copy-done.9 = s32[1,8192]{1,0:T(1,128)S(1)} copy-done((s32[1,8192]{1,0:T(1,128)S(1)}, s32[1,8192]{1,0:T(1,128)}, u32[]{:S(2)}) %copy-start.9) | copy-done | bytes 32792
  14.1 0.8 %copy-done.11 = s32[1,8192]{1,0:T(1,128)S(1)} copy-done((s32[1,8192]{1,0:T(1,128)S(1)}, s32[1,8192]{1,0:T(1,128)}, u32[]{:S(2)}) %copy-start.11) | copy-done | bytes 32792
  14.9 2.0 %shard_map.87 = (bf16[256,16384]{1,0:T(8,128)(2,1)S(1)}, bf16[256,8192]{1,0:T(8,128)(2,1)S(1)}, bf16[256,8192]{1,0:T(8,128)(2,1)S(1)}) custom-call(s32[1,16384]{1,0:T(1,128)S(1)} %bitcast.10, s32[1,8192]{1,0:T(1,128)S(1)} %copy-done.9, s32[1,8192]{1,0:T(1,128)S(1)} %copy-done.11), custom_call_target="tpu_custom_call" | custom-call | flops 4000000000 | bytes 1048576 | tf_op jit(solution)/shard_map/pallas_call | solution.py:167
  16.9 0.0 copy-start
  16.9 3.2 %copy-done = bf16[256,16384]{1,0:T(8,128)(2,1)} copy-done((bf16[256,16384]{1,0:T(8,128)(2,1)}, bf16[256,16384]{1,0:T(8,128)(2,1)S(1)}, u32[]{:S(2)}) %copy-start) | copy-done | bytes 8388632
  20.1 2.0 %copy-done.2 = bf16[256,8192]{1,0:T(8,128)(2,1)} copy-done((bf16[256,8192]{1,0:T(8,128)(2,1)}, bf16[256,8192]{1,0:T(8,128)(2,1)S(1)}, u32[]{:S(2)}) %copy-start.2) | copy-done | bytes 4194328
  22.1 1.9 %copy-done.4 = bf16[256,8192]{1,0:T(8,128)(2,1)} copy-done((bf16[256,8192]{1,0:T(8,128)(2,1)}, bf16[256,8192]{1,0:T(8,128)(2,1)S(1)}, u32[]{:S(2)}) %copy-start.4) | copy-done | bytes 4194328
  24.0 3.4 %all-to-all-done = f32[32,7,4,128]{3,2,1,0:T(4,128)S(1)} async-done(((f32[32,7,4,128]{3,2,1,0:T(4,128)}), f32[32,7,4,128]{3,2,1,0:T(4,128)S(1)}, u32[]{:S(2)}, u32[]{:S(2)}) %all-to-all-start) | async-done | bytes 458784 | tf_op jit(solution)/shard_map/all_to_all | solution.py:454
  27.5 0.0 copy-done.6
  27.5 0.0 copy-done.8
  27.5 3.4 %copy-done.1 = bf16[256,16384]{1,0:T(8,128)(2,1)S(1)} copy-done((bf16[256,16384]{1,0:T(8,128)(2,1)S(1)}, bf16[256,16384]{1,0:T(8,128)(2,1)}, u32[]{:S(2)}) %copy-start.1) | copy-done | bytes 8388632
  30.8 5.5 %shard_map.88 = (f32[7,4,16,128]{3,2,1,0:T(8,128)S(1)}, f32[28,4,128]{2,1,0:T(4,128)S(1)}, f32[29,4,128]{2,1,0:T(4,128)S(1)}) custom-call(f32[896,128]{1,0:T(8,128)S(1)} %bitcast.7, s32[1,16384]{1,0:T(1,128)S(1)} %bitcast.11, bf16[256,16384]{1,0:T(8,128)(2,1)S(1)} %copy-done.1, f32[4,16,128]{2,1,0:T(8,128)S(1)} %copy-done.6), custom_call_target="tpu_custom_call" | custom-call | tf_op jit(solution)/shard_map/pallas_call | solution.py:237
  36.3 0.0 copy-start.5
  36.3 0.0 copy-start.12
  36.4 0.8 %collective-permute-start.1 = (f32[29,4,128]{2,1,0:T(4,128)S(1)}, f32[29,4,128]{2,1,0:T(4,128)S(1)}, u32[]{:S(2)}, u32[]{:S(2)}) collective-permute-start(f32[29,4,128]{2,1,0:T(4,128)S(1)} %get-tuple-element.16), channel_id=1, source_target_pairs={{1,2},{3,4},{5,6},{2,1},{4,3},{6,5},{9,10},{11,12},{13,14},{10,9},... | collective-permute-start | bytes 178184 | tf_op jit(solution)/shard_map/ppermute | solution.py:441
  37.2 3.6 %collective-permute-start = (f32[28,4,128]{2,1,0:T(4,128)S(1)}, f32[28,4,128]{2,1,0:T(4,128)S(1)}, u32[]{:S(2)}, u32[]{:S(2)}) collective-permute-start(f32[28,4,128]{2,1,0:T(4,128)S(1)} %get-tuple-element.15), channel_id=1, source_target_pairs={{0,1},{2,3},{4,5},{6,7},{1,0},{3,2},{5,4},{7,6},{8,9},{10,11},{12,... | collective-permute-start | bytes 172040 | tf_op jit(solution)/shard_map/ppermute | solution.py:441
  40.8 2.2 %collective-permute-done.even_ref = f32[28,4,128]{2,1,0:T(4,128)S(1)} collective-permute-done((f32[28,4,128]{2,1,0:T(4,128)S(1)}, f32[28,4,128]{2,1,0:T(4,128)S(1)}, u32[]{:S(2)}, u32[]{:S(2)}) %collective-permute-start) | collective-permute-done | bytes 57376 | tf_op jit(solution)/shard_map/ppermute | solution.py:441
  43.0 0.0 collective-permute-done.1.odd_ref
  43.0 0.1 shard_map.89
  43.1 0.7 collective-permute-start.3
  43.8 2.0 %collective-permute-start.2 = (f32[7,78,128]{2,1,0:T(8,128)S(1)}, f32[7,78,128]{2,1,0:T(8,128)S(1)}, u32[]{:S(2)}, u32[]{:S(2)}) collective-permute-start(f32[7,78,128]{2,1,0:T(8,128)S(1)} %get-tuple-element.18), channel_id=1, source_target_pairs={{0,8},{16,24},{8,0},{24,16},{1,9},{17,25},{9,1},{25,17},{2,10},{18... | collective-permute-start | bytes 838664 | tf_op jit(solution)/shard_map/ppermute | solution.py:441
  45.7 1.2 %collective-permute-done.2.refs_1_ = f32[7,78,128]{2,1,0:T(8,128)S(1)} collective-permute-done((f32[7,78,128]{2,1,0:T(8,128)S(1)}, f32[7,78,128]{2,1,0:T(8,128)S(1)}, u32[]{:S(2)}, u32[]{:S(2)}) %collective-permute-start.2) | collective-permute-done | bytes 279584 | tf_op jit(solution)/shard_map/ppermute | solution.py:441
  46.9 0.0 collective-permute-done.3.refs_2_
  46.9 0.0 copy-done.10
  46.9 4.4 %shard_map.90 = (f32[7,4,16,128]{3,2,1,0:T(8,128)}, f32[192,128]{1,0:T(8,128)S(1)}) custom-call(f32[7,4,24,128]{3,2,1,0:T(8,128)S(1)} %get-tuple-element.17.refs_0_, f32[7,78,128]{2,1,0:T(8,128)S(1)} %collective-permute-done.2.refs_1_, f32[7,80,128]{2,1,0:T(8,128)S(1)} %collective-permute-done.3.refs_2_, f32[4,16,128]{2,1,0:T(8,128)S(1)} %copy-done.6, ...), custom_call_target="tpu_custom_call" | custom-call | tf_op jit(solution)/shard_map/pallas_call | solution.py:395
  51.3 15.0 %all_to_all.10 = f32[32,3,2,128]{3,2,1,0:T(2,128)S(1)} all-to-all(f32[32,3,2,128]{3,2,1,0:T(2,128)S(1)} %bitcast.9), channel_id=1, replica_groups=mesh['src'=4,'tgt'=8] {'src','tgt'}, dimensions={0} | all-to-all | bytes 196608 | tf_op jit(solution)/shard_map/all_to_all | solution.py:463
  66.3 0.0 copy-done.5
  66.3 2.3 %shard_map.91 = f32[3,8192]{1,0:T(4,128)} custom-call(f32[192,128]{1,0:T(8,128)S(1)} %bitcast.8, s32[1,8192]{1,0:T(1,128)S(1)} %copy-done.12, bf16[256,8192]{1,0:T(8,128)(2,1)S(1)} %copy-done.5), custom_call_target="tpu_custom_call" | custom-call | tf_op jit(solution)/shard_map/pallas_call | solution.py:427
  (11 shorter events, 0.0 us)
Async XLA Ops:
  5.2 22.3 %all-to-all-start = ((f32[32,7,4,128]{3,2,1,0:T(4,128)}), f32[32,7,4,128]{3,2,1,0:T(4,128)S(1)}, u32[]{:S(2)}, u32[]{:S(2)}) async-start(f32[32,7,4,128]{3,2,1,0:T(4,128)} %bitcast.12), calls=%async_computation | async-start | bytes 917504 | tf_op jit(solution)/shard_map/all_to_all | solution.py:454
  12.5 0.8 %copy-start.7 = (s32[16384]{0:T(1024)S(1)}, s32[16384]{0:T(1024)}, u32[]{:S(2)}) copy-start(s32[16384]{0:T(1024)} %param.10) | copy-start | bytes 196612
  13.3 0.8 %copy-start.9 = (s32[1,8192]{1,0:T(1,128)S(1)}, s32[1,8192]{1,0:T(1,128)}, u32[]{:S(2)}) copy-start(s32[1,8192]{1,0:T(1,128)} %refs_4_.1) | copy-start | bytes 98308
  14.1 0.8 %copy-start.11 = (s32[1,8192]{1,0:T(1,128)S(1)}, s32[1,8192]{1,0:T(1,128)}, u32[]{:S(2)}) copy-start(s32[1,8192]{1,0:T(1,128)} %order_ref.1) | copy-start | bytes 98308
  14.9 12.6 %copy-start.6 = (f32[4,16,128]{2,1,0:T(8,128)S(1)}, f32[4,16,128]{2,1,0:T(8,128)}, u32[]{:S(2)}) copy-start(f32[4,16,128]{2,1,0:T(8,128)} %refs_3_.1) | copy-start | bytes 98308
  14.9 12.6 %copy-start.8 = (s32[16384]{0:T(1024)S(1)}, s32[16384]{0:T(1024)}, u32[]{:S(2)}) copy-start(s32[16384]{0:T(1024)} %param.10) | copy-start | bytes 196612
  16.9 3.3 %copy-start = (bf16[256,16384]{1,0:T(8,128)(2,1)}, bf16[256,16384]{1,0:T(8,128)(2,1)S(1)}, u32[]{:S(2)}) copy-start(bf16[256,16384]{1,0:T(8,128)(2,1)S(1)} %get-tuple-element.13.hot_ref) | copy-start | bytes 25165828
  20.1 2.0 %copy-start.2 = (bf16[256,8192]{1,0:T(8,128)(2,1)}, bf16[256,8192]{1,0:T(8,128)(2,1)S(1)}, u32[]{:S(2)}) copy-start(bf16[256,8192]{1,0:T(8,128)(2,1)S(1)} %get-tuple-element.20.refs_5_) | copy-start | bytes 12582916
  22.1 1.9 %copy-start.4 = (bf16[256,8192]{1,0:T(8,128)(2,1)}, bf16[256,8192]{1,0:T(8,128)(2,1)S(1)}, u32[]{:S(2)}) copy-start(bf16[256,8192]{1,0:T(8,128)(2,1)S(1)} %get-tuple-element.23.hot_ref) | copy-start | bytes 12582916
  27.5 3.4 %copy-start.1 = (bf16[256,16384]{1,0:T(8,128)(2,1)S(1)}, bf16[256,16384]{1,0:T(8,128)(2,1)}, u32[]{:S(2)}) copy-start(bf16[256,16384]{1,0:T(8,128)(2,1)} %copy-done) | copy-start | bytes 25165828
  30.8 16.1 %copy-start.3 = (bf16[256,8192]{1,0:T(8,128)(2,1)S(1)}, bf16[256,8192]{1,0:T(8,128)(2,1)}, u32[]{:S(2)}) copy-start(bf16[256,8192]{1,0:T(8,128)(2,1)} %copy-done.2) | copy-start | bytes 12582916
  30.8 16.1 %copy-start.10 = (s32[1,8192]{1,0:T(1,128)S(1)}, s32[1,8192]{1,0:T(1,128)}, u32[]{:S(2)}) copy-start(s32[1,8192]{1,0:T(1,128)} %refs_4_.1) | copy-start | bytes 98308
  36.3 30.0 %copy-start.5 = (bf16[256,8192]{1,0:T(8,128)(2,1)S(1)}, bf16[256,8192]{1,0:T(8,128)(2,1)}, u32[]{:S(2)}) copy-start(bf16[256,8192]{1,0:T(8,128)(2,1)} %copy-done.4) | copy-start | bytes 12582916
  36.3 30.0 %copy-start.12 = (s32[1,8192]{1,0:T(1,128)S(1)}, s32[1,8192]{1,0:T(1,128)}, u32[]{:S(2)}) copy-start(s32[1,8192]{1,0:T(1,128)} %order_ref.1) | copy-start | bytes 98308
  36.4 6.6 %collective-permute-start.1 = (f32[29,4,128]{2,1,0:T(4,128)S(1)}, f32[29,4,128]{2,1,0:T(4,128)S(1)}, u32[]{:S(2)}, u32[]{:S(2)}) collective-permute-start(f32[29,4,128]{2,1,0:T(4,128)S(1)} %get-tuple-element.16), channel_id=1, source_target_pairs={{1,2},{3,4},{5,6},{2,1},{4,3},{6,5},{9,10},{11,12},{13,14},{10,9},... | collective-permute-start | bytes 178184 | tf_op jit(solution)/shard_map/ppermute | solution.py:441
  37.2 5.8 %collective-permute-start = (f32[28,4,128]{2,1,0:T(4,128)S(1)}, f32[28,4,128]{2,1,0:T(4,128)S(1)}, u32[]{:S(2)}, u32[]{:S(2)}) collective-permute-start(f32[28,4,128]{2,1,0:T(4,128)S(1)} %get-tuple-element.15), channel_id=1, source_target_pairs={{0,1},{2,3},{4,5},{6,7},{1,0},{3,2},{5,4},{7,6},{8,9},{10,11},{12,... | collective-permute-start | bytes 172040 | tf_op jit(solution)/shard_map/ppermute | solution.py:441
  43.1 3.9 %collective-permute-start.3 = (f32[7,80,128]{2,1,0:T(8,128)S(1)}, f32[7,80,128]{2,1,0:T(8,128)S(1)}, u32[]{:S(2)}, u32[]{:S(2)}) collective-permute-start(f32[7,80,128]{2,1,0:T(8,128)S(1)} %get-tuple-element.19), channel_id=1, source_target_pairs={{8,16},{16,8},{9,17},{17,9},{10,18},{18,10},{11,19},{19,11},{12,20... | collective-permute-start | bytes 860168 | tf_op jit(solution)/shard_map/ppermute | solution.py:441
  43.8 3.2 %collective-permute-start.2 = (f32[7,78,128]{2,1,0:T(8,128)S(1)}, f32[7,78,128]{2,1,0:T(8,128)S(1)}, u32[]{:S(2)}, u32[]{:S(2)}) collective-permute-start(f32[7,78,128]{2,1,0:T(8,128)S(1)} %get-tuple-element.18), channel_id=1, source_target_pairs={{0,8},{16,24},{8,0},{24,16},{1,9},{17,25},{9,1},{25,17},{2,10},{18... | collective-permute-start | bytes 838664 | tf_op jit(solution)/shard_map/ppermute | solution.py:441

commit v8 on v5

--- a/solution.py
+++ b/solution.py
@@ -11,7 +11,7 @@
 FIELDS = 7
 SPAN = 512
 AT_ONCE = 8
-TOGETHER = 4
+TOGETHER = 8
 WIDE = 256
 BF16 = jnp.bfloat16
 F32 = jnp.float32
@@ -98,11 +98,12 @@
         part = pl.ds(pl.multiple_of(n * rows, 8), rows)
         return pltpu.make_async_copy(out_ref.at[part], out_hbm.at[part], done.at[n])
 
-    @pl.loop(0, owners // AT_ONCE)
-    def _(n):
-        for i in range(AT_ONCE):
-            one_owner(n * AT_ONCE + i)
-        send_off(n).start()
+    @pl.loop(0, owners // AT_ONCE // 4)
+    def _(m):
+        for j in range(4):
+            for i in range(AT_ONCE):
+                one_owner((m * 4 + j) * AT_ONCE + i)
+            send_off(m * 4 + j).start()
 
     @pl.loop(0, owners // AT_ONCE)
     def _(n):
@@ -324,14 +325,13 @@
     def at_parts(index):
         return (index >> log2(hz)) & (groups - 1), ((index >> log2(groups * hz)) << log2(hz)) + (index & (hz - 1))
 
-    @pl.loop(0, groups // 4)
-    def _(q):
+    for q in range(0, groups, 4):
         lines = []
-        for i in range(4):
-            index = order_ref[:, pl.ds(pl.multiple_of((q * 4 + i) * WIDE, WIDE), WIDE)]
+        for i in range(q, q + 4):
+            index = order_ref[:, i * WIDE : (i + 1) * WIDE]
             got = lookup_rows(table, index, ids, group_ids, groups, at_parts)
             lines += [line[:, c * 128 : (c + 1) * 128] for line in got for c in range(2)]
-        out_ref[pl.ds(pl.multiple_of(q * 24, 8), 24), :] = jnp.concatenate(lines, axis=0)
+        out_ref[q * 6 : q * 6 + 24, :] = jnp.concatenate(lines, axis=0)
 
 
 def solve_call(mesh_shape, wide, even, odd, mass, order):
@@ -365,9 +365,8 @@
     ids = row_ids(WIDE, WIDE).astype(F32).astype(BF16)
     group_ids = row_ids(groups, WIDE)
 
-    @pl.loop(0, groups, unroll=8)
-    def _(q):
-        at = pl.ds(pl.multiple_of(q * WIDE, WIDE), WIDE)
+    for q in range(groups):
+        at = pl.ds(q * WIDE, WIDE)
         got = lookup_rows(
             table, order_ref[:, at], ids, group_ids, groups, lambda index: (index >> log2(WIDE), index & (WIDE - 1))
         )

time: 66.2 us -> 62.4 us (0.943)
  Pallas kernels: 17.6 us -> 13.8 us
    pallas_call x1, Pallas kernels: 5.13 us -> 3.35 us  [solve_call(): pl.pallas_call(kernel, out_shape=(jax.ShapeDtypeStruct((FIELDS, hx, hy, h...]
    pallas_call x1, Pallas kernels: 5.58 us -> 4.71 us  [scatter_call(): pl.pallas_call(scatter_kernel, out_shape=(jax.ShapeDtypeStruct((FIELDS, h...]
where the time goes in v8:
time: 62.4 us; the launch traced here: 62 us
  blocking collectives  37.2 us (60%)
  Pallas kernels  13.8 us (22%)
  starting transfers between devices  6.81 us (11%)
  waiting for transfers between devices  3.41 us (5%)
  between operations  0.7 us (1%)
    all_to_all x1, blocking collectives, on_device(): lax.all_to_all(values, both, split_axis=0, concat_axis=0, tiled=True)  22.3 us
    all_to_all x1, blocking collectives, on_device(): lax.all_to_all(outgoing, both, split_axis=0, concat_axis=0, tiled=True)  15 us
    ppermute x4, starting transfers between devices, swap(): out.append(lax.ppermute(part, axis, pairs + [(j, i) for i, j in pairs]))  6.81 us
    pallas_call x1, Pallas kernels, scatter_call(): pl.pallas_call(scatter_kernel, out_shape=(jax.ShapeDtypeStruct((FIELDS, h...  4.71 us
    pallas_call x1, Pallas kernels, gather_call(): pl.pallas_call(gather_kernel, out_shape=jax.ShapeDtypeStruct((rows, 128),...  4 us
    ppermute x4, waiting for transfers between devices, swap(): out.append(lax.ppermute(part, axis, pairs + [(j, i) for i, j in pairs]))  3.41 us
    pallas_call x1, Pallas kernels, solve_call(): pl.pallas_call(kernel, out_shape=(jax.ShapeDtypeStruct((FIELDS, hx, hy, h...  3.35 us
    pallas_call x1, Pallas kernels, place_call(): pl.pallas_call(place_kernel, out_shape=jax.ShapeDtypeStruct((3, order.sha...  1.68 us
  transfers between devices with their start and end apart: 4, of which 2 were waited for; matrix products, arithmetic and copies ran while one was open for 0% of the time, Pallas kernels for 0%

profile of v8, /device:TPU:0, one launch (start us, length us, event | category | flops | bytes accessed | tf_op | source)
XLA Modules:
  0.0 62.0 jit_solution(2378164689704661008)
XLA Ops:
  0.6 4.0 %shard_map.86 = f32[896,128]{1,0:T(8,128)} custom-call(f32[7,4096]{1,0:T(8,128)} %fields_hbm.1, s32[1,16384]{1,0:T(1,128)} %bitcast.12, f32[1,16384]{1,0:T(1,128)} %bitcast.13), custom_call_target="tpu_custom_call" | custom-call | tf_op jit(solution)/shard_map/pallas_call | solution.py:116
  4.6 0.0 copy-start
  4.7 0.0 copy-start.1
  4.7 22.3 %all_to_all.10 = f32[32,7,4,128]{3,2,1,0:T(4,128)S(1)} all-to-all(f32[32,7,4,128]{3,2,1,0:T(4,128)} %bitcast.11), channel_id=1, replica_groups=mesh['src'=4,'tgt'=8] {'src','tgt'}, dimensions={0} | all-to-all | bytes 917504 | tf_op jit(solution)/shard_map/all_to_all | solution.py:404
  26.9 0.0 copy-done
  26.9 0.0 copy-done.1
  26.9 4.7 %shard_map.87 = (f32[7,4,16,128]{3,2,1,0:T(8,128)S(1)}, f32[28,4,128]{2,1,0:T(4,128)S(1)}, f32[29,4,128]{2,1,0:T(4,128)S(1)}) custom-call(f32[896,128]{1,0:T(8,128)S(1)} %bitcast.7, s32[1,16384]{1,0:T(1,128)S(1)} %bitcast.10, f32[4,16,128]{2,1,0:T(8,128)S(1)} %copy-done), custom_call_target="tpu_custom_call" | custom-call | tf_op jit(solution)/shard_map/pallas_call | solution.py:184
  31.7 0.7 %collective-permute-start.1 = (f32[29,4,128]{2,1,0:T(4,128)S(1)}, f32[29,4,128]{2,1,0:T(4,128)S(1)}, u32[]{:S(2)}, u32[]{:S(2)}) collective-permute-start(f32[29,4,128]{2,1,0:T(4,128)S(1)} %get-tuple-element.12), channel_id=1, source_target_pairs={{1,2},{3,4},{5,6},{2,1},{4,3},{6,5},{9,10},{11,12},{13,14},{10,9},... | collective-permute-start | bytes 178184 | tf_op jit(solution)/shard_map/ppermute | solution.py:391
  32.3 3.5 %collective-permute-start = (f32[28,4,128]{2,1,0:T(4,128)S(1)}, f32[28,4,128]{2,1,0:T(4,128)S(1)}, u32[]{:S(2)}, u32[]{:S(2)}) collective-permute-start(f32[28,4,128]{2,1,0:T(4,128)S(1)} %get-tuple-element.11), channel_id=1, source_target_pairs={{0,1},{2,3},{4,5},{6,7},{1,0},{3,2},{5,4},{7,6},{8,9},{10,11},{12,... | collective-permute-start | bytes 172040 | tf_op jit(solution)/shard_map/ppermute | solution.py:391
  35.8 2.2 %collective-permute-done.even_ref = f32[28,4,128]{2,1,0:T(4,128)S(1)} collective-permute-done((f32[28,4,128]{2,1,0:T(4,128)S(1)}, f32[28,4,128]{2,1,0:T(4,128)S(1)}, u32[]{:S(2)}, u32[]{:S(2)}) %collective-permute-start) | collective-permute-done | bytes 57376 | tf_op jit(solution)/shard_map/ppermute | solution.py:391
  38.0 0.0 collective-permute-done.1.odd_ref
  38.0 0.0 copy-start.2
  38.0 0.1 shard_map.88
  38.1 0.7 %collective-permute-start.3 = (f32[7,80,128]{2,1,0:T(8,128)S(1)}, f32[7,80,128]{2,1,0:T(8,128)S(1)}, u32[]{:S(2)}, u32[]{:S(2)}) collective-permute-start(f32[7,80,128]{2,1,0:T(8,128)S(1)} %get-tuple-element.15), channel_id=1, source_target_pairs={{8,16},{16,8},{9,17},{17,9},{10,18},{18,10},{11,19},{19,11},{12,20... | collective-permute-start | bytes 860168 | tf_op jit(solution)/shard_map/ppermute | solution.py:391
  38.8 2.0 %collective-permute-start.2 = (f32[7,78,128]{2,1,0:T(8,128)S(1)}, f32[7,78,128]{2,1,0:T(8,128)S(1)}, u32[]{:S(2)}, u32[]{:S(2)}) collective-permute-start(f32[7,78,128]{2,1,0:T(8,128)S(1)} %get-tuple-element.14), channel_id=1, source_target_pairs={{0,8},{16,24},{8,0},{24,16},{1,9},{17,25},{9,1},{25,17},{2,10},{18... | collective-permute-start | bytes 838664 | tf_op jit(solution)/shard_map/ppermute | solution.py:391
  40.8 1.2 %collective-permute-done.2.refs_1_ = f32[7,78,128]{2,1,0:T(8,128)S(1)} collective-permute-done((f32[7,78,128]{2,1,0:T(8,128)S(1)}, f32[7,78,128]{2,1,0:T(8,128)S(1)}, u32[]{:S(2)}, u32[]{:S(2)}) %collective-permute-start.2) | collective-permute-done | bytes 279584 | tf_op jit(solution)/shard_map/ppermute | solution.py:391
  42.0 0.0 collective-permute-done.3.refs_2_
  42.0 0.0 copy-done.2
  42.0 3.3 %shard_map.89 = (f32[7,4,16,128]{3,2,1,0:T(8,128)}, f32[192,128]{1,0:T(8,128)S(1)}) custom-call(f32[7,4,24,128]{3,2,1,0:T(8,128)S(1)} %get-tuple-element.13.refs_0_, f32[7,78,128]{2,1,0:T(8,128)S(1)} %collective-permute-done.2.refs_1_, f32[7,80,128]{2,1,0:T(8,128)S(1)} %collective-permute-done.3.refs_2_, f32[4,16,128]{2,1,0:T(8,128)S(1)} %copy-done, ...), custom_call_target="tpu_custom_call" | custom-call | tf_op jit(solution)/shard_map/pallas_call | solution.py:343
  45.3 0.0 copy-start.3
  45.3 15.0 %all_to_all.11 = f32[32,3,2,128]{3,2,1,0:T(2,128)S(1)} all-to-all(f32[32,3,2,128]{3,2,1,0:T(2,128)S(1)} %bitcast.9), channel_id=1, replica_groups=mesh['src'=4,'tgt'=8] {'src','tgt'}, dimensions={0} | all-to-all | bytes 196608 | tf_op jit(solution)/shard_map/all_to_all | solution.py:411
  60.3 0.0 copy-done.3
  60.3 1.7 %shard_map.90 = f32[3,8192]{1,0:T(4,128)} custom-call(f32[192,128]{1,0:T(8,128)S(1)} %bitcast.8, s32[1,8192]{1,0:T(1,128)S(1)} %copy-done.3), custom_call_target="tpu_custom_call" | custom-call | tf_op jit(solution)/shard_map/pallas_call | solution.py:377
Async XLA Ops:
  4.6 22.3 %copy-start = (f32[4,16,128]{2,1,0:T(8,128)S(1)}, f32[4,16,128]{2,1,0:T(8,128)}, u32[]{:S(2)}) copy-start(f32[4,16,128]{2,1,0:T(8,128)} %refs_3_.1) | copy-start | bytes 98308
  4.7 22.3 %copy-start.1 = (s32[16384]{0:T(1024)S(1)}, s32[16384]{0:T(1024)}, u32[]{:S(2)}) copy-start(s32[16384]{0:T(1024)} %param.10) | copy-start | bytes 196612
  31.7 6.4 %collective-permute-start.1 = (f32[29,4,128]{2,1,0:T(4,128)S(1)}, f32[29,4,128]{2,1,0:T(4,128)S(1)}, u32[]{:S(2)}, u32[]{:S(2)}) collective-permute-start(f32[29,4,128]{2,1,0:T(4,128)S(1)} %get-tuple-element.12), channel_id=1, source_target_pairs={{1,2},{3,4},{5,6},{2,1},{4,3},{6,5},{9,10},{11,12},{13,14},{10,9},... | collective-permute-start | bytes 178184 | tf_op jit(solution)/shard_map/ppermute | solution.py:391
  32.3 5.7 %collective-permute-start = (f32[28,4,128]{2,1,0:T(4,128)S(1)}, f32[28,4,128]{2,1,0:T(4,128)S(1)}, u32[]{:S(2)}, u32[]{:S(2)}) collective-permute-start(f32[28,4,128]{2,1,0:T(4,128)S(1)} %get-tuple-element.11), channel_id=1, source_target_pairs={{0,1},{2,3},{4,5},{6,7},{1,0},{3,2},{5,4},{7,6},{8,9},{10,11},{12,... | collective-permute-start | bytes 172040 | tf_op jit(solution)/shard_map/ppermute | solution.py:391
  38.0 3.9 %copy-start.2 = (s32[1,8192]{1,0:T(1,128)S(1)}, s32[1,8192]{1,0:T(1,128)}, u32[]{:S(2)}) copy-start(s32[1,8192]{1,0:T(1,128)} %refs_4_.1) | copy-start | bytes 98308
  38.1 3.9 %collective-permute-start.3 = (f32[7,80,128]{2,1,0:T(8,128)S(1)}, f32[7,80,128]{2,1,0:T(8,128)S(1)}, u32[]{:S(2)}, u32[]{:S(2)}) collective-permute-start(f32[7,80,128]{2,1,0:T(8,128)S(1)} %get-tuple-element.15), channel_id=1, source_target_pairs={{8,16},{16,8},{9,17},{17,9},{10,18},{18,10},{11,19},{19,11},{12,20... | collective-permute-start | bytes 860168 | tf_op jit(solution)/shard_map/ppermute | solution.py:391
  38.8 3.2 %collective-permute-start.2 = (f32[7,78,128]{2,1,0:T(8,128)S(1)}, f32[7,78,128]{2,1,0:T(8,128)S(1)}, u32[]{:S(2)}, u32[]{:S(2)}) collective-permute-start(f32[7,78,128]{2,1,0:T(8,128)S(1)} %get-tuple-element.14), channel_id=1, source_target_pairs={{0,8},{16,24},{8,0},{24,16},{1,9},{17,25},{9,1},{25,17},{2,10},{18... | collective-permute-start | bytes 838664 | tf_op jit(solution)/shard_map/ppermute | solution.py:391
  45.3 15.0 %copy-start.3 = (s32[1,8192]{1,0:T(1,128)S(1)}, s32[1,8192]{1,0:T(1,128)}, u32[]{:S(2)}) copy-start(s32[1,8192]{1,0:T(1,128)} %order_ref.1) | copy-start | bytes 98308

commit v9 on v8

--- a/solution.py
+++ b/solution.py
@@ -9,6 +9,7 @@
 
 ITERS = 4
 FIELDS = 7
+PIECES = 4
 SPAN = 512
 AT_ONCE = 8
 TOGETHER = 8
@@ -142,8 +143,7 @@
     ids = row_ids(WIDE, span).astype(F32).astype(BF16)
     group_ids = row_ids(groups, span).astype(F32).astype(BF16)
 
-    @pl.loop(0, owners // TOGETHER)
-    def _(p):
+    def step(p):
         at = pl.multiple_of(p * span, span)
         target = target_ref[:, pl.ds(at, span)]
         low = ((target >> log2(groups * hz)) << log2(hz)) + (target & (hz - 1))
@@ -159,6 +159,11 @@
                 parts.append(jnp.where(here, half[f : f + 1], jnp.zeros((), BF16)))
         spread = jnp.concatenate(parts, axis=0)
         total[...] += lax.dot_general(spread, onehot, NT, preferred_element_type=F32)
+
+    @pl.loop(0, owners // TOGETHER // 4)
+    def _(n):
+        for i in range(4):
+            step(n * 4 + i)
 
     odd_ref[FIELDS * hx] = jnp.zeros((ITERS, hz), F32)
     scale = lax.rsqrt(mass_ref[...])
@@ -260,7 +265,7 @@
     )(v, even, odd)
 
 
-def solve_kernel(mesh_shape, wide_ref, even_ref, odd_ref, mass_ref, order_ref, projected_ref, out_ref):
+def solve_kernel(mesh_shape, wide_ref, even_ref, odd_ref, mass_ref, order_ref, projected_hbm, out_ref, projected_ref, sem):
     n_src, n_tgt = mesh_shape
     hx, hy, hz = mass_ref.shape
     k = ITERS
@@ -300,21 +305,26 @@
         for sweep in range(1, k + 1):
             new = list(u)
             for x in range(sweep, hx + 2 * k - sweep):
+                far = max(k - x, x - (k + hx - 1), 0)
+                n = rows if sweep + far < k else hy
                 w = u[x]
-                near = u[x - 1] + u[x + 1]
-                near = near + pltpu.roll(w, 1, 0) + pltpu.roll(w, rows - 1, 0)
-                near = near + pltpu.roll(w, 1, 1) * not_first + pltpu.roll(w, hz - 1, 1) * not_last
+                near = u[x - 1][:n] + u[x + 1][:n]
+                near = near + pltpu.roll(w, 1, 0)[:n] + pltpu.roll(w, rows - 1, 0)[:n]
+                w = w[:n]
+                near = near + pltpu.roll(w, 1, 1) * not_first[:n] + pltpu.roll(w, hz - 1, 1) * not_last[:n]
                 if x < k:
-                    near = near * inside_left
-                elif x < k + hx:
+                    near = near * inside_left[:n]
+                elif x >= k + hx:
+                    near = near * inside_right[:n]
+                elif n > hy:
                     near = near * inside
-                else:
-                    near = near * inside_right
-                new[x] = COEFS[k - sweep] * base[x] + near
+                new[x] = COEFS[k - sweep] * base[x][:n] + near
             u = new
         for x in range(hx):
             projected_ref[f, x] = u[k + x][:hy] * scale[x]
 
+    leave = pltpu.make_async_copy(projected_ref, projected_hbm, sem)
+    leave.start()
     groups = hx * hy * hz // WIDE
     payload = cell_moduli([projected_ref[f].reshape(hx * hy, hz) for f in range(FIELDS)])
     table = jnp.concatenate([jnp.concatenate([m[:groups], m[groups:]], axis=1) for m in payload], axis=0)
@@ -332,6 +342,7 @@
             got = lookup_rows(table, index, ids, group_ids, groups, at_parts)
             lines += [line[:, c * 128 : (c + 1) * 128] for line in got for c in range(2)]
         out_ref[q * 6 : q * 6 + 24, :] = jnp.concatenate(lines, axis=0)
+    leave.wait()
 
 
 def solve_call(mesh_shape, wide, even, odd, mass, order):
@@ -347,12 +358,13 @@
             jax.ShapeDtypeStruct((order.shape[1] // WIDE * 6, 128), F32),
         ),
         in_specs=[pl.BlockSpec(memory_space=pltpu.VMEM)] * 5,
-        out_specs=(pl.BlockSpec(memory_space=pltpu.VMEM),) * 2,
+        out_specs=(pl.BlockSpec(memory_space=pltpu.HBM), pl.BlockSpec(memory_space=pltpu.VMEM)),
+        scratch_shapes=[pltpu.VMEM((FIELDS, hx, hy, hz), F32), pltpu.SemaphoreType.DMA],
         compiler_params=pltpu.CompilerParams(vmem_limit_bytes=40 << 20),
     )(wide, even, odd, mass, order)
 
 
-def place_kernel(arrived_ref, order_ref, out_ref):
+def place_kernel(arrived_ref, order_ref, out_hbm, out_ref, sems):
     groups = arrived_ref.shape[0] // 6
     table = jnp.concatenate(
         [
@@ -365,12 +377,19 @@
     ids = row_ids(WIDE, WIDE).astype(F32).astype(BF16)
     group_ids = row_ids(groups, WIDE)
 
-    for q in range(groups):
-        at = pl.ds(q * WIDE, WIDE)
-        got = lookup_rows(
-            table, order_ref[:, at], ids, group_ids, groups, lambda index: (index >> log2(WIDE), index & (WIDE - 1))
-        )
-        out_ref[:, at] = jnp.concatenate(got, axis=0)
+    copies = []
+    for n in range(PIECES):
+        for q in range(n * groups // PIECES, (n + 1) * groups // PIECES):
+            at = pl.ds(q * WIDE, WIDE)
+            got = lookup_rows(
+                table, order_ref[:, at], ids, group_ids, groups, lambda index: (index >> log2(WIDE), index & (WIDE - 1))
+            )
+            out_ref[:, at] = jnp.concatenate(got, axis=0)
+        piece = pl.ds(n * groups // PIECES * WIDE, groups // PIECES * WIDE)
+        copies.append(pltpu.make_async_copy(out_ref.at[:, piece], out_hbm.at[:, piece], sems.at[n]))
+        copies[n].start()
+    for copy in copies:
+        copy.wait()
 
 
 def place_call(arrived, order):
@@ -378,7 +397,8 @@
         place_kernel,
         out_shape=jax.ShapeDtypeStruct((3, order.shape[1]), F32),
         in_specs=[pl.BlockSpec(memory_space=pltpu.VMEM)] * 2,
-        out_specs=pl.BlockSpec(memory_space=pltpu.VMEM),
+        out_specs=pl.BlockSpec(memory_space=pltpu.HBM),
+        scratch_shapes=[pltpu.VMEM((3, order.shape[1]), F32), pltpu.SemaphoreType.DMA((PIECES,))],
         compiler_params=pltpu.CompilerParams(vmem_limit_bytes=40 << 20),
     )(arrived, order)
 

time: 62.4 us -> 61.6 us (0.987)
  Pallas kernels: 13.8 us -> 13.1 us
    pallas_call x1, Pallas kernels: 4.71 us -> 3.98 us  [scatter_call(): pl.pallas_call(scatter_kernel, out_shape=(jax.ShapeDtypeStruct((FIELDS, h...]
where the time goes in v9:
time: 61.6 us; the launch traced here: 61.3 us
  blocking collectives  37.2 us (60%)
  Pallas kernels  13.1 us (21%)
  starting transfers between devices  6.83 us (11%)
  waiting for transfers between devices  3.4 us (6%)
  between operations  0.7 us (1%)
    all_to_all x1, blocking collectives, on_device(): lax.all_to_all(values, both, split_axis=0, concat_axis=0, tiled=True)  22.3 us
    all_to_all x1, blocking collectives, on_device(): lax.all_to_all(outgoing, both, split_axis=0, concat_axis=0, tiled=True)  15 us
    ppermute x4, starting transfers between devices, swap(): out.append(lax.ppermute(part, axis, pairs + [(j, i) for i, j in pairs]))  6.83 us
    pallas_call x1, Pallas kernels, gather_call(): pl.pallas_call(gather_kernel, out_shape=jax.ShapeDtypeStruct((rows, 128),...  4 us
    pallas_call x1, Pallas kernels, scatter_call(): pl.pallas_call(scatter_kernel, out_shape=(jax.ShapeDtypeStruct((FIELDS, h...  3.98 us
    ppermute x4, waiting for transfers between devices, swap(): out.append(lax.ppermute(part, axis, pairs + [(j, i) for i, j in pairs]))  3.4 us
    pallas_call x1, Pallas kernels, solve_call(): pl.pallas_call(kernel, out_shape=(jax.ShapeDtypeStruct((FIELDS, hx, hy, h...  3.36 us
    pallas_call x1, Pallas kernels, place_call(): pl.pallas_call(place_kernel, out_shape=jax.ShapeDtypeStruct((3, order.sha...  1.67 us
  transfers between devices with their start and end apart: 4, of which 2 were waited for; matrix products, arithmetic and copies ran while one was open for 0% of the time, Pallas kernels for 0%

profile of v9, /device:TPU:0, one launch (start us, length us, event | category | flops | bytes accessed | tf_op | source)
XLA Modules:
  0.0 61.3 jit_solution(10546805587761093915)
XLA Ops:
  0.6 4.0 %shard_map.86 = f32[896,128]{1,0:T(8,128)} custom-call(f32[7,4096]{1,0:T(8,128)} %fields_hbm.1, s32[1,16384]{1,0:T(1,128)} %bitcast.12, f32[1,16384]{1,0:T(1,128)} %bitcast.13), custom_call_target="tpu_custom_call" | custom-call | tf_op jit(solution)/shard_map/pallas_call | solution.py:117
  4.6 0.0 copy-start
  4.7 0.0 copy-start.1
  4.7 22.3 %all_to_all.10 = f32[32,7,4,128]{3,2,1,0:T(4,128)S(1)} all-to-all(f32[32,7,4,128]{3,2,1,0:T(4,128)} %bitcast.11), channel_id=1, replica_groups=mesh['src'=4,'tgt'=8] {'src','tgt'}, dimensions={0} | all-to-all | bytes 917504 | tf_op jit(solution)/shard_map/all_to_all | solution.py:424
  26.9 0.0 copy-done
  26.9 0.0 copy-done.1
  26.9 4.0 %shard_map.87 = (f32[7,4,16,128]{3,2,1,0:T(8,128)S(1)}, f32[28,4,128]{2,1,0:T(4,128)S(1)}, f32[29,4,128]{2,1,0:T(4,128)S(1)}) custom-call(f32[896,128]{1,0:T(8,128)S(1)} %bitcast.7, s32[1,16384]{1,0:T(1,128)S(1)} %bitcast.10, f32[4,16,128]{2,1,0:T(8,128)S(1)} %copy-done), custom_call_target="tpu_custom_call" | custom-call | tf_op jit(solution)/shard_map/pallas_call | solution.py:189
  30.9 0.7 %collective-permute-start.1 = (f32[29,4,128]{2,1,0:T(4,128)S(1)}, f32[29,4,128]{2,1,0:T(4,128)S(1)}, u32[]{:S(2)}, u32[]{:S(2)}) collective-permute-start(f32[29,4,128]{2,1,0:T(4,128)S(1)} %get-tuple-element.12), channel_id=1, source_target_pairs={{1,2},{3,4},{5,6},{2,1},{4,3},{6,5},{9,10},{11,12},{13,14},{10,9},... | collective-permute-start | bytes 178184 | tf_op jit(solution)/shard_map/ppermute | solution.py:411
  31.6 3.5 %collective-permute-start = (f32[28,4,128]{2,1,0:T(4,128)S(1)}, f32[28,4,128]{2,1,0:T(4,128)S(1)}, u32[]{:S(2)}, u32[]{:S(2)}) collective-permute-start(f32[28,4,128]{2,1,0:T(4,128)S(1)} %get-tuple-element.11), channel_id=1, source_target_pairs={{0,1},{2,3},{4,5},{6,7},{1,0},{3,2},{5,4},{7,6},{8,9},{10,11},{12,... | collective-permute-start | bytes 172040 | tf_op jit(solution)/shard_map/ppermute | solution.py:411
  35.1 2.2 %collective-permute-done.even_ref = f32[28,4,128]{2,1,0:T(4,128)S(1)} collective-permute-done((f32[28,4,128]{2,1,0:T(4,128)S(1)}, f32[28,4,128]{2,1,0:T(4,128)S(1)}, u32[]{:S(2)}, u32[]{:S(2)}) %collective-permute-start) | collective-permute-done | bytes 57376 | tf_op jit(solution)/shard_map/ppermute | solution.py:411
  37.3 0.0 collective-permute-done.1.odd_ref
  37.3 0.0 copy-start.2
  37.3 0.1 shard_map.88
  37.4 0.7 %collective-permute-start.3 = (f32[7,80,128]{2,1,0:T(8,128)S(1)}, f32[7,80,128]{2,1,0:T(8,128)S(1)}, u32[]{:S(2)}, u32[]{:S(2)}) collective-permute-start(f32[7,80,128]{2,1,0:T(8,128)S(1)} %get-tuple-element.15), channel_id=1, source_target_pairs={{8,16},{16,8},{9,17},{17,9},{10,18},{18,10},{11,19},{19,11},{12,20... | collective-permute-start | bytes 860168 | tf_op jit(solution)/shard_map/ppermute | solution.py:411
  38.1 2.0 %collective-permute-start.2 = (f32[7,78,128]{2,1,0:T(8,128)S(1)}, f32[7,78,128]{2,1,0:T(8,128)S(1)}, u32[]{:S(2)}, u32[]{:S(2)}) collective-permute-start(f32[7,78,128]{2,1,0:T(8,128)S(1)} %get-tuple-element.14), channel_id=1, source_target_pairs={{0,8},{16,24},{8,0},{24,16},{1,9},{17,25},{9,1},{25,17},{2,10},{18... | collective-permute-start | bytes 838664 | tf_op jit(solution)/shard_map/ppermute | solution.py:411
  40.0 1.2 %collective-permute-done.2.refs_1_ = f32[7,78,128]{2,1,0:T(8,128)S(1)} collective-permute-done((f32[7,78,128]{2,1,0:T(8,128)S(1)}, f32[7,78,128]{2,1,0:T(8,128)S(1)}, u32[]{:S(2)}, u32[]{:S(2)}) %collective-permute-start.2) | collective-permute-done | bytes 279584 | tf_op jit(solution)/shard_map/ppermute | solution.py:411
  41.2 0.0 collective-permute-done.3.refs_2_
  41.2 0.0 copy-done.2
  41.2 3.4 %shard_map.89 = (f32[7,4,16,128]{3,2,1,0:T(8,128)}, f32[192,128]{1,0:T(8,128)S(1)}) custom-call(f32[7,4,24,128]{3,2,1,0:T(8,128)S(1)} %get-tuple-element.13.refs_0_, f32[7,78,128]{2,1,0:T(8,128)S(1)} %collective-permute-done.2.refs_1_, f32[7,80,128]{2,1,0:T(8,128)S(1)} %collective-permute-done.3.refs_2_, f32[4,16,128]{2,1,0:T(8,128)S(1)} %copy-done, ...), custom_call_target="tpu_custom_call" | custom-call | tf_op jit(solution)/shard_map/pallas_call | solution.py:354
  44.6 0.0 copy-start.3
  44.6 15.0 %all_to_all.11 = f32[32,3,2,128]{3,2,1,0:T(2,128)S(1)} all-to-all(f32[32,3,2,128]{3,2,1,0:T(2,128)S(1)} %bitcast.9), channel_id=1, replica_groups=mesh['src'=4,'tgt'=8] {'src','tgt'}, dimensions={0} | all-to-all | bytes 196608 | tf_op jit(solution)/shard_map/all_to_all | solution.py:431
  59.6 0.0 copy-done.3
  59.6 1.7 %shard_map.90 = f32[3,8192]{1,0:T(4,128)} custom-call(f32[192,128]{1,0:T(8,128)S(1)} %bitcast.8, s32[1,8192]{1,0:T(1,128)S(1)} %copy-done.3), custom_call_target="tpu_custom_call" | custom-call | tf_op jit(solution)/shard_map/pallas_call | solution.py:396
Async XLA Ops:
  4.6 22.3 %copy-start = (f32[4,16,128]{2,1,0:T(8,128)S(1)}, f32[4,16,128]{2,1,0:T(8,128)}, u32[]{:S(2)}) copy-start(f32[4,16,128]{2,1,0:T(8,128)} %refs_3_.1) | copy-start | bytes 98308
  4.7 22.3 %copy-start.1 = (s32[16384]{0:T(1024)S(1)}, s32[16384]{0:T(1024)}, u32[]{:S(2)}) copy-start(s32[16384]{0:T(1024)} %param.10) | copy-start | bytes 196612
  30.9 6.4 %collective-permute-start.1 = (f32[29,4,128]{2,1,0:T(4,128)S(1)}, f32[29,4,128]{2,1,0:T(4,128)S(1)}, u32[]{:S(2)}, u32[]{:S(2)}) collective-permute-start(f32[29,4,128]{2,1,0:T(4,128)S(1)} %get-tuple-element.12), channel_id=1, source_target_pairs={{1,2},{3,4},{5,6},{2,1},{4,3},{6,5},{9,10},{11,12},{13,14},{10,9},... | collective-permute-start | bytes 178184 | tf_op jit(solution)/shard_map/ppermute | solution.py:411
  31.6 5.7 %collective-permute-start = (f32[28,4,128]{2,1,0:T(4,128)S(1)}, f32[28,4,128]{2,1,0:T(4,128)S(1)}, u32[]{:S(2)}, u32[]{:S(2)}) collective-permute-start(f32[28,4,128]{2,1,0:T(4,128)S(1)} %get-tuple-element.11), channel_id=1, source_target_pairs={{0,1},{2,3},{4,5},{6,7},{1,0},{3,2},{5,4},{7,6},{8,9},{10,11},{12,... | collective-permute-start | bytes 172040 | tf_op jit(solution)/shard_map/ppermute | solution.py:411
  37.3 3.9 %copy-start.2 = (s32[1,8192]{1,0:T(1,128)S(1)}, s32[1,8192]{1,0:T(1,128)}, u32[]{:S(2)}) copy-start(s32[1,8192]{1,0:T(1,128)} %refs_4_.1) | copy-start | bytes 98308
  37.4 3.9 %collective-permute-start.3 = (f32[7,80,128]{2,1,0:T(8,128)S(1)}, f32[7,80,128]{2,1,0:T(8,128)S(1)}, u32[]{:S(2)}, u32[]{:S(2)}) collective-permute-start(f32[7,80,128]{2,1,0:T(8,128)S(1)} %get-tuple-element.15), channel_id=1, source_target_pairs={{8,16},{16,8},{9,17},{17,9},{10,18},{18,10},{11,19},{19,11},{12,20... | collective-permute-start | bytes 860168 | tf_op jit(solution)/shard_map/ppermute | solution.py:411
  38.1 3.2 %collective-permute-start.2 = (f32[7,78,128]{2,1,0:T(8,128)S(1)}, f32[7,78,128]{2,1,0:T(8,128)S(1)}, u32[]{:S(2)}, u32[]{:S(2)}) collective-permute-start(f32[7,78,128]{2,1,0:T(8,128)S(1)} %get-tuple-element.14), channel_id=1, source_target_pairs={{0,8},{16,24},{8,0},{24,16},{1,9},{17,25},{9,1},{25,17},{2,10},{18... | collective-permute-start | bytes 838664 | tf_op jit(solution)/shard_map/ppermute | solution.py:411
  44.6 15.0 %copy-start.3 = (s32[1,8192]{1,0:T(1,128)S(1)}, s32[1,8192]{1,0:T(1,128)}, u32[]{:S(2)}) copy-start(s32[1,8192]{1,0:T(1,128)} %order_ref.1) | copy-start | bytes 98308

commit v10 on v9

--- a/solution.py
+++ b/solution.py
@@ -223,12 +223,17 @@
     return [bulk, shear, soften]
 
 
-def widen_kernel(v_ref, even_ref, odd_ref, wide_ref, to_even_ref, to_odd_ref):
-    hx, hy = v_ref.shape[1], v_ref.shape[2]
-    own = hx * hy
+def corners(sides):
+    line = row_ids(2 * ITERS, sides[0].shape[1])
+    near = pltpu.roll(sides[1], 2, 0)
+    far = jnp.where(line == 4, pltpu.roll(sides[2], 4, 0), pltpu.roll(sides[2], 6, 0))
+    return sides[0], jnp.where(line < 4, near, far)
+
+
+def sides_kernel(even_ref, odd_ref, sides_ref, to_even_ref, to_odd_ref):
+    hx = sides_ref.shape[1]
     b_odd = lax.axis_index("tgt") % 2 == 1
     a_odd = lax.axis_index("src") % 2 == 1
-    line = row_ids(2 * ITERS, v_ref.shape[3])
     for f in range(FIELDS):
         sides = []
         for x in range(hx):
@@ -236,36 +241,34 @@
             right = jnp.where(b_odd, odd_side, even_side)
             left = jnp.where(b_odd, even_side, odd_side)
             sides.append(jnp.concatenate([right, left], axis=0))
-            wide_ref[f, x, :hy] = v_ref[f, x]
-            wide_ref[f, x, hy:] = sides[x]
-            to_even_ref[f, x * hy : (x + 1) * hy] = v_ref[f, x]
-            to_odd_ref[f, x * hy : (x + 1) * hy] = v_ref[f, x]
-        extra = []
-        for first, second, third in ((sides[hx - 1], sides[hx - 2], sides[hx - 3]), (sides[0], sides[1], sides[2])):
-            near = pltpu.roll(second, 2, 0)
-            far = jnp.where(line == 4, pltpu.roll(third, 4, 0), pltpu.roll(third, 6, 0))
-            extra.append((first, jnp.where(line < 4, near, far)))
-        at = own + 2 * ITERS
-        to_even_ref[f, own:at] = jnp.where(a_odd, extra[1][0], extra[0][0])
-        to_odd_ref[f, own:at] = jnp.where(a_odd, extra[0][0], extra[1][0])
-        to_even_ref[f, at : at + 6] = jnp.where(a_odd, extra[1][1], extra[0][1])[:6]
-        to_odd_ref[f, at : at + 8] = jnp.where(a_odd, extra[0][1], extra[1][1])
-
-
-def widen_call(v, even, odd):
-    fields, hx, hy, hz = v.shape
-    even_rows = jax.ShapeDtypeStruct((fields, hx * hy + 4 * ITERS - 2, hz), F32)
-    odd_rows = jax.ShapeDtypeStruct((fields, hx * hy + 4 * ITERS, hz), F32)
+            sides_ref[f, x] = sides[x]
+        to_left, to_right = corners(sides), corners(sides[::-1])
+        to_even_ref[f, :8] = jnp.where(a_odd, to_left[0], to_right[0])
+        to_even_ref[f, 8:14] = jnp.where(a_odd, to_left[1], to_right[1])[:6]
+        to_odd_ref[f, :8] = jnp.where(a_odd, to_right[0], to_left[0])
+        to_odd_ref[f, 8:] = jnp.where(a_odd, to_right[1], to_left[1])
+
+
+def sides_call(even, odd, hx):
+    hz = even.shape[2]
     return pl.pallas_call(
-        widen_kernel,
-        out_shape=(jax.ShapeDtypeStruct((fields, hx, hy + 2 * ITERS, hz), F32), even_rows, odd_rows),
-        in_specs=[pl.BlockSpec(memory_space=pltpu.VMEM)] * 3,
+        sides_kernel,
+        out_shape=(
+            jax.ShapeDtypeStruct((FIELDS, hx, 2 * ITERS, hz), F32),
+            jax.ShapeDtypeStruct((FIELDS, 4 * ITERS - 2, hz), F32),
+            jax.ShapeDtypeStruct((FIELDS, 4 * ITERS, hz), F32),
+        ),
+        in_specs=[pl.BlockSpec(memory_space=pltpu.VMEM)] * 2,
         out_specs=(pl.BlockSpec(memory_space=pltpu.VMEM),) * 3,
-        compiler_params=pltpu.CompilerParams(vmem_limit_bytes=40 << 20),
-    )(v, even, odd)
-
-
-def solve_kernel(mesh_shape, wide_ref, even_ref, odd_ref, mass_ref, order_ref, projected_hbm, out_ref, projected_ref, sem):
+        compiler_params=pltpu.CompilerParams(vmem_limit_bytes=4 << 20),
+        cost_estimate=pl.CostEstimate(flops=40 * 10**9, bytes_accessed=40 * 10**6, transcendentals=0),
+    )(even, odd)
+
+
+def solve_kernel(
+    mesh_shape, v_ref, sides_ref, even_ref, odd_ref, even_corners_ref, odd_corners_ref, mass_ref, order_ref,
+    projected_hbm, out_ref, projected_ref, sem,
+):
     n_src, n_tgt = mesh_shape
     hx, hy, hz = mass_ref.shape
     k = ITERS
@@ -286,21 +289,25 @@
 
     line = row_ids(2 * k, hz)
 
-    def slabs(payload, from_left):
-        first = payload[hx * hy : hx * hy + 2 * k]
-        packed = payload[hx * hy + 2 * k :]
+    def slabs(own, first, packed, from_left):
         second = pltpu.roll(packed, 6, 0)
         third = jnp.where(line < 4, pltpu.roll(packed, 4, 0), pltpu.roll(packed, 2, 0))
         sides = [first, second, third] + [jnp.zeros((2 * k, hz), F32)] * (hx - 3)
-        order = reversed(sides) if from_left else sides
-        return [jnp.concatenate([payload[x * hy : (x + 1) * hy], side], axis=0) for x, side in enumerate(order)]
+        if from_left:
+            sides = sides[::-1]
+        return [jnp.concatenate([own[x], side], axis=0) for x, side in enumerate(sides)]
+
+    a_odd = a % 2 == 1
 
     @pl.loop(0, FIELDS)
     def _(f):
-        even, odd = jnp.concatenate([even_ref[f], jnp.zeros((2, hz), F32)], axis=0), odd_ref[f]
-        left = slabs(jnp.where(a % 2 == 1, even, odd), True)
-        right = slabs(jnp.where(a % 2 == 1, odd, even), False)
-        base = left + [wide_ref[f, x] for x in range(hx)] + right
+        packed = jnp.concatenate([even_corners_ref[f, 2 * k :], jnp.zeros((2, hz), F32)], axis=0)
+        even = (even_ref[f], even_corners_ref[f, : 2 * k], packed)
+        odd = (odd_ref[f], odd_corners_ref[f, : 2 * k], odd_corners_ref[f, 2 * k :])
+        left = slabs(*[jnp.where(a_odd, p, q) for p, q in zip(even, odd)], True)
+        right = slabs(*[jnp.where(a_odd, q, p) for p, q in zip(even, odd)], False)
+        own = [jnp.concatenate([v_ref[f, x], sides_ref[f, x]], axis=0) for x in range(hx)]
+        base = left + own + right
         u = [COEFS[k] * e for e in base]
         for sweep in range(1, k + 1):
             new = list(u)
@@ -345,7 +352,8 @@
     leave.wait()
 
 
-def solve_call(mesh_shape, wide, even, odd, mass, order):
+def solve_call(mesh_shape, *args):
+    mass, order = args[-2:]
     hx, hy, hz = mass.shape
 
     def kernel(*refs):
@@ -357,11 +365,11 @@
             jax.ShapeDtypeStruct((FIELDS, hx, hy, hz), F32),
             jax.ShapeDtypeStruct((order.shape[1] // WIDE * 6, 128), F32),
         ),
-        in_specs=[pl.BlockSpec(memory_space=pltpu.VMEM)] * 5,
+        in_specs=[pl.BlockSpec(memory_space=pltpu.VMEM)] * 8,
         out_specs=(pl.BlockSpec(memory_space=pltpu.HBM), pl.BlockSpec(memory_space=pltpu.VMEM)),
         scratch_shapes=[pltpu.VMEM((FIELDS, hx, hy, hz), F32), pltpu.SemaphoreType.DMA],
         compiler_params=pltpu.CompilerParams(vmem_limit_bytes=40 << 20),
-    )(wide, even, odd, mass, order)
+    )(*args)
 
 
 def place_kernel(arrived_ref, order_ref, out_hbm, out_ref, sems):
@@ -403,13 +411,9 @@
     )(arrived, order)
 
 
-def swap(x, axis):
-    count = lax.axis_size(axis)
-    out = []
-    for start, part in enumerate(x):
-        pairs = [(i, i + 1) for i in range(start, count - 1, 2)]
-        out.append(lax.ppermute(part, axis, pairs + [(j, i) for i, j in pairs]))
-    return out
+def swap(x, axis, start):
+    pairs = [(i, i + 1) for i in range(start, lax.axis_size(axis) - 1, 2)]
+    return lax.ppermute(x, axis, pairs + [(j, i) for i, j in pairs])
 
 
 def on_device(source_fields, slot_source, slot_weight, slot_target, cell_mass, send_order, place_order):
@@ -423,8 +427,13 @@
     values = values.reshape(owners, FIELDS, SPAN // 128, 128)
     values = lax.all_to_all(values, both, split_axis=0, concat_axis=0, tiled=True).reshape(-1, 128)
     v, even, odd = scatter_call(values, slot_target.reshape(1, -1), cell_mass)
-    wide, even, odd = widen_call(v, *swap((even, odd), "tgt"))
-    projected, outgoing = solve_call((n_src, n_tgt), wide, *swap((even, odd), "src"), cell_mass, send_order)
+    even_block, odd_block = swap(v, "src", 0), swap(v, "src", 1)
+    even, odd = swap(even, "tgt", 0), swap(odd, "tgt", 1)
+    sides, even, odd = sides_call(even, odd, cell_mass.shape[0])
+    even, odd = swap(even, "src", 0), swap(odd, "src", 1)
+    projected, outgoing = solve_call(
+        (n_src, n_tgt), v, sides, even_block, odd_block, even, odd, cell_mass, send_order
+    )
 
     if quota == WIDE:
         outgoing = outgoing.reshape(owners, 3, 2, 128)

time: 61.6 us -> 59.2 us (0.961)
  starting transfers between devices: 6.83 us -> 9.57 us
  blocking collectives: 37.2 us -> 34.5 us
  waiting for transfers between devices: 3.4 us -> 0.9 us
    ppermute x4 -> x6, starting transfers between devices: 6.83 us -> 9.57 us  [swap(): return lax.ppermute(x, axis, pairs + [(j, i) for i, j in pairs])]
    all_to_all x1, blocking collectives: 15 us -> 12.2 us  [on_device(): lax.all_to_all(outgoing, both, split_axis=0, concat_axis=0, tiled=True)]
    ppermute x4 -> x6, waiting for transfers between devices: 3.4 us -> 0.9 us  [swap(): return lax.ppermute(x, axis, pairs + [(j, i) for i, j in pairs])]
  transfers between devices with their start and end apart: 4 -> 6, of which waited for: 2 -> 1; matrix products, arithmetic and copies ran while one was open for 0% -> 0% of each run, Pallas kernels for 0% -> 0%
where the time goes in v10:
time: 59.2 us; the launch traced here: 58.8 us
  blocking collectives  34.5 us (58%)
  Pallas kernels  13.1 us (22%)
  starting transfers between devices  9.57 us (16%)
  waiting for transfers between devices  0.9 us (2%)
  between operations  0.73 us (1%)
    all_to_all x1, blocking collectives, on_device(): lax.all_to_all(values, both, split_axis=0, concat_axis=0, tiled=True)  22.3 us
    all_to_all x1, blocking collectives, on_device(): lax.all_to_all(outgoing, both, split_axis=0, concat_axis=0, tiled=True)  12.2 us
    ppermute x6, starting transfers between devices, swap(): return lax.ppermute(x, axis, pairs + [(j, i) for i, j in pairs])  9.57 us
    pallas_call x1, Pallas kernels, gather_call(): pl.pallas_call(gather_kernel, out_shape=jax.ShapeDtypeStruct((rows, 128),...  4.01 us
    pallas_call x1, Pallas kernels, scatter_call(): pl.pallas_call(scatter_kernel, out_shape=(jax.ShapeDtypeStruct((FIELDS, h...  3.98 us
    pallas_call x1, Pallas kernels, solve_call(): pl.pallas_call(kernel, out_shape=(jax.ShapeDtypeStruct((FIELDS, hx, hy, h...  3.36 us
    pallas_call x1, Pallas kernels, place_call(): pl.pallas_call(place_kernel, out_shape=jax.ShapeDtypeStruct((3, order.sha...  1.67 us
  transfers between devices with their start and end apart: 6, of which 1 were waited for; matrix products, arithmetic and copies ran while one was open for 0% of the time, Pallas kernels for 0%

profile of v10, /device:TPU:0, one launch (start us, length us, event | category | flops | bytes accessed | tf_op | source)
XLA Modules:
  0.0 58.8 jit_solution(10754620420927137615)
XLA Ops:
  0.6 4.0 %shard_map.86 = f32[896,128]{1,0:T(8,128)} custom-call(f32[7,4096]{1,0:T(8,128)} %fields_hbm.1, s32[1,16384]{1,0:T(1,128)} %bitcast.12, f32[1,16384]{1,0:T(1,128)} %bitcast.13), custom_call_target="tpu_custom_call" | custom-call | tf_op jit(solution)/shard_map/pallas_call | solution.py:117
  4.6 0.0 copy-start
  4.7 0.0 copy-start.1
  4.7 22.3 %all_to_all.10 = f32[32,7,4,128]{3,2,1,0:T(4,128)S(1)} all-to-all(f32[32,7,4,128]{3,2,1,0:T(4,128)} %bitcast.11), channel_id=1, replica_groups=mesh['src'=4,'tgt'=8] {'src','tgt'}, dimensions={0} | all-to-all | bytes 917504 | tf_op jit(solution)/shard_map/all_to_all | solution.py:428
  26.9 0.0 copy-done
  26.9 0.0 copy-done.1
  26.9 4.0 %shard_map.87 = (f32[7,4,16,128]{3,2,1,0:T(8,128)S(1)}, f32[28,4,128]{2,1,0:T(4,128)S(1)}, f32[29,4,128]{2,1,0:T(4,128)S(1)}) custom-call(f32[896,128]{1,0:T(8,128)S(1)} %bitcast.7, s32[1,16384]{1,0:T(1,128)S(1)} %bitcast.10, f32[4,16,128]{2,1,0:T(8,128)S(1)} %copy-done), custom_call_target="tpu_custom_call" | custom-call | tf_op jit(solution)/shard_map/pallas_call | solution.py:189
  30.9 0.7 %collective-permute-start.1 = (f32[29,4,128]{2,1,0:T(4,128)S(1)}, f32[29,4,128]{2,1,0:T(4,128)S(1)}, u32[]{:S(2)}, u32[]{:S(2)}) collective-permute-start(f32[29,4,128]{2,1,0:T(4,128)S(1)} %get-tuple-element.12), channel_id=1, source_target_pairs={{1,2},{3,4},{5,6},{2,1},{4,3},{6,5},{9,10},{11,12},{13,14},{10,9},... | collective-permute-start | bytes 178184 | tf_op jit(solution)/shard_map/ppermute | solution.py:416
  31.6 3.5 %collective-permute-start = (f32[28,4,128]{2,1,0:T(4,128)S(1)}, f32[28,4,128]{2,1,0:T(4,128)S(1)}, u32[]{:S(2)}, u32[]{:S(2)}) collective-permute-start(f32[28,4,128]{2,1,0:T(4,128)S(1)} %get-tuple-element.11), channel_id=1, source_target_pairs={{0,1},{2,3},{4,5},{6,7},{1,0},{3,2},{5,4},{7,6},{8,9},{10,11},{12,... | collective-permute-start | bytes 172040 | tf_op jit(solution)/shard_map/ppermute | solution.py:416
  35.1 0.0 copy-start.2
  35.1 0.8 %collective-permute-start.3 = (f32[7,4,16,128]{3,2,1,0:T(8,128)S(1)}, f32[7,4,16,128]{3,2,1,0:T(8,128)S(1)}, u32[]{:S(2)}, u32[]{:S(2)}) collective-permute-start(f32[7,4,16,128]{3,2,1,0:T(8,128)S(1)} %get-tuple-element.10.refs_0_), channel_id=1, source_target_pairs={{8,16},{16,8},{9,17},{17,9},{10,18},{18,10},{11,19},{19,11},{12,20... | collective-permute-start | bytes 688136 | tf_op jit(solution)/shard_map/ppermute | solution.py:416
  35.9 2.0 %collective-permute-start.2 = (f32[7,4,16,128]{3,2,1,0:T(8,128)S(1)}, f32[7,4,16,128]{3,2,1,0:T(8,128)S(1)}, u32[]{:S(2)}, u32[]{:S(2)}) collective-permute-start(f32[7,4,16,128]{3,2,1,0:T(8,128)S(1)} %get-tuple-element.10.refs_0_), channel_id=1, source_target_pairs={{0,8},{16,24},{8,0},{24,16},{1,9},{17,25},{9,1},{25,17},{2,10},{18... | collective-permute-start | bytes 688136 | tf_op jit(solution)/shard_map/ppermute | solution.py:416
  37.9 0.0 collective-permute-done.even_ref
  37.9 0.0 collective-permute-done.1.odd_ref
  37.9 0.7 %collective-permute-start.5 = (f32[7,16,128]{2,1,0:T(8,128)S(1)}, f32[7,16,128]{2,1,0:T(8,128)S(1)}, u32[]{:S(2)}, u32[]{:S(2)}) collective-permute-start(f32[7,16,128]{2,1,0:T(8,128)S(1)} %get-tuple-element.15), channel_id=1, source_target_pairs={{8,16},{16,8},{9,17},{17,9},{10,18},{18,10},{11,19},{19,11},{12,20... | collective-permute-start | bytes 172040 | tf_op jit(solution)/shard_map/ppermute | solution.py:416
  38.6 2.0 %collective-permute-start.4 = (f32[7,14,128]{2,1,0:T(8,128)S(1)}, f32[7,14,128]{2,1,0:T(8,128)S(1)}, u32[]{:S(2)}, u32[]{:S(2)}) collective-permute-start(f32[7,14,128]{2,1,0:T(8,128)S(1)} %get-tuple-element.14), channel_id=1, source_target_pairs={{0,8},{16,24},{8,0},{24,16},{1,9},{17,25},{9,1},{25,17},{2,10},{18... | collective-permute-start | bytes 150536 | tf_op jit(solution)/shard_map/ppermute | solution.py:416
  40.6 0.9 %collective-permute-done.4.refs_4_ = f32[7,14,128]{2,1,0:T(8,128)S(1)} collective-permute-done((f32[7,14,128]{2,1,0:T(8,128)S(1)}, f32[7,14,128]{2,1,0:T(8,128)S(1)}, u32[]{:S(2)}, u32[]{:S(2)}) %collective-permute-start.4) | collective-permute-done | bytes 50208 | tf_op jit(solution)/shard_map/ppermute | solution.py:416
  41.5 0.0 collective-permute-done.5.refs_5_
  41.5 0.0 collective-permute-done.3.refs_3_
  41.5 0.0 collective-permute-done.2.refs_2_
  41.5 0.0 copy-done.2
  41.5 3.4 %shard_map.89 = (f32[7,4,16,128]{3,2,1,0:T(8,128)}, f32[192,128]{1,0:T(8,128)S(1)}) custom-call(f32[7,4,16,128]{3,2,1,0:T(8,128)S(1)} %get-tuple-element.10.refs_0_, f32[7,4,8,128]{3,2,1,0:T(8,128)S(1)} %get-tuple-element.13.refs_1_, f32[7,4,16,128]{3,2,1,0:T(8,128)S(1)} %collective-permute-done.2.refs_2_, ...), custom_call_target="tpu_custom_call" | custom-call | tf_op jit(solution)/shard_map/pallas_call | solution.py:362
  44.9 0.0 copy-start.3
  44.9 12.2 %all_to_all.11 = f32[32,3,2,128]{3,2,1,0:T(2,128)S(1)} all-to-all(f32[32,3,2,128]{3,2,1,0:T(2,128)S(1)} %bitcast.9), channel_id=1, replica_groups=mesh['src'=4,'tgt'=8] {'src','tgt'}, dimensions={0} | all-to-all | bytes 196608 | tf_op jit(solution)/shard_map/all_to_all | solution.py:440
  57.1 0.0 copy-done.3
  57.1 1.7 %shard_map.90 = f32[3,8192]{1,0:T(4,128)} custom-call(f32[192,128]{1,0:T(8,128)S(1)} %bitcast.8, s32[1,8192]{1,0:T(1,128)S(1)} %copy-done.3), custom_call_target="tpu_custom_call" | custom-call | tf_op jit(solution)/shard_map/pallas_call | solution.py:404
  (1 shorter events, 0.0 us)
Async XLA Ops:
  4.6 22.3 %copy-start = (f32[4,16,128]{2,1,0:T(8,128)S(1)}, f32[4,16,128]{2,1,0:T(8,128)}, u32[]{:S(2)}) copy-start(f32[4,16,128]{2,1,0:T(8,128)} %refs_6_.1) | copy-start | bytes 98308
  4.7 22.3 %copy-start.1 = (s32[16384]{0:T(1024)S(1)}, s32[16384]{0:T(1024)}, u32[]{:S(2)}) copy-start(s32[16384]{0:T(1024)} %param.10) | copy-start | bytes 196612
  30.9 7.0 %collective-permute-start.1 = (f32[29,4,128]{2,1,0:T(4,128)S(1)}, f32[29,4,128]{2,1,0:T(4,128)S(1)}, u32[]{:S(2)}, u32[]{:S(2)}) collective-permute-start(f32[29,4,128]{2,1,0:T(4,128)S(1)} %get-tuple-element.12), channel_id=1, source_target_pairs={{1,2},{3,4},{5,6},{2,1},{4,3},{6,5},{9,10},{11,12},{13,14},{10,9},... | collective-permute-start | bytes 178184 | tf_op jit(solution)/shard_map/ppermute | solution.py:416
  31.6 6.3 %collective-permute-start = (f32[28,4,128]{2,1,0:T(4,128)S(1)}, f32[28,4,128]{2,1,0:T(4,128)S(1)}, u32[]{:S(2)}, u32[]{:S(2)}) collective-permute-start(f32[28,4,128]{2,1,0:T(4,128)S(1)} %get-tuple-element.11), channel_id=1, source_target_pairs={{0,1},{2,3},{4,5},{6,7},{1,0},{3,2},{5,4},{7,6},{8,9},{10,11},{12,... | collective-permute-start | bytes 172040 | tf_op jit(solution)/shard_map/ppermute | solution.py:416
  35.1 6.4 %copy-start.2 = (s32[1,8192]{1,0:T(1,128)S(1)}, s32[1,8192]{1,0:T(1,128)}, u32[]{:S(2)}) copy-start(s32[1,8192]{1,0:T(1,128)} %refs_7_.1) | copy-start | bytes 98308
  35.1 6.4 %collective-permute-start.3 = (f32[7,4,16,128]{3,2,1,0:T(8,128)S(1)}, f32[7,4,16,128]{3,2,1,0:T(8,128)S(1)}, u32[]{:S(2)}, u32[]{:S(2)}) collective-permute-start(f32[7,4,16,128]{3,2,1,0:T(8,128)S(1)} %get-tuple-element.10.refs_0_), channel_id=1, source_target_pairs={{8,16},{16,8},{9,17},{17,9},{10,18},{18,10},{11,19},{19,11},{12,20... | collective-permute-start | bytes 688136 | tf_op jit(solution)/shard_map/ppermute | solution.py:416
  35.9 5.6 %collective-permute-start.2 = (f32[7,4,16,128]{3,2,1,0:T(8,128)S(1)}, f32[7,4,16,128]{3,2,1,0:T(8,128)S(1)}, u32[]{:S(2)}, u32[]{:S(2)}) collective-permute-start(f32[7,4,16,128]{3,2,1,0:T(8,128)S(1)} %get-tuple-element.10.refs_0_), channel_id=1, source_target_pairs={{0,8},{16,24},{8,0},{24,16},{1,9},{17,25},{9,1},{25,17},{2,10},{18... | collective-permute-start | bytes 688136 | tf_op jit(solution)/shard_map/ppermute | solution.py:416
  37.9 3.5 %collective-permute-start.5 = (f32[7,16,128]{2,1,0:T(8,128)S(1)}, f32[7,16,128]{2,1,0:T(8,128)S(1)}, u32[]{:S(2)}, u32[]{:S(2)}) collective-permute-start(f32[7,16,128]{2,1,0:T(8,128)S(1)} %get-tuple-element.15), channel_id=1, source_target_pairs={{8,16},{16,8},{9,17},{17,9},{10,18},{18,10},{11,19},{19,11},{12,20... | collective-permute-start | bytes 172040 | tf_op jit(solution)/shard_map/ppermute | solution.py:416
  38.6 2.9 %collective-permute-start.4 = (f32[7,14,128]{2,1,0:T(8,128)S(1)}, f32[7,14,128]{2,1,0:T(8,128)S(1)}, u32[]{:S(2)}, u32[]{:S(2)}) collective-permute-start(f32[7,14,128]{2,1,0:T(8,128)S(1)} %get-tuple-element.14), channel_id=1, source_target_pairs={{0,8},{16,24},{8,0},{24,16},{1,9},{17,25},{9,1},{25,17},{2,10},{18... | collective-permute-start | bytes 150536 | tf_op jit(solution)/shard_map/ppermute | solution.py:416
  44.9 12.3 %copy-start.3 = (s32[1,8192]{1,0:T(1,128)S(1)}, s32[1,8192]{1,0:T(1,128)}, u32[]{:S(2)}) copy-start(s32[1,8192]{1,0:T(1,128)} %order_ref.1) | copy-start | bytes 98308

commit v11 on v10

--- a/solution.py
+++ b/solution.py
@@ -11,7 +11,7 @@
 FIELDS = 7
 PIECES = 4
 SPAN = 512
-AT_ONCE = 8
+AT_ONCE = 32
 TOGETHER = 8
 WIDE = 256
 BF16 = jnp.bfloat16
@@ -57,7 +57,7 @@
     return jnp.where(ids == low.astype(F32).astype(BF16), jnp.ones((), BF16), jnp.zeros((), BF16))
 
 
-def gather_kernel(fields_hbm, index_hbm, weight_hbm, out_hbm, table, fields_ref, index_ref, weight_ref, out_ref, sems, done):
+def gather_kernel(fields_hbm, index_hbm, weight_hbm, out_ref, table, fields_ref, index_ref, weight_ref, sems):
     pairs = ((fields_hbm, fields_ref), (index_hbm, index_ref), (weight_hbm, weight_ref))
     copies = [pltpu.make_async_copy(src, dst, sems.at[i]) for i, (src, dst) in enumerate(pairs)]
     for copy in copies:
@@ -94,42 +94,28 @@
                 :FIELDS, t * lanes : (t + 1) * lanes
             ]
 
-    def send_off(n):
-        rows = AT_ONCE * FIELDS * tiles
-        part = pl.ds(pl.multiple_of(n * rows, 8), rows)
-        return pltpu.make_async_copy(out_ref.at[part], out_hbm.at[part], done.at[n])
-
-    @pl.loop(0, owners // AT_ONCE // 4)
+    @pl.loop(0, owners // AT_ONCE)
     def _(m):
-        for j in range(4):
-            for i in range(AT_ONCE):
-                one_owner((m * 4 + j) * AT_ONCE + i)
-            send_off(m * 4 + j).start()
-
-    @pl.loop(0, owners // AT_ONCE)
-    def _(n):
-        send_off(n).wait()
+        for i in range(AT_ONCE):
+            one_owner(m * AT_ONCE + i)
 
 
 def gather_call(fields, index, weight):
-    owners = index.shape[1] // SPAN
     rows = FIELDS * index.shape[1] // 128
     return pl.pallas_call(
         gather_kernel,
         out_shape=jax.ShapeDtypeStruct((rows, 128), F32),
         in_specs=[pl.BlockSpec(memory_space=pltpu.HBM)] * 3,
-        out_specs=pl.BlockSpec(memory_space=pltpu.HBM),
+        out_specs=pl.BlockSpec(memory_space=pltpu.VMEM),
         scratch_shapes=[
             pltpu.VMEM((fields.shape[1] // WIDE * 8, WIDE), F32),
             pltpu.VMEM(fields.shape, F32),
             pltpu.VMEM(index.shape, jnp.int32),
             pltpu.VMEM(weight.shape, F32),
-            pltpu.VMEM((rows, 128), F32),
             pltpu.SemaphoreType.DMA((3,)),
-            pltpu.SemaphoreType.DMA((owners // AT_ONCE,)),
         ],
-        compiler_params=pltpu.CompilerParams(vmem_limit_bytes=60 << 20),
-    )(fields, index, weight)
+        compiler_params=pltpu.CompilerParams(vmem_limit_bytes=40 << 20),
+    )(*[pltpu.with_memory_space_constraint(x, pltpu.HBM) for x in (fields, index, weight)])
 
 
 def scatter_kernel(value_ref, target_ref, mass_ref, v_ref, even_ref, odd_ref, total):
@@ -299,8 +285,7 @@
 
     a_odd = a % 2 == 1
 
-    @pl.loop(0, FIELDS)
-    def _(f):
+    for f in range(FIELDS):
         packed = jnp.concatenate([even_corners_ref[f, 2 * k :], jnp.zeros((2, hz), F32)], axis=0)
         even = (even_ref[f], even_corners_ref[f, : 2 * k], packed)
         odd = (odd_ref[f], odd_corners_ref[f, : 2 * k], odd_corners_ref[f, 2 * k :])

time: 59.2 us -> 57.4 us (0.970)
  Pallas kernels: 13.1 us -> 11.5 us
    pallas_call x1, Pallas kernels: 3.36 us -> 2.51 us  [solve_call(): pl.pallas_call(kernel, out_shape=(jax.ShapeDtypeStruct((FIELDS, hx, hy, h...]
    pallas_call x1, Pallas kernels: 4.01 us -> 3.32 us  [gather_call(): pl.pallas_call(gather_kernel, out_shape=jax.ShapeDtypeStruct((rows, 128),...]
where the time goes in v11:
time: 57.4 us; the launch traced here: 57.1 us
  blocking collectives  34.3 us (60%)
  Pallas kernels  11.5 us (20%)
  starting transfers between devices  9.57 us (17%)
  waiting for transfers between devices  0.9 us (2%)
  between operations  0.73 us (1%)
    all_to_all x1, blocking collectives, on_device(): lax.all_to_all(values, both, split_axis=0, concat_axis=0, tiled=True)  22.1 us
    all_to_all x1, blocking collectives, on_device(): lax.all_to_all(outgoing, both, split_axis=0, concat_axis=0, tiled=True)  12.3 us
    ppermute x6, starting transfers between devices, swap(): return lax.ppermute(x, axis, pairs + [(j, i) for i, j in pairs])  9.57 us
    pallas_call x1, Pallas kernels, scatter_call(): pl.pallas_call(scatter_kernel, out_shape=(jax.ShapeDtypeStruct((FIELDS, h...  3.98 us
    pallas_call x1, Pallas kernels, gather_call(): pl.pallas_call(gather_kernel, out_shape=jax.ShapeDtypeStruct((rows, 128),...  3.32 us
    pallas_call x1, Pallas kernels, solve_call(): pl.pallas_call(kernel, out_shape=(jax.ShapeDtypeStruct((FIELDS, hx, hy, h...  2.51 us
    pallas_call x1, Pallas kernels, place_call(): pl.pallas_call(place_kernel, out_shape=jax.ShapeDtypeStruct((3, order.sha...  1.67 us
  transfers between devices with their start and end apart: 6, of which 1 were waited for; matrix products, arithmetic and copies ran while one was open for 0% of the time, Pallas kernels for 0%

profile of v11, /device:TPU:0, one launch (start us, length us, event | category | flops | bytes accessed | tf_op | source)
XLA Modules:
  0.0 57.1 jit_solution(3415729789309355112)
XLA Ops:
  0.6 3.3 %shard_map.86 = f32[896,128]{1,0:T(8,128)S(1)} custom-call(f32[7,4096]{1,0:T(8,128)} %fields_hbm.1, s32[1,16384]{1,0:T(1,128)} %bitcast.12, f32[1,16384]{1,0:T(1,128)} %bitcast.13), custom_call_target="tpu_custom_call" | custom-call | tf_op jit(solution)/shard_map/pallas_call | solution.py:105
  4.0 0.0 copy-start
  4.0 0.0 copy-start.1
  4.0 22.1 %all_to_all.10 = f32[32,7,4,128]{3,2,1,0:T(4,128)S(1)} all-to-all(f32[32,7,4,128]{3,2,1,0:T(4,128)S(1)} %bitcast.8), channel_id=1, replica_groups=mesh['src'=4,'tgt'=8] {'src','tgt'}, dimensions={0} | all-to-all | bytes 917504 | tf_op jit(solution)/shard_map/all_to_all | solution.py:413
  26.0 0.0 copy-done
  26.0 0.0 copy-done.1
  26.0 4.0 %shard_map.87 = (f32[7,4,16,128]{3,2,1,0:T(8,128)S(1)}, f32[28,4,128]{2,1,0:T(4,128)S(1)}, f32[29,4,128]{2,1,0:T(4,128)S(1)}) custom-call(f32[896,128]{1,0:T(8,128)S(1)} %bitcast.7, s32[1,16384]{1,0:T(1,128)S(1)} %bitcast.11, f32[4,16,128]{2,1,0:T(8,128)S(1)} %copy-done), custom_call_target="tpu_custom_call" | custom-call | tf_op jit(solution)/shard_map/pallas_call | solution.py:175
  30.0 0.7 %collective-permute-start.1 = (f32[29,4,128]{2,1,0:T(4,128)S(1)}, f32[29,4,128]{2,1,0:T(4,128)S(1)}, u32[]{:S(2)}, u32[]{:S(2)}) collective-permute-start(f32[29,4,128]{2,1,0:T(4,128)S(1)} %get-tuple-element.12), channel_id=1, source_target_pairs={{1,2},{3,4},{5,6},{2,1},{4,3},{6,5},{9,10},{11,12},{13,14},{10,9},... | collective-permute-start | bytes 178184 | tf_op jit(solution)/shard_map/ppermute | solution.py:401
  30.7 3.5 %collective-permute-start = (f32[28,4,128]{2,1,0:T(4,128)S(1)}, f32[28,4,128]{2,1,0:T(4,128)S(1)}, u32[]{:S(2)}, u32[]{:S(2)}) collective-permute-start(f32[28,4,128]{2,1,0:T(4,128)S(1)} %get-tuple-element.11), channel_id=1, source_target_pairs={{0,1},{2,3},{4,5},{6,7},{1,0},{3,2},{5,4},{7,6},{8,9},{10,11},{12,... | collective-permute-start | bytes 172040 | tf_op jit(solution)/shard_map/ppermute | solution.py:401
  34.2 0.0 copy-start.2
  34.2 0.8 %collective-permute-start.3 = (f32[7,4,16,128]{3,2,1,0:T(8,128)S(1)}, f32[7,4,16,128]{3,2,1,0:T(8,128)S(1)}, u32[]{:S(2)}, u32[]{:S(2)}) collective-permute-start(f32[7,4,16,128]{3,2,1,0:T(8,128)S(1)} %get-tuple-element.10.refs_0_), channel_id=1, source_target_pairs={{8,16},{16,8},{9,17},{17,9},{10,18},{18,10},{11,19},{19,11},{12,20... | collective-permute-start | bytes 688136 | tf_op jit(solution)/shard_map/ppermute | solution.py:401
  35.0 2.0 %collective-permute-start.2 = (f32[7,4,16,128]{3,2,1,0:T(8,128)S(1)}, f32[7,4,16,128]{3,2,1,0:T(8,128)S(1)}, u32[]{:S(2)}, u32[]{:S(2)}) collective-permute-start(f32[7,4,16,128]{3,2,1,0:T(8,128)S(1)} %get-tuple-element.10.refs_0_), channel_id=1, source_target_pairs={{0,8},{16,24},{8,0},{24,16},{1,9},{17,25},{9,1},{25,17},{2,10},{18... | collective-permute-start | bytes 688136 | tf_op jit(solution)/shard_map/ppermute | solution.py:401
  37.0 0.0 collective-permute-done.even_ref
  37.0 0.0 collective-permute-done.1.odd_ref
  37.0 0.7 %collective-permute-start.5 = (f32[7,16,128]{2,1,0:T(8,128)S(1)}, f32[7,16,128]{2,1,0:T(8,128)S(1)}, u32[]{:S(2)}, u32[]{:S(2)}) collective-permute-start(f32[7,16,128]{2,1,0:T(8,128)S(1)} %get-tuple-element.15), channel_id=1, source_target_pairs={{8,16},{16,8},{9,17},{17,9},{10,18},{18,10},{11,19},{19,11},{12,20... | collective-permute-start | bytes 172040 | tf_op jit(solution)/shard_map/ppermute | solution.py:401
  37.7 2.0 %collective-permute-start.4 = (f32[7,14,128]{2,1,0:T(8,128)S(1)}, f32[7,14,128]{2,1,0:T(8,128)S(1)}, u32[]{:S(2)}, u32[]{:S(2)}) collective-permute-start(f32[7,14,128]{2,1,0:T(8,128)S(1)} %get-tuple-element.14), channel_id=1, source_target_pairs={{0,8},{16,24},{8,0},{24,16},{1,9},{17,25},{9,1},{25,17},{2,10},{18... | collective-permute-start | bytes 150536 | tf_op jit(solution)/shard_map/ppermute | solution.py:401
  39.7 0.9 %collective-permute-done.4.refs_4_ = f32[7,14,128]{2,1,0:T(8,128)S(1)} collective-permute-done((f32[7,14,128]{2,1,0:T(8,128)S(1)}, f32[7,14,128]{2,1,0:T(8,128)S(1)}, u32[]{:S(2)}, u32[]{:S(2)}) %collective-permute-start.4) | collective-permute-done | bytes 50208 | tf_op jit(solution)/shard_map/ppermute | solution.py:401
  40.6 0.0 collective-permute-done.5.refs_5_
  40.6 0.0 collective-permute-done.3.refs_3_
  40.6 0.0 collective-permute-done.2.refs_2_
  40.6 0.0 copy-done.2
  40.6 2.5 %shard_map.89 = (f32[7,4,16,128]{3,2,1,0:T(8,128)}, f32[192,128]{1,0:T(8,128)S(1)}) custom-call(f32[7,4,16,128]{3,2,1,0:T(8,128)S(1)} %get-tuple-element.10.refs_0_, f32[7,4,8,128]{3,2,1,0:T(8,128)S(1)} %get-tuple-element.13.refs_1_, f32[7,4,16,128]{3,2,1,0:T(8,128)S(1)} %collective-permute-done.2.refs_2_, ...), custom_call_target="tpu_custom_call" | custom-call | tf_op jit(solution)/shard_map/pallas_call | solution.py:347
  43.1 0.0 copy-start.3
  43.1 12.3 %all_to_all.11 = f32[32,3,2,128]{3,2,1,0:T(2,128)S(1)} all-to-all(f32[32,3,2,128]{3,2,1,0:T(2,128)S(1)} %bitcast.10), channel_id=1, replica_groups=mesh['src'=4,'tgt'=8] {'src','tgt'}, dimensions={0} | all-to-all | bytes 196608 | tf_op jit(solution)/shard_map/all_to_all | solution.py:425
  55.4 0.0 copy-done.3
  55.4 1.7 %shard_map.90 = f32[3,8192]{1,0:T(4,128)} custom-call(f32[192,128]{1,0:T(8,128)S(1)} %bitcast.9, s32[1,8192]{1,0:T(1,128)S(1)} %copy-done.3), custom_call_target="tpu_custom_call" | custom-call | tf_op jit(solution)/shard_map/pallas_call | solution.py:389
  (1 shorter events, 0.0 us)
Async XLA Ops:
  4.0 22.1 %copy-start = (f32[4,16,128]{2,1,0:T(8,128)S(1)}, f32[4,16,128]{2,1,0:T(8,128)}, u32[]{:S(2)}) copy-start(f32[4,16,128]{2,1,0:T(8,128)} %refs_6_.1) | copy-start | bytes 98308
  4.0 22.1 %copy-start.1 = (s32[16384]{0:T(1024)S(1)}, s32[16384]{0:T(1024)}, u32[]{:S(2)}) copy-start(s32[16384]{0:T(1024)} %param.10) | copy-start | bytes 196612
  30.0 7.0 %collective-permute-start.1 = (f32[29,4,128]{2,1,0:T(4,128)S(1)}, f32[29,4,128]{2,1,0:T(4,128)S(1)}, u32[]{:S(2)}, u32[]{:S(2)}) collective-permute-start(f32[29,4,128]{2,1,0:T(4,128)S(1)} %get-tuple-element.12), channel_id=1, source_target_pairs={{1,2},{3,4},{5,6},{2,1},{4,3},{6,5},{9,10},{11,12},{13,14},{10,9},... | collective-permute-start | bytes 178184 | tf_op jit(solution)/shard_map/ppermute | solution.py:401
  30.7 6.3 %collective-permute-start = (f32[28,4,128]{2,1,0:T(4,128)S(1)}, f32[28,4,128]{2,1,0:T(4,128)S(1)}, u32[]{:S(2)}, u32[]{:S(2)}) collective-permute-start(f32[28,4,128]{2,1,0:T(4,128)S(1)} %get-tuple-element.11), channel_id=1, source_target_pairs={{0,1},{2,3},{4,5},{6,7},{1,0},{3,2},{5,4},{7,6},{8,9},{10,11},{12,... | collective-permute-start | bytes 172040 | tf_op jit(solution)/shard_map/ppermute | solution.py:401
  34.2 6.4 %copy-start.2 = (s32[1,8192]{1,0:T(1,128)S(1)}, s32[1,8192]{1,0:T(1,128)}, u32[]{:S(2)}) copy-start(s32[1,8192]{1,0:T(1,128)} %refs_7_.1) | copy-start | bytes 98308
  34.2 6.4 %collective-permute-start.3 = (f32[7,4,16,128]{3,2,1,0:T(8,128)S(1)}, f32[7,4,16,128]{3,2,1,0:T(8,128)S(1)}, u32[]{:S(2)}, u32[]{:S(2)}) collective-permute-start(f32[7,4,16,128]{3,2,1,0:T(8,128)S(1)} %get-tuple-element.10.refs_0_), channel_id=1, source_target_pairs={{8,16},{16,8},{9,17},{17,9},{10,18},{18,10},{11,19},{19,11},{12,20... | collective-permute-start | bytes 688136 | tf_op jit(solution)/shard_map/ppermute | solution.py:401
  35.0 5.6 %collective-permute-start.2 = (f32[7,4,16,128]{3,2,1,0:T(8,128)S(1)}, f32[7,4,16,128]{3,2,1,0:T(8,128)S(1)}, u32[]{:S(2)}, u32[]{:S(2)}) collective-permute-start(f32[7,4,16,128]{3,2,1,0:T(8,128)S(1)} %get-tuple-element.10.refs_0_), channel_id=1, source_target_pairs={{0,8},{16,24},{8,0},{24,16},{1,9},{17,25},{9,1},{25,17},{2,10},{18... | collective-permute-start | bytes 688136 | tf_op jit(solution)/shard_map/ppermute | solution.py:401
  37.0 3.5 %collective-permute-start.5 = (f32[7,16,128]{2,1,0:T(8,128)S(1)}, f32[7,16,128]{2,1,0:T(8,128)S(1)}, u32[]{:S(2)}, u32[]{:S(2)}) collective-permute-start(f32[7,16,128]{2,1,0:T(8,128)S(1)} %get-tuple-element.15), channel_id=1, source_target_pairs={{8,16},{16,8},{9,17},{17,9},{10,18},{18,10},{11,19},{19,11},{12,20... | collective-permute-start | bytes 172040 | tf_op jit(solution)/shard_map/ppermute | solution.py:401
  37.7 2.9 %collective-permute-start.4 = (f32[7,14,128]{2,1,0:T(8,128)S(1)}, f32[7,14,128]{2,1,0:T(8,128)S(1)}, u32[]{:S(2)}, u32[]{:S(2)}) collective-permute-start(f32[7,14,128]{2,1,0:T(8,128)S(1)} %get-tuple-element.14), channel_id=1, source_target_pairs={{0,8},{16,24},{8,0},{24,16},{1,9},{17,25},{9,1},{25,17},{2,10},{18... | collective-permute-start | bytes 150536 | tf_op jit(solution)/shard_map/ppermute | solution.py:401
  43.1 12.3 %copy-start.3 = (s32[1,8192]{1,0:T(1,128)S(1)}, s32[1,8192]{1,0:T(1,128)}, u32[]{:S(2)}) copy-start(s32[1,8192]{1,0:T(1,128)} %order_ref.1) | copy-start | bytes 98308

commit v12 on v11

--- a/solution.py
+++ b/solution.py
@@ -9,6 +9,7 @@
 
 ITERS = 4
 FIELDS = 7
+HEAD = 4
 PIECES = 4
 SPAN = 512
 AT_ONCE = 32
@@ -252,7 +253,7 @@
 
 
 def solve_kernel(
-    mesh_shape, v_ref, sides_ref, even_ref, odd_ref, even_corners_ref, odd_corners_ref, mass_ref, order_ref,
+    mesh_shape, v_ref, sides_ref, even_ref, head_ref, tail_ref, even_corners_ref, odd_corners_ref, mass_ref, order_ref,
     projected_hbm, out_ref, projected_ref, sem,
 ):
     n_src, n_tgt = mesh_shape
@@ -288,7 +289,8 @@
     for f in range(FIELDS):
         packed = jnp.concatenate([even_corners_ref[f, 2 * k :], jnp.zeros((2, hz), F32)], axis=0)
         even = (even_ref[f], even_corners_ref[f, : 2 * k], packed)
-        odd = (odd_ref[f], odd_corners_ref[f, : 2 * k], odd_corners_ref[f, 2 * k :])
+        odd_block = head_ref[f] if f < HEAD else tail_ref[f - HEAD]
+        odd = (odd_block, odd_corners_ref[f, : 2 * k], odd_corners_ref[f, 2 * k :])
         left = slabs(*[jnp.where(a_odd, p, q) for p, q in zip(even, odd)], True)
         right = slabs(*[jnp.where(a_odd, q, p) for p, q in zip(even, odd)], False)
         own = [jnp.concatenate([v_ref[f, x], sides_ref[f, x]], axis=0) for x in range(hx)]
@@ -350,7 +352,7 @@
             jax.ShapeDtypeStruct((FIELDS, hx, hy, hz), F32),
             jax.ShapeDtypeStruct((order.shape[1] // WIDE * 6, 128), F32),
         ),
-        in_specs=[pl.BlockSpec(memory_space=pltpu.VMEM)] * 8,
+        in_specs=[pl.BlockSpec(memory_space=pltpu.VMEM)] * 9,
         out_specs=(pl.BlockSpec(memory_space=pltpu.HBM), pl.BlockSpec(memory_space=pltpu.VMEM)),
         scratch_shapes=[pltpu.VMEM((FIELDS, hx, hy, hz), F32), pltpu.SemaphoreType.DMA],
         compiler_params=pltpu.CompilerParams(vmem_limit_bytes=40 << 20),
@@ -412,12 +414,14 @@
     values = values.reshape(owners, FIELDS, SPAN // 128, 128)
     values = lax.all_to_all(values, both, split_axis=0, concat_axis=0, tiled=True).reshape(-1, 128)
     v, even, odd = scatter_call(values, slot_target.reshape(1, -1), cell_mass)
-    even_block, odd_block = swap(v, "src", 0), swap(v, "src", 1)
+    even_block, head = swap(v, "src", 0), swap(v[:HEAD], "src", 1)
+    across = [(i, i + 2 if i % 2 == 0 else i - 2) for i in range(n_src)]
+    tail = lax.ppermute(even_block[HEAD:], "src", [(i, j) for i, j in across if 0 <= j < n_src])
     even, odd = swap(even, "tgt", 0), swap(odd, "tgt", 1)
     sides, even, odd = sides_call(even, odd, cell_mass.shape[0])
     even, odd = swap(even, "src", 0), swap(odd, "src", 1)
     projected, outgoing = solve_call(
-        (n_src, n_tgt), v, sides, even_block, odd_block, even, odd, cell_mass, send_order
+        (n_src, n_tgt), v, sides, even_block, head, tail, even, odd, cell_mass, send_order
     )
 
     if quota == WIDE:

time: 57.4 us -> 58.3 us (1.016)
  starting transfers between devices: 9.57 us -> 11.1 us
  blocking collectives: 34.3 us -> 33.5 us
    ppermute x0 -> x1, starting transfers between devices: none -> 4.65 us  [on_device(): lax.ppermute(even_block[HEAD:], 'src', [(i, j) for i, j in across if 0 <=...]
    ppermute x6, starting transfers between devices: 9.57 us -> 6.47 us  [swap(): return lax.ppermute(x, axis, pairs + [(j, i) for i, j in pairs])]
    all_to_all x1, blocking collectives: 12.3 us -> 11.5 us  [on_device(): lax.all_to_all(outgoing, both, split_axis=0, concat_axis=0, tiled=True)]
  transfers between devices with their start and end apart: 6 -> 7, of which waited for: 1 -> 1; matrix products, arithmetic and copies ran while one was open for 0% -> 0% of each run, Pallas kernels for 0% -> 0%
where the time goes in v12:
time: 58.3 us; the launch traced here: 57.9 us
  blocking collectives  33.5 us (57%)
  Pallas kernels  11.5 us (20%)
  starting transfers between devices  11.1 us (19%)
  waiting for transfers between devices  0.91 us (2%)
  between operations  0.78 us (1%)
    all_to_all x1, blocking collectives, on_device(): lax.all_to_all(values, both, split_axis=0, concat_axis=0, tiled=True)  22.1 us
    all_to_all x1, blocking collectives, on_device(): lax.all_to_all(outgoing, both, split_axis=0, concat_axis=0, tiled=True)  11.5 us
    ppermute x6, starting transfers between devices, swap(): return lax.ppermute(x, axis, pairs + [(j, i) for i, j in pairs])  6.47 us
    ppermute x1, starting transfers between devices, on_device(): lax.ppermute(even_block[HEAD:], 'src', [(i, j) for i, j in across if 0 <=...  4.65 us
    pallas_call x1, Pallas kernels, scatter_call(): pl.pallas_call(scatter_kernel, out_shape=(jax.ShapeDtypeStruct((FIELDS, h...  3.98 us
    pallas_call x1, Pallas kernels, gather_call(): pl.pallas_call(gather_kernel, out_shape=jax.ShapeDtypeStruct((rows, 128),...  3.32 us
    pallas_call x1, Pallas kernels, solve_call(): pl.pallas_call(kernel, out_shape=(jax.ShapeDtypeStruct((FIELDS, hx, hy, h...  2.51 us
    pallas_call x1, Pallas kernels, place_call(): pl.pallas_call(place_kernel, out_shape=jax.ShapeDtypeStruct((3, order.sha...  1.67 us
  transfers between devices with their start and end apart: 7, of which 1 were waited for; matrix products, arithmetic and copies ran while one was open for 0% of the time, Pallas kernels for 0%

profile of v12, /device:TPU:0, one launch (start us, length us, event | category | flops | bytes accessed | tf_op | source)
XLA Modules:
  0.0 57.9 jit_solution(5076831435659802611)
XLA Ops:
  0.6 3.3 %shard_map.86 = f32[896,128]{1,0:T(8,128)S(1)} custom-call(f32[7,4096]{1,0:T(8,128)} %fields_hbm.1, s32[1,16384]{1,0:T(1,128)} %bitcast.12, f32[1,16384]{1,0:T(1,128)} %bitcast.13), custom_call_target="tpu_custom_call" | custom-call | tf_op jit(solution)/shard_map/pallas_call | solution.py:106
  4.0 0.0 copy-start
  4.0 0.0 copy-start.1
  4.0 22.1 %all_to_all.10 = f32[32,7,4,128]{3,2,1,0:T(4,128)S(1)} all-to-all(f32[32,7,4,128]{3,2,1,0:T(4,128)S(1)} %bitcast.8), channel_id=1, replica_groups=mesh['src'=4,'tgt'=8] {'src','tgt'}, dimensions={0} | all-to-all | bytes 917504 | tf_op jit(solution)/shard_map/all_to_all | solution.py:415
  26.0 0.0 copy-done
  26.0 0.0 copy-done.1
  26.0 4.0 %shard_map.87 = (f32[7,4,16,128]{3,2,1,0:T(8,128)S(1)}, f32[28,4,128]{2,1,0:T(4,128)S(1)}, f32[29,4,128]{2,1,0:T(4,128)S(1)}) custom-call(f32[896,128]{1,0:T(8,128)S(1)} %bitcast.7, s32[1,16384]{1,0:T(1,128)S(1)} %bitcast.11, f32[4,16,128]{2,1,0:T(8,128)S(1)} %copy-done), custom_call_target="tpu_custom_call" | custom-call | tf_op jit(solution)/shard_map/pallas_call | solution.py:176
  30.0 0.1 collective-permute-start.2
  30.1 0.7 %collective-permute-start.1 = (f32[29,4,128]{2,1,0:T(4,128)S(1)}, f32[29,4,128]{2,1,0:T(4,128)S(1)}, u32[]{:S(2)}, u32[]{:S(2)}) collective-permute-start(f32[29,4,128]{2,1,0:T(4,128)S(1)} %get-tuple-element.12), channel_id=1, source_target_pairs={{1,2},{3,4},{5,6},{2,1},{4,3},{6,5},{9,10},{11,12},{13,14},{10,9},... | collective-permute-start | bytes 178184 | tf_op jit(solution)/shard_map/ppermute | solution.py:403
  30.8 3.6 %collective-permute-start = (f32[28,4,128]{2,1,0:T(4,128)S(1)}, f32[28,4,128]{2,1,0:T(4,128)S(1)}, u32[]{:S(2)}, u32[]{:S(2)}) collective-permute-start(f32[28,4,128]{2,1,0:T(4,128)S(1)} %get-tuple-element.11), channel_id=1, source_target_pairs={{0,1},{2,3},{4,5},{6,7},{1,0},{3,2},{5,4},{7,6},{8,9},{10,11},{12,... | collective-permute-start | bytes 172040 | tf_op jit(solution)/shard_map/ppermute | solution.py:403
  34.4 0.7 %collective-permute-start.3 = (f32[4,4,16,128]{3,2,1,0:T(8,128)S(1)}, f32[4,4,16,128]{3,2,1,0:T(8,128)S(1)}, u32[]{:S(2)}, u32[]{:S(2)}) collective-permute-start(f32[4,4,16,128]{3,2,1,0:T(8,128)S(1)} %slice.6), channel_id=1, source_target_pairs={{8,16},{16,8},{9,17},{17,9},{10,18},{18,10},{11,19},{19,11},{12,20... | collective-permute-start | bytes 393224 | tf_op jit(solution)/shard_map/ppermute | solution.py:403
  35.1 0.0 collective-permute-done.2.refs_2_
  35.1 0.0 copy-start.2
  35.1 4.6 %collective-permute-start.4 = (f32[3,4,16,128]{3,2,1,0:T(8,128)S(1)}, f32[3,4,16,128]{3,2,1,0:T(8,128)S(1)}, u32[]{:S(2)}, u32[]{:S(2)}) collective-permute-start(f32[3,4,16,128]{3,2,1,0:T(8,128)S(1)} %slice.8), channel_id=1, source_target_pairs={{0,16},{24,8},{1,17},{25,9},{2,18},{26,10},{3,19},{27,11},{4,20},{... | collective-permute-start | bytes 294920 | tf_op jit(solution)/shard_map/ppermute | solution.py:419
  39.8 0.0 collective-permute-done.even_ref
  39.8 0.0 collective-permute-done.1.odd_ref
  39.8 0.7 %collective-permute-start.6 = (f32[7,16,128]{2,1,0:T(8,128)S(1)}, f32[7,16,128]{2,1,0:T(8,128)S(1)}, u32[]{:S(2)}, u32[]{:S(2)}) collective-permute-start(f32[7,16,128]{2,1,0:T(8,128)S(1)} %get-tuple-element.15), channel_id=1, source_target_pairs={{8,16},{16,8},{9,17},{17,9},{10,18},{18,10},{11,19},{19,11},{12,20... | collective-permute-start | bytes 172040 | tf_op jit(solution)/shard_map/ppermute | solution.py:403
  40.5 0.8 %collective-permute-start.5 = (f32[7,14,128]{2,1,0:T(8,128)S(1)}, f32[7,14,128]{2,1,0:T(8,128)S(1)}, u32[]{:S(2)}, u32[]{:S(2)}) collective-permute-start(f32[7,14,128]{2,1,0:T(8,128)S(1)} %get-tuple-element.14), channel_id=1, source_target_pairs={{0,8},{16,24},{8,0},{24,16},{1,9},{17,25},{9,1},{25,17},{2,10},{18... | collective-permute-start | bytes 150536 | tf_op jit(solution)/shard_map/ppermute | solution.py:403
  41.3 0.9 %collective-permute-done.5.refs_5_ = f32[7,14,128]{2,1,0:T(8,128)S(1)} collective-permute-done((f32[7,14,128]{2,1,0:T(8,128)S(1)}, f32[7,14,128]{2,1,0:T(8,128)S(1)}, u32[]{:S(2)}, u32[]{:S(2)}) %collective-permute-start.5) | collective-permute-done | bytes 50208 | tf_op jit(solution)/shard_map/ppermute | solution.py:403
  42.2 0.0 collective-permute-done.6.refs_6_
  42.2 0.0 collective-permute-done.3.refs_3_
  42.2 0.0 collective-permute-done.4.refs_4_
  42.2 0.0 copy-done.2
  42.2 2.5 %shard_map.89 = (f32[7,4,16,128]{3,2,1,0:T(8,128)}, f32[192,128]{1,0:T(8,128)S(1)}) custom-call(f32[7,4,16,128]{3,2,1,0:T(8,128)S(1)} %get-tuple-element.10.refs_0_, f32[7,4,8,128]{3,2,1,0:T(8,128)S(1)} %get-tuple-element.13.refs_1_, f32[7,4,16,128]{3,2,1,0:T(8,128)S(1)} %collective-permute-done.2.refs_2_, ...), custom_call_target="tpu_custom_call" | custom-call | tf_op jit(solution)/shard_map/pallas_call | solution.py:349
  44.8 0.0 copy-start.3
  44.8 11.5 %all_to_all.11 = f32[32,3,2,128]{3,2,1,0:T(2,128)S(1)} all-to-all(f32[32,3,2,128]{3,2,1,0:T(2,128)S(1)} %bitcast.10), channel_id=1, replica_groups=mesh['src'=4,'tgt'=8] {'src','tgt'}, dimensions={0} | all-to-all | bytes 196608 | tf_op jit(solution)/shard_map/all_to_all | solution.py:429
  56.2 0.0 copy-done.3
  56.2 1.7 %shard_map.90 = f32[3,8192]{1,0:T(4,128)} custom-call(f32[192,128]{1,0:T(8,128)S(1)} %bitcast.9, s32[1,8192]{1,0:T(1,128)S(1)} %copy-done.3), custom_call_target="tpu_custom_call" | custom-call | tf_op jit(solution)/shard_map/pallas_call | solution.py:391
  (3 shorter events, 0.1 us)
Async XLA Ops:
  4.0 22.1 %copy-start = (f32[4,16,128]{2,1,0:T(8,128)S(1)}, f32[4,16,128]{2,1,0:T(8,128)}, u32[]{:S(2)}) copy-start(f32[4,16,128]{2,1,0:T(8,128)} %refs_7_.1) | copy-start | bytes 98308
  4.0 22.1 %copy-start.1 = (s32[16384]{0:T(1024)S(1)}, s32[16384]{0:T(1024)}, u32[]{:S(2)}) copy-start(s32[16384]{0:T(1024)} %param.10) | copy-start | bytes 196612
  30.0 5.0 %collective-permute-start.2 = (f32[7,4,16,128]{3,2,1,0:T(8,128)S(1)}, f32[7,4,16,128]{3,2,1,0:T(8,128)S(1)}, u32[]{:S(2)}, u32[]{:S(2)}) collective-permute-start(f32[7,4,16,128]{3,2,1,0:T(8,128)S(1)} %get-tuple-element.10.refs_0_), channel_id=1, source_target_pairs={{0,8},{16,24},{8,0},{24,16},{1,9},{17,25},{9,1},{25,17},{2,10},{18... | collective-permute-start | bytes 688136 | tf_op jit(solution)/shard_map/ppermute | solution.py:403
  30.1 9.7 %collective-permute-start.1 = (f32[29,4,128]{2,1,0:T(4,128)S(1)}, f32[29,4,128]{2,1,0:T(4,128)S(1)}, u32[]{:S(2)}, u32[]{:S(2)}) collective-permute-start(f32[29,4,128]{2,1,0:T(4,128)S(1)} %get-tuple-element.12), channel_id=1, source_target_pairs={{1,2},{3,4},{5,6},{2,1},{4,3},{6,5},{9,10},{11,12},{13,14},{10,9},... | collective-permute-start | bytes 178184 | tf_op jit(solution)/shard_map/ppermute | solution.py:403
  30.8 9.0 %collective-permute-start = (f32[28,4,128]{2,1,0:T(4,128)S(1)}, f32[28,4,128]{2,1,0:T(4,128)S(1)}, u32[]{:S(2)}, u32[]{:S(2)}) collective-permute-start(f32[28,4,128]{2,1,0:T(4,128)S(1)} %get-tuple-element.11), channel_id=1, source_target_pairs={{0,1},{2,3},{4,5},{6,7},{1,0},{3,2},{5,4},{7,6},{8,9},{10,11},{12,... | collective-permute-start | bytes 172040 | tf_op jit(solution)/shard_map/ppermute | solution.py:403
  34.4 7.8 %collective-permute-start.3 = (f32[4,4,16,128]{3,2,1,0:T(8,128)S(1)}, f32[4,4,16,128]{3,2,1,0:T(8,128)S(1)}, u32[]{:S(2)}, u32[]{:S(2)}) collective-permute-start(f32[4,4,16,128]{3,2,1,0:T(8,128)S(1)} %slice.6), channel_id=1, source_target_pairs={{8,16},{16,8},{9,17},{17,9},{10,18},{18,10},{11,19},{19,11},{12,20... | collective-permute-start | bytes 393224 | tf_op jit(solution)/shard_map/ppermute | solution.py:403
  35.1 7.1 %copy-start.2 = (s32[1,8192]{1,0:T(1,128)S(1)}, s32[1,8192]{1,0:T(1,128)}, u32[]{:S(2)}) copy-start(s32[1,8192]{1,0:T(1,128)} %refs_8_.1) | copy-start | bytes 98308
  35.1 7.1 %collective-permute-start.4 = (f32[3,4,16,128]{3,2,1,0:T(8,128)S(1)}, f32[3,4,16,128]{3,2,1,0:T(8,128)S(1)}, u32[]{:S(2)}, u32[]{:S(2)}) collective-permute-start(f32[3,4,16,128]{3,2,1,0:T(8,128)S(1)} %slice.8), channel_id=1, source_target_pairs={{0,16},{24,8},{1,17},{25,9},{2,18},{26,10},{3,19},{27,11},{4,20},{... | collective-permute-start | bytes 294920 | tf_op jit(solution)/shard_map/ppermute | solution.py:419
  39.8 2.4 %collective-permute-start.6 = (f32[7,16,128]{2,1,0:T(8,128)S(1)}, f32[7,16,128]{2,1,0:T(8,128)S(1)}, u32[]{:S(2)}, u32[]{:S(2)}) collective-permute-start(f32[7,16,128]{2,1,0:T(8,128)S(1)} %get-tuple-element.15), channel_id=1, source_target_pairs={{8,16},{16,8},{9,17},{17,9},{10,18},{18,10},{11,19},{19,11},{12,20... | collective-permute-start | bytes 172040 | tf_op jit(solution)/shard_map/ppermute | solution.py:403
  40.5 1.7 %collective-permute-start.5 = (f32[7,14,128]{2,1,0:T(8,128)S(1)}, f32[7,14,128]{2,1,0:T(8,128)S(1)}, u32[]{:S(2)}, u32[]{:S(2)}) collective-permute-start(f32[7,14,128]{2,1,0:T(8,128)S(1)} %get-tuple-element.14), channel_id=1, source_target_pairs={{0,8},{16,24},{8,0},{24,16},{1,9},{17,25},{9,1},{25,17},{2,10},{18... | collective-permute-start | bytes 150536 | tf_op jit(solution)/shard_map/ppermute | solution.py:403
  44.8 11.5 %copy-start.3 = (s32[1,8192]{1,0:T(1,128)S(1)}, s32[1,8192]{1,0:T(1,128)}, u32[]{:S(2)}) copy-start(s32[1,8192]{1,0:T(1,128)} %order_ref.1) | copy-start | bytes 98308

commit v13 on v11

--- a/solution.py
+++ b/solution.py
@@ -1,3 +1,5 @@
+import functools
+
 import numpy as np
 
 import jax
@@ -118,7 +120,7 @@
     )(*[pltpu.with_memory_space_constraint(x, pltpu.HBM) for x in (fields, index, weight)])
 
 
-def scatter_kernel(value_ref, target_ref, mass_ref, v_ref, even_ref, odd_ref, total):
+def scatter_kernel(value_ref, target_ref, mass_ref, v_ref, strips_ref, total):
     lanes = value_ref.shape[1]
     tiles = SPAN // lanes
     owners = target_ref.shape[1] // SPAN
@@ -151,7 +153,6 @@
         for i in range(4):
             step(n * 4 + i)
 
-    odd_ref[FIELDS * hx] = jnp.zeros((ITERS, hz), F32)
     scale = lax.rsqrt(mass_ref[...])
     half_x = hx // 2
     odd = lax.axis_index("tgt") % 2 == 1
@@ -163,20 +164,19 @@
                 v = s[x * hy : (x + 1) * hy, b * hz : (b + 1) * hz] * scale[at]
                 v_ref[f, at] = v
                 first, last = v[:ITERS], v[hy - ITERS :]
-                even_ref[f * hx + at] = jnp.where(odd, first, last)
-                odd_ref[f * hx + at] = jnp.where(odd, last, first)
+                strips_ref[0, f * hx + at] = jnp.where(odd, first, last)
+                strips_ref[1, f * hx + at] = jnp.where(odd, last, first)
 
 
 def scatter_call(values, target, mass):
     hx, hy, hz = mass.shape
     groups = hx * hy * hz // WIDE
-    even = jax.ShapeDtypeStruct((FIELDS * hx, ITERS, hz), F32)
-    odd = jax.ShapeDtypeStruct((FIELDS * hx + 1, ITERS, hz), F32)
+    strips = jax.ShapeDtypeStruct((2, FIELDS * hx, ITERS, hz), F32)
     return pl.pallas_call(
         scatter_kernel,
-        out_shape=(jax.ShapeDtypeStruct((FIELDS, hx, hy, hz), F32), even, odd),
+        out_shape=(jax.ShapeDtypeStruct((FIELDS, hx, hy, hz), F32), strips),
         in_specs=[pl.BlockSpec(memory_space=pltpu.VMEM)] * 3,
-        out_specs=(pl.BlockSpec(memory_space=pltpu.VMEM),) * 3,
+        out_specs=(pl.BlockSpec(memory_space=pltpu.VMEM),) * 2,
         scratch_shapes=[pltpu.VMEM((2 * FIELDS * groups, WIDE), F32)],
         compiler_params=pltpu.CompilerParams(vmem_limit_bytes=40 << 20),
     )(values, target, mass)
@@ -209,46 +209,59 @@
     return [bulk, shear, soften]
 
 
-def corners(sides):
-    line = row_ids(2 * ITERS, sides[0].shape[1])
-    near = pltpu.roll(sides[1], 2, 0)
-    far = jnp.where(line == 4, pltpu.roll(sides[2], 4, 0), pltpu.roll(sides[2], 6, 0))
-    return sides[0], jnp.where(line < 4, near, far)
-
-
-def sides_kernel(even_ref, odd_ref, sides_ref, to_even_ref, to_odd_ref):
+def pack_corners(sides):
+    first, second, third = sides[:3]
+    line = row_ids(2 * ITERS, first.shape[1])
+    far = jnp.where(line == 3, pltpu.roll(third, 3, 0), pltpu.roll(third, 5, 0))
+    first = jnp.where((line == 3) | (line == 4), far, first)
+    return first[:4], first[4:], pltpu.roll(second, 2, 0)[:4]
+
+
+def unpack_corners(pieces):
+    first = jnp.concatenate([pieces[0], pieces[1]], axis=0)
+    line = row_ids(2 * ITERS, first.shape[1])
+    second = pltpu.roll(jnp.concatenate([pieces[2], pieces[2]], axis=0), 6, 0)
+    third = jnp.where(line < 4, pltpu.roll(first, 5, 0), pltpu.roll(first, 3, 0))
+    return [first, second, third]
+
+
+def inner(axis, count):
+    index = lax.axis_index(axis)
+    return (index > 0) & (index < count - 1)
+
+
+def sides_kernel(n_tgt, even_ref, odd_ref, block_ref, sides_ref, corners_ref):
+    del block_ref
     hx = sides_ref.shape[1]
     b_odd = lax.axis_index("tgt") % 2 == 1
     a_odd = lax.axis_index("src") % 2 == 1
+    has_odd = inner("tgt", n_tgt)
     for f in range(FIELDS):
         sides = []
         for x in range(hx):
-            even_side, odd_side = even_ref[f * hx + x], odd_ref[f * hx + x]
+            even_side = even_ref[0, f * hx + x]
+            odd_side = jnp.where(has_odd, odd_ref[f * hx + x], 0.0)
             right = jnp.where(b_odd, odd_side, even_side)
             left = jnp.where(b_odd, even_side, odd_side)
             sides.append(jnp.concatenate([right, left], axis=0))
             sides_ref[f, x] = sides[x]
-        to_left, to_right = corners(sides), corners(sides[::-1])
-        to_even_ref[f, :8] = jnp.where(a_odd, to_left[0], to_right[0])
-        to_even_ref[f, 8:14] = jnp.where(a_odd, to_left[1], to_right[1])[:6]
-        to_odd_ref[f, :8] = jnp.where(a_odd, to_right[0], to_left[0])
-        to_odd_ref[f, 8:] = jnp.where(a_odd, to_right[1], to_left[1])
-
-
-def sides_call(even, odd, hx):
-    hz = even.shape[2]
+        for i, (to_left, to_right) in enumerate(zip(pack_corners(sides), pack_corners(sides[::-1]))):
+            corners_ref[0, f * 3 + i] = jnp.where(a_odd, to_left, to_right)
+            corners_ref[1, f * 3 + i] = jnp.where(a_odd, to_right, to_left)
+
+
+def sides_call(n_tgt, even, odd, block):
+    hx, _, hz = block.shape[1:]
     return pl.pallas_call(
-        sides_kernel,
+        functools.partial(sides_kernel, n_tgt),
         out_shape=(
             jax.ShapeDtypeStruct((FIELDS, hx, 2 * ITERS, hz), F32),
-            jax.ShapeDtypeStruct((FIELDS, 4 * ITERS - 2, hz), F32),
-            jax.ShapeDtypeStruct((FIELDS, 4 * ITERS, hz), F32),
+            jax.ShapeDtypeStruct((2, FIELDS * 3, 4, hz), F32),
         ),
-        in_specs=[pl.BlockSpec(memory_space=pltpu.VMEM)] * 2,
-        out_specs=(pl.BlockSpec(memory_space=pltpu.VMEM),) * 3,
+        in_specs=[pl.BlockSpec(memory_space=pltpu.VMEM)] * 2 + [pl.BlockSpec(memory_space=pl.ANY)],
+        out_specs=(pl.BlockSpec(memory_space=pltpu.VMEM),) * 2,
         compiler_params=pltpu.CompilerParams(vmem_limit_bytes=4 << 20),
-        cost_estimate=pl.CostEstimate(flops=40 * 10**9, bytes_accessed=40 * 10**6, transcendentals=0),
-    )(even, odd)
+    )(even, odd, block)
 
 
 def solve_kernel(
@@ -275,22 +288,21 @@
 
     line = row_ids(2 * k, hz)
 
-    def slabs(own, first, packed, from_left):
-        second = pltpu.roll(packed, 6, 0)
-        third = jnp.where(line < 4, pltpu.roll(packed, 4, 0), pltpu.roll(packed, 2, 0))
-        sides = [first, second, third] + [jnp.zeros((2 * k, hz), F32)] * (hx - 3)
+    def slabs(own, ends, from_left):
+        sides = unpack_corners(ends) + [jnp.zeros((2 * k, hz), F32)] * (hx - 3)
         if from_left:
             sides = sides[::-1]
         return [jnp.concatenate([own[x], side], axis=0) for x, side in enumerate(sides)]
 
     a_odd = a % 2 == 1
+    has_odd = inner("src", n_src)
 
     for f in range(FIELDS):
-        packed = jnp.concatenate([even_corners_ref[f, 2 * k :], jnp.zeros((2, hz), F32)], axis=0)
-        even = (even_ref[f], even_corners_ref[f, : 2 * k], packed)
-        odd = (odd_ref[f], odd_corners_ref[f, : 2 * k], odd_corners_ref[f, 2 * k :])
-        left = slabs(*[jnp.where(a_odd, p, q) for p, q in zip(even, odd)], True)
-        right = slabs(*[jnp.where(a_odd, q, p) for p, q in zip(even, odd)], False)
+        even = [even_corners_ref[0, f * 3 + i] for i in range(3)]
+        odd = [jnp.where(has_odd, odd_corners_ref[f * 3 + i], 0.0) for i in range(3)]
+        odd_block = jnp.where(has_odd, odd_ref[f], 0.0)
+        left = slabs(jnp.where(a_odd, even_ref[f], odd_block), [jnp.where(a_odd, p, q) for p, q in zip(even, odd)], True)
+        right = slabs(jnp.where(a_odd, odd_block, even_ref[f]), [jnp.where(a_odd, q, p) for p, q in zip(even, odd)], False)
         own = [jnp.concatenate([v_ref[f, x], sides_ref[f, x]], axis=0) for x in range(hx)]
         base = left + own + right
         u = [COEFS[k] * e for e in base]
@@ -396,9 +408,17 @@
     )(arrived, order)
 
 
-def swap(x, axis, start):
-    pairs = [(i, i + 1) for i in range(start, lax.axis_size(axis) - 1, 2)]
-    return lax.ppermute(x, axis, pairs + [(j, i) for i, j in pairs])
+def swap(x, axis):
+    return lax.ppermute(x, axis, [(i, i ^ 1) for i in range(lax.axis_size(axis))])
+
+
+def ring(x, axis, evens):
+    count = lax.axis_size(axis)
+    pairs = []
+    for i in range(count):
+        to = i + (evens if i % 2 == 0 else -evens)
+        pairs.append((i, to if 0 <= to < count else i ^ 1))
+    return lax.ppermute(x, axis, pairs)
 
 
 def on_device(source_fields, slot_source, slot_weight, slot_target, cell_mass, send_order, place_order):
@@ -411,13 +431,17 @@
     values = gather_call(source_fields, slot_source.reshape(1, -1), slot_weight.reshape(1, -1))
     values = values.reshape(owners, FIELDS, SPAN // 128, 128)
     values = lax.all_to_all(values, both, split_axis=0, concat_axis=0, tiled=True).reshape(-1, 128)
-    v, even, odd = scatter_call(values, slot_target.reshape(1, -1), cell_mass)
-    even_block, odd_block = swap(v, "src", 0), swap(v, "src", 1)
-    even, odd = swap(even, "tgt", 0), swap(odd, "tgt", 1)
-    sides, even, odd = sides_call(even, odd, cell_mass.shape[0])
-    even, odd = swap(even, "src", 0), swap(odd, "src", 1)
+    v, strips = scatter_call(values, slot_target.reshape(1, -1), cell_mass)
+    strips = swap(strips, "tgt")
+    even_block = swap(v, "src")
+    far_block = ring(v, "src", -2)
+    odd_strips = ring(strips[1], "tgt", 2)
+    sides, ends = sides_call(n_tgt, strips, odd_strips, far_block)
+    ends = swap(ends, "src")
+    odd_ends = ring(ends[1], "src", 2)
+    odd_block = swap(far_block, "src")
     projected, outgoing = solve_call(
-        (n_src, n_tgt), v, sides, even_block, odd_block, even, odd, cell_mass, send_order
+        (n_src, n_tgt), v, sides, even_block, odd_block, ends, odd_ends, cell_mass, send_order
     )
 
     if quota == WIDE:

time: 57.4 us -> 58.9 us (1.026)
  waiting for transfers between devices: 0.9 us -> 9.39 us
  starting transfers between devices: 9.57 us -> 3.8 us
  blocking collectives: 34.3 us -> 33.2 us
    ppermute x6 -> x7, waiting for transfers between devices: 0.9 us -> 9.39 us  [the longest x3 4.76 us: ring(): return lax.ppermute(x, axis, pairs)]
    ppermute x6 -> x7, starting transfers between devices: 9.57 us -> 3.8 us  [the longest x3 2.23 us: ring(): return lax.ppermute(x, axis, pairs)]
    all_to_all x1, blocking collectives: 12.3 us -> 11.2 us  [on_device(): lax.all_to_all(outgoing, both, split_axis=0, concat_axis=0, tiled=True)]
  transfers between devices with their start and end apart: 6 -> 7, of which waited for: 1 -> 4; matrix products, arithmetic and copies ran while one was open for 0% -> 0% of each run, Pallas kernels for 0% -> 0%
where the time goes in v13:
time: 58.9 us; the launch traced here: 58.7 us
  blocking collectives  33.2 us (56%)
  Pallas kernels  11.5 us (20%)
  waiting for transfers between devices  9.39 us (16%)
  starting transfers between devices  3.8 us (6%)
  between operations  0.71 us (1%)
    all_to_all x1, blocking collectives, on_device(): lax.all_to_all(values, both, split_axis=0, concat_axis=0, tiled=True)  22.1 us
    all_to_all x1, blocking collectives, on_device(): lax.all_to_all(outgoing, both, split_axis=0, concat_axis=0, tiled=True)  11.2 us
    ppermute x3, waiting for transfers between devices, ring(): return lax.ppermute(x, axis, pairs)  4.76 us
    ppermute x4, waiting for transfers between devices, swap(): lax.ppermute(x, axis, [(i, i ^ 1) for i in range(lax.axis_size(axis))])  4.63 us
    pallas_call x1, Pallas kernels, scatter_call(): pl.pallas_call(scatter_kernel, out_shape=(jax.ShapeDtypeStruct((FIELDS, h...  3.98 us
    pallas_call x1, Pallas kernels, gather_call(): pl.pallas_call(gather_kernel, out_shape=jax.ShapeDtypeStruct((rows, 128),...  3.32 us
    pallas_call x1, Pallas kernels, solve_call(): pl.pallas_call(kernel, out_shape=(jax.ShapeDtypeStruct((FIELDS, hx, hy, h...  2.51 us
    ppermute x3, starting transfers between devices, ring(): return lax.ppermute(x, axis, pairs)  2.23 us
  transfers between devices with their start and end apart: 7, of which 4 were waited for; matrix products, arithmetic and copies ran while one was open for 0% of the time, Pallas kernels for 0%

profile of v13, /device:TPU:0, one launch (start us, length us, event | category | flops | bytes accessed | tf_op | source)
XLA Modules:
  0.0 58.7 jit_solution(17747237548638642912)
XLA Ops:
  0.6 3.3 %shard_map.86 = f32[896,128]{1,0:T(8,128)S(1)} custom-call(f32[7,4096]{1,0:T(8,128)} %fields_hbm.1, s32[1,16384]{1,0:T(1,128)} %bitcast.16, f32[1,16384]{1,0:T(1,128)} %bitcast.17), custom_call_target="tpu_custom_call" | custom-call | tf_op jit(solution)/shard_map/pallas_call | solution.py:107
  4.0 0.0 copy-start
  4.0 0.0 copy-start.1
  4.0 22.1 %all_to_all.10 = f32[32,7,4,128]{3,2,1,0:T(4,128)S(1)} all-to-all(f32[32,7,4,128]{3,2,1,0:T(4,128)S(1)} %bitcast.12), channel_id=1, replica_groups=mesh['src'=4,'tgt'=8] {'src','tgt'}, dimensions={0} | all-to-all | bytes 917504 | tf_op jit(solution)/shard_map/all_to_all | solution.py:433
  26.0 0.0 copy-done
  26.0 0.0 copy-done.1
  26.0 4.0 %shard_map.87 = (f32[7,4,16,128]{3,2,1,0:T(8,128)S(1)}, f32[2,28,4,128]{3,2,1,0:T(4,128)S(1)}) custom-call(f32[896,128]{1,0:T(8,128)S(1)} %bitcast.11, s32[1,16384]{1,0:T(1,128)S(1)} %bitcast.15, f32[4,16,128]{2,1,0:T(8,128)S(1)} %copy-done), custom_call_target="tpu_custom_call" | custom-call | tf_op jit(solution)/shard_map/pallas_call | solution.py:175
  30.0 0.9 %collective-permute-start = (f32[2,28,4,128]{3,2,1,0:T(4,128)S(1)}, f32[2,28,4,128]{3,2,1,0:T(4,128)S(1)}, u32[]{:S(2)}, u32[]{:S(2)}) collective-permute-start(f32[2,28,4,128]{3,2,1,0:T(4,128)S(1)} %get-tuple-element.9), channel_id=1, source_target_pairs={{0,1},{1,0},{2,3},{3,2},{4,5},{5,4},{6,7},{7,6},{8,9},{9,8},{10,11... | collective-permute-start | bytes 344072 | tf_op jit(solution)/shard_map/ppermute | solution.py:412
  31.0 0.0 collective-permute-start.2
  31.0 3.9 %collective-permute-done.even_ref = f32[2,28,4,128]{3,2,1,0:T(4,128)S(1)} collective-permute-done((f32[2,28,4,128]{3,2,1,0:T(4,128)S(1)}, f32[2,28,4,128]{3,2,1,0:T(4,128)S(1)}, u32[]{:S(2)}, u32[]{:S(2)}) %collective-permute-start) | collective-permute-done | bytes 114720 | tf_op jit(solution)/shard_map/ppermute | solution.py:412
  34.9 1.1 %collective-permute-start.1 = (f32[28,4,128]{2,1,0:T(4,128)S(1)}, f32[28,4,128]{2,1,0:T(4,128)S(1)}, u32[]{:S(2)}, u32[]{:S(2)}) collective-permute-start(f32[28,4,128]{2,1,0:T(4,128)S(1)} %slice_bitcast_fusion), channel_id=1, source_target_pairs={{0,2},{1,0},{2,4},{3,1},{4,6},{5,3},{6,7},{7,5},{8,10},{9,8},{10,1... | collective-permute-start | bytes 172040 | tf_op jit(solution)/shard_map/ppermute | solution.py:421
  36.0 3.1 %collective-permute-done.1.odd_ref = f32[28,4,128]{2,1,0:T(4,128)S(1)} collective-permute-done((f32[28,4,128]{2,1,0:T(4,128)S(1)}, f32[28,4,128]{2,1,0:T(4,128)S(1)}, u32[]{:S(2)}, u32[]{:S(2)}) %collective-permute-start.1) | collective-permute-done | bytes 57376 | tf_op jit(solution)/shard_map/ppermute | solution.py:421
  39.1 0.0 collective-permute-done.2.block_ref
  39.1 0.0 copy-start.2
  39.1 0.1 collective-permute-start.5
  39.2 0.5 collective-permute-start.3
  39.7 0.1 collective-permute-start.4
  39.8 0.7 %collective-permute-done.5.refs_4_ = f32[2,21,4,128]{3,2,1,0:T(4,128)S(1)} collective-permute-done((f32[2,21,4,128]{3,2,1,0:T(4,128)S(1)}, f32[2,21,4,128]{3,2,1,0:T(4,128)S(1)}, u32[]{:S(2)}, u32[]{:S(2)}) %collective-permute-start.5) | collective-permute-done | bytes 86048 | tf_op jit(solution)/shard_map/ppermute | solution.py:412
  40.5 1.1 %collective-permute-start.6 = (f32[21,4,128]{2,1,0:T(4,128)S(1)}, f32[21,4,128]{2,1,0:T(4,128)S(1)}, u32[]{:S(2)}, u32[]{:S(2)}) collective-permute-start(f32[21,4,128]{2,1,0:T(4,128)S(1)} %slice_bitcast_fusion.1), channel_id=1, source_target_pairs={{0,16},{8,0},{16,24},{24,8},{1,17},{9,1},{17,25},{25,9},{2,18},{10... | collective-permute-start | bytes 129032 | tf_op jit(solution)/shard_map/ppermute | solution.py:421
  41.6 0.0 collective-permute-done.3.refs_2_
  41.6 1.7 %collective-permute-done.6.refs_5_ = f32[21,4,128]{2,1,0:T(4,128)S(1)} collective-permute-done((f32[21,4,128]{2,1,0:T(4,128)S(1)}, f32[21,4,128]{2,1,0:T(4,128)S(1)}, u32[]{:S(2)}, u32[]{:S(2)}) %collective-permute-start.6) | collective-permute-done | bytes 43040 | tf_op jit(solution)/shard_map/ppermute | solution.py:421
  43.3 0.0 collective-permute-done.4.refs_3_
  43.3 0.0 copy-done.2
  43.3 2.5 %shard_map.89 = (f32[7,4,16,128]{3,2,1,0:T(8,128)}, f32[192,128]{1,0:T(8,128)S(1)}) custom-call(f32[7,4,16,128]{3,2,1,0:T(8,128)S(1)} %get-tuple-element.8.refs_0_, f32[7,4,8,128]{3,2,1,0:T(8,128)S(1)} %get-tuple-element.10.refs_1_, f32[7,4,16,128]{3,2,1,0:T(8,128)S(1)} %collective-permute-done.3.refs_2_, ...), custom_call_target="tpu_custom_call" | custom-call | tf_op jit(solution)/shard_map/pallas_call | solution.py:359
  45.8 0.0 copy-start.3
  45.8 11.2 %all_to_all.11 = f32[32,3,2,128]{3,2,1,0:T(2,128)S(1)} all-to-all(f32[32,3,2,128]{3,2,1,0:T(2,128)S(1)} %bitcast.14), channel_id=1, replica_groups=mesh['src'=4,'tgt'=8] {'src','tgt'}, dimensions={0} | all-to-all | bytes 196608 | tf_op jit(solution)/shard_map/all_to_all | solution.py:449
  57.0 0.0 copy-done.3
  57.0 1.7 %shard_map.90 = f32[3,8192]{1,0:T(4,128)} custom-call(f32[192,128]{1,0:T(8,128)S(1)} %bitcast.13, s32[1,8192]{1,0:T(1,128)S(1)} %copy-done.3), custom_call_target="tpu_custom_call" | custom-call | tf_op jit(solution)/shard_map/pallas_call | solution.py:401
  (3 shorter events, 0.1 us)
Async XLA Ops:
  4.0 22.1 %copy-start = (f32[4,16,128]{2,1,0:T(8,128)S(1)}, f32[4,16,128]{2,1,0:T(8,128)}, u32[]{:S(2)}) copy-start(f32[4,16,128]{2,1,0:T(8,128)} %refs_6_.1) | copy-start | bytes 98308
  4.0 22.1 %copy-start.1 = (s32[16384]{0:T(1024)S(1)}, s32[16384]{0:T(1024)}, u32[]{:S(2)}) copy-start(s32[16384]{0:T(1024)} %param.10) | copy-start | bytes 196612
  30.0 4.9 %collective-permute-start = (f32[2,28,4,128]{3,2,1,0:T(4,128)S(1)}, f32[2,28,4,128]{3,2,1,0:T(4,128)S(1)}, u32[]{:S(2)}, u32[]{:S(2)}) collective-permute-start(f32[2,28,4,128]{3,2,1,0:T(4,128)S(1)} %get-tuple-element.9), channel_id=1, source_target_pairs={{0,1},{1,0},{2,3},{3,2},{4,5},{5,4},{6,7},{7,6},{8,9},{9,8},{10,11... | collective-permute-start | bytes 344072 | tf_op jit(solution)/shard_map/ppermute | solution.py:412
  31.0 8.1 %collective-permute-start.2 = (f32[7,4,16,128]{3,2,1,0:T(8,128)S(1)}, f32[7,4,16,128]{3,2,1,0:T(8,128)S(1)}, u32[]{:S(2)}, u32[]{:S(2)}) collective-permute-start(f32[7,4,16,128]{3,2,1,0:T(8,128)S(1)} %get-tuple-element.8.refs_0_), channel_id=1, source_target_pairs={{0,8},{8,24},{16,0},{24,16},{1,9},{9,25},{17,1},{25,17},{2,10},{10... | collective-permute-start | bytes 688136 | tf_op jit(solution)/shard_map/ppermute | solution.py:421
  34.9 4.2 %collective-permute-start.1 = (f32[28,4,128]{2,1,0:T(4,128)S(1)}, f32[28,4,128]{2,1,0:T(4,128)S(1)}, u32[]{:S(2)}, u32[]{:S(2)}) collective-permute-start(f32[28,4,128]{2,1,0:T(4,128)S(1)} %slice_bitcast_fusion), channel_id=1, source_target_pairs={{0,2},{1,0},{2,4},{3,1},{4,6},{5,3},{6,7},{7,5},{8,10},{9,8},{10,1... | collective-permute-start | bytes 172040 | tf_op jit(solution)/shard_map/ppermute | solution.py:421
  39.1 4.2 %copy-start.2 = (s32[1,8192]{1,0:T(1,128)S(1)}, s32[1,8192]{1,0:T(1,128)}, u32[]{:S(2)}) copy-start(s32[1,8192]{1,0:T(1,128)} %refs_7_.1) | copy-start | bytes 98308
  39.1 1.3 %collective-permute-start.5 = (f32[2,21,4,128]{3,2,1,0:T(4,128)S(1)}, f32[2,21,4,128]{3,2,1,0:T(4,128)S(1)}, u32[]{:S(2)}, u32[]{:S(2)}) collective-permute-start(f32[2,21,4,128]{3,2,1,0:T(4,128)S(1)} %get-tuple-element.11), channel_id=1, source_target_pairs={{0,8},{8,0},{16,24},{24,16},{1,9},{9,1},{17,25},{25,17},{2,10},{10... | collective-permute-start | bytes 258056 | tf_op jit(solution)/shard_map/ppermute | solution.py:412
  39.2 2.4 %collective-permute-start.3 = (f32[7,4,16,128]{3,2,1,0:T(8,128)S(1)}, f32[7,4,16,128]{3,2,1,0:T(8,128)S(1)}, u32[]{:S(2)}, u32[]{:S(2)}) collective-permute-start(f32[7,4,16,128]{3,2,1,0:T(8,128)S(1)} %get-tuple-element.8.refs_0_), channel_id=1, source_target_pairs={{0,8},{8,0},{16,24},{24,16},{1,9},{9,1},{17,25},{25,17},{2,10},{10... | collective-permute-start | bytes 688136 | tf_op jit(solution)/shard_map/ppermute | solution.py:412
  39.7 3.6 %collective-permute-start.4 = (f32[7,4,16,128]{3,2,1,0:T(8,128)S(1)}, f32[7,4,16,128]{3,2,1,0:T(8,128)S(1)}, u32[]{:S(2)}, u32[]{:S(2)}) collective-permute-start(f32[7,4,16,128]{3,2,1,0:T(8,128)S(1)} %collective-permute-done.2.block_ref), channel_id=1, source_target_pairs={{0,8},{8,0},{16,24},{24,16},{1,9},{9,1},{17,25},{25,17},{2,10},{10... | collective-permute-start | bytes 688136 | tf_op jit(solution)/shard_map/ppermute | solution.py:412
  40.5 2.8 %collective-permute-start.6 = (f32[21,4,128]{2,1,0:T(4,128)S(1)}, f32[21,4,128]{2,1,0:T(4,128)S(1)}, u32[]{:S(2)}, u32[]{:S(2)}) collective-permute-start(f32[21,4,128]{2,1,0:T(4,128)S(1)} %slice_bitcast_fusion.1), channel_id=1, source_target_pairs={{0,16},{8,0},{16,24},{24,8},{1,17},{9,1},{17,25},{25,9},{2,18},{10... | collective-permute-start | bytes 129032 | tf_op jit(solution)/shard_map/ppermute | solution.py:421
  45.8 11.2 %copy-start.3 = (s32[1,8192]{1,0:T(1,128)S(1)}, s32[1,8192]{1,0:T(1,128)}, u32[]{:S(2)}) copy-start(s32[1,8192]{1,0:T(1,128)} %order_ref.1) | copy-start | bytes 98308

commit v14 on v11

--- a/solution.py
+++ b/solution.py
@@ -151,7 +151,7 @@
         for i in range(4):
             step(n * 4 + i)
 
-    odd_ref[FIELDS * hx] = jnp.zeros((ITERS, hz), F32)
+    even_ref[FIELDS * hx] = jnp.zeros((ITERS, hz), F32)
     scale = lax.rsqrt(mass_ref[...])
     half_x = hx // 2
     odd = lax.axis_index("tgt") % 2 == 1
@@ -170,8 +170,8 @@
 def scatter_call(values, target, mass):
     hx, hy, hz = mass.shape
     groups = hx * hy * hz // WIDE
-    even = jax.ShapeDtypeStruct((FIELDS * hx, ITERS, hz), F32)
-    odd = jax.ShapeDtypeStruct((FIELDS * hx + 1, ITERS, hz), F32)
+    even = jax.ShapeDtypeStruct((FIELDS * hx + 1, ITERS, hz), F32)
+    odd = jax.ShapeDtypeStruct((FIELDS * hx, ITERS, hz), F32)
     return pl.pallas_call(
         scatter_kernel,
         out_shape=(jax.ShapeDtypeStruct((FIELDS, hx, hy, hz), F32), even, odd),

time: 57.4 us -> 57.1 us (level)
  starting transfers between devices: 9.57 us -> 7.15 us
  blocking collectives: 34.3 us -> 36.4 us
    ppermute x6, starting transfers between devices: 9.57 us -> 7.15 us  [swap(): return lax.ppermute(x, axis, pairs + [(j, i) for i, j in pairs])]
    all_to_all x1, blocking collectives: 12.3 us -> 14.4 us  [on_device(): lax.all_to_all(outgoing, both, split_axis=0, concat_axis=0, tiled=True)]
where the time goes in v14:
time: 57.1 us; the launch traced here: 56.7 us
  blocking collectives  36.4 us (64%)
  Pallas kernels  11.5 us (20%)
  starting transfers between devices  7.15 us (13%)
  waiting for transfers between devices  0.91 us (2%)
  between operations  0.73 us (1%)
    all_to_all x1, blocking collectives, on_device(): lax.all_to_all(values, both, split_axis=0, concat_axis=0, tiled=True)  22.1 us
    all_to_all x1, blocking collectives, on_device(): lax.all_to_all(outgoing, both, split_axis=0, concat_axis=0, tiled=True)  14.4 us
    ppermute x6, starting transfers between devices, swap(): return lax.ppermute(x, axis, pairs + [(j, i) for i, j in pairs])  7.15 us
    pallas_call x1, Pallas kernels, scatter_call(): pl.pallas_call(scatter_kernel, out_shape=(jax.ShapeDtypeStruct((FIELDS, h...  3.98 us
    pallas_call x1, Pallas kernels, gather_call(): pl.pallas_call(gather_kernel, out_shape=jax.ShapeDtypeStruct((rows, 128),...  3.32 us
    pallas_call x1, Pallas kernels, solve_call(): pl.pallas_call(kernel, out_shape=(jax.ShapeDtypeStruct((FIELDS, hx, hy, h...  2.51 us
    pallas_call x1, Pallas kernels, place_call(): pl.pallas_call(place_kernel, out_shape=jax.ShapeDtypeStruct((3, order.sha...  1.67 us
  transfers between devices with their start and end apart: 6, of which 1 were waited for; matrix products, arithmetic and copies ran while one was open for 0% of the time, Pallas kernels for 0%

profile of v14, /device:TPU:0, one launch (start us, length us, event | category | flops | bytes accessed | tf_op | source)
XLA Modules:
  0.0 56.7 jit_solution(11257978121163862340)
XLA Ops:
  0.6 3.3 %shard_map.86 = f32[896,128]{1,0:T(8,128)S(1)} custom-call(f32[7,4096]{1,0:T(8,128)} %fields_hbm.1, s32[1,16384]{1,0:T(1,128)} %bitcast.12, f32[1,16384]{1,0:T(1,128)} %bitcast.13), custom_call_target="tpu_custom_call" | custom-call | tf_op jit(solution)/shard_map/pallas_call | solution.py:105
  4.0 0.0 copy-start
  4.0 0.0 copy-start.1
  4.0 22.1 %all_to_all.10 = f32[32,7,4,128]{3,2,1,0:T(4,128)S(1)} all-to-all(f32[32,7,4,128]{3,2,1,0:T(4,128)S(1)} %bitcast.8), channel_id=1, replica_groups=mesh['src'=4,'tgt'=8] {'src','tgt'}, dimensions={0} | all-to-all | bytes 917504 | tf_op jit(solution)/shard_map/all_to_all | solution.py:413
  26.0 0.0 copy-done
  26.0 0.0 copy-done.1
  26.0 4.0 %shard_map.87 = (f32[7,4,16,128]{3,2,1,0:T(8,128)S(1)}, f32[29,4,128]{2,1,0:T(4,128)S(1)}, f32[28,4,128]{2,1,0:T(4,128)S(1)}) custom-call(f32[896,128]{1,0:T(8,128)S(1)} %bitcast.7, s32[1,16384]{1,0:T(1,128)S(1)} %bitcast.11, f32[4,16,128]{2,1,0:T(8,128)S(1)} %copy-done), custom_call_target="tpu_custom_call" | custom-call | tf_op jit(solution)/shard_map/pallas_call | solution.py:175
  30.0 0.9 %collective-permute-start = (f32[29,4,128]{2,1,0:T(4,128)S(1)}, f32[29,4,128]{2,1,0:T(4,128)S(1)}, u32[]{:S(2)}, u32[]{:S(2)}) collective-permute-start(f32[29,4,128]{2,1,0:T(4,128)S(1)} %get-tuple-element.11), channel_id=1, source_target_pairs={{0,1},{2,3},{4,5},{6,7},{1,0},{3,2},{5,4},{7,6},{8,9},{10,11},{12,... | collective-permute-start | bytes 178184 | tf_op jit(solution)/shard_map/ppermute | solution.py:401
  31.0 0.7 %collective-permute-start.1 = (f32[28,4,128]{2,1,0:T(4,128)S(1)}, f32[28,4,128]{2,1,0:T(4,128)S(1)}, u32[]{:S(2)}, u32[]{:S(2)}) collective-permute-start(f32[28,4,128]{2,1,0:T(4,128)S(1)} %get-tuple-element.12), channel_id=1, source_target_pairs={{1,2},{3,4},{5,6},{2,1},{4,3},{6,5},{9,10},{11,12},{13,14},{10,9},... | collective-permute-start | bytes 172040 | tf_op jit(solution)/shard_map/ppermute | solution.py:401
  31.6 0.0 copy-start.2
  31.6 0.7 %collective-permute-start.3 = (f32[7,4,16,128]{3,2,1,0:T(8,128)S(1)}, f32[7,4,16,128]{3,2,1,0:T(8,128)S(1)}, u32[]{:S(2)}, u32[]{:S(2)}) collective-permute-start(f32[7,4,16,128]{3,2,1,0:T(8,128)S(1)} %get-tuple-element.10.refs_0_), channel_id=1, source_target_pairs={{8,16},{16,8},{9,17},{17,9},{10,18},{18,10},{11,19},{19,11},{12,20... | collective-permute-start | bytes 688136 | tf_op jit(solution)/shard_map/ppermute | solution.py:401
  32.3 2.0 %collective-permute-start.2 = (f32[7,4,16,128]{3,2,1,0:T(8,128)S(1)}, f32[7,4,16,128]{3,2,1,0:T(8,128)S(1)}, u32[]{:S(2)}, u32[]{:S(2)}) collective-permute-start(f32[7,4,16,128]{3,2,1,0:T(8,128)S(1)} %get-tuple-element.10.refs_0_), channel_id=1, source_target_pairs={{0,8},{16,24},{8,0},{24,16},{1,9},{17,25},{9,1},{25,17},{2,10},{18... | collective-permute-start | bytes 688136 | tf_op jit(solution)/shard_map/ppermute | solution.py:401
  34.3 0.0 collective-permute-done.1.odd_ref
  34.3 0.0 collective-permute-done.even_ref
  34.3 0.7 %collective-permute-start.5 = (f32[7,16,128]{2,1,0:T(8,128)S(1)}, f32[7,16,128]{2,1,0:T(8,128)S(1)}, u32[]{:S(2)}, u32[]{:S(2)}) collective-permute-start(f32[7,16,128]{2,1,0:T(8,128)S(1)} %get-tuple-element.15), channel_id=1, source_target_pairs={{8,16},{16,8},{9,17},{17,9},{10,18},{18,10},{11,19},{19,11},{12,20... | collective-permute-start | bytes 172040 | tf_op jit(solution)/shard_map/ppermute | solution.py:401
  35.0 2.3 %collective-permute-start.4 = (f32[7,14,128]{2,1,0:T(8,128)S(1)}, f32[7,14,128]{2,1,0:T(8,128)S(1)}, u32[]{:S(2)}, u32[]{:S(2)}) collective-permute-start(f32[7,14,128]{2,1,0:T(8,128)S(1)} %get-tuple-element.14), channel_id=1, source_target_pairs={{0,8},{16,24},{8,0},{24,16},{1,9},{17,25},{9,1},{25,17},{2,10},{18... | collective-permute-start | bytes 150536 | tf_op jit(solution)/shard_map/ppermute | solution.py:401
  37.3 0.9 %collective-permute-done.4.refs_4_ = f32[7,14,128]{2,1,0:T(8,128)S(1)} collective-permute-done((f32[7,14,128]{2,1,0:T(8,128)S(1)}, f32[7,14,128]{2,1,0:T(8,128)S(1)}, u32[]{:S(2)}, u32[]{:S(2)}) %collective-permute-start.4) | collective-permute-done | bytes 50208 | tf_op jit(solution)/shard_map/ppermute | solution.py:401
  38.2 0.0 collective-permute-done.5.refs_5_
  38.2 0.0 collective-permute-done.3.refs_3_
  38.2 0.0 collective-permute-done.2.refs_2_
  38.2 0.0 copy-done.2
  38.2 2.5 %shard_map.89 = (f32[7,4,16,128]{3,2,1,0:T(8,128)}, f32[192,128]{1,0:T(8,128)S(1)}) custom-call(f32[7,4,16,128]{3,2,1,0:T(8,128)S(1)} %get-tuple-element.10.refs_0_, f32[7,4,8,128]{3,2,1,0:T(8,128)S(1)} %get-tuple-element.13.refs_1_, f32[7,4,16,128]{3,2,1,0:T(8,128)S(1)} %collective-permute-done.2.refs_2_, ...), custom_call_target="tpu_custom_call" | custom-call | tf_op jit(solution)/shard_map/pallas_call | solution.py:347
  40.7 0.0 copy-start.3
  40.7 14.4 %all_to_all.11 = f32[32,3,2,128]{3,2,1,0:T(2,128)S(1)} all-to-all(f32[32,3,2,128]{3,2,1,0:T(2,128)S(1)} %bitcast.10), channel_id=1, replica_groups=mesh['src'=4,'tgt'=8] {'src','tgt'}, dimensions={0} | all-to-all | bytes 196608 | tf_op jit(solution)/shard_map/all_to_all | solution.py:425
  55.1 0.0 copy-done.3
  55.1 1.7 %shard_map.90 = f32[3,8192]{1,0:T(4,128)} custom-call(f32[192,128]{1,0:T(8,128)S(1)} %bitcast.9, s32[1,8192]{1,0:T(1,128)S(1)} %copy-done.3), custom_call_target="tpu_custom_call" | custom-call | tf_op jit(solution)/shard_map/pallas_call | solution.py:389
  (1 shorter events, 0.0 us)
Async XLA Ops:
  4.0 22.1 %copy-start = (f32[4,16,128]{2,1,0:T(8,128)S(1)}, f32[4,16,128]{2,1,0:T(8,128)}, u32[]{:S(2)}) copy-start(f32[4,16,128]{2,1,0:T(8,128)} %refs_6_.1) | copy-start | bytes 98308
  4.0 22.1 %copy-start.1 = (s32[16384]{0:T(1024)S(1)}, s32[16384]{0:T(1024)}, u32[]{:S(2)}) copy-start(s32[16384]{0:T(1024)} %param.10) | copy-start | bytes 196612
  30.0 4.3 %collective-permute-start = (f32[29,4,128]{2,1,0:T(4,128)S(1)}, f32[29,4,128]{2,1,0:T(4,128)S(1)}, u32[]{:S(2)}, u32[]{:S(2)}) collective-permute-start(f32[29,4,128]{2,1,0:T(4,128)S(1)} %get-tuple-element.11), channel_id=1, source_target_pairs={{0,1},{2,3},{4,5},{6,7},{1,0},{3,2},{5,4},{7,6},{8,9},{10,11},{12,... | collective-permute-start | bytes 178184 | tf_op jit(solution)/shard_map/ppermute | solution.py:401
  31.0 3.3 %collective-permute-start.1 = (f32[28,4,128]{2,1,0:T(4,128)S(1)}, f32[28,4,128]{2,1,0:T(4,128)S(1)}, u32[]{:S(2)}, u32[]{:S(2)}) collective-permute-start(f32[28,4,128]{2,1,0:T(4,128)S(1)} %get-tuple-element.12), channel_id=1, source_target_pairs={{1,2},{3,4},{5,6},{2,1},{4,3},{6,5},{9,10},{11,12},{13,14},{10,9},... | collective-permute-start | bytes 172040 | tf_op jit(solution)/shard_map/ppermute | solution.py:401
  31.6 6.6 %copy-start.2 = (s32[1,8192]{1,0:T(1,128)S(1)}, s32[1,8192]{1,0:T(1,128)}, u32[]{:S(2)}) copy-start(s32[1,8192]{1,0:T(1,128)} %refs_7_.1) | copy-start | bytes 98308
  31.6 6.5 %collective-permute-start.3 = (f32[7,4,16,128]{3,2,1,0:T(8,128)S(1)}, f32[7,4,16,128]{3,2,1,0:T(8,128)S(1)}, u32[]{:S(2)}, u32[]{:S(2)}) collective-permute-start(f32[7,4,16,128]{3,2,1,0:T(8,128)S(1)} %get-tuple-element.10.refs_0_), channel_id=1, source_target_pairs={{8,16},{16,8},{9,17},{17,9},{10,18},{18,10},{11,19},{19,11},{12,20... | collective-permute-start | bytes 688136 | tf_op jit(solution)/shard_map/ppermute | solution.py:401
  32.3 5.9 %collective-permute-start.2 = (f32[7,4,16,128]{3,2,1,0:T(8,128)S(1)}, f32[7,4,16,128]{3,2,1,0:T(8,128)S(1)}, u32[]{:S(2)}, u32[]{:S(2)}) collective-permute-start(f32[7,4,16,128]{3,2,1,0:T(8,128)S(1)} %get-tuple-element.10.refs_0_), channel_id=1, source_target_pairs={{0,8},{16,24},{8,0},{24,16},{1,9},{17,25},{9,1},{25,17},{2,10},{18... | collective-permute-start | bytes 688136 | tf_op jit(solution)/shard_map/ppermute | solution.py:401
  34.3 3.8 %collective-permute-start.5 = (f32[7,16,128]{2,1,0:T(8,128)S(1)}, f32[7,16,128]{2,1,0:T(8,128)S(1)}, u32[]{:S(2)}, u32[]{:S(2)}) collective-permute-start(f32[7,16,128]{2,1,0:T(8,128)S(1)} %get-tuple-element.15), channel_id=1, source_target_pairs={{8,16},{16,8},{9,17},{17,9},{10,18},{18,10},{11,19},{19,11},{12,20... | collective-permute-start | bytes 172040 | tf_op jit(solution)/shard_map/ppermute | solution.py:401
  35.0 3.1 %collective-permute-start.4 = (f32[7,14,128]{2,1,0:T(8,128)S(1)}, f32[7,14,128]{2,1,0:T(8,128)S(1)}, u32[]{:S(2)}, u32[]{:S(2)}) collective-permute-start(f32[7,14,128]{2,1,0:T(8,128)S(1)} %get-tuple-element.14), channel_id=1, source_target_pairs={{0,8},{16,24},{8,0},{24,16},{1,9},{17,25},{9,1},{25,17},{2,10},{18... | collective-permute-start | bytes 150536 | tf_op jit(solution)/shard_map/ppermute | solution.py:401
  40.7 14.4 %copy-start.3 = (s32[1,8192]{1,0:T(1,128)S(1)}, s32[1,8192]{1,0:T(1,128)}, u32[]{:S(2)}) copy-start(s32[1,8192]{1,0:T(1,128)} %order_ref.1) | copy-start | bytes 98308

commit v15 on v14

--- a/solution.py
+++ b/solution.py
@@ -1,3 +1,5 @@
+import functools
+
 import numpy as np
 
 import jax
@@ -73,21 +75,19 @@
     for g in range(groups):
         table[g * 8 : g * 8 + FIELDS, :] = fields_ref[:, g * WIDE : (g + 1) * WIDE]
     high, low = halves(table[...])
-    both = jnp.concatenate([high, low], axis=0)
     ids = row_ids(WIDE, span).astype(F32).astype(BF16)
-    rows = groups * 8
 
     def one_owner(q):
         at = pl.multiple_of(q * span, span)
         index = index_ref[:, pl.ds(at, span)]
         weight = weight_ref[:, pl.ds(at, span)]
         onehot = low_onehot(index & (WIDE - 1), ids)
-        got = jnp.dot(both, onehot, preferred_element_type=F32)
+        got = jnp.dot(high, onehot, preferred_element_type=F32)
+        got = got + jnp.dot(low, onehot, preferred_element_type=F32)
         group = jnp.broadcast_to(index >> log2(WIDE), (8, span))
         value = jnp.zeros((8, span), F32)
         for g in range(groups):
-            part = got[g * 8 : (g + 1) * 8] + got[rows + g * 8 : rows + (g + 1) * 8]
-            value = jnp.where(group == g, part, value)
+            value = jnp.where(group == g, got[g * 8 : (g + 1) * 8], value)
         value = value * weight
         for t in range(tiles):
             out_ref[pl.ds(q * (FIELDS * tiles) + t, FIELDS, stride=tiles), :] = value[
@@ -144,12 +144,11 @@
             for f in range(FIELDS):
                 parts.append(jnp.where(here, half[f : f + 1], jnp.zeros((), BF16)))
         spread = jnp.concatenate(parts, axis=0)
-        total[...] += lax.dot_general(spread, onehot, NT, preferred_element_type=F32)
+        return lax.dot_general(spread, onehot, NT, preferred_element_type=F32)
 
     @pl.loop(0, owners // TOGETHER // 4)
     def _(n):
-        for i in range(4):
-            step(n * 4 + i)
+        total[...] += functools.reduce(lambda sums, i: sums + step(n * 4 + i), range(1, 4), step(n * 4))
 
     even_ref[FIELDS * hx] = jnp.zeros((ITERS, hz), F32)
     scale = lax.rsqrt(mass_ref[...])
@@ -184,12 +183,13 @@
 
 def lookup_rows(table, index, ids, group_ids, groups, at_parts):
     group, low = at_parts(index)
-    got = jnp.dot(table, low_onehot(low, ids), preferred_element_type=F32)
+    onehot = low_onehot(low, ids)
+    got = jnp.dot(table[0], onehot, preferred_element_type=F32)
+    got = got + jnp.dot(table[1], onehot, preferred_element_type=F32)
     here = group_ids == group
-    rows = 3 * groups
     out = []
     for m in range(3):
-        part = got[m * groups : (m + 1) * groups] + got[rows + m * groups : rows + (m + 1) * groups]
+        part = got[m * groups : (m + 1) * groups]
         out.append(jnp.sum(jnp.where(here, part, 0.0), axis=0, keepdims=True))
     return out
 
@@ -320,7 +320,7 @@
     groups = hx * hy * hz // WIDE
     payload = cell_moduli([projected_ref[f].reshape(hx * hy, hz) for f in range(FIELDS)])
     table = jnp.concatenate([jnp.concatenate([m[:groups], m[groups:]], axis=1) for m in payload], axis=0)
-    table = jnp.concatenate(halves(table), axis=0)
+    table = halves(table)
     ids = row_ids(WIDE, WIDE).astype(F32).astype(BF16)
     group_ids = row_ids(groups, WIDE)
 
@@ -366,7 +366,7 @@
         ],
         axis=0,
     )
-    table = jnp.concatenate(halves(table), axis=0)
+    table = halves(table)
     ids = row_ids(WIDE, WIDE).astype(F32).astype(BF16)
     group_ids = row_ids(groups, WIDE)
 

time: 57.1 us -> 58.1 us (1.018)
  Pallas kernels: 11.5 us -> 12.5 us
where the time goes in v15:
time: 58.1 us; the launch traced here: 57.7 us
  blocking collectives  36.4 us (63%)
  Pallas kernels  12.5 us (22%)
  starting transfers between devices  7.14 us (12%)
  waiting for transfers between devices  0.91 us (2%)
  between operations  0.73 us (1%)
    all_to_all x1, blocking collectives, on_device(): lax.all_to_all(values, both, split_axis=0, concat_axis=0, tiled=True)  22.1 us
    all_to_all x1, blocking collectives, on_device(): lax.all_to_all(outgoing, both, split_axis=0, concat_axis=0, tiled=True)  14.4 us
    ppermute x6, starting transfers between devices, swap(): return lax.ppermute(x, axis, pairs + [(j, i) for i, j in pairs])  7.14 us
    pallas_call x1, Pallas kernels, scatter_call(): pl.pallas_call(scatter_kernel, out_shape=(jax.ShapeDtypeStruct((FIELDS, h...  3.98 us
    pallas_call x1, Pallas kernels, gather_call(): pl.pallas_call(gather_kernel, out_shape=jax.ShapeDtypeStruct((rows, 128),...  3.33 us
    pallas_call x1, Pallas kernels, solve_call(): pl.pallas_call(kernel, out_shape=(jax.ShapeDtypeStruct((FIELDS, hx, hy, h...  3.02 us
    pallas_call x1, Pallas kernels, place_call(): pl.pallas_call(place_kernel, out_shape=jax.ShapeDtypeStruct((3, order.sha...  2.14 us
  transfers between devices with their start and end apart: 6, of which 1 were waited for; matrix products, arithmetic and copies ran while one was open for 0% of the time, Pallas kernels for 0%

profile of v15, /device:TPU:0, one launch (start us, length us, event | category | flops | bytes accessed | tf_op | source)
XLA Modules:
  0.0 57.7 jit_solution(12384121471517959198)
XLA Ops:
  0.6 3.3 %shard_map.86 = f32[896,128]{1,0:T(8,128)S(1)} custom-call(f32[7,4096]{1,0:T(8,128)} %fields_hbm.1, s32[1,16384]{1,0:T(1,128)} %bitcast.12, f32[1,16384]{1,0:T(1,128)} %bitcast.13), custom_call_target="tpu_custom_call" | custom-call | tf_op jit(solution)/shard_map/pallas_call | solution.py:105
  4.0 0.0 copy-start
  4.0 0.0 copy-start.1
  4.0 22.1 %all_to_all.10 = f32[32,7,4,128]{3,2,1,0:T(4,128)S(1)} all-to-all(f32[32,7,4,128]{3,2,1,0:T(4,128)S(1)} %bitcast.8), channel_id=1, replica_groups=mesh['src'=4,'tgt'=8] {'src','tgt'}, dimensions={0} | all-to-all | bytes 917504 | tf_op jit(solution)/shard_map/all_to_all | solution.py:413
  26.0 0.0 copy-done
  26.0 0.0 copy-done.1
  26.1 4.0 %shard_map.87 = (f32[7,4,16,128]{3,2,1,0:T(8,128)S(1)}, f32[29,4,128]{2,1,0:T(4,128)S(1)}, f32[28,4,128]{2,1,0:T(4,128)S(1)}) custom-call(f32[896,128]{1,0:T(8,128)S(1)} %bitcast.7, s32[1,16384]{1,0:T(1,128)S(1)} %bitcast.11, f32[4,16,128]{2,1,0:T(8,128)S(1)} %copy-done), custom_call_target="tpu_custom_call" | custom-call | tf_op jit(solution)/shard_map/pallas_call | solution.py:174
  30.0 0.9 %collective-permute-start = (f32[29,4,128]{2,1,0:T(4,128)S(1)}, f32[29,4,128]{2,1,0:T(4,128)S(1)}, u32[]{:S(2)}, u32[]{:S(2)}) collective-permute-start(f32[29,4,128]{2,1,0:T(4,128)S(1)} %get-tuple-element.11), channel_id=1, source_target_pairs={{0,1},{2,3},{4,5},{6,7},{1,0},{3,2},{5,4},{7,6},{8,9},{10,11},{12,... | collective-permute-start | bytes 178184 | tf_op jit(solution)/shard_map/ppermute | solution.py:401
  31.0 0.7 %collective-permute-start.1 = (f32[28,4,128]{2,1,0:T(4,128)S(1)}, f32[28,4,128]{2,1,0:T(4,128)S(1)}, u32[]{:S(2)}, u32[]{:S(2)}) collective-permute-start(f32[28,4,128]{2,1,0:T(4,128)S(1)} %get-tuple-element.12), channel_id=1, source_target_pairs={{1,2},{3,4},{5,6},{2,1},{4,3},{6,5},{9,10},{11,12},{13,14},{10,9},... | collective-permute-start | bytes 172040 | tf_op jit(solution)/shard_map/ppermute | solution.py:401
  31.6 0.0 copy-start.2
  31.6 0.7 %collective-permute-start.3 = (f32[7,4,16,128]{3,2,1,0:T(8,128)S(1)}, f32[7,4,16,128]{3,2,1,0:T(8,128)S(1)}, u32[]{:S(2)}, u32[]{:S(2)}) collective-permute-start(f32[7,4,16,128]{3,2,1,0:T(8,128)S(1)} %get-tuple-element.10.refs_0_), channel_id=1, source_target_pairs={{8,16},{16,8},{9,17},{17,9},{10,18},{18,10},{11,19},{19,11},{12,20... | collective-permute-start | bytes 688136 | tf_op jit(solution)/shard_map/ppermute | solution.py:401
  32.3 2.0 %collective-permute-start.2 = (f32[7,4,16,128]{3,2,1,0:T(8,128)S(1)}, f32[7,4,16,128]{3,2,1,0:T(8,128)S(1)}, u32[]{:S(2)}, u32[]{:S(2)}) collective-permute-start(f32[7,4,16,128]{3,2,1,0:T(8,128)S(1)} %get-tuple-element.10.refs_0_), channel_id=1, source_target_pairs={{0,8},{16,24},{8,0},{24,16},{1,9},{17,25},{9,1},{25,17},{2,10},{18... | collective-permute-start | bytes 688136 | tf_op jit(solution)/shard_map/ppermute | solution.py:401
  34.3 0.0 collective-permute-done.1.odd_ref
  34.3 0.0 collective-permute-done.even_ref
  34.4 0.7 %collective-permute-start.5 = (f32[7,16,128]{2,1,0:T(8,128)S(1)}, f32[7,16,128]{2,1,0:T(8,128)S(1)}, u32[]{:S(2)}, u32[]{:S(2)}) collective-permute-start(f32[7,16,128]{2,1,0:T(8,128)S(1)} %get-tuple-element.15), channel_id=1, source_target_pairs={{8,16},{16,8},{9,17},{17,9},{10,18},{18,10},{11,19},{19,11},{12,20... | collective-permute-start | bytes 172040 | tf_op jit(solution)/shard_map/ppermute | solution.py:401
  35.0 2.3 %collective-permute-start.4 = (f32[7,14,128]{2,1,0:T(8,128)S(1)}, f32[7,14,128]{2,1,0:T(8,128)S(1)}, u32[]{:S(2)}, u32[]{:S(2)}) collective-permute-start(f32[7,14,128]{2,1,0:T(8,128)S(1)} %get-tuple-element.14), channel_id=1, source_target_pairs={{0,8},{16,24},{8,0},{24,16},{1,9},{17,25},{9,1},{25,17},{2,10},{18... | collective-permute-start | bytes 150536 | tf_op jit(solution)/shard_map/ppermute | solution.py:401
  37.3 0.9 %collective-permute-done.4.refs_4_ = f32[7,14,128]{2,1,0:T(8,128)S(1)} collective-permute-done((f32[7,14,128]{2,1,0:T(8,128)S(1)}, f32[7,14,128]{2,1,0:T(8,128)S(1)}, u32[]{:S(2)}, u32[]{:S(2)}) %collective-permute-start.4) | collective-permute-done | bytes 50208 | tf_op jit(solution)/shard_map/ppermute | solution.py:401
  38.2 0.0 collective-permute-done.5.refs_5_
  38.2 0.0 collective-permute-done.3.refs_3_
  38.2 0.0 collective-permute-done.2.refs_2_
  38.2 0.0 copy-done.2
  38.2 3.0 %shard_map.89 = (f32[7,4,16,128]{3,2,1,0:T(8,128)}, f32[192,128]{1,0:T(8,128)S(1)}) custom-call(f32[7,4,16,128]{3,2,1,0:T(8,128)S(1)} %get-tuple-element.10.refs_0_, f32[7,4,8,128]{3,2,1,0:T(8,128)S(1)} %get-tuple-element.13.refs_1_, f32[7,4,16,128]{3,2,1,0:T(8,128)S(1)} %collective-permute-done.2.refs_2_, ...), custom_call_target="tpu_custom_call" | custom-call | tf_op jit(solution)/shard_map/pallas_call | solution.py:347
  41.2 0.0 copy-start.3
  41.2 14.4 %all_to_all.11 = f32[32,3,2,128]{3,2,1,0:T(2,128)S(1)} all-to-all(f32[32,3,2,128]{3,2,1,0:T(2,128)S(1)} %bitcast.10), channel_id=1, replica_groups=mesh['src'=4,'tgt'=8] {'src','tgt'}, dimensions={0} | all-to-all | bytes 196608 | tf_op jit(solution)/shard_map/all_to_all | solution.py:425
  55.6 0.0 copy-done.3
  55.6 2.1 %shard_map.90 = f32[3,8192]{1,0:T(4,128)} custom-call(f32[192,128]{1,0:T(8,128)S(1)} %bitcast.9, s32[1,8192]{1,0:T(1,128)S(1)} %copy-done.3), custom_call_target="tpu_custom_call" | custom-call | tf_op jit(solution)/shard_map/pallas_call | solution.py:389
  (1 shorter events, 0.0 us)
Async XLA Ops:
  4.0 22.1 %copy-start = (f32[4,16,128]{2,1,0:T(8,128)S(1)}, f32[4,16,128]{2,1,0:T(8,128)}, u32[]{:S(2)}) copy-start(f32[4,16,128]{2,1,0:T(8,128)} %refs_6_.1) | copy-start | bytes 98308
  4.0 22.1 %copy-start.1 = (s32[16384]{0:T(1024)S(1)}, s32[16384]{0:T(1024)}, u32[]{:S(2)}) copy-start(s32[16384]{0:T(1024)} %param.10) | copy-start | bytes 196612
  30.0 4.3 %collective-permute-start = (f32[29,4,128]{2,1,0:T(4,128)S(1)}, f32[29,4,128]{2,1,0:T(4,128)S(1)}, u32[]{:S(2)}, u32[]{:S(2)}) collective-permute-start(f32[29,4,128]{2,1,0:T(4,128)S(1)} %get-tuple-element.11), channel_id=1, source_target_pairs={{0,1},{2,3},{4,5},{6,7},{1,0},{3,2},{5,4},{7,6},{8,9},{10,11},{12,... | collective-permute-start | bytes 178184 | tf_op jit(solution)/shard_map/ppermute | solution.py:401
  31.0 3.3 %collective-permute-start.1 = (f32[28,4,128]{2,1,0:T(4,128)S(1)}, f32[28,4,128]{2,1,0:T(4,128)S(1)}, u32[]{:S(2)}, u32[]{:S(2)}) collective-permute-start(f32[28,4,128]{2,1,0:T(4,128)S(1)} %get-tuple-element.12), channel_id=1, source_target_pairs={{1,2},{3,4},{5,6},{2,1},{4,3},{6,5},{9,10},{11,12},{13,14},{10,9},... | collective-permute-start | bytes 172040 | tf_op jit(solution)/shard_map/ppermute | solution.py:401
  31.6 6.6 %copy-start.2 = (s32[1,8192]{1,0:T(1,128)S(1)}, s32[1,8192]{1,0:T(1,128)}, u32[]{:S(2)}) copy-start(s32[1,8192]{1,0:T(1,128)} %refs_7_.1) | copy-start | bytes 98308
  31.6 6.5 %collective-permute-start.3 = (f32[7,4,16,128]{3,2,1,0:T(8,128)S(1)}, f32[7,4,16,128]{3,2,1,0:T(8,128)S(1)}, u32[]{:S(2)}, u32[]{:S(2)}) collective-permute-start(f32[7,4,16,128]{3,2,1,0:T(8,128)S(1)} %get-tuple-element.10.refs_0_), channel_id=1, source_target_pairs={{8,16},{16,8},{9,17},{17,9},{10,18},{18,10},{11,19},{19,11},{12,20... | collective-permute-start | bytes 688136 | tf_op jit(solution)/shard_map/ppermute | solution.py:401
  32.3 5.9 %collective-permute-start.2 = (f32[7,4,16,128]{3,2,1,0:T(8,128)S(1)}, f32[7,4,16,128]{3,2,1,0:T(8,128)S(1)}, u32[]{:S(2)}, u32[]{:S(2)}) collective-permute-start(f32[7,4,16,128]{3,2,1,0:T(8,128)S(1)} %get-tuple-element.10.refs_0_), channel_id=1, source_target_pairs={{0,8},{16,24},{8,0},{24,16},{1,9},{17,25},{9,1},{25,17},{2,10},{18... | collective-permute-start | bytes 688136 | tf_op jit(solution)/shard_map/ppermute | solution.py:401
  34.4 3.8 %collective-permute-start.5 = (f32[7,16,128]{2,1,0:T(8,128)S(1)}, f32[7,16,128]{2,1,0:T(8,128)S(1)}, u32[]{:S(2)}, u32[]{:S(2)}) collective-permute-start(f32[7,16,128]{2,1,0:T(8,128)S(1)} %get-tuple-element.15), channel_id=1, source_target_pairs={{8,16},{16,8},{9,17},{17,9},{10,18},{18,10},{11,19},{19,11},{12,20... | collective-permute-start | bytes 172040 | tf_op jit(solution)/shard_map/ppermute | solution.py:401
  35.0 3.1 %collective-permute-start.4 = (f32[7,14,128]{2,1,0:T(8,128)S(1)}, f32[7,14,128]{2,1,0:T(8,128)S(1)}, u32[]{:S(2)}, u32[]{:S(2)}) collective-permute-start(f32[7,14,128]{2,1,0:T(8,128)S(1)} %get-tuple-element.14), channel_id=1, source_target_pairs={{0,8},{16,24},{8,0},{24,16},{1,9},{17,25},{9,1},{25,17},{2,10},{18... | collective-permute-start | bytes 150536 | tf_op jit(solution)/shard_map/ppermute | solution.py:401
  41.2 14.4 %copy-start.3 = (s32[1,8192]{1,0:T(1,128)S(1)}, s32[1,8192]{1,0:T(1,128)}, u32[]{:S(2)}) copy-start(s32[1,8192]{1,0:T(1,128)} %order_ref.1) | copy-start | bytes 98308

commit v16 on v15

--- a/solution.py
+++ b/solution.py
@@ -181,16 +181,18 @@
     )(values, target, mass)
 
 
-def lookup_rows(table, index, ids, group_ids, groups, at_parts):
-    group, low = at_parts(index)
-    onehot = low_onehot(low, ids)
-    got = jnp.dot(table[0], onehot, preferred_element_type=F32)
-    got = got + jnp.dot(table[1], onehot, preferred_element_type=F32)
-    here = group_ids == group
+def lookup_rows(tables, row, lane):
+    row = jnp.broadcast_to(row, (8, 128))
+    lane = jnp.broadcast_to(lane, (8, 128))
+    tile = row >> 3
+    here = row_ids(8, 128) == (row & 7)
     out = []
-    for m in range(3):
-        part = got[m * groups : (m + 1) * groups]
-        out.append(jnp.sum(jnp.where(here, part, 0.0), axis=0, keepdims=True))
+    for table in tables:
+        got = jnp.zeros((8, 128), F32)
+        for v in range(table.shape[0] // 8):
+            piece = jnp.take_along_axis(table[v * 8 : (v + 1) * 8], lane, axis=1, mode="promise_in_bounds")
+            got = jnp.where(tile == v, piece, got)
+        out.append(jnp.sum(jnp.where(here, got, 0.0), axis=0, keepdims=True))
     return out
 
 
@@ -317,22 +319,15 @@
 
     leave = pltpu.make_async_copy(projected_ref, projected_hbm, sem)
     leave.start()
-    groups = hx * hy * hz // WIDE
-    payload = cell_moduli([projected_ref[f].reshape(hx * hy, hz) for f in range(FIELDS)])
-    table = jnp.concatenate([jnp.concatenate([m[:groups], m[groups:]], axis=1) for m in payload], axis=0)
-    table = halves(table)
-    ids = row_ids(WIDE, WIDE).astype(F32).astype(BF16)
-    group_ids = row_ids(groups, WIDE)
-
-    def at_parts(index):
-        return (index >> log2(hz)) & (groups - 1), ((index >> log2(groups * hz)) << log2(hz)) + (index & (hz - 1))
-
-    for q in range(0, groups, 4):
+    tables = cell_moduli([projected_ref[f].reshape(hx * hy, hz) for f in range(FIELDS)])
+    for q in range(0, order_ref.shape[1] // WIDE, 4):
         lines = []
         for i in range(q, q + 4):
-            index = order_ref[:, i * WIDE : (i + 1) * WIDE]
-            got = lookup_rows(table, index, ids, group_ids, groups, at_parts)
-            lines += [line[:, c * 128 : (c + 1) * 128] for line in got for c in range(2)]
+            got = []
+            for c in range(2):
+                index = order_ref[:, i * WIDE + c * 128 : i * WIDE + (c + 1) * 128]
+                got.append(lookup_rows(tables, index >> log2(hz), index & (hz - 1)))
+            lines += [got[c][m] for m in range(3) for c in range(2)]
         out_ref[q * 6 : q * 6 + 24, :] = jnp.concatenate(lines, axis=0)
     leave.wait()
 
@@ -359,25 +354,18 @@
 
 def place_kernel(arrived_ref, order_ref, out_hbm, out_ref, sems):
     groups = arrived_ref.shape[0] // 6
-    table = jnp.concatenate(
-        [
-            jnp.concatenate([arrived_ref[pl.ds(2 * m + c, groups, stride=6), :] for c in range(2)], axis=1)
-            for m in range(3)
-        ],
-        axis=0,
-    )
-    table = halves(table)
-    ids = row_ids(WIDE, WIDE).astype(F32).astype(BF16)
-    group_ids = row_ids(groups, WIDE)
+    tables = [
+        jnp.concatenate([arrived_ref[pl.ds(2 * m + c, groups, stride=6), :] for c in range(2)], axis=0)
+        for m in range(3)
+    ]
 
     copies = []
     for n in range(PIECES):
-        for q in range(n * groups // PIECES, (n + 1) * groups // PIECES):
-            at = pl.ds(q * WIDE, WIDE)
-            got = lookup_rows(
-                table, order_ref[:, at], ids, group_ids, groups, lambda index: (index >> log2(WIDE), index & (WIDE - 1))
-            )
-            out_ref[:, at] = jnp.concatenate(got, axis=0)
+        for q in range(n * groups // PIECES * 2, (n + 1) * groups // PIECES * 2):
+            at = pl.ds(q * 128, 128)
+            index = order_ref[:, at]
+            row = ((index >> 7) & 1) * groups + (index >> log2(WIDE))
+            out_ref[:, at] = jnp.concatenate(lookup_rows(tables, row, index & 127), axis=0)
         piece = pl.ds(n * groups // PIECES * WIDE, groups // PIECES * WIDE)
         copies.append(pltpu.make_async_copy(out_ref.at[:, piece], out_hbm.at[:, piece], sems.at[n]))
         copies[n].start()

time: 58.1 us -> 59.2 us (1.019)
  Pallas kernels: 12.5 us -> 13.7 us
    pallas_call x1, Pallas kernels: 3.02 us -> 3.77 us  [solve_call(): pl.pallas_call(kernel, out_shape=(jax.ShapeDtypeStruct((FIELDS, hx, hy, h...]
where the time goes in v16:
time: 59.2 us; the launch traced here: 58.9 us
  blocking collectives  36.4 us (61%)
  Pallas kernels  13.7 us (23%)
  starting transfers between devices  7.14 us (12%)
  waiting for transfers between devices  0.91 us (2%)
  between operations  0.73 us (1%)
    all_to_all x1, blocking collectives, on_device(): lax.all_to_all(values, both, split_axis=0, concat_axis=0, tiled=True)  22.1 us
    all_to_all x1, blocking collectives, on_device(): lax.all_to_all(outgoing, both, split_axis=0, concat_axis=0, tiled=True)  14.4 us
    ppermute x6, starting transfers between devices, swap(): return lax.ppermute(x, axis, pairs + [(j, i) for i, j in pairs])  7.14 us
    pallas_call x1, Pallas kernels, scatter_call(): pl.pallas_call(scatter_kernel, out_shape=(jax.ShapeDtypeStruct((FIELDS, h...  3.98 us
    pallas_call x1, Pallas kernels, solve_call(): pl.pallas_call(kernel, out_shape=(jax.ShapeDtypeStruct((FIELDS, hx, hy, h...  3.77 us
    pallas_call x1, Pallas kernels, gather_call(): pl.pallas_call(gather_kernel, out_shape=jax.ShapeDtypeStruct((rows, 128),...  3.33 us
    pallas_call x1, Pallas kernels, place_call(): pl.pallas_call(place_kernel, out_shape=jax.ShapeDtypeStruct((3, order.sha...  2.55 us
  transfers between devices with their start and end apart: 6, of which 1 were waited for; matrix products, arithmetic and copies ran while one was open for 0% of the time, Pallas kernels for 0%

profile of v16, /device:TPU:0, one launch (start us, length us, event | category | flops | bytes accessed | tf_op | source)
XLA Modules:
  0.0 58.9 jit_solution(12321365857048553828)
XLA Ops:
  0.6 3.3 %shard_map.86 = f32[896,128]{1,0:T(8,128)S(1)} custom-call(f32[7,4096]{1,0:T(8,128)} %fields_hbm.1, s32[1,16384]{1,0:T(1,128)} %bitcast.12, f32[1,16384]{1,0:T(1,128)} %bitcast.13), custom_call_target="tpu_custom_call" | custom-call | tf_op jit(solution)/shard_map/pallas_call | solution.py:105
  4.0 0.0 copy-start
  4.0 0.0 copy-start.1
  4.0 22.1 %all_to_all.10 = f32[32,7,4,128]{3,2,1,0:T(4,128)S(1)} all-to-all(f32[32,7,4,128]{3,2,1,0:T(4,128)S(1)} %bitcast.8), channel_id=1, replica_groups=mesh['src'=4,'tgt'=8] {'src','tgt'}, dimensions={0} | all-to-all | bytes 917504 | tf_op jit(solution)/shard_map/all_to_all | solution.py:401
  26.0 0.0 copy-done
  26.0 0.0 copy-done.1
  26.1 4.0 %shard_map.87 = (f32[7,4,16,128]{3,2,1,0:T(8,128)S(1)}, f32[29,4,128]{2,1,0:T(4,128)S(1)}, f32[28,4,128]{2,1,0:T(4,128)S(1)}) custom-call(f32[896,128]{1,0:T(8,128)S(1)} %bitcast.7, s32[1,16384]{1,0:T(1,128)S(1)} %bitcast.11, f32[4,16,128]{2,1,0:T(8,128)S(1)} %copy-done), custom_call_target="tpu_custom_call" | custom-call | tf_op jit(solution)/shard_map/pallas_call | solution.py:174
  30.0 0.9 %collective-permute-start = (f32[29,4,128]{2,1,0:T(4,128)S(1)}, f32[29,4,128]{2,1,0:T(4,128)S(1)}, u32[]{:S(2)}, u32[]{:S(2)}) collective-permute-start(f32[29,4,128]{2,1,0:T(4,128)S(1)} %get-tuple-element.11), channel_id=1, source_target_pairs={{0,1},{2,3},{4,5},{6,7},{1,0},{3,2},{5,4},{7,6},{8,9},{10,11},{12,... | collective-permute-start | bytes 178184 | tf_op jit(solution)/shard_map/ppermute | solution.py:389
  31.0 0.7 %collective-permute-start.1 = (f32[28,4,128]{2,1,0:T(4,128)S(1)}, f32[28,4,128]{2,1,0:T(4,128)S(1)}, u32[]{:S(2)}, u32[]{:S(2)}) collective-permute-start(f32[28,4,128]{2,1,0:T(4,128)S(1)} %get-tuple-element.12), channel_id=1, source_target_pairs={{1,2},{3,4},{5,6},{2,1},{4,3},{6,5},{9,10},{11,12},{13,14},{10,9},... | collective-permute-start | bytes 172040 | tf_op jit(solution)/shard_map/ppermute | solution.py:389
  31.6 0.0 copy-start.2
  31.6 0.7 %collective-permute-start.3 = (f32[7,4,16,128]{3,2,1,0:T(8,128)S(1)}, f32[7,4,16,128]{3,2,1,0:T(8,128)S(1)}, u32[]{:S(2)}, u32[]{:S(2)}) collective-permute-start(f32[7,4,16,128]{3,2,1,0:T(8,128)S(1)} %get-tuple-element.10.refs_0_), channel_id=1, source_target_pairs={{8,16},{16,8},{9,17},{17,9},{10,18},{18,10},{11,19},{19,11},{12,20... | collective-permute-start | bytes 688136 | tf_op jit(solution)/shard_map/ppermute | solution.py:389
  32.3 2.0 %collective-permute-start.2 = (f32[7,4,16,128]{3,2,1,0:T(8,128)S(1)}, f32[7,4,16,128]{3,2,1,0:T(8,128)S(1)}, u32[]{:S(2)}, u32[]{:S(2)}) collective-permute-start(f32[7,4,16,128]{3,2,1,0:T(8,128)S(1)} %get-tuple-element.10.refs_0_), channel_id=1, source_target_pairs={{0,8},{16,24},{8,0},{24,16},{1,9},{17,25},{9,1},{25,17},{2,10},{18... | collective-permute-start | bytes 688136 | tf_op jit(solution)/shard_map/ppermute | solution.py:389
  34.3 0.0 collective-permute-done.1.odd_ref
  34.3 0.0 collective-permute-done.even_ref
  34.4 0.7 %collective-permute-start.5 = (f32[7,16,128]{2,1,0:T(8,128)S(1)}, f32[7,16,128]{2,1,0:T(8,128)S(1)}, u32[]{:S(2)}, u32[]{:S(2)}) collective-permute-start(f32[7,16,128]{2,1,0:T(8,128)S(1)} %get-tuple-element.15), channel_id=1, source_target_pairs={{8,16},{16,8},{9,17},{17,9},{10,18},{18,10},{11,19},{19,11},{12,20... | collective-permute-start | bytes 172040 | tf_op jit(solution)/shard_map/ppermute | solution.py:389
  35.0 2.3 %collective-permute-start.4 = (f32[7,14,128]{2,1,0:T(8,128)S(1)}, f32[7,14,128]{2,1,0:T(8,128)S(1)}, u32[]{:S(2)}, u32[]{:S(2)}) collective-permute-start(f32[7,14,128]{2,1,0:T(8,128)S(1)} %get-tuple-element.14), channel_id=1, source_target_pairs={{0,8},{16,24},{8,0},{24,16},{1,9},{17,25},{9,1},{25,17},{2,10},{18... | collective-permute-start | bytes 150536 | tf_op jit(solution)/shard_map/ppermute | solution.py:389
  37.3 0.9 %collective-permute-done.4.refs_4_ = f32[7,14,128]{2,1,0:T(8,128)S(1)} collective-permute-done((f32[7,14,128]{2,1,0:T(8,128)S(1)}, f32[7,14,128]{2,1,0:T(8,128)S(1)}, u32[]{:S(2)}, u32[]{:S(2)}) %collective-permute-start.4) | collective-permute-done | bytes 50208 | tf_op jit(solution)/shard_map/ppermute | solution.py:389
  38.2 0.0 collective-permute-done.5.refs_5_
  38.2 0.0 collective-permute-done.3.refs_3_
  38.2 0.0 collective-permute-done.2.refs_2_
  38.2 0.0 copy-done.2
  38.2 3.8 %shard_map.89 = (f32[7,4,16,128]{3,2,1,0:T(8,128)}, f32[192,128]{1,0:T(8,128)S(1)}) custom-call(f32[7,4,16,128]{3,2,1,0:T(8,128)S(1)} %get-tuple-element.10.refs_0_, f32[7,4,8,128]{3,2,1,0:T(8,128)S(1)} %get-tuple-element.13.refs_1_, f32[7,4,16,128]{3,2,1,0:T(8,128)S(1)} %collective-permute-done.2.refs_2_, ...), custom_call_target="tpu_custom_call" | custom-call | tf_op jit(solution)/shard_map/pallas_call | solution.py:342
  42.0 0.0 copy-start.3
  42.0 14.4 %all_to_all.11 = f32[32,3,2,128]{3,2,1,0:T(2,128)S(1)} all-to-all(f32[32,3,2,128]{3,2,1,0:T(2,128)S(1)} %bitcast.10), channel_id=1, replica_groups=mesh['src'=4,'tgt'=8] {'src','tgt'}, dimensions={0} | all-to-all | bytes 196608 | tf_op jit(solution)/shard_map/all_to_all | solution.py:413
  56.3 0.0 copy-done.3
  56.3 2.5 %shard_map.90 = f32[3,8192]{1,0:T(4,128)} custom-call(f32[192,128]{1,0:T(8,128)S(1)} %bitcast.9, s32[1,8192]{1,0:T(1,128)S(1)} %copy-done.3), custom_call_target="tpu_custom_call" | custom-call | tf_op jit(solution)/shard_map/pallas_call | solution.py:377
  (1 shorter events, 0.0 us)
Async XLA Ops:
  4.0 22.1 %copy-start = (f32[4,16,128]{2,1,0:T(8,128)S(1)}, f32[4,16,128]{2,1,0:T(8,128)}, u32[]{:S(2)}) copy-start(f32[4,16,128]{2,1,0:T(8,128)} %refs_6_.1) | copy-start | bytes 98308
  4.0 22.1 %copy-start.1 = (s32[16384]{0:T(1024)S(1)}, s32[16384]{0:T(1024)}, u32[]{:S(2)}) copy-start(s32[16384]{0:T(1024)} %param.10) | copy-start | bytes 196612
  30.0 4.3 %collective-permute-start = (f32[29,4,128]{2,1,0:T(4,128)S(1)}, f32[29,4,128]{2,1,0:T(4,128)S(1)}, u32[]{:S(2)}, u32[]{:S(2)}) collective-permute-start(f32[29,4,128]{2,1,0:T(4,128)S(1)} %get-tuple-element.11), channel_id=1, source_target_pairs={{0,1},{2,3},{4,5},{6,7},{1,0},{3,2},{5,4},{7,6},{8,9},{10,11},{12,... | collective-permute-start | bytes 178184 | tf_op jit(solution)/shard_map/ppermute | solution.py:389
  31.0 3.3 %collective-permute-start.1 = (f32[28,4,128]{2,1,0:T(4,128)S(1)}, f32[28,4,128]{2,1,0:T(4,128)S(1)}, u32[]{:S(2)}, u32[]{:S(2)}) collective-permute-start(f32[28,4,128]{2,1,0:T(4,128)S(1)} %get-tuple-element.12), channel_id=1, source_target_pairs={{1,2},{3,4},{5,6},{2,1},{4,3},{6,5},{9,10},{11,12},{13,14},{10,9},... | collective-permute-start | bytes 172040 | tf_op jit(solution)/shard_map/ppermute | solution.py:389
  31.6 6.6 %copy-start.2 = (s32[1,8192]{1,0:T(1,128)S(1)}, s32[1,8192]{1,0:T(1,128)}, u32[]{:S(2)}) copy-start(s32[1,8192]{1,0:T(1,128)} %refs_7_.1) | copy-start | bytes 98308
  31.6 6.5 %collective-permute-start.3 = (f32[7,4,16,128]{3,2,1,0:T(8,128)S(1)}, f32[7,4,16,128]{3,2,1,0:T(8,128)S(1)}, u32[]{:S(2)}, u32[]{:S(2)}) collective-permute-start(f32[7,4,16,128]{3,2,1,0:T(8,128)S(1)} %get-tuple-element.10.refs_0_), channel_id=1, source_target_pairs={{8,16},{16,8},{9,17},{17,9},{10,18},{18,10},{11,19},{19,11},{12,20... | collective-permute-start | bytes 688136 | tf_op jit(solution)/shard_map/ppermute | solution.py:389
  32.3 5.9 %collective-permute-start.2 = (f32[7,4,16,128]{3,2,1,0:T(8,128)S(1)}, f32[7,4,16,128]{3,2,1,0:T(8,128)S(1)}, u32[]{:S(2)}, u32[]{:S(2)}) collective-permute-start(f32[7,4,16,128]{3,2,1,0:T(8,128)S(1)} %get-tuple-element.10.refs_0_), channel_id=1, source_target_pairs={{0,8},{16,24},{8,0},{24,16},{1,9},{17,25},{9,1},{25,17},{2,10},{18... | collective-permute-start | bytes 688136 | tf_op jit(solution)/shard_map/ppermute | solution.py:389
  34.4 3.8 %collective-permute-start.5 = (f32[7,16,128]{2,1,0:T(8,128)S(1)}, f32[7,16,128]{2,1,0:T(8,128)S(1)}, u32[]{:S(2)}, u32[]{:S(2)}) collective-permute-start(f32[7,16,128]{2,1,0:T(8,128)S(1)} %get-tuple-element.15), channel_id=1, source_target_pairs={{8,16},{16,8},{9,17},{17,9},{10,18},{18,10},{11,19},{19,11},{12,20... | collective-permute-start | bytes 172040 | tf_op jit(solution)/shard_map/ppermute | solution.py:389
  35.0 3.1 %collective-permute-start.4 = (f32[7,14,128]{2,1,0:T(8,128)S(1)}, f32[7,14,128]{2,1,0:T(8,128)S(1)}, u32[]{:S(2)}, u32[]{:S(2)}) collective-permute-start(f32[7,14,128]{2,1,0:T(8,128)S(1)} %get-tuple-element.14), channel_id=1, source_target_pairs={{0,8},{16,24},{8,0},{24,16},{1,9},{17,25},{9,1},{25,17},{2,10},{18... | collective-permute-start | bytes 150536 | tf_op jit(solution)/shard_map/ppermute | solution.py:389
  42.0 14.4 %copy-start.3 = (s32[1,8192]{1,0:T(1,128)S(1)}, s32[1,8192]{1,0:T(1,128)}, u32[]{:S(2)}) copy-start(s32[1,8192]{1,0:T(1,128)} %order_ref.1) | copy-start | bytes 98308

commit v17 on v14

--- a/solution.py
+++ b/solution.py
@@ -1,3 +1,5 @@
+import functools
+
 import numpy as np
 
 import jax
@@ -57,7 +59,7 @@
     return jnp.where(ids == low.astype(F32).astype(BF16), jnp.ones((), BF16), jnp.zeros((), BF16))
 
 
-def gather_kernel(fields_hbm, index_hbm, weight_hbm, out_ref, table, fields_ref, index_ref, weight_ref, sems):
+def gather_kernel(fields_hbm, index_hbm, weight_hbm, out_ref, table, padded, fields_ref, index_ref, weight_ref, sems):
     pairs = ((fields_hbm, fields_ref), (index_hbm, index_ref), (weight_hbm, weight_ref))
     copies = [pltpu.make_async_copy(src, dst, sems.at[i]) for i, (src, dst) in enumerate(pairs)]
     for copy in copies:
@@ -68,27 +70,43 @@
     owners = index_ref.shape[1] // span
     groups = fields_ref.shape[1] // WIDE
     table[...] = jnp.zeros_like(table)
+    padded[...] = jnp.zeros_like(padded)
     for copy in copies:
         copy.wait()
     for g in range(groups):
         table[g * 8 : g * 8 + FIELDS, :] = fields_ref[:, g * WIDE : (g + 1) * WIDE]
-    high, low = halves(table[...])
-    both = jnp.concatenate([high, low], axis=0)
-    ids = row_ids(WIDE, span).astype(F32).astype(BF16)
+    both = jnp.concatenate(halves(table[...]), axis=0)
     rows = groups * 8
-
-    def one_owner(q):
-        at = pl.multiple_of(q * span, span)
-        index = index_ref[:, pl.ds(at, span)]
-        weight = weight_ref[:, pl.ds(at, span)]
-        onehot = low_onehot(index & (WIDE - 1), ids)
-        got = jnp.dot(both, onehot, preferred_element_type=F32)
-        group = jnp.broadcast_to(index >> log2(WIDE), (8, span))
-        value = jnp.zeros((8, span), F32)
+    ids = row_ids(WIDE, WIDE).astype(F32).astype(BF16)
+    padded[:FIELDS, :] = fields_ref[...]
+
+    def by_matmul(index):
+        got = jnp.dot(both, low_onehot(index & (WIDE - 1), ids), preferred_element_type=F32)
+        group = jnp.broadcast_to(index >> log2(WIDE), (8, WIDE))
+        value = jnp.zeros((8, WIDE), F32)
         for g in range(groups):
             part = got[g * 8 : (g + 1) * 8] + got[rows + g * 8 : rows + (g + 1) * 8]
             value = jnp.where(group == g, part, value)
-        value = value * weight
+        return value
+
+    def by_lanes(index):
+        lane = jnp.broadcast_to(index & 127, (8, 128))
+        tile = jnp.broadcast_to(index >> 7, (8, 128))
+        value = jnp.zeros((8, 128), F32)
+        for g in range(padded.shape[1] // 128):
+            piece = padded[:, g * 128 : (g + 1) * 128]
+            piece = jnp.take_along_axis(piece, lane, axis=1, mode="promise_in_bounds")
+            value = jnp.where(tile == g, piece, value)
+        return value
+
+    def one_owner(q, matmuls):
+        at = pl.multiple_of(q * SPAN, SPAN)
+        index = index_ref[:, pl.ds(at, SPAN)]
+        weight = weight_ref[:, pl.ds(at, SPAN)]
+        values = [by_matmul(index[:, i * WIDE : (i + 1) * WIDE]) for i in range(matmuls)]
+        for t in range(matmuls * WIDE // 128, tiles):
+            values.append(by_lanes(index[:, t * 128 : (t + 1) * 128]))
+        value = jnp.concatenate(values, axis=1) * weight
         for t in range(tiles):
             out_ref[pl.ds(q * (FIELDS * tiles) + t, FIELDS, stride=tiles), :] = value[
                 :FIELDS, t * lanes : (t + 1) * lanes
@@ -97,7 +115,7 @@
     @pl.loop(0, owners // AT_ONCE)
     def _(m):
         for i in range(AT_ONCE):
-            one_owner(m * AT_ONCE + i)
+            one_owner(m * AT_ONCE + i, SPAN // WIDE - i % 2)
 
 
 def gather_call(fields, index, weight):
@@ -109,6 +127,7 @@
         out_specs=pl.BlockSpec(memory_space=pltpu.VMEM),
         scratch_shapes=[
             pltpu.VMEM((fields.shape[1] // WIDE * 8, WIDE), F32),
+            pltpu.VMEM((8, fields.shape[1]), F32),
             pltpu.VMEM(fields.shape, F32),
             pltpu.VMEM(index.shape, jnp.int32),
             pltpu.VMEM(weight.shape, F32),
@@ -144,12 +163,11 @@
             for f in range(FIELDS):
                 parts.append(jnp.where(here, half[f : f + 1], jnp.zeros((), BF16)))
         spread = jnp.concatenate(parts, axis=0)
-        total[...] += lax.dot_general(spread, onehot, NT, preferred_element_type=F32)
+        return lax.dot_general(spread, onehot, NT, preferred_element_type=F32)
 
     @pl.loop(0, owners // TOGETHER // 4)
     def _(n):
-        for i in range(4):
-            step(n * 4 + i)
+        total[...] += functools.reduce(lambda sums, i: sums + step(n * 4 + i), range(1, 4), step(n * 4))
 
     even_ref[FIELDS * hx] = jnp.zeros((ITERS, hz), F32)
     scale = lax.rsqrt(mass_ref[...])
@@ -192,6 +210,30 @@
         part = got[m * groups : (m + 1) * groups] + got[rows + m * groups : rows + (m + 1) * groups]
         out.append(jnp.sum(jnp.where(here, part, 0.0), axis=0, keepdims=True))
     return out
+
+
+def pick_rows(tables, row, lane):
+    row = jnp.broadcast_to(row, (8, 128))
+    lane = jnp.broadcast_to(lane, (8, 128))
+    tile = row >> 3
+    here = row_ids(8, 128) == (row & 7)
+    out = []
+    for table in tables:
+        got = jnp.zeros((8, 128), F32)
+        for v in range(table.shape[0] // 8):
+            piece = jnp.take_along_axis(table[v * 8 : (v + 1) * 8], lane, axis=1, mode="promise_in_bounds")
+            got = jnp.where(tile == v, piece, got)
+        out.append(jnp.sum(jnp.where(here, got, 0.0), axis=0, keepdims=True))
+    return out
+
+
+def either_way(i, index, table, ids, group_ids, groups, at_parts, tables, row_and_lane):
+    halves_of = [slice(c * 128, (c + 1) * 128) for c in range(2)]
+    if i % 8 in (2, 5, 7):
+        got = [pick_rows(tables, *row_and_lane(index[:, c])) for c in halves_of]
+        return [got[c][m] for m in range(3) for c in range(2)]
+    got = lookup_rows(table, index, ids, group_ids, groups, at_parts)
+    return [line[:, c] for line in got for c in halves_of]
 
 
 def cell_moduli(vals):
@@ -327,12 +369,14 @@
     def at_parts(index):
         return (index >> log2(hz)) & (groups - 1), ((index >> log2(groups * hz)) << log2(hz)) + (index & (hz - 1))
 
+    def row_and_lane(index):
+        return index >> log2(hz), index & (hz - 1)
+
     for q in range(0, groups, 4):
         lines = []
         for i in range(q, q + 4):
             index = order_ref[:, i * WIDE : (i + 1) * WIDE]
-            got = lookup_rows(table, index, ids, group_ids, groups, at_parts)
-            lines += [line[:, c * 128 : (c + 1) * 128] for line in got for c in range(2)]
+            lines += either_way(i, index, table, ids, group_ids, groups, at_parts, payload, row_and_lane)
         out_ref[q * 6 : q * 6 + 24, :] = jnp.concatenate(lines, axis=0)
     leave.wait()
 
@@ -359,25 +403,26 @@
 
 def place_kernel(arrived_ref, order_ref, out_hbm, out_ref, sems):
     groups = arrived_ref.shape[0] // 6
-    table = jnp.concatenate(
-        [
-            jnp.concatenate([arrived_ref[pl.ds(2 * m + c, groups, stride=6), :] for c in range(2)], axis=1)
-            for m in range(3)
-        ],
-        axis=0,
-    )
+    parts = [[arrived_ref[pl.ds(2 * m + c, groups, stride=6), :] for c in range(2)] for m in range(3)]
+    table = jnp.concatenate([jnp.concatenate(part, axis=1) for part in parts], axis=0)
     table = jnp.concatenate(halves(table), axis=0)
+    tables = [jnp.concatenate(part, axis=0) for part in parts]
     ids = row_ids(WIDE, WIDE).astype(F32).astype(BF16)
     group_ids = row_ids(groups, WIDE)
+
+    def at_parts(index):
+        return index >> log2(WIDE), index & (WIDE - 1)
+
+    def row_and_lane(index):
+        return ((index >> 7) & 1) * groups + (index >> log2(WIDE)), index & 127
 
     copies = []
     for n in range(PIECES):
         for q in range(n * groups // PIECES, (n + 1) * groups // PIECES):
-            at = pl.ds(q * WIDE, WIDE)
-            got = lookup_rows(
-                table, order_ref[:, at], ids, group_ids, groups, lambda index: (index >> log2(WIDE), index & (WIDE - 1))
-            )
-            out_ref[:, at] = jnp.concatenate(got, axis=0)
+            index = order_ref[:, q * WIDE : (q + 1) * WIDE]
+            lines = either_way(q, index, table, ids, group_ids, groups, at_parts, tables, row_and_lane)
+            for c in range(2):
+                out_ref[:, q * WIDE + c * 128 : q * WIDE + (c + 1) * 128] = jnp.concatenate(lines[c::2], axis=0)
         piece = pl.ds(n * groups // PIECES * WIDE, groups // PIECES * WIDE)
         copies.append(pltpu.make_async_copy(out_ref.at[:, piece], out_hbm.at[:, piece], sems.at[n]))
         copies[n].start()

time: 57.1 us -> 57.4 us (level)
    pallas_call x1, Pallas kernels: 2.51 us -> 3.46 us  [solve_call(): pl.pallas_call(kernel, out_shape=(jax.ShapeDtypeStruct((FIELDS, hx, hy, h...]
where the time goes in v17:
time: 57.4 us; the launch traced here: 57.1 us
  blocking collectives  36.4 us (63%)
  Pallas kernels  11.8 us (21%)
  starting transfers between devices  7.14 us (12%)
  waiting for transfers between devices  0.9 us (2%)
  between operations  0.73 us (1%)
    all_to_all x1, blocking collectives, on_device(): lax.all_to_all(values, both, split_axis=0, concat_axis=0, tiled=True)  22.1 us
    all_to_all x1, blocking collectives, on_device(): lax.all_to_all(outgoing, both, split_axis=0, concat_axis=0, tiled=True)  14.4 us
    ppermute x6, starting transfers between devices, swap(): return lax.ppermute(x, axis, pairs + [(j, i) for i, j in pairs])  7.14 us
    pallas_call x1, Pallas kernels, scatter_call(): pl.pallas_call(scatter_kernel, out_shape=(jax.ShapeDtypeStruct((FIELDS, h...  3.98 us
    pallas_call x1, Pallas kernels, solve_call(): pl.pallas_call(kernel, out_shape=(jax.ShapeDtypeStruct((FIELDS, hx, hy, h...  3.46 us
    pallas_call x1, Pallas kernels, gather_call(): pl.pallas_call(gather_kernel, out_shape=jax.ShapeDtypeStruct((rows, 128),...  2.8 us
    pallas_call x1, Pallas kernels, place_call(): pl.pallas_call(place_kernel, out_shape=jax.ShapeDtypeStruct((3, order.sha...  1.54 us
  transfers between devices with their start and end apart: 6, of which 1 were waited for; matrix products, arithmetic and copies ran while one was open for 0% of the time, Pallas kernels for 0%

profile of v17, /device:TPU:0, one launch (start us, length us, event | category | flops | bytes accessed | tf_op | source)
XLA Modules:
  0.0 57.1 jit_solution(5684001893268508888)
XLA Ops:
  0.6 2.8 %shard_map.86 = f32[896,128]{1,0:T(8,128)S(1)} custom-call(f32[7,4096]{1,0:T(8,128)} %fields_hbm.1, s32[1,16384]{1,0:T(1,128)} %bitcast.12, f32[1,16384]{1,0:T(1,128)} %bitcast.13), custom_call_target="tpu_custom_call" | custom-call | tf_op jit(solution)/shard_map/pallas_call | solution.py:123
  3.4 0.0 copy-start
  3.5 0.0 copy-start.1
  3.5 22.1 %all_to_all.10 = f32[32,7,4,128]{3,2,1,0:T(4,128)S(1)} all-to-all(f32[32,7,4,128]{3,2,1,0:T(4,128)S(1)} %bitcast.8), channel_id=1, replica_groups=mesh['src'=4,'tgt'=8] {'src','tgt'}, dimensions={0} | all-to-all | bytes 917504 | tf_op jit(solution)/shard_map/all_to_all | solution.py:458
  25.5 0.0 copy-done
  25.5 0.0 copy-done.1
  25.5 4.0 %shard_map.87 = (f32[7,4,16,128]{3,2,1,0:T(8,128)S(1)}, f32[29,4,128]{2,1,0:T(4,128)S(1)}, f32[28,4,128]{2,1,0:T(4,128)S(1)}) custom-call(f32[896,128]{1,0:T(8,128)S(1)} %bitcast.7, s32[1,16384]{1,0:T(1,128)S(1)} %bitcast.11, f32[4,16,128]{2,1,0:T(8,128)S(1)} %copy-done), custom_call_target="tpu_custom_call" | custom-call | tf_op jit(solution)/shard_map/pallas_call | solution.py:193
  29.5 0.9 %collective-permute-start = (f32[29,4,128]{2,1,0:T(4,128)S(1)}, f32[29,4,128]{2,1,0:T(4,128)S(1)}, u32[]{:S(2)}, u32[]{:S(2)}) collective-permute-start(f32[29,4,128]{2,1,0:T(4,128)S(1)} %get-tuple-element.11), channel_id=1, source_target_pairs={{0,1},{2,3},{4,5},{6,7},{1,0},{3,2},{5,4},{7,6},{8,9},{10,11},{12,... | collective-permute-start | bytes 178184 | tf_op jit(solution)/shard_map/ppermute | solution.py:446
  30.4 0.7 %collective-permute-start.1 = (f32[28,4,128]{2,1,0:T(4,128)S(1)}, f32[28,4,128]{2,1,0:T(4,128)S(1)}, u32[]{:S(2)}, u32[]{:S(2)}) collective-permute-start(f32[28,4,128]{2,1,0:T(4,128)S(1)} %get-tuple-element.12), channel_id=1, source_target_pairs={{1,2},{3,4},{5,6},{2,1},{4,3},{6,5},{9,10},{11,12},{13,14},{10,9},... | collective-permute-start | bytes 172040 | tf_op jit(solution)/shard_map/ppermute | solution.py:446
  31.1 0.0 copy-start.2
  31.1 0.7 %collective-permute-start.3 = (f32[7,4,16,128]{3,2,1,0:T(8,128)S(1)}, f32[7,4,16,128]{3,2,1,0:T(8,128)S(1)}, u32[]{:S(2)}, u32[]{:S(2)}) collective-permute-start(f32[7,4,16,128]{3,2,1,0:T(8,128)S(1)} %get-tuple-element.10.refs_0_), channel_id=1, source_target_pairs={{8,16},{16,8},{9,17},{17,9},{10,18},{18,10},{11,19},{19,11},{12,20... | collective-permute-start | bytes 688136 | tf_op jit(solution)/shard_map/ppermute | solution.py:446
  31.8 2.0 %collective-permute-start.2 = (f32[7,4,16,128]{3,2,1,0:T(8,128)S(1)}, f32[7,4,16,128]{3,2,1,0:T(8,128)S(1)}, u32[]{:S(2)}, u32[]{:S(2)}) collective-permute-start(f32[7,4,16,128]{3,2,1,0:T(8,128)S(1)} %get-tuple-element.10.refs_0_), channel_id=1, source_target_pairs={{0,8},{16,24},{8,0},{24,16},{1,9},{17,25},{9,1},{25,17},{2,10},{18... | collective-permute-start | bytes 688136 | tf_op jit(solution)/shard_map/ppermute | solution.py:446
  33.8 0.0 collective-permute-done.1.odd_ref
  33.8 0.0 collective-permute-done.even_ref
  33.8 0.7 %collective-permute-start.5 = (f32[7,16,128]{2,1,0:T(8,128)S(1)}, f32[7,16,128]{2,1,0:T(8,128)S(1)}, u32[]{:S(2)}, u32[]{:S(2)}) collective-permute-start(f32[7,16,128]{2,1,0:T(8,128)S(1)} %get-tuple-element.15), channel_id=1, source_target_pairs={{8,16},{16,8},{9,17},{17,9},{10,18},{18,10},{11,19},{19,11},{12,20... | collective-permute-start | bytes 172040 | tf_op jit(solution)/shard_map/ppermute | solution.py:446
  34.5 2.2 %collective-permute-start.4 = (f32[7,14,128]{2,1,0:T(8,128)S(1)}, f32[7,14,128]{2,1,0:T(8,128)S(1)}, u32[]{:S(2)}, u32[]{:S(2)}) collective-permute-start(f32[7,14,128]{2,1,0:T(8,128)S(1)} %get-tuple-element.14), channel_id=1, source_target_pairs={{0,8},{16,24},{8,0},{24,16},{1,9},{17,25},{9,1},{25,17},{2,10},{18... | collective-permute-start | bytes 150536 | tf_op jit(solution)/shard_map/ppermute | solution.py:446
  36.8 0.9 %collective-permute-done.4.refs_4_ = f32[7,14,128]{2,1,0:T(8,128)S(1)} collective-permute-done((f32[7,14,128]{2,1,0:T(8,128)S(1)}, f32[7,14,128]{2,1,0:T(8,128)S(1)}, u32[]{:S(2)}, u32[]{:S(2)}) %collective-permute-start.4) | collective-permute-done | bytes 50208 | tf_op jit(solution)/shard_map/ppermute | solution.py:446
  37.6 0.0 collective-permute-done.5.refs_5_
  37.6 0.0 collective-permute-done.3.refs_3_
  37.6 0.0 collective-permute-done.2.refs_2_
  37.7 0.0 copy-done.2
  37.7 3.5 %shard_map.89 = (f32[7,4,16,128]{3,2,1,0:T(8,128)}, f32[192,128]{1,0:T(8,128)S(1)}) custom-call(f32[7,4,16,128]{3,2,1,0:T(8,128)S(1)} %get-tuple-element.10.refs_0_, f32[7,4,8,128]{3,2,1,0:T(8,128)S(1)} %get-tuple-element.13.refs_1_, f32[7,4,16,128]{3,2,1,0:T(8,128)S(1)} %collective-permute-done.2.refs_2_, ...), custom_call_target="tpu_custom_call" | custom-call | tf_op jit(solution)/shard_map/pallas_call | solution.py:391
  41.1 0.0 copy-start.3
  41.1 14.4 %all_to_all.11 = f32[32,3,2,128]{3,2,1,0:T(2,128)S(1)} all-to-all(f32[32,3,2,128]{3,2,1,0:T(2,128)S(1)} %bitcast.10), channel_id=1, replica_groups=mesh['src'=4,'tgt'=8] {'src','tgt'}, dimensions={0} | all-to-all | bytes 196608 | tf_op jit(solution)/shard_map/all_to_all | solution.py:470
  55.5 0.0 copy-done.3
  55.5 1.5 %shard_map.90 = f32[3,8192]{1,0:T(4,128)} custom-call(f32[192,128]{1,0:T(8,128)S(1)} %bitcast.9, s32[1,8192]{1,0:T(1,128)S(1)} %copy-done.3), custom_call_target="tpu_custom_call" | custom-call | tf_op jit(solution)/shard_map/pallas_call | solution.py:434
  (1 shorter events, 0.0 us)
Async XLA Ops:
  3.4 22.1 %copy-start = (f32[4,16,128]{2,1,0:T(8,128)S(1)}, f32[4,16,128]{2,1,0:T(8,128)}, u32[]{:S(2)}) copy-start(f32[4,16,128]{2,1,0:T(8,128)} %refs_6_.1) | copy-start | bytes 98308
  3.5 22.1 %copy-start.1 = (s32[16384]{0:T(1024)S(1)}, s32[16384]{0:T(1024)}, u32[]{:S(2)}) copy-start(s32[16384]{0:T(1024)} %param.10) | copy-start | bytes 196612
  29.5 4.3 %collective-permute-start = (f32[29,4,128]{2,1,0:T(4,128)S(1)}, f32[29,4,128]{2,1,0:T(4,128)S(1)}, u32[]{:S(2)}, u32[]{:S(2)}) collective-permute-start(f32[29,4,128]{2,1,0:T(4,128)S(1)} %get-tuple-element.11), channel_id=1, source_target_pairs={{0,1},{2,3},{4,5},{6,7},{1,0},{3,2},{5,4},{7,6},{8,9},{10,11},{12,... | collective-permute-start | bytes 178184 | tf_op jit(solution)/shard_map/ppermute | solution.py:446
  30.4 3.3 %collective-permute-start.1 = (f32[28,4,128]{2,1,0:T(4,128)S(1)}, f32[28,4,128]{2,1,0:T(4,128)S(1)}, u32[]{:S(2)}, u32[]{:S(2)}) collective-permute-start(f32[28,4,128]{2,1,0:T(4,128)S(1)} %get-tuple-element.12), channel_id=1, source_target_pairs={{1,2},{3,4},{5,6},{2,1},{4,3},{6,5},{9,10},{11,12},{13,14},{10,9},... | collective-permute-start | bytes 172040 | tf_op jit(solution)/shard_map/ppermute | solution.py:446
  31.1 6.5 %copy-start.2 = (s32[1,8192]{1,0:T(1,128)S(1)}, s32[1,8192]{1,0:T(1,128)}, u32[]{:S(2)}) copy-start(s32[1,8192]{1,0:T(1,128)} %refs_7_.1) | copy-start | bytes 98308
  31.1 6.5 %collective-permute-start.3 = (f32[7,4,16,128]{3,2,1,0:T(8,128)S(1)}, f32[7,4,16,128]{3,2,1,0:T(8,128)S(1)}, u32[]{:S(2)}, u32[]{:S(2)}) collective-permute-start(f32[7,4,16,128]{3,2,1,0:T(8,128)S(1)} %get-tuple-element.10.refs_0_), channel_id=1, source_target_pairs={{8,16},{16,8},{9,17},{17,9},{10,18},{18,10},{11,19},{19,11},{12,20... | collective-permute-start | bytes 688136 | tf_op jit(solution)/shard_map/ppermute | solution.py:446
  31.8 5.8 %collective-permute-start.2 = (f32[7,4,16,128]{3,2,1,0:T(8,128)S(1)}, f32[7,4,16,128]{3,2,1,0:T(8,128)S(1)}, u32[]{:S(2)}, u32[]{:S(2)}) collective-permute-start(f32[7,4,16,128]{3,2,1,0:T(8,128)S(1)} %get-tuple-element.10.refs_0_), channel_id=1, source_target_pairs={{0,8},{16,24},{8,0},{24,16},{1,9},{17,25},{9,1},{25,17},{2,10},{18... | collective-permute-start | bytes 688136 | tf_op jit(solution)/shard_map/ppermute | solution.py:446
  33.8 3.8 %collective-permute-start.5 = (f32[7,16,128]{2,1,0:T(8,128)S(1)}, f32[7,16,128]{2,1,0:T(8,128)S(1)}, u32[]{:S(2)}, u32[]{:S(2)}) collective-permute-start(f32[7,16,128]{2,1,0:T(8,128)S(1)} %get-tuple-element.15), channel_id=1, source_target_pairs={{8,16},{16,8},{9,17},{17,9},{10,18},{18,10},{11,19},{19,11},{12,20... | collective-permute-start | bytes 172040 | tf_op jit(solution)/shard_map/ppermute | solution.py:446
  34.5 3.1 %collective-permute-start.4 = (f32[7,14,128]{2,1,0:T(8,128)S(1)}, f32[7,14,128]{2,1,0:T(8,128)S(1)}, u32[]{:S(2)}, u32[]{:S(2)}) collective-permute-start(f32[7,14,128]{2,1,0:T(8,128)S(1)} %get-tuple-element.14), channel_id=1, source_target_pairs={{0,8},{16,24},{8,0},{24,16},{1,9},{17,25},{9,1},{25,17},{2,10},{18... | collective-permute-start | bytes 150536 | tf_op jit(solution)/shard_map/ppermute | solution.py:446
  41.1 14.4 %copy-start.3 = (s32[1,8192]{1,0:T(1,128)S(1)}, s32[1,8192]{1,0:T(1,128)}, u32[]{:S(2)}) copy-start(s32[1,8192]{1,0:T(1,128)} %order_ref.1) | copy-start | bytes 98308

commit v18 on v17

--- a/solution.py
+++ b/solution.py
@@ -115,7 +115,7 @@
     @pl.loop(0, owners // AT_ONCE)
     def _(m):
         for i in range(AT_ONCE):
-            one_owner(m * AT_ONCE + i, SPAN // WIDE - i % 2)
+            one_owner(m * AT_ONCE + i, SPAN // WIDE - (i % 4 > 0))
 
 
 def gather_call(fields, index, weight):
@@ -369,14 +369,12 @@
     def at_parts(index):
         return (index >> log2(hz)) & (groups - 1), ((index >> log2(groups * hz)) << log2(hz)) + (index & (hz - 1))
 
-    def row_and_lane(index):
-        return index >> log2(hz), index & (hz - 1)
-
     for q in range(0, groups, 4):
         lines = []
         for i in range(q, q + 4):
             index = order_ref[:, i * WIDE : (i + 1) * WIDE]
-            lines += either_way(i, index, table, ids, group_ids, groups, at_parts, payload, row_and_lane)
+            got = lookup_rows(table, index, ids, group_ids, groups, at_parts)
+            lines += [line[:, c * 128 : (c + 1) * 128] for line in got for c in range(2)]
         out_ref[q * 6 : q * 6 + 24, :] = jnp.concatenate(lines, axis=0)
     leave.wait()
 

time: 57.4 us -> 56.5 us (0.984)
  Pallas kernels: 11.8 us -> 10.9 us
    pallas_call x1, Pallas kernels: 3.46 us -> 2.51 us  [solve_call(): pl.pallas_call(kernel, out_shape=(jax.ShapeDtypeStruct((FIELDS, hx, hy, h...]
where the time goes in v18:
time: 56.5 us; the launch traced here: 56.2 us
  blocking collectives  36.4 us (64%)
  Pallas kernels  10.9 us (19%)
  starting transfers between devices  7.15 us (13%)
  waiting for transfers between devices  0.91 us (2%)
  between operations  0.73 us (1%)
    all_to_all x1, blocking collectives, on_device(): lax.all_to_all(values, both, split_axis=0, concat_axis=0, tiled=True)  22.1 us
    all_to_all x1, blocking collectives, on_device(): lax.all_to_all(outgoing, both, split_axis=0, concat_axis=0, tiled=True)  14.4 us
    ppermute x6, starting transfers between devices, swap(): return lax.ppermute(x, axis, pairs + [(j, i) for i, j in pairs])  7.15 us
    pallas_call x1, Pallas kernels, scatter_call(): pl.pallas_call(scatter_kernel, out_shape=(jax.ShapeDtypeStruct((FIELDS, h...  3.98 us
    pallas_call x1, Pallas kernels, gather_call(): pl.pallas_call(gather_kernel, out_shape=jax.ShapeDtypeStruct((rows, 128),...  2.86 us
    pallas_call x1, Pallas kernels, solve_call(): pl.pallas_call(kernel, out_shape=(jax.ShapeDtypeStruct((FIELDS, hx, hy, h...  2.51 us
    pallas_call x1, Pallas kernels, place_call(): pl.pallas_call(place_kernel, out_shape=jax.ShapeDtypeStruct((3, order.sha...  1.54 us
  transfers between devices with their start and end apart: 6, of which 1 were waited for; matrix products, arithmetic and copies ran while one was open for 0% of the time, Pallas kernels for 0%

profile of v18, /device:TPU:0, one launch (start us, length us, event | category | flops | bytes accessed | tf_op | source)
XLA Modules:
  0.0 56.2 jit_solution(18039568925975229529)
XLA Ops:
  0.6 2.9 %shard_map.86 = f32[896,128]{1,0:T(8,128)S(1)} custom-call(f32[7,4096]{1,0:T(8,128)} %fields_hbm.1, s32[1,16384]{1,0:T(1,128)} %bitcast.12, f32[1,16384]{1,0:T(1,128)} %bitcast.13), custom_call_target="tpu_custom_call" | custom-call | tf_op jit(solution)/shard_map/pallas_call | solution.py:123
  3.5 0.0 copy-start
  3.5 0.0 copy-start.1
  3.5 22.1 %all_to_all.10 = f32[32,7,4,128]{3,2,1,0:T(4,128)S(1)} all-to-all(f32[32,7,4,128]{3,2,1,0:T(4,128)S(1)} %bitcast.8), channel_id=1, replica_groups=mesh['src'=4,'tgt'=8] {'src','tgt'}, dimensions={0} | all-to-all | bytes 917504 | tf_op jit(solution)/shard_map/all_to_all | solution.py:456
  25.6 0.0 copy-done
  25.6 0.0 copy-done.1
  25.6 4.0 %shard_map.87 = (f32[7,4,16,128]{3,2,1,0:T(8,128)S(1)}, f32[29,4,128]{2,1,0:T(4,128)S(1)}, f32[28,4,128]{2,1,0:T(4,128)S(1)}) custom-call(f32[896,128]{1,0:T(8,128)S(1)} %bitcast.7, s32[1,16384]{1,0:T(1,128)S(1)} %bitcast.11, f32[4,16,128]{2,1,0:T(8,128)S(1)} %copy-done), custom_call_target="tpu_custom_call" | custom-call | tf_op jit(solution)/shard_map/pallas_call | solution.py:193
  29.6 0.9 %collective-permute-start = (f32[29,4,128]{2,1,0:T(4,128)S(1)}, f32[29,4,128]{2,1,0:T(4,128)S(1)}, u32[]{:S(2)}, u32[]{:S(2)}) collective-permute-start(f32[29,4,128]{2,1,0:T(4,128)S(1)} %get-tuple-element.11), channel_id=1, source_target_pairs={{0,1},{2,3},{4,5},{6,7},{1,0},{3,2},{5,4},{7,6},{8,9},{10,11},{12,... | collective-permute-start | bytes 178184 | tf_op jit(solution)/shard_map/ppermute | solution.py:444
  30.5 0.7 %collective-permute-start.1 = (f32[28,4,128]{2,1,0:T(4,128)S(1)}, f32[28,4,128]{2,1,0:T(4,128)S(1)}, u32[]{:S(2)}, u32[]{:S(2)}) collective-permute-start(f32[28,4,128]{2,1,0:T(4,128)S(1)} %get-tuple-element.12), channel_id=1, source_target_pairs={{1,2},{3,4},{5,6},{2,1},{4,3},{6,5},{9,10},{11,12},{13,14},{10,9},... | collective-permute-start | bytes 172040 | tf_op jit(solution)/shard_map/ppermute | solution.py:444
  31.2 0.0 copy-start.2
  31.2 0.7 %collective-permute-start.3 = (f32[7,4,16,128]{3,2,1,0:T(8,128)S(1)}, f32[7,4,16,128]{3,2,1,0:T(8,128)S(1)}, u32[]{:S(2)}, u32[]{:S(2)}) collective-permute-start(f32[7,4,16,128]{3,2,1,0:T(8,128)S(1)} %get-tuple-element.10.refs_0_), channel_id=1, source_target_pairs={{8,16},{16,8},{9,17},{17,9},{10,18},{18,10},{11,19},{19,11},{12,20... | collective-permute-start | bytes 688136 | tf_op jit(solution)/shard_map/ppermute | solution.py:444
  31.9 2.0 %collective-permute-start.2 = (f32[7,4,16,128]{3,2,1,0:T(8,128)S(1)}, f32[7,4,16,128]{3,2,1,0:T(8,128)S(1)}, u32[]{:S(2)}, u32[]{:S(2)}) collective-permute-start(f32[7,4,16,128]{3,2,1,0:T(8,128)S(1)} %get-tuple-element.10.refs_0_), channel_id=1, source_target_pairs={{0,8},{16,24},{8,0},{24,16},{1,9},{17,25},{9,1},{25,17},{2,10},{18... | collective-permute-start | bytes 688136 | tf_op jit(solution)/shard_map/ppermute | solution.py:444
  33.8 0.0 collective-permute-done.1.odd_ref
  33.8 0.0 collective-permute-done.even_ref
  33.9 0.7 %collective-permute-start.5 = (f32[7,16,128]{2,1,0:T(8,128)S(1)}, f32[7,16,128]{2,1,0:T(8,128)S(1)}, u32[]{:S(2)}, u32[]{:S(2)}) collective-permute-start(f32[7,16,128]{2,1,0:T(8,128)S(1)} %get-tuple-element.15), channel_id=1, source_target_pairs={{8,16},{16,8},{9,17},{17,9},{10,18},{18,10},{11,19},{19,11},{12,20... | collective-permute-start | bytes 172040 | tf_op jit(solution)/shard_map/ppermute | solution.py:444
  34.6 2.3 %collective-permute-start.4 = (f32[7,14,128]{2,1,0:T(8,128)S(1)}, f32[7,14,128]{2,1,0:T(8,128)S(1)}, u32[]{:S(2)}, u32[]{:S(2)}) collective-permute-start(f32[7,14,128]{2,1,0:T(8,128)S(1)} %get-tuple-element.14), channel_id=1, source_target_pairs={{0,8},{16,24},{8,0},{24,16},{1,9},{17,25},{9,1},{25,17},{2,10},{18... | collective-permute-start | bytes 150536 | tf_op jit(solution)/shard_map/ppermute | solution.py:444
  36.8 0.9 %collective-permute-done.4.refs_4_ = f32[7,14,128]{2,1,0:T(8,128)S(1)} collective-permute-done((f32[7,14,128]{2,1,0:T(8,128)S(1)}, f32[7,14,128]{2,1,0:T(8,128)S(1)}, u32[]{:S(2)}, u32[]{:S(2)}) %collective-permute-start.4) | collective-permute-done | bytes 50208 | tf_op jit(solution)/shard_map/ppermute | solution.py:444
  37.7 0.0 collective-permute-done.5.refs_5_
  37.7 0.0 collective-permute-done.3.refs_3_
  37.7 0.0 collective-permute-done.2.refs_2_
  37.7 0.0 copy-done.2
  37.7 2.5 %shard_map.89 = (f32[7,4,16,128]{3,2,1,0:T(8,128)}, f32[192,128]{1,0:T(8,128)S(1)}) custom-call(f32[7,4,16,128]{3,2,1,0:T(8,128)S(1)} %get-tuple-element.10.refs_0_, f32[7,4,8,128]{3,2,1,0:T(8,128)S(1)} %get-tuple-element.13.refs_1_, f32[7,4,16,128]{3,2,1,0:T(8,128)S(1)} %collective-permute-done.2.refs_2_, ...), custom_call_target="tpu_custom_call" | custom-call | tf_op jit(solution)/shard_map/pallas_call | solution.py:389
  40.2 0.0 copy-start.3
  40.3 14.4 %all_to_all.11 = f32[32,3,2,128]{3,2,1,0:T(2,128)S(1)} all-to-all(f32[32,3,2,128]{3,2,1,0:T(2,128)S(1)} %bitcast.10), channel_id=1, replica_groups=mesh['src'=4,'tgt'=8] {'src','tgt'}, dimensions={0} | all-to-all | bytes 196608 | tf_op jit(solution)/shard_map/all_to_all | solution.py:468
  54.6 0.0 copy-done.3
  54.6 1.5 %shard_map.90 = f32[3,8192]{1,0:T(4,128)} custom-call(f32[192,128]{1,0:T(8,128)S(1)} %bitcast.9, s32[1,8192]{1,0:T(1,128)S(1)} %copy-done.3), custom_call_target="tpu_custom_call" | custom-call | tf_op jit(solution)/shard_map/pallas_call | solution.py:432
  (1 shorter events, 0.0 us)
Async XLA Ops:
  3.5 22.1 %copy-start = (f32[4,16,128]{2,1,0:T(8,128)S(1)}, f32[4,16,128]{2,1,0:T(8,128)}, u32[]{:S(2)}) copy-start(f32[4,16,128]{2,1,0:T(8,128)} %refs_6_.1) | copy-start | bytes 98308
  3.5 22.1 %copy-start.1 = (s32[16384]{0:T(1024)S(1)}, s32[16384]{0:T(1024)}, u32[]{:S(2)}) copy-start(s32[16384]{0:T(1024)} %param.10) | copy-start | bytes 196612
  29.6 4.3 %collective-permute-start = (f32[29,4,128]{2,1,0:T(4,128)S(1)}, f32[29,4,128]{2,1,0:T(4,128)S(1)}, u32[]{:S(2)}, u32[]{:S(2)}) collective-permute-start(f32[29,4,128]{2,1,0:T(4,128)S(1)} %get-tuple-element.11), channel_id=1, source_target_pairs={{0,1},{2,3},{4,5},{6,7},{1,0},{3,2},{5,4},{7,6},{8,9},{10,11},{12,... | collective-permute-start | bytes 178184 | tf_op jit(solution)/shard_map/ppermute | solution.py:444
  30.5 3.3 %collective-permute-start.1 = (f32[28,4,128]{2,1,0:T(4,128)S(1)}, f32[28,4,128]{2,1,0:T(4,128)S(1)}, u32[]{:S(2)}, u32[]{:S(2)}) collective-permute-start(f32[28,4,128]{2,1,0:T(4,128)S(1)} %get-tuple-element.12), channel_id=1, source_target_pairs={{1,2},{3,4},{5,6},{2,1},{4,3},{6,5},{9,10},{11,12},{13,14},{10,9},... | collective-permute-start | bytes 172040 | tf_op jit(solution)/shard_map/ppermute | solution.py:444
  31.2 6.6 %copy-start.2 = (s32[1,8192]{1,0:T(1,128)S(1)}, s32[1,8192]{1,0:T(1,128)}, u32[]{:S(2)}) copy-start(s32[1,8192]{1,0:T(1,128)} %refs_7_.1) | copy-start | bytes 98308
  31.2 6.5 %collective-permute-start.3 = (f32[7,4,16,128]{3,2,1,0:T(8,128)S(1)}, f32[7,4,16,128]{3,2,1,0:T(8,128)S(1)}, u32[]{:S(2)}, u32[]{:S(2)}) collective-permute-start(f32[7,4,16,128]{3,2,1,0:T(8,128)S(1)} %get-tuple-element.10.refs_0_), channel_id=1, source_target_pairs={{8,16},{16,8},{9,17},{17,9},{10,18},{18,10},{11,19},{19,11},{12,20... | collective-permute-start | bytes 688136 | tf_op jit(solution)/shard_map/ppermute | solution.py:444
  31.9 5.9 %collective-permute-start.2 = (f32[7,4,16,128]{3,2,1,0:T(8,128)S(1)}, f32[7,4,16,128]{3,2,1,0:T(8,128)S(1)}, u32[]{:S(2)}, u32[]{:S(2)}) collective-permute-start(f32[7,4,16,128]{3,2,1,0:T(8,128)S(1)} %get-tuple-element.10.refs_0_), channel_id=1, source_target_pairs={{0,8},{16,24},{8,0},{24,16},{1,9},{17,25},{9,1},{25,17},{2,10},{18... | collective-permute-start | bytes 688136 | tf_op jit(solution)/shard_map/ppermute | solution.py:444
  33.9 3.8 %collective-permute-start.5 = (f32[7,16,128]{2,1,0:T(8,128)S(1)}, f32[7,16,128]{2,1,0:T(8,128)S(1)}, u32[]{:S(2)}, u32[]{:S(2)}) collective-permute-start(f32[7,16,128]{2,1,0:T(8,128)S(1)} %get-tuple-element.15), channel_id=1, source_target_pairs={{8,16},{16,8},{9,17},{17,9},{10,18},{18,10},{11,19},{19,11},{12,20... | collective-permute-start | bytes 172040 | tf_op jit(solution)/shard_map/ppermute | solution.py:444
  34.6 3.1 %collective-permute-start.4 = (f32[7,14,128]{2,1,0:T(8,128)S(1)}, f32[7,14,128]{2,1,0:T(8,128)S(1)}, u32[]{:S(2)}, u32[]{:S(2)}) collective-permute-start(f32[7,14,128]{2,1,0:T(8,128)S(1)} %get-tuple-element.14), channel_id=1, source_target_pairs={{0,8},{16,24},{8,0},{24,16},{1,9},{17,25},{9,1},{25,17},{2,10},{18... | collective-permute-start | bytes 150536 | tf_op jit(solution)/shard_map/ppermute | solution.py:444
  40.2 14.4 %copy-start.3 = (s32[1,8192]{1,0:T(1,128)S(1)}, s32[1,8192]{1,0:T(1,128)}, u32[]{:S(2)}) copy-start(s32[1,8192]{1,0:T(1,128)} %order_ref.1) | copy-start | bytes 98308

commit v19 on v18

--- a/solution.py
+++ b/solution.py
@@ -107,15 +107,21 @@
         for t in range(matmuls * WIDE // 128, tiles):
             values.append(by_lanes(index[:, t * 128 : (t + 1) * 128]))
         value = jnp.concatenate(values, axis=1) * weight
-        for t in range(tiles):
-            out_ref[pl.ds(q * (FIELDS * tiles) + t, FIELDS, stride=tiles), :] = value[
-                :FIELDS, t * lanes : (t + 1) * lanes
-            ]
+        return [value[:FIELDS, t * lanes : (t + 1) * lanes] for t in range(tiles)]
 
     @pl.loop(0, owners // AT_ONCE)
     def _(m):
+        lines = []
         for i in range(AT_ONCE):
-            one_owner(m * AT_ONCE + i, SPAN // WIDE - (i % 4 > 0))
+            q = m * AT_ONCE + i
+            value = one_owner(q, SPAN // WIDE - (i % 4 > 0))
+            if i < AT_ONCE - 2:
+                for t in range(tiles):
+                    out_ref[pl.ds(q * (FIELDS * tiles) + t, FIELDS, stride=tiles), :] = value[t]
+            else:
+                lines += [value[t][f : f + 1] for f in range(FIELDS) for t in range(tiles)]
+        at = pl.multiple_of((m * AT_ONCE + AT_ONCE - 2) * (FIELDS * tiles), 8)
+        out_ref[pl.ds(at, len(lines)), :] = jnp.concatenate(lines, axis=0)
 
 
 def gather_call(fields, index, weight):
@@ -148,7 +154,7 @@
     ids = row_ids(WIDE, span).astype(F32).astype(BF16)
     group_ids = row_ids(groups, span).astype(F32).astype(BF16)
 
-    def step(p):
+    def step(p, last):
         at = pl.multiple_of(p * span, span)
         target = target_ref[:, pl.ds(at, span)]
         low = ((target >> log2(groups * hz)) << log2(hz)) + (target & (hz - 1))
@@ -156,8 +162,16 @@
         group = ((target >> log2(hz)) & (groups - 1)).astype(F32).astype(BF16)
         here = group_ids == group
         row = p * (TOGETHER * FIELDS * tiles)
-        pieces = [i * FIELDS * tiles + t for i in range(TOGETHER) for t in range(tiles)]
-        value = jnp.concatenate([value_ref[pl.ds(row + i, FIELDS, stride=tiles), :] for i in pieces], axis=1)
+        plain = TOGETHER - 2 if last else TOGETHER
+        pieces = [i * FIELDS * tiles + t for i in range(plain) for t in range(tiles)]
+        pieces = [value_ref[pl.ds(row + i, FIELDS, stride=tiles), :] for i in pieces]
+        if last:
+            at_end = pl.multiple_of(row + plain * FIELDS * tiles, 8)
+            block = value_ref[pl.ds(at_end, 2 * FIELDS * tiles), :]
+            for first in [i * FIELDS * tiles + t for i in range(2) for t in range(tiles)]:
+                lines = [first + f * tiles for f in range(FIELDS)]
+                pieces.append(jnp.concatenate([block[r : r + 1] for r in lines], axis=0))
+        value = jnp.concatenate(pieces, axis=1)
         parts = []
         for half in halves(value):
             for f in range(FIELDS):
@@ -167,7 +181,7 @@
 
     @pl.loop(0, owners // TOGETHER // 4)
     def _(n):
-        total[...] += functools.reduce(lambda sums, i: sums + step(n * 4 + i), range(1, 4), step(n * 4))
+        total[...] += functools.reduce(lambda sums, i: sums + step(n * 4 + i, i == 3), range(1, 4), step(n * 4, False))
 
     even_ref[FIELDS * hx] = jnp.zeros((ITERS, hz), F32)
     scale = lax.rsqrt(mass_ref[...])

time: 56.5 us -> 56.5 us (level)
  no operation moved by 1% of the time
where the time goes in v19:
time: 56.5 us; the launch traced here: 56.2 us
  blocking collectives  36.4 us (64%)
  Pallas kernels  10.9 us (19%)
  starting transfers between devices  7.13 us (13%)
  waiting for transfers between devices  0.92 us (2%)
  between operations  0.73 us (1%)
    all_to_all x1, blocking collectives, on_device(): lax.all_to_all(values, both, split_axis=0, concat_axis=0, tiled=True)  22.1 us
    all_to_all x1, blocking collectives, on_device(): lax.all_to_all(outgoing, both, split_axis=0, concat_axis=0, tiled=True)  14.4 us
    ppermute x6, starting transfers between devices, swap(): return lax.ppermute(x, axis, pairs + [(j, i) for i, j in pairs])  7.13 us
    pallas_call x1, Pallas kernels, scatter_call(): pl.pallas_call(scatter_kernel, out_shape=(jax.ShapeDtypeStruct((FIELDS, h...  3.99 us
    pallas_call x1, Pallas kernels, gather_call(): pl.pallas_call(gather_kernel, out_shape=jax.ShapeDtypeStruct((rows, 128),...  2.85 us
    pallas_call x1, Pallas kernels, solve_call(): pl.pallas_call(kernel, out_shape=(jax.ShapeDtypeStruct((FIELDS, hx, hy, h...  2.51 us
    pallas_call x1, Pallas kernels, place_call(): pl.pallas_call(place_kernel, out_shape=jax.ShapeDtypeStruct((3, order.sha...  1.55 us
  transfers between devices with their start and end apart: 6, of which 1 were waited for; matrix products, arithmetic and copies ran while one was open for 0% of the time, Pallas kernels for 0%

profile of v19, /device:TPU:0, one launch (start us, length us, event | category | flops | bytes accessed | tf_op | source)
XLA Modules:
  0.0 56.2 jit_solution(13759511586123244980)
XLA Ops:
  0.6 2.8 %shard_map.86 = f32[896,128]{1,0:T(8,128)S(1)} custom-call(f32[7,4096]{1,0:T(8,128)} %fields_hbm.1, s32[1,16384]{1,0:T(1,128)} %bitcast.12, f32[1,16384]{1,0:T(1,128)} %bitcast.13), custom_call_target="tpu_custom_call" | custom-call | tf_op jit(solution)/shard_map/pallas_call | solution.py:129
  3.5 0.0 copy-start
  3.5 0.0 copy-start.1
  3.5 22.1 %all_to_all.10 = f32[32,7,4,128]{3,2,1,0:T(4,128)S(1)} all-to-all(f32[32,7,4,128]{3,2,1,0:T(4,128)S(1)} %bitcast.8), channel_id=1, replica_groups=mesh['src'=4,'tgt'=8] {'src','tgt'}, dimensions={0} | all-to-all | bytes 917504 | tf_op jit(solution)/shard_map/all_to_all | solution.py:470
  25.6 0.0 copy-done
  25.6 0.0 copy-done.1
  25.6 4.0 %shard_map.87 = (f32[7,4,16,128]{3,2,1,0:T(8,128)S(1)}, f32[29,4,128]{2,1,0:T(4,128)S(1)}, f32[28,4,128]{2,1,0:T(4,128)S(1)}) custom-call(f32[896,128]{1,0:T(8,128)S(1)} %bitcast.7, s32[1,16384]{1,0:T(1,128)S(1)} %bitcast.11, f32[4,16,128]{2,1,0:T(8,128)S(1)} %copy-done), custom_call_target="tpu_custom_call" | custom-call | tf_op jit(solution)/shard_map/pallas_call | solution.py:207
  29.6 0.9 %collective-permute-start = (f32[29,4,128]{2,1,0:T(4,128)S(1)}, f32[29,4,128]{2,1,0:T(4,128)S(1)}, u32[]{:S(2)}, u32[]{:S(2)}) collective-permute-start(f32[29,4,128]{2,1,0:T(4,128)S(1)} %get-tuple-element.11), channel_id=1, source_target_pairs={{0,1},{2,3},{4,5},{6,7},{1,0},{3,2},{5,4},{7,6},{8,9},{10,11},{12,... | collective-permute-start | bytes 178184 | tf_op jit(solution)/shard_map/ppermute | solution.py:458
  30.5 0.7 %collective-permute-start.1 = (f32[28,4,128]{2,1,0:T(4,128)S(1)}, f32[28,4,128]{2,1,0:T(4,128)S(1)}, u32[]{:S(2)}, u32[]{:S(2)}) collective-permute-start(f32[28,4,128]{2,1,0:T(4,128)S(1)} %get-tuple-element.12), channel_id=1, source_target_pairs={{1,2},{3,4},{5,6},{2,1},{4,3},{6,5},{9,10},{11,12},{13,14},{10,9},... | collective-permute-start | bytes 172040 | tf_op jit(solution)/shard_map/ppermute | solution.py:458
  31.1 0.0 copy-start.2
  31.2 0.7 %collective-permute-start.3 = (f32[7,4,16,128]{3,2,1,0:T(8,128)S(1)}, f32[7,4,16,128]{3,2,1,0:T(8,128)S(1)}, u32[]{:S(2)}, u32[]{:S(2)}) collective-permute-start(f32[7,4,16,128]{3,2,1,0:T(8,128)S(1)} %get-tuple-element.10.refs_0_), channel_id=1, source_target_pairs={{8,16},{16,8},{9,17},{17,9},{10,18},{18,10},{11,19},{19,11},{12,20... | collective-permute-start | bytes 688136 | tf_op jit(solution)/shard_map/ppermute | solution.py:458
  31.8 2.0 %collective-permute-start.2 = (f32[7,4,16,128]{3,2,1,0:T(8,128)S(1)}, f32[7,4,16,128]{3,2,1,0:T(8,128)S(1)}, u32[]{:S(2)}, u32[]{:S(2)}) collective-permute-start(f32[7,4,16,128]{3,2,1,0:T(8,128)S(1)} %get-tuple-element.10.refs_0_), channel_id=1, source_target_pairs={{0,8},{16,24},{8,0},{24,16},{1,9},{17,25},{9,1},{25,17},{2,10},{18... | collective-permute-start | bytes 688136 | tf_op jit(solution)/shard_map/ppermute | solution.py:458
  33.8 0.0 collective-permute-done.1.odd_ref
  33.8 0.0 collective-permute-done.even_ref
  33.9 0.7 %collective-permute-start.5 = (f32[7,16,128]{2,1,0:T(8,128)S(1)}, f32[7,16,128]{2,1,0:T(8,128)S(1)}, u32[]{:S(2)}, u32[]{:S(2)}) collective-permute-start(f32[7,16,128]{2,1,0:T(8,128)S(1)} %get-tuple-element.15), channel_id=1, source_target_pairs={{8,16},{16,8},{9,17},{17,9},{10,18},{18,10},{11,19},{19,11},{12,20... | collective-permute-start | bytes 172040 | tf_op jit(solution)/shard_map/ppermute | solution.py:458
  34.5 2.2 %collective-permute-start.4 = (f32[7,14,128]{2,1,0:T(8,128)S(1)}, f32[7,14,128]{2,1,0:T(8,128)S(1)}, u32[]{:S(2)}, u32[]{:S(2)}) collective-permute-start(f32[7,14,128]{2,1,0:T(8,128)S(1)} %get-tuple-element.14), channel_id=1, source_target_pairs={{0,8},{16,24},{8,0},{24,16},{1,9},{17,25},{9,1},{25,17},{2,10},{18... | collective-permute-start | bytes 150536 | tf_op jit(solution)/shard_map/ppermute | solution.py:458
  36.8 0.9 %collective-permute-done.4.refs_4_ = f32[7,14,128]{2,1,0:T(8,128)S(1)} collective-permute-done((f32[7,14,128]{2,1,0:T(8,128)S(1)}, f32[7,14,128]{2,1,0:T(8,128)S(1)}, u32[]{:S(2)}, u32[]{:S(2)}) %collective-permute-start.4) | collective-permute-done | bytes 50208 | tf_op jit(solution)/shard_map/ppermute | solution.py:458
  37.7 0.0 collective-permute-done.5.refs_5_
  37.7 0.0 collective-permute-done.3.refs_3_
  37.7 0.0 collective-permute-done.2.refs_2_
  37.7 0.0 copy-done.2
  37.7 2.5 %shard_map.89 = (f32[7,4,16,128]{3,2,1,0:T(8,128)}, f32[192,128]{1,0:T(8,128)S(1)}) custom-call(f32[7,4,16,128]{3,2,1,0:T(8,128)S(1)} %get-tuple-element.10.refs_0_, f32[7,4,8,128]{3,2,1,0:T(8,128)S(1)} %get-tuple-element.13.refs_1_, f32[7,4,16,128]{3,2,1,0:T(8,128)S(1)} %collective-permute-done.2.refs_2_, ...), custom_call_target="tpu_custom_call" | custom-call | tf_op jit(solution)/shard_map/pallas_call | solution.py:403
  40.2 0.0 copy-start.3
  40.2 14.4 %all_to_all.11 = f32[32,3,2,128]{3,2,1,0:T(2,128)S(1)} all-to-all(f32[32,3,2,128]{3,2,1,0:T(2,128)S(1)} %bitcast.10), channel_id=1, replica_groups=mesh['src'=4,'tgt'=8] {'src','tgt'}, dimensions={0} | all-to-all | bytes 196608 | tf_op jit(solution)/shard_map/all_to_all | solution.py:482
  54.6 0.0 copy-done.3
  54.6 1.5 %shard_map.90 = f32[3,8192]{1,0:T(4,128)} custom-call(f32[192,128]{1,0:T(8,128)S(1)} %bitcast.9, s32[1,8192]{1,0:T(1,128)S(1)} %copy-done.3), custom_call_target="tpu_custom_call" | custom-call | tf_op jit(solution)/shard_map/pallas_call | solution.py:446
  (1 shorter events, 0.0 us)
Async XLA Ops:
  3.5 22.1 %copy-start = (f32[4,16,128]{2,1,0:T(8,128)S(1)}, f32[4,16,128]{2,1,0:T(8,128)}, u32[]{:S(2)}) copy-start(f32[4,16,128]{2,1,0:T(8,128)} %refs_6_.1) | copy-start | bytes 98308
  3.5 22.1 %copy-start.1 = (s32[16384]{0:T(1024)S(1)}, s32[16384]{0:T(1024)}, u32[]{:S(2)}) copy-start(s32[16384]{0:T(1024)} %param.10) | copy-start | bytes 196612
  29.6 4.3 %collective-permute-start = (f32[29,4,128]{2,1,0:T(4,128)S(1)}, f32[29,4,128]{2,1,0:T(4,128)S(1)}, u32[]{:S(2)}, u32[]{:S(2)}) collective-permute-start(f32[29,4,128]{2,1,0:T(4,128)S(1)} %get-tuple-element.11), channel_id=1, source_target_pairs={{0,1},{2,3},{4,5},{6,7},{1,0},{3,2},{5,4},{7,6},{8,9},{10,11},{12,... | collective-permute-start | bytes 178184 | tf_op jit(solution)/shard_map/ppermute | solution.py:458
  30.5 3.3 %collective-permute-start.1 = (f32[28,4,128]{2,1,0:T(4,128)S(1)}, f32[28,4,128]{2,1,0:T(4,128)S(1)}, u32[]{:S(2)}, u32[]{:S(2)}) collective-permute-start(f32[28,4,128]{2,1,0:T(4,128)S(1)} %get-tuple-element.12), channel_id=1, source_target_pairs={{1,2},{3,4},{5,6},{2,1},{4,3},{6,5},{9,10},{11,12},{13,14},{10,9},... | collective-permute-start | bytes 172040 | tf_op jit(solution)/shard_map/ppermute | solution.py:458
  31.1 6.6 %copy-start.2 = (s32[1,8192]{1,0:T(1,128)S(1)}, s32[1,8192]{1,0:T(1,128)}, u32[]{:S(2)}) copy-start(s32[1,8192]{1,0:T(1,128)} %refs_7_.1) | copy-start | bytes 98308
  31.2 6.5 %collective-permute-start.3 = (f32[7,4,16,128]{3,2,1,0:T(8,128)S(1)}, f32[7,4,16,128]{3,2,1,0:T(8,128)S(1)}, u32[]{:S(2)}, u32[]{:S(2)}) collective-permute-start(f32[7,4,16,128]{3,2,1,0:T(8,128)S(1)} %get-tuple-element.10.refs_0_), channel_id=1, source_target_pairs={{8,16},{16,8},{9,17},{17,9},{10,18},{18,10},{11,19},{19,11},{12,20... | collective-permute-start | bytes 688136 | tf_op jit(solution)/shard_map/ppermute | solution.py:458
  31.8 5.9 %collective-permute-start.2 = (f32[7,4,16,128]{3,2,1,0:T(8,128)S(1)}, f32[7,4,16,128]{3,2,1,0:T(8,128)S(1)}, u32[]{:S(2)}, u32[]{:S(2)}) collective-permute-start(f32[7,4,16,128]{3,2,1,0:T(8,128)S(1)} %get-tuple-element.10.refs_0_), channel_id=1, source_target_pairs={{0,8},{16,24},{8,0},{24,16},{1,9},{17,25},{9,1},{25,17},{2,10},{18... | collective-permute-start | bytes 688136 | tf_op jit(solution)/shard_map/ppermute | solution.py:458
  33.9 3.8 %collective-permute-start.5 = (f32[7,16,128]{2,1,0:T(8,128)S(1)}, f32[7,16,128]{2,1,0:T(8,128)S(1)}, u32[]{:S(2)}, u32[]{:S(2)}) collective-permute-start(f32[7,16,128]{2,1,0:T(8,128)S(1)} %get-tuple-element.15), channel_id=1, source_target_pairs={{8,16},{16,8},{9,17},{17,9},{10,18},{18,10},{11,19},{19,11},{12,20... | collective-permute-start | bytes 172040 | tf_op jit(solution)/shard_map/ppermute | solution.py:458
  34.5 3.1 %collective-permute-start.4 = (f32[7,14,128]{2,1,0:T(8,128)S(1)}, f32[7,14,128]{2,1,0:T(8,128)S(1)}, u32[]{:S(2)}, u32[]{:S(2)}) collective-permute-start(f32[7,14,128]{2,1,0:T(8,128)S(1)} %get-tuple-element.14), channel_id=1, source_target_pairs={{0,8},{16,24},{8,0},{24,16},{1,9},{17,25},{9,1},{25,17},{2,10},{18... | collective-permute-start | bytes 150536 | tf_op jit(solution)/shard_map/ppermute | solution.py:458
  40.2 14.4 %copy-start.3 = (s32[1,8192]{1,0:T(1,128)S(1)}, s32[1,8192]{1,0:T(1,128)}, u32[]{:S(2)}) copy-start(s32[1,8192]{1,0:T(1,128)} %order_ref.1) | copy-start | bytes 98308

commit v20 on v19

--- a/solution.py
+++ b/solution.py
@@ -321,12 +321,22 @@
         return jnp.where(flag, 1.0, 0.0).astype(F32)
 
     row = row_ids(rows, hz)
-    lane = lax.broadcasted_iota(jnp.int32, (rows, hz), 1)
     inside = jnp.where(row < hy, 1.0, jnp.where(row < hy + k, exists(b < n_tgt - 1), exists(b > 0)))
     inside_left = inside * exists(a > 0)
     inside_right = inside * exists(a < n_src - 1)
-    not_first = jnp.where(lane == 0, 0.0, 1.0)
-    not_last = jnp.where(lane == hz - 1, 0.0, 1.0)
+    gap = row_ids(hz, hz) - lax.broadcasted_iota(jnp.int32, (hz, hz), 1)
+    beside = jnp.where(jnp.abs(gap) == 1, 1.0, 0.0).astype(BF16)
+    beside = jnp.concatenate([beside, beside], axis=0)
+
+    def rows_of(sweep, x):
+        return rows if sweep + max(k - x, x - (k + hx - 1), 0) < k else hy
+
+    def deep_sums(parts):
+        both = jnp.concatenate(halves(jnp.concatenate(parts, axis=0)), axis=1)
+        sums = jnp.dot(both, beside, preferred_element_type=F32)
+        starts = np.cumsum([0] + [part.shape[0] for part in parts])
+        return [sums[at : at + part.shape[0]] for at, part in zip(starts, parts)]
+
     scale = lax.rsqrt(mass_ref[...])
 
     line = row_ids(2 * k, hz)
@@ -352,14 +362,14 @@
         u = [COEFS[k] * e for e in base]
         for sweep in range(1, k + 1):
             new = list(u)
-            for x in range(sweep, hx + 2 * k - sweep):
-                far = max(k - x, x - (k + hx - 1), 0)
-                n = rows if sweep + far < k else hy
+            xs = range(sweep, hx + 2 * k - sweep)
+            deep = deep_sums([u[x][: rows_of(sweep, x)] for x in xs])
+            for x in xs:
+                n = rows_of(sweep, x)
                 w = u[x]
                 near = u[x - 1][:n] + u[x + 1][:n]
                 near = near + pltpu.roll(w, 1, 0)[:n] + pltpu.roll(w, rows - 1, 0)[:n]
-                w = w[:n]
-                near = near + pltpu.roll(w, 1, 1) * not_first[:n] + pltpu.roll(w, hz - 1, 1) * not_last[:n]
+                near = near + deep[x - sweep]
                 if x < k:
                     near = near * inside_left[:n]
                 elif x >= k + hx:

time: 56.5 us -> 58.1 us (1.028)
  Pallas kernels: 10.9 us -> 12.5 us
    pallas_call x1, Pallas kernels: 2.51 us -> 4.09 us  [solve_call(): pl.pallas_call(kernel, out_shape=(jax.ShapeDtypeStruct((FIELDS, hx, hy, h...]
where the time goes in v20:
time: 58.1 us; the launch traced here: 57.7 us
  blocking collectives  36.4 us (63%)
  Pallas kernels  12.5 us (22%)
  starting transfers between devices  7.13 us (12%)
  waiting for transfers between devices  0.92 us (2%)
  between operations  0.73 us (1%)
    all_to_all x1, blocking collectives, on_device(): lax.all_to_all(values, both, split_axis=0, concat_axis=0, tiled=True)  22.1 us
    all_to_all x1, blocking collectives, on_device(): lax.all_to_all(outgoing, both, split_axis=0, concat_axis=0, tiled=True)  14.4 us
    ppermute x6, starting transfers between devices, swap(): return lax.ppermute(x, axis, pairs + [(j, i) for i, j in pairs])  7.13 us
    pallas_call x1, Pallas kernels, solve_call(): pl.pallas_call(kernel, out_shape=(jax.ShapeDtypeStruct((FIELDS, hx, hy, h...  4.09 us
    pallas_call x1, Pallas kernels, scatter_call(): pl.pallas_call(scatter_kernel, out_shape=(jax.ShapeDtypeStruct((FIELDS, h...  3.99 us
    pallas_call x1, Pallas kernels, gather_call(): pl.pallas_call(gather_kernel, out_shape=jax.ShapeDtypeStruct((rows, 128),...  2.85 us
    pallas_call x1, Pallas kernels, place_call(): pl.pallas_call(place_kernel, out_shape=jax.ShapeDtypeStruct((3, order.sha...  1.54 us
  transfers between devices with their start and end apart: 6, of which 1 were waited for; matrix products, arithmetic and copies ran while one was open for 0% of the time, Pallas kernels for 0%

profile of v20, /device:TPU:0, one launch (start us, length us, event | category | flops | bytes accessed | tf_op | source)
XLA Modules:
  0.0 57.7 jit_solution(10861401683019709475)
XLA Ops:
  0.6 2.8 %shard_map.86 = f32[896,128]{1,0:T(8,128)S(1)} custom-call(f32[7,4096]{1,0:T(8,128)} %fields_hbm.1, s32[1,16384]{1,0:T(1,128)} %bitcast.12, f32[1,16384]{1,0:T(1,128)} %bitcast.13), custom_call_target="tpu_custom_call" | custom-call | tf_op jit(solution)/shard_map/pallas_call | solution.py:129
  3.5 0.0 copy-start
  3.5 0.0 copy-start.1
  3.5 22.1 %all_to_all.10 = f32[32,7,4,128]{3,2,1,0:T(4,128)S(1)} all-to-all(f32[32,7,4,128]{3,2,1,0:T(4,128)S(1)} %bitcast.8), channel_id=1, replica_groups=mesh['src'=4,'tgt'=8] {'src','tgt'}, dimensions={0} | all-to-all | bytes 917504 | tf_op jit(solution)/shard_map/all_to_all | solution.py:480
  25.6 0.0 copy-done
  25.6 0.0 copy-done.1
  25.6 4.0 %shard_map.87 = (f32[7,4,16,128]{3,2,1,0:T(8,128)S(1)}, f32[29,4,128]{2,1,0:T(4,128)S(1)}, f32[28,4,128]{2,1,0:T(4,128)S(1)}) custom-call(f32[896,128]{1,0:T(8,128)S(1)} %bitcast.7, s32[1,16384]{1,0:T(1,128)S(1)} %bitcast.11, f32[4,16,128]{2,1,0:T(8,128)S(1)} %copy-done), custom_call_target="tpu_custom_call" | custom-call | tf_op jit(solution)/shard_map/pallas_call | solution.py:207
  29.6 0.9 %collective-permute-start = (f32[29,4,128]{2,1,0:T(4,128)S(1)}, f32[29,4,128]{2,1,0:T(4,128)S(1)}, u32[]{:S(2)}, u32[]{:S(2)}) collective-permute-start(f32[29,4,128]{2,1,0:T(4,128)S(1)} %get-tuple-element.11), channel_id=1, source_target_pairs={{0,1},{2,3},{4,5},{6,7},{1,0},{3,2},{5,4},{7,6},{8,9},{10,11},{12,... | collective-permute-start | bytes 178184 | tf_op jit(solution)/shard_map/ppermute | solution.py:468
  30.5 0.7 %collective-permute-start.1 = (f32[28,4,128]{2,1,0:T(4,128)S(1)}, f32[28,4,128]{2,1,0:T(4,128)S(1)}, u32[]{:S(2)}, u32[]{:S(2)}) collective-permute-start(f32[28,4,128]{2,1,0:T(4,128)S(1)} %get-tuple-element.12), channel_id=1, source_target_pairs={{1,2},{3,4},{5,6},{2,1},{4,3},{6,5},{9,10},{11,12},{13,14},{10,9},... | collective-permute-start | bytes 172040 | tf_op jit(solution)/shard_map/ppermute | solution.py:468
  31.1 0.0 copy-start.2
  31.2 0.7 %collective-permute-start.3 = (f32[7,4,16,128]{3,2,1,0:T(8,128)S(1)}, f32[7,4,16,128]{3,2,1,0:T(8,128)S(1)}, u32[]{:S(2)}, u32[]{:S(2)}) collective-permute-start(f32[7,4,16,128]{3,2,1,0:T(8,128)S(1)} %get-tuple-element.10.refs_0_), channel_id=1, source_target_pairs={{8,16},{16,8},{9,17},{17,9},{10,18},{18,10},{11,19},{19,11},{12,20... | collective-permute-start | bytes 688136 | tf_op jit(solution)/shard_map/ppermute | solution.py:468
  31.8 2.0 %collective-permute-start.2 = (f32[7,4,16,128]{3,2,1,0:T(8,128)S(1)}, f32[7,4,16,128]{3,2,1,0:T(8,128)S(1)}, u32[]{:S(2)}, u32[]{:S(2)}) collective-permute-start(f32[7,4,16,128]{3,2,1,0:T(8,128)S(1)} %get-tuple-element.10.refs_0_), channel_id=1, source_target_pairs={{0,8},{16,24},{8,0},{24,16},{1,9},{17,25},{9,1},{25,17},{2,10},{18... | collective-permute-start | bytes 688136 | tf_op jit(solution)/shard_map/ppermute | solution.py:468
  33.8 0.0 collective-permute-done.1.odd_ref
  33.8 0.0 collective-permute-done.even_ref
  33.9 0.7 %collective-permute-start.5 = (f32[7,16,128]{2,1,0:T(8,128)S(1)}, f32[7,16,128]{2,1,0:T(8,128)S(1)}, u32[]{:S(2)}, u32[]{:S(2)}) collective-permute-start(f32[7,16,128]{2,1,0:T(8,128)S(1)} %get-tuple-element.15), channel_id=1, source_target_pairs={{8,16},{16,8},{9,17},{17,9},{10,18},{18,10},{11,19},{19,11},{12,20... | collective-permute-start | bytes 172040 | tf_op jit(solution)/shard_map/ppermute | solution.py:468
  34.5 2.2 %collective-permute-start.4 = (f32[7,14,128]{2,1,0:T(8,128)S(1)}, f32[7,14,128]{2,1,0:T(8,128)S(1)}, u32[]{:S(2)}, u32[]{:S(2)}) collective-permute-start(f32[7,14,128]{2,1,0:T(8,128)S(1)} %get-tuple-element.14), channel_id=1, source_target_pairs={{0,8},{16,24},{8,0},{24,16},{1,9},{17,25},{9,1},{25,17},{2,10},{18... | collective-permute-start | bytes 150536 | tf_op jit(solution)/shard_map/ppermute | solution.py:468
  36.8 0.9 %collective-permute-done.4.refs_4_ = f32[7,14,128]{2,1,0:T(8,128)S(1)} collective-permute-done((f32[7,14,128]{2,1,0:T(8,128)S(1)}, f32[7,14,128]{2,1,0:T(8,128)S(1)}, u32[]{:S(2)}, u32[]{:S(2)}) %collective-permute-start.4) | collective-permute-done | bytes 50208 | tf_op jit(solution)/shard_map/ppermute | solution.py:468
  37.7 0.0 collective-permute-done.5.refs_5_
  37.7 0.0 collective-permute-done.3.refs_3_
  37.7 0.0 collective-permute-done.2.refs_2_
  37.7 0.0 copy-done.2
  37.7 4.1 %shard_map.89 = (f32[7,4,16,128]{3,2,1,0:T(8,128)}, f32[192,128]{1,0:T(8,128)S(1)}) custom-call(f32[7,4,16,128]{3,2,1,0:T(8,128)S(1)} %get-tuple-element.10.refs_0_, f32[7,4,8,128]{3,2,1,0:T(8,128)S(1)} %get-tuple-element.13.refs_1_, f32[7,4,16,128]{3,2,1,0:T(8,128)S(1)} %collective-permute-done.2.refs_2_, ...), custom_call_target="tpu_custom_call" | custom-call | tf_op jit(solution)/shard_map/pallas_call | solution.py:413
  41.8 0.0 copy-start.3
  41.8 14.4 %all_to_all.11 = f32[32,3,2,128]{3,2,1,0:T(2,128)S(1)} all-to-all(f32[32,3,2,128]{3,2,1,0:T(2,128)S(1)} %bitcast.10), channel_id=1, replica_groups=mesh['src'=4,'tgt'=8] {'src','tgt'}, dimensions={0} | all-to-all | bytes 196608 | tf_op jit(solution)/shard_map/all_to_all | solution.py:492
  56.2 0.0 copy-done.3
  56.2 1.5 %shard_map.90 = f32[3,8192]{1,0:T(4,128)} custom-call(f32[192,128]{1,0:T(8,128)S(1)} %bitcast.9, s32[1,8192]{1,0:T(1,128)S(1)} %copy-done.3), custom_call_target="tpu_custom_call" | custom-call | tf_op jit(solution)/shard_map/pallas_call | solution.py:456
  (1 shorter events, 0.0 us)
Async XLA Ops:
  3.5 22.1 %copy-start = (f32[4,16,128]{2,1,0:T(8,128)S(1)}, f32[4,16,128]{2,1,0:T(8,128)}, u32[]{:S(2)}) copy-start(f32[4,16,128]{2,1,0:T(8,128)} %refs_6_.1) | copy-start | bytes 98308
  3.5 22.1 %copy-start.1 = (s32[16384]{0:T(1024)S(1)}, s32[16384]{0:T(1024)}, u32[]{:S(2)}) copy-start(s32[16384]{0:T(1024)} %param.10) | copy-start | bytes 196612
  29.6 4.3 %collective-permute-start = (f32[29,4,128]{2,1,0:T(4,128)S(1)}, f32[29,4,128]{2,1,0:T(4,128)S(1)}, u32[]{:S(2)}, u32[]{:S(2)}) collective-permute-start(f32[29,4,128]{2,1,0:T(4,128)S(1)} %get-tuple-element.11), channel_id=1, source_target_pairs={{0,1},{2,3},{4,5},{6,7},{1,0},{3,2},{5,4},{7,6},{8,9},{10,11},{12,... | collective-permute-start | bytes 178184 | tf_op jit(solution)/shard_map/ppermute | solution.py:468
  30.5 3.3 %collective-permute-start.1 = (f32[28,4,128]{2,1,0:T(4,128)S(1)}, f32[28,4,128]{2,1,0:T(4,128)S(1)}, u32[]{:S(2)}, u32[]{:S(2)}) collective-permute-start(f32[28,4,128]{2,1,0:T(4,128)S(1)} %get-tuple-element.12), channel_id=1, source_target_pairs={{1,2},{3,4},{5,6},{2,1},{4,3},{6,5},{9,10},{11,12},{13,14},{10,9},... | collective-permute-start | bytes 172040 | tf_op jit(solution)/shard_map/ppermute | solution.py:468
  31.1 6.6 %copy-start.2 = (s32[1,8192]{1,0:T(1,128)S(1)}, s32[1,8192]{1,0:T(1,128)}, u32[]{:S(2)}) copy-start(s32[1,8192]{1,0:T(1,128)} %refs_7_.1) | copy-start | bytes 98308
  31.2 6.5 %collective-permute-start.3 = (f32[7,4,16,128]{3,2,1,0:T(8,128)S(1)}, f32[7,4,16,128]{3,2,1,0:T(8,128)S(1)}, u32[]{:S(2)}, u32[]{:S(2)}) collective-permute-start(f32[7,4,16,128]{3,2,1,0:T(8,128)S(1)} %get-tuple-element.10.refs_0_), channel_id=1, source_target_pairs={{8,16},{16,8},{9,17},{17,9},{10,18},{18,10},{11,19},{19,11},{12,20... | collective-permute-start | bytes 688136 | tf_op jit(solution)/shard_map/ppermute | solution.py:468
  31.8 5.9 %collective-permute-start.2 = (f32[7,4,16,128]{3,2,1,0:T(8,128)S(1)}, f32[7,4,16,128]{3,2,1,0:T(8,128)S(1)}, u32[]{:S(2)}, u32[]{:S(2)}) collective-permute-start(f32[7,4,16,128]{3,2,1,0:T(8,128)S(1)} %get-tuple-element.10.refs_0_), channel_id=1, source_target_pairs={{0,8},{16,24},{8,0},{24,16},{1,9},{17,25},{9,1},{25,17},{2,10},{18... | collective-permute-start | bytes 688136 | tf_op jit(solution)/shard_map/ppermute | solution.py:468
  33.9 3.8 %collective-permute-start.5 = (f32[7,16,128]{2,1,0:T(8,128)S(1)}, f32[7,16,128]{2,1,0:T(8,128)S(1)}, u32[]{:S(2)}, u32[]{:S(2)}) collective-permute-start(f32[7,16,128]{2,1,0:T(8,128)S(1)} %get-tuple-element.15), channel_id=1, source_target_pairs={{8,16},{16,8},{9,17},{17,9},{10,18},{18,10},{11,19},{19,11},{12,20... | collective-permute-start | bytes 172040 | tf_op jit(solution)/shard_map/ppermute | solution.py:468
  34.5 3.1 %collective-permute-start.4 = (f32[7,14,128]{2,1,0:T(8,128)S(1)}, f32[7,14,128]{2,1,0:T(8,128)S(1)}, u32[]{:S(2)}, u32[]{:S(2)}) collective-permute-start(f32[7,14,128]{2,1,0:T(8,128)S(1)} %get-tuple-element.14), channel_id=1, source_target_pairs={{0,8},{16,24},{8,0},{24,16},{1,9},{17,25},{9,1},{25,17},{2,10},{18... | collective-permute-start | bytes 150536 | tf_op jit(solution)/shard_map/ppermute | solution.py:468
  41.8 14.4 %copy-start.3 = (s32[1,8192]{1,0:T(1,128)S(1)}, s32[1,8192]{1,0:T(1,128)}, u32[]{:S(2)}) copy-start(s32[1,8192]{1,0:T(1,128)} %order_ref.1) | copy-start | bytes 98308

commit v21 on v19

--- a/solution.py
+++ b/solution.py
@@ -341,35 +341,43 @@
 
     a_odd = a % 2 == 1
 
-    for f in range(FIELDS):
+    def slabs_of(f):
         packed = jnp.concatenate([even_corners_ref[f, 2 * k :], jnp.zeros((2, hz), F32)], axis=0)
         even = (even_ref[f], even_corners_ref[f, : 2 * k], packed)
         odd = (odd_ref[f], odd_corners_ref[f, : 2 * k], odd_corners_ref[f, 2 * k :])
         left = slabs(*[jnp.where(a_odd, p, q) for p, q in zip(even, odd)], True)
         right = slabs(*[jnp.where(a_odd, q, p) for p, q in zip(even, odd)], False)
         own = [jnp.concatenate([v_ref[f, x], sides_ref[f, x]], axis=0) for x in range(hx)]
-        base = left + own + right
-        u = [COEFS[k] * e for e in base]
+        return left + own + right
+
+    def one_sweep(sweep, base, u):
+        new = list(u)
+        for x in range(sweep, hx + 2 * k - sweep):
+            far = max(k - x, x - (k + hx - 1), 0)
+            n = rows if sweep + far < k else hy
+            w = u[x]
+            near = u[x - 1][:n] + u[x + 1][:n]
+            near = near + pltpu.roll(w, 1, 0)[:n] + pltpu.roll(w, rows - 1, 0)[:n]
+            w = w[:n]
+            near = near + pltpu.roll(w, 1, 1) * not_first[:n] + pltpu.roll(w, hz - 1, 1) * not_last[:n]
+            if x < k:
+                near = near * inside_left[:n]
+            elif x >= k + hx:
+                near = near * inside_right[:n]
+            elif n > hy:
+                near = near * inside
+            new[x] = COEFS[k - sweep] * base[x][:n] + near
+        return new
+
+    for first in range(0, FIELDS, 2):
+        pair = range(first, min(first + 2, FIELDS))
+        bases = [slabs_of(f) for f in pair]
+        us = [[COEFS[k] * e for e in base] for base in bases]
         for sweep in range(1, k + 1):
-            new = list(u)
-            for x in range(sweep, hx + 2 * k - sweep):
-                far = max(k - x, x - (k + hx - 1), 0)
-                n = rows if sweep + far < k else hy
-                w = u[x]
-                near = u[x - 1][:n] + u[x + 1][:n]
-                near = near + pltpu.roll(w, 1, 0)[:n] + pltpu.roll(w, rows - 1, 0)[:n]
-                w = w[:n]
-                near = near + pltpu.roll(w, 1, 1) * not_first[:n] + pltpu.roll(w, hz - 1, 1) * not_last[:n]
-                if x < k:
-                    near = near * inside_left[:n]
-                elif x >= k + hx:
-                    near = near * inside_right[:n]
-                elif n > hy:
-                    near = near * inside
-                new[x] = COEFS[k - sweep] * base[x][:n] + near
-            u = new
-        for x in range(hx):
-            projected_ref[f, x] = u[k + x][:hy] * scale[x]
+            us = [one_sweep(sweep, base, u) for base, u in zip(bases, us)]
+        for f, u in zip(pair, us):
+            for x in range(hx):
+                projected_ref[f, x] = u[k + x][:hy] * scale[x]
 
     leave = pltpu.make_async_copy(projected_ref, projected_hbm, sem)
     leave.start()

time: 56.5 us -> 56.5 us (level)
  no operation moved by 1% of the time
where the time goes in v21:
time: 56.5 us; the launch traced here: 56.2 us
  blocking collectives  36.4 us (64%)
  Pallas kernels  10.9 us (19%)
  starting transfers between devices  7.13 us (13%)
  waiting for transfers between devices  0.92 us (2%)
  between operations  0.73 us (1%)
    all_to_all x1, blocking collectives, on_device(): lax.all_to_all(values, both, split_axis=0, concat_axis=0, tiled=True)  22.1 us
    all_to_all x1, blocking collectives, on_device(): lax.all_to_all(outgoing, both, split_axis=0, concat_axis=0, tiled=True)  14.4 us
    ppermute x6, starting transfers between devices, swap(): return lax.ppermute(x, axis, pairs + [(j, i) for i, j in pairs])  7.13 us
    pallas_call x1, Pallas kernels, scatter_call(): pl.pallas_call(scatter_kernel, out_shape=(jax.ShapeDtypeStruct((FIELDS, h...  3.99 us
    pallas_call x1, Pallas kernels, gather_call(): pl.pallas_call(gather_kernel, out_shape=jax.ShapeDtypeStruct((rows, 128),...  2.85 us
    pallas_call x1, Pallas kernels, solve_call(): pl.pallas_call(kernel, out_shape=(jax.ShapeDtypeStruct((FIELDS, hx, hy, h...  2.51 us
    pallas_call x1, Pallas kernels, place_call(): pl.pallas_call(place_kernel, out_shape=jax.ShapeDtypeStruct((3, order.sha...  1.55 us
  transfers between devices with their start and end apart: 6, of which 1 were waited for; matrix products, arithmetic and copies ran while one was open for 0% of the time, Pallas kernels for 0%

profile of v21, /device:TPU:0, one launch (start us, length us, event | category | flops | bytes accessed | tf_op | source)
XLA Modules:
  0.0 56.2 jit_solution(13759511586123244980)
XLA Ops:
  0.6 2.8 %shard_map.86 = f32[896,128]{1,0:T(8,128)S(1)} custom-call(f32[7,4096]{1,0:T(8,128)} %fields_hbm.1, s32[1,16384]{1,0:T(1,128)} %bitcast.12, f32[1,16384]{1,0:T(1,128)} %bitcast.13), custom_call_target="tpu_custom_call" | custom-call | tf_op jit(solution)/shard_map/pallas_call | solution.py:129
  3.5 0.0 copy-start
  3.5 0.0 copy-start.1
  3.5 22.1 %all_to_all.10 = f32[32,7,4,128]{3,2,1,0:T(4,128)S(1)} all-to-all(f32[32,7,4,128]{3,2,1,0:T(4,128)S(1)} %bitcast.8), channel_id=1, replica_groups=mesh['src'=4,'tgt'=8] {'src','tgt'}, dimensions={0} | all-to-all | bytes 917504 | tf_op jit(solution)/shard_map/all_to_all | solution.py:478
  25.6 0.0 copy-done
  25.6 0.0 copy-done.1
  25.6 4.0 %shard_map.87 = (f32[7,4,16,128]{3,2,1,0:T(8,128)S(1)}, f32[29,4,128]{2,1,0:T(4,128)S(1)}, f32[28,4,128]{2,1,0:T(4,128)S(1)}) custom-call(f32[896,128]{1,0:T(8,128)S(1)} %bitcast.7, s32[1,16384]{1,0:T(1,128)S(1)} %bitcast.11, f32[4,16,128]{2,1,0:T(8,128)S(1)} %copy-done), custom_call_target="tpu_custom_call" | custom-call | tf_op jit(solution)/shard_map/pallas_call | solution.py:207
  29.6 0.9 %collective-permute-start = (f32[29,4,128]{2,1,0:T(4,128)S(1)}, f32[29,4,128]{2,1,0:T(4,128)S(1)}, u32[]{:S(2)}, u32[]{:S(2)}) collective-permute-start(f32[29,4,128]{2,1,0:T(4,128)S(1)} %get-tuple-element.11), channel_id=1, source_target_pairs={{0,1},{2,3},{4,5},{6,7},{1,0},{3,2},{5,4},{7,6},{8,9},{10,11},{12,... | collective-permute-start | bytes 178184 | tf_op jit(solution)/shard_map/ppermute | solution.py:466
  30.5 0.7 %collective-permute-start.1 = (f32[28,4,128]{2,1,0:T(4,128)S(1)}, f32[28,4,128]{2,1,0:T(4,128)S(1)}, u32[]{:S(2)}, u32[]{:S(2)}) collective-permute-start(f32[28,4,128]{2,1,0:T(4,128)S(1)} %get-tuple-element.12), channel_id=1, source_target_pairs={{1,2},{3,4},{5,6},{2,1},{4,3},{6,5},{9,10},{11,12},{13,14},{10,9},... | collective-permute-start | bytes 172040 | tf_op jit(solution)/shard_map/ppermute | solution.py:466
  31.1 0.0 copy-start.2
  31.2 0.7 %collective-permute-start.3 = (f32[7,4,16,128]{3,2,1,0:T(8,128)S(1)}, f32[7,4,16,128]{3,2,1,0:T(8,128)S(1)}, u32[]{:S(2)}, u32[]{:S(2)}) collective-permute-start(f32[7,4,16,128]{3,2,1,0:T(8,128)S(1)} %get-tuple-element.10.refs_0_), channel_id=1, source_target_pairs={{8,16},{16,8},{9,17},{17,9},{10,18},{18,10},{11,19},{19,11},{12,20... | collective-permute-start | bytes 688136 | tf_op jit(solution)/shard_map/ppermute | solution.py:466
  31.8 2.0 %collective-permute-start.2 = (f32[7,4,16,128]{3,2,1,0:T(8,128)S(1)}, f32[7,4,16,128]{3,2,1,0:T(8,128)S(1)}, u32[]{:S(2)}, u32[]{:S(2)}) collective-permute-start(f32[7,4,16,128]{3,2,1,0:T(8,128)S(1)} %get-tuple-element.10.refs_0_), channel_id=1, source_target_pairs={{0,8},{16,24},{8,0},{24,16},{1,9},{17,25},{9,1},{25,17},{2,10},{18... | collective-permute-start | bytes 688136 | tf_op jit(solution)/shard_map/ppermute | solution.py:466
  33.8 0.0 collective-permute-done.1.odd_ref
  33.8 0.0 collective-permute-done.even_ref
  33.9 0.7 %collective-permute-start.5 = (f32[7,16,128]{2,1,0:T(8,128)S(1)}, f32[7,16,128]{2,1,0:T(8,128)S(1)}, u32[]{:S(2)}, u32[]{:S(2)}) collective-permute-start(f32[7,16,128]{2,1,0:T(8,128)S(1)} %get-tuple-element.15), channel_id=1, source_target_pairs={{8,16},{16,8},{9,17},{17,9},{10,18},{18,10},{11,19},{19,11},{12,20... | collective-permute-start | bytes 172040 | tf_op jit(solution)/shard_map/ppermute | solution.py:466
  34.5 2.2 %collective-permute-start.4 = (f32[7,14,128]{2,1,0:T(8,128)S(1)}, f32[7,14,128]{2,1,0:T(8,128)S(1)}, u32[]{:S(2)}, u32[]{:S(2)}) collective-permute-start(f32[7,14,128]{2,1,0:T(8,128)S(1)} %get-tuple-element.14), channel_id=1, source_target_pairs={{0,8},{16,24},{8,0},{24,16},{1,9},{17,25},{9,1},{25,17},{2,10},{18... | collective-permute-start | bytes 150536 | tf_op jit(solution)/shard_map/ppermute | solution.py:466
  36.8 0.9 %collective-permute-done.4.refs_4_ = f32[7,14,128]{2,1,0:T(8,128)S(1)} collective-permute-done((f32[7,14,128]{2,1,0:T(8,128)S(1)}, f32[7,14,128]{2,1,0:T(8,128)S(1)}, u32[]{:S(2)}, u32[]{:S(2)}) %collective-permute-start.4) | collective-permute-done | bytes 50208 | tf_op jit(solution)/shard_map/ppermute | solution.py:466
  37.7 0.0 collective-permute-done.5.refs_5_
  37.7 0.0 collective-permute-done.3.refs_3_
  37.7 0.0 collective-permute-done.2.refs_2_
  37.7 0.0 copy-done.2
  37.7 2.5 %shard_map.89 = (f32[7,4,16,128]{3,2,1,0:T(8,128)}, f32[192,128]{1,0:T(8,128)S(1)}) custom-call(f32[7,4,16,128]{3,2,1,0:T(8,128)S(1)} %get-tuple-element.10.refs_0_, f32[7,4,8,128]{3,2,1,0:T(8,128)S(1)} %get-tuple-element.13.refs_1_, f32[7,4,16,128]{3,2,1,0:T(8,128)S(1)} %collective-permute-done.2.refs_2_, ...), custom_call_target="tpu_custom_call" | custom-call | tf_op jit(solution)/shard_map/pallas_call | solution.py:411
  40.2 0.0 copy-start.3
  40.2 14.4 %all_to_all.11 = f32[32,3,2,128]{3,2,1,0:T(2,128)S(1)} all-to-all(f32[32,3,2,128]{3,2,1,0:T(2,128)S(1)} %bitcast.10), channel_id=1, replica_groups=mesh['src'=4,'tgt'=8] {'src','tgt'}, dimensions={0} | all-to-all | bytes 196608 | tf_op jit(solution)/shard_map/all_to_all | solution.py:490
  54.6 0.0 copy-done.3
  54.6 1.5 %shard_map.90 = f32[3,8192]{1,0:T(4,128)} custom-call(f32[192,128]{1,0:T(8,128)S(1)} %bitcast.9, s32[1,8192]{1,0:T(1,128)S(1)} %copy-done.3), custom_call_target="tpu_custom_call" | custom-call | tf_op jit(solution)/shard_map/pallas_call | solution.py:454
  (1 shorter events, 0.0 us)
Async XLA Ops:
  3.5 22.1 %copy-start = (f32[4,16,128]{2,1,0:T(8,128)S(1)}, f32[4,16,128]{2,1,0:T(8,128)}, u32[]{:S(2)}) copy-start(f32[4,16,128]{2,1,0:T(8,128)} %refs_6_.1) | copy-start | bytes 98308
  3.5 22.1 %copy-start.1 = (s32[16384]{0:T(1024)S(1)}, s32[16384]{0:T(1024)}, u32[]{:S(2)}) copy-start(s32[16384]{0:T(1024)} %param.10) | copy-start | bytes 196612
  29.6 4.3 %collective-permute-start = (f32[29,4,128]{2,1,0:T(4,128)S(1)}, f32[29,4,128]{2,1,0:T(4,128)S(1)}, u32[]{:S(2)}, u32[]{:S(2)}) collective-permute-start(f32[29,4,128]{2,1,0:T(4,128)S(1)} %get-tuple-element.11), channel_id=1, source_target_pairs={{0,1},{2,3},{4,5},{6,7},{1,0},{3,2},{5,4},{7,6},{8,9},{10,11},{12,... | collective-permute-start | bytes 178184 | tf_op jit(solution)/shard_map/ppermute | solution.py:466
  30.5 3.3 %collective-permute-start.1 = (f32[28,4,128]{2,1,0:T(4,128)S(1)}, f32[28,4,128]{2,1,0:T(4,128)S(1)}, u32[]{:S(2)}, u32[]{:S(2)}) collective-permute-start(f32[28,4,128]{2,1,0:T(4,128)S(1)} %get-tuple-element.12), channel_id=1, source_target_pairs={{1,2},{3,4},{5,6},{2,1},{4,3},{6,5},{9,10},{11,12},{13,14},{10,9},... | collective-permute-start | bytes 172040 | tf_op jit(solution)/shard_map/ppermute | solution.py:466
  31.1 6.6 %copy-start.2 = (s32[1,8192]{1,0:T(1,128)S(1)}, s32[1,8192]{1,0:T(1,128)}, u32[]{:S(2)}) copy-start(s32[1,8192]{1,0:T(1,128)} %refs_7_.1) | copy-start | bytes 98308
  31.2 6.5 %collective-permute-start.3 = (f32[7,4,16,128]{3,2,1,0:T(8,128)S(1)}, f32[7,4,16,128]{3,2,1,0:T(8,128)S(1)}, u32[]{:S(2)}, u32[]{:S(2)}) collective-permute-start(f32[7,4,16,128]{3,2,1,0:T(8,128)S(1)} %get-tuple-element.10.refs_0_), channel_id=1, source_target_pairs={{8,16},{16,8},{9,17},{17,9},{10,18},{18,10},{11,19},{19,11},{12,20... | collective-permute-start | bytes 688136 | tf_op jit(solution)/shard_map/ppermute | solution.py:466
  31.8 5.9 %collective-permute-start.2 = (f32[7,4,16,128]{3,2,1,0:T(8,128)S(1)}, f32[7,4,16,128]{3,2,1,0:T(8,128)S(1)}, u32[]{:S(2)}, u32[]{:S(2)}) collective-permute-start(f32[7,4,16,128]{3,2,1,0:T(8,128)S(1)} %get-tuple-element.10.refs_0_), channel_id=1, source_target_pairs={{0,8},{16,24},{8,0},{24,16},{1,9},{17,25},{9,1},{25,17},{2,10},{18... | collective-permute-start | bytes 688136 | tf_op jit(solution)/shard_map/ppermute | solution.py:466
  33.9 3.8 %collective-permute-start.5 = (f32[7,16,128]{2,1,0:T(8,128)S(1)}, f32[7,16,128]{2,1,0:T(8,128)S(1)}, u32[]{:S(2)}, u32[]{:S(2)}) collective-permute-start(f32[7,16,128]{2,1,0:T(8,128)S(1)} %get-tuple-element.15), channel_id=1, source_target_pairs={{8,16},{16,8},{9,17},{17,9},{10,18},{18,10},{11,19},{19,11},{12,20... | collective-permute-start | bytes 172040 | tf_op jit(solution)/shard_map/ppermute | solution.py:466
  34.5 3.1 %collective-permute-start.4 = (f32[7,14,128]{2,1,0:T(8,128)S(1)}, f32[7,14,128]{2,1,0:T(8,128)S(1)}, u32[]{:S(2)}, u32[]{:S(2)}) collective-permute-start(f32[7,14,128]{2,1,0:T(8,128)S(1)} %get-tuple-element.14), channel_id=1, source_target_pairs={{0,8},{16,24},{8,0},{24,16},{1,9},{17,25},{9,1},{25,17},{2,10},{18... | collective-permute-start | bytes 150536 | tf_op jit(solution)/shard_map/ppermute | solution.py:466
  40.2 14.4 %copy-start.3 = (s32[1,8192]{1,0:T(1,128)S(1)}, s32[1,8192]{1,0:T(1,128)}, u32[]{:S(2)}) copy-start(s32[1,8192]{1,0:T(1,128)} %order_ref.1) | copy-start | bytes 98308

commit v22 on v19

--- a/solution.py
+++ b/solution.py
@@ -49,6 +49,18 @@
 def log2(n):
     assert n & (n - 1) == 0
     return n.bit_length() - 1
+
+
+def choose(part, index, count):
+    bits = [(index & (1 << bit)) != 0 for bit in range(log2(count))]
+
+    def among(first, depth):
+        if depth == 0:
+            return part(first)
+        low = among(first, depth - 1)
+        return jnp.where(bits[depth - 1], among(first + (1 << (depth - 1)), depth - 1), low)
+
+    return among(0, log2(count))
 
 
 def row_ids(rows, lanes):
@@ -83,21 +95,17 @@
     def by_matmul(index):
         got = jnp.dot(both, low_onehot(index & (WIDE - 1), ids), preferred_element_type=F32)
         group = jnp.broadcast_to(index >> log2(WIDE), (8, WIDE))
-        value = jnp.zeros((8, WIDE), F32)
-        for g in range(groups):
-            part = got[g * 8 : (g + 1) * 8] + got[rows + g * 8 : rows + (g + 1) * 8]
-            value = jnp.where(group == g, part, value)
-        return value
+        return choose(lambda g: got[g * 8 : (g + 1) * 8] + got[rows + g * 8 : rows + (g + 1) * 8], group, groups)
 
     def by_lanes(index):
         lane = jnp.broadcast_to(index & 127, (8, 128))
         tile = jnp.broadcast_to(index >> 7, (8, 128))
-        value = jnp.zeros((8, 128), F32)
-        for g in range(padded.shape[1] // 128):
-            piece = padded[:, g * 128 : (g + 1) * 128]
-            piece = jnp.take_along_axis(piece, lane, axis=1, mode="promise_in_bounds")
-            value = jnp.where(tile == g, piece, value)
-        return value
+
+        def piece(g):
+            columns = padded[:, g * 128 : (g + 1) * 128]
+            return jnp.take_along_axis(columns, lane, axis=1, mode="promise_in_bounds")
+
+        return choose(piece, tile, padded.shape[1] // 128)
 
     def one_owner(q, matmuls):
         at = pl.multiple_of(q * SPAN, SPAN)
@@ -233,10 +241,11 @@
     here = row_ids(8, 128) == (row & 7)
     out = []
     for table in tables:
-        got = jnp.zeros((8, 128), F32)
-        for v in range(table.shape[0] // 8):
-            piece = jnp.take_along_axis(table[v * 8 : (v + 1) * 8], lane, axis=1, mode="promise_in_bounds")
-            got = jnp.where(tile == v, piece, got)
+
+        def piece(v, table=table):
+            return jnp.take_along_axis(table[v * 8 : (v + 1) * 8], lane, axis=1, mode="promise_in_bounds")
+
+        got = choose(piece, tile, table.shape[0] // 8)
         out.append(jnp.sum(jnp.where(here, got, 0.0), axis=0, keepdims=True))
     return out
 

time: 56.5 us -> 56.5 us (level)
  no operation moved by 1% of the time
where the time goes in v22:
time: 56.5 us; the launch traced here: 56.1 us
  blocking collectives  36.4 us (64%)
  Pallas kernels  10.9 us (19%)
  starting transfers between devices  7.14 us (13%)
  waiting for transfers between devices  0.91 us (2%)
  between operations  0.73 us (1%)
    all_to_all x1, blocking collectives, on_device(): lax.all_to_all(values, both, split_axis=0, concat_axis=0, tiled=True)  22.1 us
    all_to_all x1, blocking collectives, on_device(): lax.all_to_all(outgoing, both, split_axis=0, concat_axis=0, tiled=True)  14.4 us
    ppermute x6, starting transfers between devices, swap(): return lax.ppermute(x, axis, pairs + [(j, i) for i, j in pairs])  7.14 us
    pallas_call x1, Pallas kernels, scatter_call(): pl.pallas_call(scatter_kernel, out_shape=(jax.ShapeDtypeStruct((FIELDS, h...  3.98 us
    pallas_call x1, Pallas kernels, gather_call(): pl.pallas_call(gather_kernel, out_shape=jax.ShapeDtypeStruct((rows, 128),...  2.85 us
    pallas_call x1, Pallas kernels, solve_call(): pl.pallas_call(kernel, out_shape=(jax.ShapeDtypeStruct((FIELDS, hx, hy, h...  2.51 us
    pallas_call x1, Pallas kernels, place_call(): pl.pallas_call(place_kernel, out_shape=jax.ShapeDtypeStruct((3, order.sha...  1.5 us
  transfers between devices with their start and end apart: 6, of which 1 were waited for; matrix products, arithmetic and copies ran while one was open for 0% of the time, Pallas kernels for 0%

profile of v22, /device:TPU:0, one launch (start us, length us, event | category | flops | bytes accessed | tf_op | source)
XLA Modules:
  0.0 56.1 jit_solution(2611360761810862334)
XLA Ops:
  0.6 2.9 %shard_map.86 = f32[896,128]{1,0:T(8,128)S(1)} custom-call(f32[7,4096]{1,0:T(8,128)} %fields_hbm.1, s32[1,16384]{1,0:T(1,128)} %bitcast.12, f32[1,16384]{1,0:T(1,128)} %bitcast.13), custom_call_target="tpu_custom_call" | custom-call | tf_op jit(solution)/shard_map/pallas_call | solution.py:137
  3.5 0.0 copy-start
  3.5 0.0 copy-start.1
  3.5 22.1 %all_to_all.10 = f32[32,7,4,128]{3,2,1,0:T(4,128)S(1)} all-to-all(f32[32,7,4,128]{3,2,1,0:T(4,128)S(1)} %bitcast.8), channel_id=1, replica_groups=mesh['src'=4,'tgt'=8] {'src','tgt'}, dimensions={0} | all-to-all | bytes 917504 | tf_op jit(solution)/shard_map/all_to_all | solution.py:479
  25.6 0.0 copy-done
  25.6 0.0 copy-done.1
  25.6 4.0 %shard_map.87 = (f32[7,4,16,128]{3,2,1,0:T(8,128)S(1)}, f32[29,4,128]{2,1,0:T(4,128)S(1)}, f32[28,4,128]{2,1,0:T(4,128)S(1)}) custom-call(f32[896,128]{1,0:T(8,128)S(1)} %bitcast.7, s32[1,16384]{1,0:T(1,128)S(1)} %bitcast.11, f32[4,16,128]{2,1,0:T(8,128)S(1)} %copy-done), custom_call_target="tpu_custom_call" | custom-call | tf_op jit(solution)/shard_map/pallas_call | solution.py:215
  29.6 0.9 %collective-permute-start = (f32[29,4,128]{2,1,0:T(4,128)S(1)}, f32[29,4,128]{2,1,0:T(4,128)S(1)}, u32[]{:S(2)}, u32[]{:S(2)}) collective-permute-start(f32[29,4,128]{2,1,0:T(4,128)S(1)} %get-tuple-element.11), channel_id=1, source_target_pairs={{0,1},{2,3},{4,5},{6,7},{1,0},{3,2},{5,4},{7,6},{8,9},{10,11},{12,... | collective-permute-start | bytes 178184 | tf_op jit(solution)/shard_map/ppermute | solution.py:467
  30.5 0.7 %collective-permute-start.1 = (f32[28,4,128]{2,1,0:T(4,128)S(1)}, f32[28,4,128]{2,1,0:T(4,128)S(1)}, u32[]{:S(2)}, u32[]{:S(2)}) collective-permute-start(f32[28,4,128]{2,1,0:T(4,128)S(1)} %get-tuple-element.12), channel_id=1, source_target_pairs={{1,2},{3,4},{5,6},{2,1},{4,3},{6,5},{9,10},{11,12},{13,14},{10,9},... | collective-permute-start | bytes 172040 | tf_op jit(solution)/shard_map/ppermute | solution.py:467
  31.1 0.0 copy-start.2
  31.2 0.7 %collective-permute-start.3 = (f32[7,4,16,128]{3,2,1,0:T(8,128)S(1)}, f32[7,4,16,128]{3,2,1,0:T(8,128)S(1)}, u32[]{:S(2)}, u32[]{:S(2)}) collective-permute-start(f32[7,4,16,128]{3,2,1,0:T(8,128)S(1)} %get-tuple-element.10.refs_0_), channel_id=1, source_target_pairs={{8,16},{16,8},{9,17},{17,9},{10,18},{18,10},{11,19},{19,11},{12,20... | collective-permute-start | bytes 688136 | tf_op jit(solution)/shard_map/ppermute | solution.py:467
  31.8 2.0 %collective-permute-start.2 = (f32[7,4,16,128]{3,2,1,0:T(8,128)S(1)}, f32[7,4,16,128]{3,2,1,0:T(8,128)S(1)}, u32[]{:S(2)}, u32[]{:S(2)}) collective-permute-start(f32[7,4,16,128]{3,2,1,0:T(8,128)S(1)} %get-tuple-element.10.refs_0_), channel_id=1, source_target_pairs={{0,8},{16,24},{8,0},{24,16},{1,9},{17,25},{9,1},{25,17},{2,10},{18... | collective-permute-start | bytes 688136 | tf_op jit(solution)/shard_map/ppermute | solution.py:467
  33.8 0.0 collective-permute-done.1.odd_ref
  33.8 0.0 collective-permute-done.even_ref
  33.9 0.7 %collective-permute-start.5 = (f32[7,16,128]{2,1,0:T(8,128)S(1)}, f32[7,16,128]{2,1,0:T(8,128)S(1)}, u32[]{:S(2)}, u32[]{:S(2)}) collective-permute-start(f32[7,16,128]{2,1,0:T(8,128)S(1)} %get-tuple-element.15), channel_id=1, source_target_pairs={{8,16},{16,8},{9,17},{17,9},{10,18},{18,10},{11,19},{19,11},{12,20... | collective-permute-start | bytes 172040 | tf_op jit(solution)/shard_map/ppermute | solution.py:467
  34.5 2.3 %collective-permute-start.4 = (f32[7,14,128]{2,1,0:T(8,128)S(1)}, f32[7,14,128]{2,1,0:T(8,128)S(1)}, u32[]{:S(2)}, u32[]{:S(2)}) collective-permute-start(f32[7,14,128]{2,1,0:T(8,128)S(1)} %get-tuple-element.14), channel_id=1, source_target_pairs={{0,8},{16,24},{8,0},{24,16},{1,9},{17,25},{9,1},{25,17},{2,10},{18... | collective-permute-start | bytes 150536 | tf_op jit(solution)/shard_map/ppermute | solution.py:467
  36.8 0.9 %collective-permute-done.4.refs_4_ = f32[7,14,128]{2,1,0:T(8,128)S(1)} collective-permute-done((f32[7,14,128]{2,1,0:T(8,128)S(1)}, f32[7,14,128]{2,1,0:T(8,128)S(1)}, u32[]{:S(2)}, u32[]{:S(2)}) %collective-permute-start.4) | collective-permute-done | bytes 50208 | tf_op jit(solution)/shard_map/ppermute | solution.py:467
  37.7 0.0 collective-permute-done.5.refs_5_
  37.7 0.0 collective-permute-done.3.refs_3_
  37.7 0.0 collective-permute-done.2.refs_2_
  37.7 0.0 copy-done.2
  37.7 2.5 %shard_map.89 = (f32[7,4,16,128]{3,2,1,0:T(8,128)}, f32[192,128]{1,0:T(8,128)S(1)}) custom-call(f32[7,4,16,128]{3,2,1,0:T(8,128)S(1)} %get-tuple-element.10.refs_0_, f32[7,4,8,128]{3,2,1,0:T(8,128)S(1)} %get-tuple-element.13.refs_1_, f32[7,4,16,128]{3,2,1,0:T(8,128)S(1)} %collective-permute-done.2.refs_2_, ...), custom_call_target="tpu_custom_call" | custom-call | tf_op jit(solution)/shard_map/pallas_call | solution.py:412
  40.2 0.0 copy-start.3
  40.2 14.4 %all_to_all.11 = f32[32,3,2,128]{3,2,1,0:T(2,128)S(1)} all-to-all(f32[32,3,2,128]{3,2,1,0:T(2,128)S(1)} %bitcast.10), channel_id=1, replica_groups=mesh['src'=4,'tgt'=8] {'src','tgt'}, dimensions={0} | all-to-all | bytes 196608 | tf_op jit(solution)/shard_map/all_to_all | solution.py:491
  54.6 0.0 copy-done.3
  54.6 1.5 %shard_map.90 = f32[3,8192]{1,0:T(4,128)} custom-call(f32[192,128]{1,0:T(8,128)S(1)} %bitcast.9, s32[1,8192]{1,0:T(1,128)S(1)} %copy-done.3), custom_call_target="tpu_custom_call" | custom-call | tf_op jit(solution)/shard_map/pallas_call | solution.py:455
  (1 shorter events, 0.0 us)
Async XLA Ops:
  3.5 22.1 %copy-start = (f32[4,16,128]{2,1,0:T(8,128)S(1)}, f32[4,16,128]{2,1,0:T(8,128)}, u32[]{:S(2)}) copy-start(f32[4,16,128]{2,1,0:T(8,128)} %refs_6_.1) | copy-start | bytes 98308
  3.5 22.1 %copy-start.1 = (s32[16384]{0:T(1024)S(1)}, s32[16384]{0:T(1024)}, u32[]{:S(2)}) copy-start(s32[16384]{0:T(1024)} %param.10) | copy-start | bytes 196612
  29.6 4.3 %collective-permute-start = (f32[29,4,128]{2,1,0:T(4,128)S(1)}, f32[29,4,128]{2,1,0:T(4,128)S(1)}, u32[]{:S(2)}, u32[]{:S(2)}) collective-permute-start(f32[29,4,128]{2,1,0:T(4,128)S(1)} %get-tuple-element.11), channel_id=1, source_target_pairs={{0,1},{2,3},{4,5},{6,7},{1,0},{3,2},{5,4},{7,6},{8,9},{10,11},{12,... | collective-permute-start | bytes 178184 | tf_op jit(solution)/shard_map/ppermute | solution.py:467
  30.5 3.3 %collective-permute-start.1 = (f32[28,4,128]{2,1,0:T(4,128)S(1)}, f32[28,4,128]{2,1,0:T(4,128)S(1)}, u32[]{:S(2)}, u32[]{:S(2)}) collective-permute-start(f32[28,4,128]{2,1,0:T(4,128)S(1)} %get-tuple-element.12), channel_id=1, source_target_pairs={{1,2},{3,4},{5,6},{2,1},{4,3},{6,5},{9,10},{11,12},{13,14},{10,9},... | collective-permute-start | bytes 172040 | tf_op jit(solution)/shard_map/ppermute | solution.py:467
  31.1 6.6 %copy-start.2 = (s32[1,8192]{1,0:T(1,128)S(1)}, s32[1,8192]{1,0:T(1,128)}, u32[]{:S(2)}) copy-start(s32[1,8192]{1,0:T(1,128)} %refs_7_.1) | copy-start | bytes 98308
  31.2 6.5 %collective-permute-start.3 = (f32[7,4,16,128]{3,2,1,0:T(8,128)S(1)}, f32[7,4,16,128]{3,2,1,0:T(8,128)S(1)}, u32[]{:S(2)}, u32[]{:S(2)}) collective-permute-start(f32[7,4,16,128]{3,2,1,0:T(8,128)S(1)} %get-tuple-element.10.refs_0_), channel_id=1, source_target_pairs={{8,16},{16,8},{9,17},{17,9},{10,18},{18,10},{11,19},{19,11},{12,20... | collective-permute-start | bytes 688136 | tf_op jit(solution)/shard_map/ppermute | solution.py:467
  31.8 5.9 %collective-permute-start.2 = (f32[7,4,16,128]{3,2,1,0:T(8,128)S(1)}, f32[7,4,16,128]{3,2,1,0:T(8,128)S(1)}, u32[]{:S(2)}, u32[]{:S(2)}) collective-permute-start(f32[7,4,16,128]{3,2,1,0:T(8,128)S(1)} %get-tuple-element.10.refs_0_), channel_id=1, source_target_pairs={{0,8},{16,24},{8,0},{24,16},{1,9},{17,25},{9,1},{25,17},{2,10},{18... | collective-permute-start | bytes 688136 | tf_op jit(solution)/shard_map/ppermute | solution.py:467
  33.9 3.8 %collective-permute-start.5 = (f32[7,16,128]{2,1,0:T(8,128)S(1)}, f32[7,16,128]{2,1,0:T(8,128)S(1)}, u32[]{:S(2)}, u32[]{:S(2)}) collective-permute-start(f32[7,16,128]{2,1,0:T(8,128)S(1)} %get-tuple-element.15), channel_id=1, source_target_pairs={{8,16},{16,8},{9,17},{17,9},{10,18},{18,10},{11,19},{19,11},{12,20... | collective-permute-start | bytes 172040 | tf_op jit(solution)/shard_map/ppermute | solution.py:467
  34.5 3.1 %collective-permute-start.4 = (f32[7,14,128]{2,1,0:T(8,128)S(1)}, f32[7,14,128]{2,1,0:T(8,128)S(1)}, u32[]{:S(2)}, u32[]{:S(2)}) collective-permute-start(f32[7,14,128]{2,1,0:T(8,128)S(1)} %get-tuple-element.14), channel_id=1, source_target_pairs={{0,8},{16,24},{8,0},{24,16},{1,9},{17,25},{9,1},{25,17},{2,10},{18... | collective-permute-start | bytes 150536 | tf_op jit(solution)/shard_map/ppermute | solution.py:467
  40.2 14.4 %copy-start.3 = (s32[1,8192]{1,0:T(1,128)S(1)}, s32[1,8192]{1,0:T(1,128)}, u32[]{:S(2)}) copy-start(s32[1,8192]{1,0:T(1,128)} %order_ref.1) | copy-start | bytes 98308

commit v23 on v19

--- a/solution.py
+++ b/solution.py
@@ -14,7 +14,7 @@
 PIECES = 4
 SPAN = 512
 AT_ONCE = 32
-TOGETHER = 8
+TOGETHER = 16
 WIDE = 256
 BF16 = jnp.bfloat16
 F32 = jnp.float32
@@ -71,14 +71,15 @@
     groups = fields_ref.shape[1] // WIDE
     table[...] = jnp.zeros_like(table)
     padded[...] = jnp.zeros_like(padded)
-    for copy in copies:
-        copy.wait()
+    copies[0].wait()
     for g in range(groups):
         table[g * 8 : g * 8 + FIELDS, :] = fields_ref[:, g * WIDE : (g + 1) * WIDE]
     both = jnp.concatenate(halves(table[...]), axis=0)
     rows = groups * 8
     ids = row_ids(WIDE, WIDE).astype(F32).astype(BF16)
     padded[:FIELDS, :] = fields_ref[...]
+    copies[1].wait()
+    copies[2].wait()
 
     def by_matmul(index):
         got = jnp.dot(both, low_onehot(index & (WIDE - 1), ids), preferred_element_type=F32)
@@ -179,9 +180,9 @@
         spread = jnp.concatenate(parts, axis=0)
         return lax.dot_general(spread, onehot, NT, preferred_element_type=F32)
 
-    @pl.loop(0, owners // TOGETHER // 4)
+    @pl.loop(0, owners // TOGETHER // 2)
     def _(n):
-        total[...] += functools.reduce(lambda sums, i: sums + step(n * 4 + i, i == 3), range(1, 4), step(n * 4, False))
+        total[...] += step(n * 2, False) + step(n * 2 + 1, True)
 
     even_ref[FIELDS * hx] = jnp.zeros((ITERS, hz), F32)
     scale = lax.rsqrt(mass_ref[...])

time: 56.5 us -> 56.5 us (level)
  no operation moved by 1% of the time
where the time goes in v23:
time: 56.5 us; the launch traced here: 56.2 us
  blocking collectives  36.4 us (64%)
  Pallas kernels  10.9 us (19%)
  starting transfers between devices  7.13 us (13%)
  waiting for transfers between devices  0.91 us (2%)
  between operations  0.73 us (1%)
    all_to_all x1, blocking collectives, on_device(): lax.all_to_all(values, both, split_axis=0, concat_axis=0, tiled=True)  22.1 us
    all_to_all x1, blocking collectives, on_device(): lax.all_to_all(outgoing, both, split_axis=0, concat_axis=0, tiled=True)  14.4 us
    ppermute x6, starting transfers between devices, swap(): return lax.ppermute(x, axis, pairs + [(j, i) for i, j in pairs])  7.13 us
    pallas_call x1, Pallas kernels, scatter_call(): pl.pallas_call(scatter_kernel, out_shape=(jax.ShapeDtypeStruct((FIELDS, h...  3.99 us
    pallas_call x1, Pallas kernels, gather_call(): pl.pallas_call(gather_kernel, out_shape=jax.ShapeDtypeStruct((rows, 128),...  2.86 us
    pallas_call x1, Pallas kernels, solve_call(): pl.pallas_call(kernel, out_shape=(jax.ShapeDtypeStruct((FIELDS, hx, hy, h...  2.52 us
    pallas_call x1, Pallas kernels, place_call(): pl.pallas_call(place_kernel, out_shape=jax.ShapeDtypeStruct((3, order.sha...  1.54 us
  transfers between devices with their start and end apart: 6, of which 1 were waited for; matrix products, arithmetic and copies ran while one was open for 0% of the time, Pallas kernels for 0%

profile of v23, /device:TPU:0, one launch (start us, length us, event | category | flops | bytes accessed | tf_op | source)
XLA Modules:
  0.0 56.2 jit_solution(10671175566124173247)
XLA Ops:
  0.6 2.9 %shard_map.86 = f32[896,128]{1,0:T(8,128)S(1)} custom-call(f32[7,4096]{1,0:T(8,128)} %fields_hbm.1, s32[1,16384]{1,0:T(1,128)} %bitcast.12, f32[1,16384]{1,0:T(1,128)} %bitcast.13), custom_call_target="tpu_custom_call" | custom-call | tf_op jit(solution)/shard_map/pallas_call | solution.py:130
  3.5 0.0 copy-start
  3.5 0.0 copy-start.1
  3.5 22.1 %all_to_all.10 = f32[32,7,4,128]{3,2,1,0:T(4,128)S(1)} all-to-all(f32[32,7,4,128]{3,2,1,0:T(4,128)S(1)} %bitcast.8), channel_id=1, replica_groups=mesh['src'=4,'tgt'=8] {'src','tgt'}, dimensions={0} | all-to-all | bytes 917504 | tf_op jit(solution)/shard_map/all_to_all | solution.py:471
  25.6 0.0 copy-done
  25.6 0.0 copy-done.1
  25.6 4.0 %shard_map.87 = (f32[7,4,16,128]{3,2,1,0:T(8,128)S(1)}, f32[29,4,128]{2,1,0:T(4,128)S(1)}, f32[28,4,128]{2,1,0:T(4,128)S(1)}) custom-call(f32[896,128]{1,0:T(8,128)S(1)} %bitcast.7, s32[1,16384]{1,0:T(1,128)S(1)} %bitcast.11, f32[4,16,128]{2,1,0:T(8,128)S(1)} %copy-done), custom_call_target="tpu_custom_call" | custom-call | tf_op jit(solution)/shard_map/pallas_call | solution.py:208
  29.6 0.9 %collective-permute-start = (f32[29,4,128]{2,1,0:T(4,128)S(1)}, f32[29,4,128]{2,1,0:T(4,128)S(1)}, u32[]{:S(2)}, u32[]{:S(2)}) collective-permute-start(f32[29,4,128]{2,1,0:T(4,128)S(1)} %get-tuple-element.11), channel_id=1, source_target_pairs={{0,1},{2,3},{4,5},{6,7},{1,0},{3,2},{5,4},{7,6},{8,9},{10,11},{12,... | collective-permute-start | bytes 178184 | tf_op jit(solution)/shard_map/ppermute | solution.py:459
  30.5 0.7 %collective-permute-start.1 = (f32[28,4,128]{2,1,0:T(4,128)S(1)}, f32[28,4,128]{2,1,0:T(4,128)S(1)}, u32[]{:S(2)}, u32[]{:S(2)}) collective-permute-start(f32[28,4,128]{2,1,0:T(4,128)S(1)} %get-tuple-element.12), channel_id=1, source_target_pairs={{1,2},{3,4},{5,6},{2,1},{4,3},{6,5},{9,10},{11,12},{13,14},{10,9},... | collective-permute-start | bytes 172040 | tf_op jit(solution)/shard_map/ppermute | solution.py:459
  31.2 0.0 copy-start.2
  31.2 0.7 %collective-permute-start.3 = (f32[7,4,16,128]{3,2,1,0:T(8,128)S(1)}, f32[7,4,16,128]{3,2,1,0:T(8,128)S(1)}, u32[]{:S(2)}, u32[]{:S(2)}) collective-permute-start(f32[7,4,16,128]{3,2,1,0:T(8,128)S(1)} %get-tuple-element.10.refs_0_), channel_id=1, source_target_pairs={{8,16},{16,8},{9,17},{17,9},{10,18},{18,10},{11,19},{19,11},{12,20... | collective-permute-start | bytes 688136 | tf_op jit(solution)/shard_map/ppermute | solution.py:459
  31.9 2.0 %collective-permute-start.2 = (f32[7,4,16,128]{3,2,1,0:T(8,128)S(1)}, f32[7,4,16,128]{3,2,1,0:T(8,128)S(1)}, u32[]{:S(2)}, u32[]{:S(2)}) collective-permute-start(f32[7,4,16,128]{3,2,1,0:T(8,128)S(1)} %get-tuple-element.10.refs_0_), channel_id=1, source_target_pairs={{0,8},{16,24},{8,0},{24,16},{1,9},{17,25},{9,1},{25,17},{2,10},{18... | collective-permute-start | bytes 688136 | tf_op jit(solution)/shard_map/ppermute | solution.py:459
  33.8 0.0 collective-permute-done.1.odd_ref
  33.8 0.0 collective-permute-done.even_ref
  33.9 0.7 %collective-permute-start.5 = (f32[7,16,128]{2,1,0:T(8,128)S(1)}, f32[7,16,128]{2,1,0:T(8,128)S(1)}, u32[]{:S(2)}, u32[]{:S(2)}) collective-permute-start(f32[7,16,128]{2,1,0:T(8,128)S(1)} %get-tuple-element.15), channel_id=1, source_target_pairs={{8,16},{16,8},{9,17},{17,9},{10,18},{18,10},{11,19},{19,11},{12,20... | collective-permute-start | bytes 172040 | tf_op jit(solution)/shard_map/ppermute | solution.py:459
  34.6 2.2 %collective-permute-start.4 = (f32[7,14,128]{2,1,0:T(8,128)S(1)}, f32[7,14,128]{2,1,0:T(8,128)S(1)}, u32[]{:S(2)}, u32[]{:S(2)}) collective-permute-start(f32[7,14,128]{2,1,0:T(8,128)S(1)} %get-tuple-element.14), channel_id=1, source_target_pairs={{0,8},{16,24},{8,0},{24,16},{1,9},{17,25},{9,1},{25,17},{2,10},{18... | collective-permute-start | bytes 150536 | tf_op jit(solution)/shard_map/ppermute | solution.py:459
  36.8 0.9 %collective-permute-done.4.refs_4_ = f32[7,14,128]{2,1,0:T(8,128)S(1)} collective-permute-done((f32[7,14,128]{2,1,0:T(8,128)S(1)}, f32[7,14,128]{2,1,0:T(8,128)S(1)}, u32[]{:S(2)}, u32[]{:S(2)}) %collective-permute-start.4) | collective-permute-done | bytes 50208 | tf_op jit(solution)/shard_map/ppermute | solution.py:459
  37.7 0.0 collective-permute-done.5.refs_5_
  37.7 0.0 collective-permute-done.3.refs_3_
  37.7 0.0 collective-permute-done.2.refs_2_
  37.7 0.0 copy-done.2
  37.7 2.5 %shard_map.89 = (f32[7,4,16,128]{3,2,1,0:T(8,128)}, f32[192,128]{1,0:T(8,128)S(1)}) custom-call(f32[7,4,16,128]{3,2,1,0:T(8,128)S(1)} %get-tuple-element.10.refs_0_, f32[7,4,8,128]{3,2,1,0:T(8,128)S(1)} %get-tuple-element.13.refs_1_, f32[7,4,16,128]{3,2,1,0:T(8,128)S(1)} %collective-permute-done.2.refs_2_, ...), custom_call_target="tpu_custom_call" | custom-call | tf_op jit(solution)/shard_map/pallas_call | solution.py:404
  40.2 0.0 copy-start.3
  40.3 14.4 %all_to_all.11 = f32[32,3,2,128]{3,2,1,0:T(2,128)S(1)} all-to-all(f32[32,3,2,128]{3,2,1,0:T(2,128)S(1)} %bitcast.10), channel_id=1, replica_groups=mesh['src'=4,'tgt'=8] {'src','tgt'}, dimensions={0} | all-to-all | bytes 196608 | tf_op jit(solution)/shard_map/all_to_all | solution.py:483
  54.6 0.0 copy-done.3
  54.6 1.5 %shard_map.90 = f32[3,8192]{1,0:T(4,128)} custom-call(f32[192,128]{1,0:T(8,128)S(1)} %bitcast.9, s32[1,8192]{1,0:T(1,128)S(1)} %copy-done.3), custom_call_target="tpu_custom_call" | custom-call | tf_op jit(solution)/shard_map/pallas_call | solution.py:447
  (1 shorter events, 0.0 us)
Async XLA Ops:
  3.5 22.1 %copy-start = (f32[4,16,128]{2,1,0:T(8,128)S(1)}, f32[4,16,128]{2,1,0:T(8,128)}, u32[]{:S(2)}) copy-start(f32[4,16,128]{2,1,0:T(8,128)} %refs_6_.1) | copy-start | bytes 98308
  3.5 22.1 %copy-start.1 = (s32[16384]{0:T(1024)S(1)}, s32[16384]{0:T(1024)}, u32[]{:S(2)}) copy-start(s32[16384]{0:T(1024)} %param.10) | copy-start | bytes 196612
  29.6 4.3 %collective-permute-start = (f32[29,4,128]{2,1,0:T(4,128)S(1)}, f32[29,4,128]{2,1,0:T(4,128)S(1)}, u32[]{:S(2)}, u32[]{:S(2)}) collective-permute-start(f32[29,4,128]{2,1,0:T(4,128)S(1)} %get-tuple-element.11), channel_id=1, source_target_pairs={{0,1},{2,3},{4,5},{6,7},{1,0},{3,2},{5,4},{7,6},{8,9},{10,11},{12,... | collective-permute-start | bytes 178184 | tf_op jit(solution)/shard_map/ppermute | solution.py:459
  30.5 3.3 %collective-permute-start.1 = (f32[28,4,128]{2,1,0:T(4,128)S(1)}, f32[28,4,128]{2,1,0:T(4,128)S(1)}, u32[]{:S(2)}, u32[]{:S(2)}) collective-permute-start(f32[28,4,128]{2,1,0:T(4,128)S(1)} %get-tuple-element.12), channel_id=1, source_target_pairs={{1,2},{3,4},{5,6},{2,1},{4,3},{6,5},{9,10},{11,12},{13,14},{10,9},... | collective-permute-start | bytes 172040 | tf_op jit(solution)/shard_map/ppermute | solution.py:459
  31.2 6.5 %copy-start.2 = (s32[1,8192]{1,0:T(1,128)S(1)}, s32[1,8192]{1,0:T(1,128)}, u32[]{:S(2)}) copy-start(s32[1,8192]{1,0:T(1,128)} %refs_7_.1) | copy-start | bytes 98308
  31.2 6.5 %collective-permute-start.3 = (f32[7,4,16,128]{3,2,1,0:T(8,128)S(1)}, f32[7,4,16,128]{3,2,1,0:T(8,128)S(1)}, u32[]{:S(2)}, u32[]{:S(2)}) collective-permute-start(f32[7,4,16,128]{3,2,1,0:T(8,128)S(1)} %get-tuple-element.10.refs_0_), channel_id=1, source_target_pairs={{8,16},{16,8},{9,17},{17,9},{10,18},{18,10},{11,19},{19,11},{12,20... | collective-permute-start | bytes 688136 | tf_op jit(solution)/shard_map/ppermute | solution.py:459
  31.9 5.8 %collective-permute-start.2 = (f32[7,4,16,128]{3,2,1,0:T(8,128)S(1)}, f32[7,4,16,128]{3,2,1,0:T(8,128)S(1)}, u32[]{:S(2)}, u32[]{:S(2)}) collective-permute-start(f32[7,4,16,128]{3,2,1,0:T(8,128)S(1)} %get-tuple-element.10.refs_0_), channel_id=1, source_target_pairs={{0,8},{16,24},{8,0},{24,16},{1,9},{17,25},{9,1},{25,17},{2,10},{18... | collective-permute-start | bytes 688136 | tf_op jit(solution)/shard_map/ppermute | solution.py:459
  33.9 3.8 %collective-permute-start.5 = (f32[7,16,128]{2,1,0:T(8,128)S(1)}, f32[7,16,128]{2,1,0:T(8,128)S(1)}, u32[]{:S(2)}, u32[]{:S(2)}) collective-permute-start(f32[7,16,128]{2,1,0:T(8,128)S(1)} %get-tuple-element.15), channel_id=1, source_target_pairs={{8,16},{16,8},{9,17},{17,9},{10,18},{18,10},{11,19},{19,11},{12,20... | collective-permute-start | bytes 172040 | tf_op jit(solution)/shard_map/ppermute | solution.py:459
  34.6 3.1 %collective-permute-start.4 = (f32[7,14,128]{2,1,0:T(8,128)S(1)}, f32[7,14,128]{2,1,0:T(8,128)S(1)}, u32[]{:S(2)}, u32[]{:S(2)}) collective-permute-start(f32[7,14,128]{2,1,0:T(8,128)S(1)} %get-tuple-element.14), channel_id=1, source_target_pairs={{0,8},{16,24},{8,0},{24,16},{1,9},{17,25},{9,1},{25,17},{2,10},{18... | collective-permute-start | bytes 150536 | tf_op jit(solution)/shard_map/ppermute | solution.py:459
  40.2 14.4 %copy-start.3 = (s32[1,8192]{1,0:T(1,128)S(1)}, s32[1,8192]{1,0:T(1,128)}, u32[]{:S(2)}) copy-start(s32[1,8192]{1,0:T(1,128)} %order_ref.1) | copy-start | bytes 98308
